TPU v7x, 32 devices: a whole 2x2x4 slice. The times are simulated.
32 devices in a mesh: stu: 4 (over y, x), que: 8 (over z, core).
Axes of the slice: x: 2, y: 2, z: 4, core: 2. Of those that a mesh axis runs over, the one named last changes fastest.
Arguments:
- codes: int32 [1024, 1024], P('stu', 'que'), may hold values from 0 to 2
- theta: float32 [1024, 64], P(('stu', 'que')), may hold values from -6 to 6
- disc: float32 [1024, 64], P(('que', 'stu')), may hold values from -0.75 to 0.75
- intercept: float32 [1024], P(('que', 'stu')), may hold values from -5 to 5
Outputs:
- step_abilities: float32 [1024, 64], P(('stu', 'que'))
- step_disc: float32 [1024, 64], P(('que', 'stu'))
- step_intercept: float32 [1024], P(('que', 'stu'))
All inputs are finite; a program needn't handle non-finite values.
Results may differ from a plain program's by a relative error of at most 0.0003.
Values sent between devices are 32-bit elements; how exact they have to be, the bound alone decides.
No kernel may reach another device: no remote copies, remote signals or barrier semaphores. Data moves between devices by JAX's collectives and lax.ppermute only.
A program may use at most 64 MiB of HBM per device.

v0:
```python
import jax
import jax.numpy as jnp
from jax import lax
from jax.sharding import PartitionSpec as P

ITERS = 2


HIGH = lax.Precision.HIGHEST


def matmul(left, right):
    return jnp.dot(left, right, precision=HIGH, preferred_element_type=jnp.float32)


def contract_rows(left, right):
    return lax.dot_general(
        left, right, (((0,), (0,)), ((), ())), precision=HIGH, preferred_element_type=jnp.float32
    )


def local_inner(left, right):
    first = jnp.where(lax.axis_index("que") == 0, jnp.sum(left[0] * right[0]), 0.0)
    second = jnp.where(
        lax.axis_index("stu") == 0, jnp.sum(left[1] * right[1]) + jnp.sum(left[2] * right[2]), 0.0
    )
    return first + second


def squared(residual, precond):
    return lax.psum(local_inner(residual, precond), ("stu", "que"))


def combine(first, factor, second):
    return jax.tree.map(lambda u, v: u + factor * v, first, second)


def shards(codes, theta, disc, intercept):
    theta_rows = lax.all_gather(theta, "que", axis=0, tiled=True)
    disc_cols, icpt_cols = (
        lax.all_gather(disc, "stu", axis=0, tiled=True),
        lax.all_gather(intercept, "stu", axis=0, tiled=True),
    )
    logit = matmul(theta_rows, disc_cols.T) + icpt_cols[None, :]
    prob = jax.nn.sigmoid(logit)
    observed = (codes > 0).astype(jnp.float32)
    correct = (codes == 2).astype(jnp.float32)
    resid = observed * (prob - correct)
    weight = observed * prob * (1.0 - prob)
    row_one = matmul(resid, disc_cols)
    row_two = matmul(weight, disc_cols * disc_cols)
    col_one = contract_rows(resid, theta_rows)
    col_two = contract_rows(weight, theta_rows * theta_rows)
    col_three = jnp.sum(resid, 0)
    col_four = jnp.sum(weight, 0)
    row_sum = lax.psum((row_one, row_two), "que")
    col_sum = lax.psum((col_one, col_two, col_three, col_four), "stu")
    own = (theta_rows, disc_cols, icpt_cols)
    grad = (row_sum[0] + own[0], col_sum[0] + own[1], col_sum[2] + own[2])
    diag = (row_sum[1] + 1.0, col_sum[1] + 1.0, col_sum[3] + 1.0)
    solution = jax.tree.map(jnp.zeros_like, grad)
    residual = jax.tree.map(lambda u: -u, grad)
    precond = jax.tree.map(lambda u, d: u / d, residual, diag)
    direction = precond
    norm_now = squared(residual, precond)
    for step in range(ITERS):
        vt_rows, va_cols, vb_cols = direction
        left = jnp.concatenate([vt_rows, theta_rows], 1)
        right = jnp.concatenate([disc_cols, va_cols], 1)
        change = matmul(left, right.T) + vb_cols[None, :]
        scaled = weight * change
        part_rows = matmul(scaled, disc_cols)
        part_disc = contract_rows(scaled, theta_rows)
        part_icpt = jnp.sum(scaled, 0)
        summed_rows = lax.psum(part_rows, "que")
        summed_disc, summed_icpt = lax.psum((part_disc, part_icpt), "stu")
        image = (summed_rows + direction[0], summed_disc + direction[1], summed_icpt + direction[2])
        alpha = norm_now / lax.psum(local_inner(direction, image), ("stu", "que"))
        solution = combine(solution, alpha, direction)
        residual = combine(residual, -alpha, image)
        if step + 1 < ITERS:
            precond = jax.tree.map(lambda u, d: u / d, residual, diag)
            norm_next = squared(residual, precond)
            ratio = norm_next / norm_now
            direction = combine(precond, ratio, direction)
            norm_now = norm_next
    result = jax.tree.map(lambda u, d: u * jnp.sqrt(d), solution, diag)
    rows_dev = theta.shape[0]
    cols_dev = disc.shape[0]
    row_start = lax.axis_index("que") * rows_dev
    col_start = lax.axis_index("stu") * cols_dev
    step_abilities = lax.dynamic_slice_in_dim(result[0], row_start, rows_dev, 0)
    step_disc = lax.dynamic_slice_in_dim(result[1], col_start, cols_dev, 0)
    step_intercept = lax.dynamic_slice_in_dim(result[2], col_start, cols_dev, 0)
    return (step_abilities, step_disc, step_intercept)


def solution(mesh):
    placed = (P("stu", "que"), P(("stu", "que"), None), P(("que", "stu"), None), P(("que", "stu")))
    return jax.shard_map(
        shards,
        mesh=mesh,
        in_specs=placed,
        out_specs=(P(("stu", "que"), None), P(("que", "stu"), None), P(("que", "stu"))),
        check_vma=False,
    )
```

profile of v0, /device:TPU:0, one launch (start us, length us, event | category | flops | bytes accessed | tf_op | source)
XLA Modules:
  0.0 414.1 jit_solution(9904862962335800048)
XLA Ops:
  9.1 0.9 dynamic-update-slice
  9.9 11.3 %all-reduce = f32[128]{0:T(128)S(1)} all-reduce(f32[128]{0:T(128)S(1)} %dynamic-update-slice), channel_id=1, replica_groups=mesh['stu'=4,'que'=8] {'stu'}, use_global_device_ids=true, to_apply=%add | all-reduce | flops 128 | bytes 1024
  21.3 7.3 %all_gather.10 = f32[128,64]{1,0:T(8,128)S(1)} all-gather(f32[32,64]{1,0:T(8,128)S(1)} %copy-done.3), channel_id=1, replica_groups=mesh['stu'=4,'que'=8] {'stu'}, dimensions={0}, use_global_device_ids=true | all-gather | bytes 40960 | tf_op jit(solution)/shard_map/all_gather | solution.py:41
  28.5 14.5 %all_gather.9 = f32[256,64]{1,0:T(8,128)S(1)} all-gather(f32[32,64]{1,0:T(8,128)} %param.5), channel_id=1, replica_groups=mesh['stu'=4,'que'=8] {'que'}, dimensions={0}, use_global_device_ids=true | all-gather | bytes 73728 | tf_op jit(solution)/shard_map/all_gather | solution.py:39
  43.0 0.9 fusion.33
  43.9 0.9 fusion.31
  44.8 0.9 fusion.13
  45.8 1.0 fusion.30
  46.8 1.0 fusion.8
  48.0 52.3 %all-reduce.15.cloned.1.call-done = (f32[256,64]{0,1:T(8,128)}, f32[256,64]{0,1:T(8,128)}) async-done(((f32[256,64]{0,1:T(8,128)}, f32[256,64]{0,1:T(8,128)}), (f32[256,64]{0,1:T(8,128)}, f32[256,64]{0,1:T(8,128)})) %all-reduce.15.cloned.1.call-update) | async-done | bytes 131088 | tf_op jit(solution)/shard_map/psum | solution.py:56
  100.3 0.9 fusion.28
  101.2 43.1 %all-reduce.17.cloned.1.call-done = (f32[128,64]{0,1:T(8,128)}, f32[128,64]{0,1:T(8,128)}, f32[128]{0:T(128)}, f32[128]{0:T(128)}) async-done(((f32[128,64]{0,1:T(8,128)}, f32[128,64]{0,1:T(8,128)}, f32[128]{0:T(128)}, f32[128]{0:T(128)}), (f32[128,64]{0,1:T(8,128)}, f32[128,64]{0,1:T(8,128)}, f32[128]{0:T(128)}, f32[128]{0:T(128)})) %all-reduce.17.cloned.1.call-update) | async-done | bytes 66576 | tf_op jit(solution)/shard_map/psum | solution.py:57
  144.9 0.8 fusion.27
  146.5 0.9 fusion.36
  147.5 17.4 %all-reduce.4 = (f32[128,64]{0,1:T(8,128)S(1)}, f32[128]{0:T(128)S(1)}) all-reduce(f32[128,64]{0,1:T(8,128)S(1)} %fusion.37, f32[128]{0:T(128)S(1)} %get-tuple-element.45), channel_id=1, replica_groups=mesh['stu'=4,'que'=8] {'stu'}, use_global_device_ids=true, to_apply=%region_14.15 | all-reduce | flops 8320 | bytes 66560 | tf_op jit(solution)/shard_map/psum | solution.py:76
  164.9 0.6 multiply_reduce_fusion.4
  165.5 0.7 multiply_reduce_fusion.7
  168.8 34.2 %all-reduce.11.cloned.1.call-done = f32[256,64]{0,1:T(8,128)} async-done(((f32[256,64]{0,1:T(8,128)}), f32[256,64]{0,1:T(8,128)}) %all-reduce.11.cloned.1.call-update) | async-done | bytes 65552 | tf_op jit(solution)/shard_map/psum | solution.py:75
  202.9 1.5 multiply_reduce_fusion.1
  205.8 39.3 %all-reduce.1 = (f32[]{:T(128)}, f32[]{:T(128)}) all-reduce(f32[]{:T(128)S(6)} %add.175, f32[]{:T(128)S(6)} %add.182), channel_id=1, replica_groups=mesh['stu'=4,'que'=8] {'stu','que'}, use_global_device_ids=true, to_apply=%region_11.12 | all-reduce | flops 2 | bytes 16 | tf_op jit(solution)/shard_map/psum | solution.py:31
  246.4 0.6 multiply_reduce_fusion.3
  247.0 0.6 multiply_reduce_fusion
  248.3 0.6 multiply_reduce_fusion.6
  250.2 40.1 %psum.123 = f32[]{:T(128)} all-reduce(f32[]{:T(128)S(6)} %add.187), channel_id=1, replica_groups=mesh['stu'=4,'que'=8] {'stu','que'}, use_global_device_ids=true, to_apply=%region_23.24 | all-reduce | flops 1 | bytes 8 | tf_op jit(solution)/shard_map/psum | solution.py:31
  292.5 0.9 fusion.38
  293.4 17.6 %all-reduce.3 = (f32[128,64]{0,1:T(8,128)S(1)}, f32[128]{0:T(128)S(1)}) all-reduce(f32[128,64]{0,1:T(8,128)S(1)} %fusion.39, f32[128]{0:T(128)S(1)} %get-tuple-element.47), channel_id=1, replica_groups=mesh['stu'=4,'que'=8] {'stu'}, use_global_device_ids=true, to_apply=%region_26.27 | all-reduce | flops 8320 | bytes 66560 | tf_op jit(solution)/shard_map/psum | solution.py:76
  311.1 0.6 fusion.15
  313.6 49.2 %all-reduce.13.cloned.1.call-done = f32[256,64]{0,1:T(8,128)} async-done(((f32[256,64]{0,1:T(8,128)}), f32[256,64]{0,1:T(8,128)}) %all-reduce.13.cloned.1.call-update) | async-done | bytes 65552 | tf_op jit(solution)/shard_map/psum | solution.py:75
  362.8 1.5 fusion.10
  364.9 39.2 %psum.127 = f32[]{:T(128)} all-reduce(f32[]{:T(128)S(6)} %add.197), channel_id=1, replica_groups=mesh['stu'=4,'que'=8] {'stu','que'}, use_global_device_ids=true, to_apply=%region_31.32 | all-reduce | flops 1 | bytes 8 | tf_op jit(solution)/shard_map/psum | solution.py:78
  406.2 0.7 copy.18
  406.9 0.7 copy.17
  (38 shorter events, 5.2 us)
Async XLA Ops:
  7.2 0.7 copy-start.6
  7.2 14.1 %copy-start.3 = (f32[32,64]{1,0:T(8,128)S(1)}, f32[32,64]{1,0:T(8,128)}, u32[]{:S(2)}) copy-start(f32[32,64]{1,0:T(8,128)} %param.6) | copy-start | bytes 24580
  7.2 35.8 %copy-start.1 = (s32[256,128]{1,0:T(8,128)S(1)}, s32[256,128]{1,0:T(8,128)}, u32[]{:S(2)}) copy-start(s32[256,128]{1,0:T(8,128)} %param.4) | copy-start | bytes 393220
  7.2 93.1 %all-reduce.15.cloned.1.call-start = ((), (), s32[]{:S(2)}) async-start(), calls=%async_computation.2 | async-start | bytes 262144 | tf_op jit(solution)/shard_map/psum | solution.py:56
  45.7 98.5 %all-reduce.17.cloned.1.call-start = ((), (), s32[]{:S(2)}) async-start(), calls=%async_computation.3 | async-start | bytes 133120 | tf_op jit(solution)/shard_map/psum | solution.py:57
  47.8 155.2 %all-reduce.11.cloned.1.call-start = ((), (), s32[]{:S(2)}) async-start(), calls=%async_computation | async-start | bytes 131072 | tf_op jit(solution)/shard_map/psum | solution.py:75
  144.2 0.6 copy-start.4
  144.2 0.7 copy-start.5
  147.4 215.3 %all-reduce.13.cloned.1.call-start = ((), (), s32[]{:S(2)}) async-start(), calls=%async_computation.1 | async-start | bytes 131072 | tf_op jit(solution)/shard_map/psum | solution.py:75
  202.9 43.4 %copy-start.2 = (f32[128,64]{0,1:T(8,128)S(1)}, f32[128,64]{0,1:T(8,128)}, u32[]{:S(2)}) copy-start(f32[128,64]{0,1:T(8,128)} %get-tuple-element.24) | copy-start | bytes 98308
  204.4 42.6 %copy-start = (f32[256,64]{0,1:T(8,128)S(1)}, f32[256,64]{0,1:T(8,128)}, u32[]{:S(2)}) copy-start(f32[256,64]{0,1:T(8,128)} %get-tuple-element.17) | copy-start | bytes 196612
Sparse Core Ops, SparseCore 0:
  45.8 54.4 all-reduce.14
  104.4 39.8 all-reduce.16
  147.5 55.3 all-reduce.10
  311.8 50.8 all-reduce.12
where the time goes:
time: 415 us; the launch traced here: 414 us
  blocking collectives  187 us (45%)
  waiting for transfers between devices  179 us (43%)
  between operations  26.4 us (6%)
  other arithmetic  9.15 us (2%)
  matrix products  8.03 us (2%)
  local copies, waits for them, and re-layouts  4.81 us (1%)
    psum x2, waiting for transfers between devices, shards(): summed_rows = lax.psum(part_rows, 'que')  83.3 us
    psum x2, blocking collectives, squared(): return lax.psum(local_inner(residual, precond), ('stu', 'que'))  79.4 us
    psum x1, waiting for transfers between devices, shards(): row_sum = lax.psum((row_one, row_two), 'que')  52.3 us
    psum x1, waiting for transfers between devices, shards(): col_sum = lax.psum((col_one, col_two, col_three, col_four), 'stu')  43.1 us
    psum x1, blocking collectives, shards(): alpha = norm_now / lax.psum(local_inner(direction, image), ('stu', 'que'))  39.2 us
    psum x2, blocking collectives, shards(): summed_disc, summed_icpt = lax.psum((part_disc, part_icpt), 'stu')  35 us
    all_gather x1, blocking collectives, shards(): theta_rows = lax.all_gather(theta, 'que', axis=0, tiled=True)  14.5 us
    unnamed x1, blocking collectives  11.3 us
  transfers between devices with their start and end apart: 4, of which 4 were waited for; matrix products, arithmetic and copies ran while one was open for 1% of the time, Pallas kernels for 0%

commit v1 on v0

v1 whole, which is shorter than its diff:
```python
import functools

import jax
import jax.numpy as jnp
from jax import lax
from jax.experimental import pallas as pl
from jax.experimental.pallas import tpu as pltpu
from jax.sharding import PartitionSpec as P

HIGH = lax.Precision.HIGHEST
AXES = ("stu", "que")
LANES = 128
BIAS = 8


def dot_nt(left, right):
    return lax.dot_general(
        left, right, (((1,), (1,)), ((), ())), precision=HIGH, preferred_element_type=jnp.float32
    )


def dot_nn(left, right):
    return jnp.dot(left, right, precision=HIGH, preferred_element_type=jnp.float32)


def position():
    que = lax.axis_index("que")
    return lax.rem(que, 2), que // 2, lax.axis_index("stu")


def block_of(side, core, line, plane, group):
    return jnp.where(side == 0, line * 2 + core, core * group + plane)


def low_lanes(shape):
    return lax.broadcasted_iota(jnp.int32, shape, 1) < LANES // 2


def turn(value):
    return pltpu.roll(value, LANES // 2, 1)


def pack(value):
    half = value.shape[0] // 2
    low = low_lanes((half, LANES))
    return jnp.where(low, value[:half], turn(value[half:]))


def bias_rows(lanes, mine):
    return jnp.where(mine, jnp.concatenate([lanes[0:1, :LANES], lanes[0:1, LANES:]], 0), 0.0)


def column(rows):
    wide = jnp.concatenate([rows, jnp.zeros((LANES - 2, LANES), jnp.float32)], 0)
    tall = wide.T
    return jnp.concatenate([tall[:, 0:1], tall[:, 1:2]], 0)


def arrange_kernel(own_ref, peer_ref, out_ref):
    core, _, _ = position()
    cols = own_ref.shape[1]

    @pl.when(core == 0)
    def _():
        out_ref[:, :cols] = own_ref[...].astype(jnp.float32)
        out_ref[:, cols:] = peer_ref[...].astype(jnp.float32)

    @pl.when(core == 1)
    def _():
        out_ref[:cols, :] = peer_ref[...].astype(jnp.float32).T
        out_ref[cols:, :] = own_ref[...].astype(jnp.float32).T


def place(src_ref, dst_ref, side, core, line, plane, group):
    rows = src_ref.shape[0] // (2 * group)
    for k in range(group):
        for j in range(2):
            at = block_of(side, core ^ j, line ^ k, plane ^ k, group) * rows
            first = (k * 2 + j) * rows
            dst_ref[pl.ds(pl.multiple_of(at, rows), rows), :] = src_ref[first : first + rows, :]


def gradient_kernel(group, mine_ref, other_ref, code_ref, sums_ref, left_ref, right_ref, weight_ref, icpt_ref):
    core, line, plane = position()
    place(mine_ref, left_ref, core, core, line, plane, group)
    place(other_ref, right_ref, 1 - core, 1 - core, line, plane, group)
    left = left_ref[...]
    right = right_ref[...]
    prob = 1.0 / (1.0 + jnp.exp(-dot_nt(left, right)))
    code = code_ref[...]
    seen = code > 0.0
    resid = jnp.where(seen, prob - jnp.where(code == 2.0, 1.0, 0.0), 0.0)
    weight = jnp.where(seen, prob * (1.0 - prob), 0.0)
    weight_ref[...] = weight
    rows = left.shape[0]
    grad = dot_nn(resid, right)
    diag = dot_nn(weight, right * right)
    sums_ref[:rows, :] = jnp.where(low_lanes((rows, LANES)), grad, turn(diag))
    ones = jnp.ones((8, rows), jnp.float32)
    mine = core == 1
    sums_ref[rows:, :] = jnp.concatenate(
        [
            bias_rows(dot_nt(ones, resid), mine),
            bias_rows(dot_nt(ones, weight), mine),
            jnp.zeros((BIAS - 4, LANES), jnp.float32),
        ],
        0,
    )
    pick = (lax.broadcasted_iota(jnp.int32, (8, LANES), 1) == LANES // 2).astype(jnp.float32)
    icpt = bias_rows(dot_nt(pick, left), mine)
    icpt_ref[...] = jnp.concatenate([icpt, jnp.zeros((BIAS - 2, LANES), jnp.float32)], 0)


def start_kernel(group, parts, *refs):
    sum_refs, (left_ref, icpt_ref, send_ref, diag_ref, root_ref) = refs[:parts], refs[parts:]
    core, line, plane = position()
    total = sum_refs[0][...]
    for ref in sum_refs[1:]:
        total = total + ref[...]
    rows = left_ref.shape[0]
    half = rows // 2
    low = low_lanes((rows, LANES))
    main = total[:rows]
    diag = jnp.where(low, turn(main) + 1.0, 1.0)
    first = jnp.where(low, -(main + left_ref[...]) / diag, 0.0)
    grad_b = total[rows : rows + 2] + icpt_ref[:2]
    diag_b = total[rows + 2 : rows + 4] + 1.0
    first_b = -grad_b / diag_b
    root_ref[...] = jnp.sqrt(diag)
    send_ref[:half, :] = pack(first)
    send_ref[half : half + BIAS, :] = jnp.concatenate(
        [first_b, jnp.sqrt(diag_b), jnp.zeros((BIAS - 4, LANES), jnp.float32)], 0
    )
    diag_ref[:half, :] = pack(diag)
    diag_ref[half:, :] = jnp.concatenate([diag_b, jnp.ones((BIAS - 2, LANES), jnp.float32)], 0)
    size = rows // (2 * group)
    at = block_of(core, 1 - core, line, plane, group) * size
    send_ref[half + BIAS :, :] = root_ref[pl.ds(pl.multiple_of(at, size), size), :]


def change_of(mine_ref, other_ref, left, right, half):
    low = low_lanes((half, LANES))
    mine = mine_ref[:half, :]
    other = other_ref[:half, :]
    lhs = jnp.concatenate(
        [
            jnp.where(low, mine, turn(left[:half])),
            jnp.where(low, turn(mine), turn(left[half:])),
        ],
        0,
    )
    rhs = jnp.concatenate(
        [
            jnp.where(low, right[:half], turn(other)),
            jnp.where(low, right[half:], other),
        ],
        0,
    )
    lanes = jnp.concatenate([other_ref[half : half + 1, :], other_ref[half + 1 : half + 2, :]], 1)
    return dot_nt(lhs, rhs) + lanes + column(mine_ref[half : half + 2, :])


def image_kernel(mine_ref, other_ref, left_ref, right_ref, weight_ref, sums_ref):
    core, _, _ = position()
    rows = left_ref.shape[0]
    half = rows // 2
    right = right_ref[...]
    scaled = weight_ref[...] * change_of(mine_ref, other_ref, left_ref[...], right, half)
    sums_ref[:half, :] = pack(dot_nn(scaled, right))
    ones = jnp.ones((8, rows), jnp.float32)
    sums_ref[half:, :] = jnp.concatenate(
        [bias_rows(dot_nt(ones, scaled), core == 1), jnp.zeros((BIAS - 2, LANES), jnp.float32)], 0
    )


def second_kernel(group, parts, *refs):
    sum_refs, (send_ref, diag_ref, second_ref, dots_ref) = refs[:parts], refs[parts:]
    total = sum_refs[0][...]
    for ref in sum_refs[1:]:
        total = total + ref[...]
    half = total.shape[0] - BIAS
    row = lax.broadcasted_iota(jnp.int32, total.shape, 0)
    used = row < half + 2
    first = jnp.where(used, send_ref[: half + BIAS, :], 0.0)
    diag = diag_ref[...]
    lift = jnp.where(used, total + first - diag * first, 0.0)
    second = lift / diag
    second_ref[...] = second
    scale = 1.0 / group
    lane = lax.broadcasted_iota(jnp.int32, (8, LANES), 1)
    dots = jnp.zeros((8, LANES), jnp.float32)
    for at, value in enumerate((first * first * diag, first * lift, second * lift, second * second)):
        dots = jnp.where(lane == at, jnp.sum(value) * scale, dots)
    dots_ref[...] = dots


def form_kernel(mine_ref, other_ref, left_ref, right_ref, weight_ref, dots_ref, out_ref):
    half = left_ref.shape[0] // 2
    change = change_of(mine_ref, other_ref, left_ref[...], right_ref[...], half)
    form = 0.5 * jnp.sum(weight_ref[...] * change * change)
    lane = lax.broadcasted_iota(jnp.int32, (1, LANES), 1)
    value = dots_ref[0:1, :] + jnp.where(lane == 3, form, 0.0)
    out_ref[...] = jnp.broadcast_to(value[None], out_ref.shape)


def finish_kernel(
    group, dots_ref, send_ref, peer_ref, second_ref, peer_second_ref, root_ref, theta_ref, disc_ref, icpt_ref
):
    core, line, plane = position()
    dots = jnp.sum(dots_ref[...], axis=0)
    lane = lax.broadcasted_iota(jnp.int32, (1, LANES), 1)
    a, f, h, d = [jnp.sum(jnp.where(lane == at, dots, 0.0), axis=1, keepdims=True) for at in range(4)]
    b = a + f
    e = f + h
    det = b * d - e * e
    s = (a * d - e * f) / det
    t = (f * f - a * h) / det
    rows = root_ref.shape[0]
    half = rows // 2
    size = rows // (2 * group)

    def direction(first_ref, next_ref, at):
        upper = at // group
        rows_at = pl.ds(pl.multiple_of(lax.rem(at, group) * size, size), size)
        value = s * first_ref[rows_at, :] + t * next_ref[rows_at, :]
        return jnp.where(upper == 1, turn(value), value)

    mine_at = block_of(core, core, line, plane, group)
    other_at = block_of(1 - core, core, line, plane, group)
    mine = direction(send_ref, second_ref, mine_at)
    mine = mine * root_ref[pl.ds(pl.multiple_of(mine_at * size, size), size), :]
    other = direction(peer_ref, peer_second_ref, other_at) * peer_ref[half + BIAS :, :]
    theta_ref[...] = jnp.where(core == 0, mine, other)[:, : LANES // 2]
    disc_ref[...] = jnp.where(core == 0, other, mine)[:, : LANES // 2]
    ask = jnp.where(core == 0, peer_ref[half : half + BIAS, :], send_ref[half : half + BIAS, :])
    ask_next = jnp.where(core == 0, peer_second_ref[half : half + 2, :], second_ref[half : half + 2, :])
    bias = (s * ask[0:2] + t * ask_next) * ask[2:4]
    disc_at = jnp.where(core == 0, other_at, mine_at)
    row = jnp.where(disc_at // group == 1, bias[1:2], bias[0:1])
    back = lax.rem(LANES - lax.rem(disc_at, group) * size, LANES)
    icpt_ref[...] = jnp.broadcast_to(pltpu.roll(row, back, 1), icpt_ref.shape)


def call(kernel, shapes, *args):
    out = [jax.ShapeDtypeStruct(shape, jnp.float32) for shape in shapes]
    return pl.pallas_call(
        kernel,
        out_shape=out,
        in_specs=[pl.BlockSpec(memory_space=pltpu.VMEM)] * len(args),
        out_specs=[pl.BlockSpec(memory_space=pltpu.VMEM)] * len(out),
        compiler_params=pltpu.CompilerParams(vmem_limit_bytes=32 * 2**20),
    )(*args)


def swap_cores(value, n_stu, n_que):
    return lax.ppermute(value, AXES, [(i, i ^ 1) for i in range(n_stu * n_que)])


def send_over(value, step, n_stu, n_que):
    pairs = []
    for stu in range(n_stu):
        for que in range(n_que):
            there = (stu, que ^ (2 * step)) if que % 2 == 0 else (stu ^ step, que)
            pairs.append((stu * n_que + que, there[0] * n_que + there[1]))
    return lax.ppermute(value, AXES, pairs)


def stages(group):
    base = 1
    while base < group:
        width = min(4, group // base)
        yield [base * k for k in range(1, width)]
        base *= width


def shards(n_stu, n_que, codes, theta, disc, intercept):
    group = n_stu
    assert n_que == 2 * group
    send = functools.partial(send_over, n_stu=n_stu, n_que=n_que)
    swap = functools.partial(swap_cores, n_stu=n_stu, n_que=n_que)
    size, width = theta.shape
    rows = 2 * group * size
    half = rows // 2
    assert width == LANES // 2 and rows == 2 * LANES
    assert disc.shape == theta.shape and codes.shape == (rows, half)
    core = lax.rem(lax.axis_index("que"), 2)
    pad = jnp.zeros((size, LANES - width - 1), jnp.float32)
    students = jnp.concatenate([theta, jnp.ones((size, 1), jnp.float32), pad], 1)
    questions = jnp.concatenate([disc, intercept[:, None], pad], 1)
    (code,) = call(arrange_kernel, [(rows, rows)], codes, swap(codes))
    kept = jnp.where(core == 0, students, questions)
    given = jnp.where(core == 0, questions, students)
    mine = jnp.concatenate([kept, swap(given)], 0)
    for steps in stages(group):
        for step in steps:
            if step & (step - 1) == 0:
                mine = jnp.concatenate([mine, send(mine, step)], 0)
    other = swap(mine)

    def totals(value):
        parts = [value]
        for number, steps in enumerate(stages(group)):
            if number:
                parts = [functools.reduce(jnp.add, parts)]
            parts = parts + [send(parts[0], step) for step in steps]
        return parts

    sums, left, right, weight, icpt = call(
        functools.partial(gradient_kernel, group),
        [(rows + BIAS, LANES), (rows, LANES), (rows, LANES), (rows, rows), (BIAS, LANES)],
        mine,
        other,
        code,
    )
    parts = totals(sums)
    first, diag, root = call(
        functools.partial(start_kernel, group, len(parts)),
        [(half + BIAS + size, LANES), (half + BIAS, LANES), (rows, LANES)],
        *parts,
        left,
        icpt,
    )
    peer = swap(first)
    (sums,) = call(image_kernel, [(half + BIAS, LANES)], first, peer, left, right, weight)
    parts = totals(sums)
    second, dots = call(
        functools.partial(second_kernel, group, len(parts)),
        [(half + BIAS, LANES), (8, LANES)],
        *parts,
        first,
        diag,
    )
    peer_second = swap(second)
    devices = n_stu * n_que
    (dots,) = call(form_kernel, [(devices, 1, LANES)], second, peer_second, left, right, weight, dots)
    dots = lax.all_to_all(dots, AXES, 0, 0, tiled=True)
    abilities, discs, icpts = call(
        functools.partial(finish_kernel, group),
        [(size, width), (size, width), (8, LANES)],
        dots,
        first,
        peer,
        second,
        peer_second,
        root,
    )
    return abilities, discs, icpts[0, :size]


def solution(mesh):
    placed = (P("stu", "que"), P(("stu", "que"), None), P(("que", "stu"), None), P(("que", "stu")))
    return jax.shard_map(
        functools.partial(shards, mesh.shape["stu"], mesh.shape["que"]),
        mesh=mesh,
        in_specs=placed,
        out_specs=(P(("stu", "que"), None), P(("que", "stu"), None), P(("que", "stu"))),
        check_vma=False,
    )
```

time: 415 us -> 52.5 us (0.13)
  blocking collectives: 187 us -> 11.2 us
  waiting for transfers between devices: 179 us -> 18.3 us
  between operations: 26.4 us -> 0.75 us
  starting transfers between devices: 0.16 us -> 16.2 us
  other arithmetic: 9.15 us -> 0.1 us
  matrix products: 8.03 us -> 0 us
  Pallas kernels: 0 us -> 4.52 us
    psum x4 -> x0, waiting for transfers between devices: 179 us -> none  [the longest x2 83.3 us: shards(): summed_rows = lax.psum(part_rows, 'que')]
    psum x5 -> x0, blocking collectives: 154 us -> none  [the longest x2 79.4 us: squared(): return lax.psum(local_inner(residual, precond), ('stu', 'que'))]
    all_gather x2 -> x0, blocking collectives: 21.7 us -> none  [the longest x1 14.5 us: shards(): theta_rows = lax.all_gather(theta, 'que', axis=0, tiled=True)]
    ppermute x0 -> x13, waiting for transfers between devices: none -> 18.3 us  [the longest x8 13.6 us: send_over(): return lax.ppermute(value, AXES, pairs)]
    ppermute x0 -> x13, starting transfers between devices: none -> 16.2 us  [the longest x8 15.5 us: send_over(): return lax.ppermute(value, AXES, pairs)]
    unnamed x1 -> x0, blocking collectives: 11.3 us -> none
    all_to_all x0 -> x1, blocking collectives: none -> 11.2 us  [shards(): dots = lax.all_to_all(dots, AXES, 0, 0, tiled=True)]
    dot_general x11 -> x0, matrix products: 8.03 us -> none  [the longest x7 5.32 us: matmul(): jnp.dot(left, right, precision=HIGH, preferred_element_type=jnp.float32)]
  transfers between devices with their start and end apart: 4 -> 13, of which waited for: 4 -> 12; matrix products, arithmetic and copies ran while one was open for 1% -> 0% of each run, Pallas kernels for 0% -> 0%
where the time goes in v1:
time: 52.5 us; the launch traced here: 52.3 us
  waiting for transfers between devices  18.3 us (35%)
  starting transfers between devices  16.2 us (31%)
  blocking collectives  11.2 us (21%)
  Pallas kernels  4.52 us (9%)
  local copies, waits for them, and re-layouts  1.24 us (2%)
  between operations  0.75 us (1%)
    ppermute x8, starting transfers between devices, send_over(): return lax.ppermute(value, AXES, pairs)  15.5 us
    ppermute x8, waiting for transfers between devices, send_over(): return lax.ppermute(value, AXES, pairs)  13.6 us
    all_to_all x1, blocking collectives, shards(): dots = lax.all_to_all(dots, AXES, 0, 0, tiled=True)  11.2 us
    ppermute x5, waiting for transfers between devices, swap_cores(): return lax.ppermute(value, AXES, [(i, i ^ 1) for i in range(n_stu * n_que)])  4.64 us
    pallas_call x7, Pallas kernels, call(): pl.pallas_call(kernel, out_shape=out, in_specs=[pl.BlockSpec(memory_space...  4.52 us
  transfers between devices with their start and end apart: 13, of which 12 were waited for; matrix products, arithmetic and copies ran while one was open for 0% of the time, Pallas kernels for 0%

profile of v1, /device:TPU:0, one launch (start us, length us, event | category | flops | bytes accessed | tf_op | source)
XLA Modules:
  0.0 52.3 jit_solution(8126144843623656165)
XLA Ops:
  0.7 0.1 pad.14.clone
  0.8 0.5 copy-done.3
  1.3 0.1 copy.7
  1.4 0.1 fusion.1
  1.5 0.5 collective-permute-start
  1.9 0.8 %collective-permute-done = f32[32,128]{1,0:T(8,128)S(1)} collective-permute-done((f32[32,128]{1,0:T(8,128)S(1)}, f32[32,128]{1,0:T(8,128)S(1)}, u32[]{:S(2)}, u32[]{:S(2)}) %collective-permute-start) | collective-permute-done | bytes 16416 | tf_op jit(solution)/shard_map/ppermute | solution.py:256
  2.8 2.9 %collective-permute-start.1 = (f32[64,128]{1,0:T(8,128)S(1)}, f32[64,128]{1,0:T(8,128)S(1)}, u32[]{:S(2)}, u32[]{:S(2)}) collective-permute-start(f32[64,128]{1,0:T(8,128)S(1)} %pad_maximum_fusion.2), channel_id=1, source_target_pairs={{0,2},{1,9},{2,0},{3,11},{4,6},{5,13},{6,4},{7,15},{8,10},{9,1},{1... | collective-permute-start | bytes 98312 | tf_op jit(solution)/shard_map/ppermute | solution.py:265
  5.7 1.9 %collective-permute-done.1 = f32[64,128]{1,0:T(8,128)S(1)} collective-permute-done((f32[64,128]{1,0:T(8,128)S(1)}, f32[64,128]{1,0:T(8,128)S(1)}, u32[]{:S(2)}, u32[]{:S(2)}) %collective-permute-start.1) | collective-permute-done | bytes 32800 | tf_op jit(solution)/shard_map/ppermute | solution.py:265
  7.6 3.0 %collective-permute-start.2 = (f32[128,128]{1,0:T(8,128)S(1)}, f32[128,128]{1,0:T(8,128)S(1)}, u32[]{:S(2)}, u32[]{:S(2)}) collective-permute-start(f32[128,128]{1,0:T(8,128)S(1)} %pad_maximum_fusion.1), channel_id=1, source_target_pairs={{0,4},{1,17},{2,6},{3,19},{4,0},{5,21},{6,2},{7,23},{8,12},{9,25},... | collective-permute-start | bytes 196616 | tf_op jit(solution)/shard_map/ppermute | solution.py:265
  10.6 2.2 %collective-permute-done.2 = f32[128,128]{1,0:T(8,128)S(1)} collective-permute-done((f32[128,128]{1,0:T(8,128)S(1)}, f32[128,128]{1,0:T(8,128)S(1)}, u32[]{:S(2)}, u32[]{:S(2)}) %collective-permute-start.2) | collective-permute-done | bytes 65568 | tf_op jit(solution)/shard_map/ppermute | solution.py:265
  13.0 1.3 %collective-permute-done.3.other_ref = f32[256,128]{1,0:T(8,128)S(1)} collective-permute-done((f32[256,128]{1,0:T(8,128)S(1)}, f32[256,128]{1,0:T(8,128)S(1)}, u32[]{:S(2)}, u32[]{:S(2)}) %collective-permute-start.3) | collective-permute-done | bytes 131104 | tf_op jit(solution)/shard_map/ppermute | solution.py:256
  14.3 1.6 %shard_map.68 = (f32[264,128]{1,0:T(8,128)S(1)}, f32[256,128]{1,0:T(8,128)S(1)}, f32[256,128]{1,0:T(8,128)S(1)}, f32[256,256]{1,0:T(8,128)S(1)}, f32[8,128]{1,0:T(8,128)S(1)}) custom-call(f32[256,128]{1,0:T(8,128)S(1)} %pad_maximum_fusion.mine_ref, f32[256,128]{1,0:T(8,128)S(1)} %collective-permute-done.3.other_ref, f32[256,256]{1,0:T(8,128)S(1)} %shard_map.67.code_ref), custom_call_target="tpu_custom_call" | custom-call | tf_op jit(solution)/shard_map/pallas_call | solution.py:246
  15.9 4.6 %collective-permute-start.7 = (f32[264,128]{1,0:T(8,128)S(1)}, f32[264,128]{1,0:T(8,128)S(1)}, u32[]{:S(2)}, u32[]{:S(2)}) collective-permute-start(f32[264,128]{1,0:T(8,128)S(1)} %get-tuple-element.16.refs_0_), channel_id=1, source_target_pairs={{0,6},{1,25},{2,4},{3,27},{4,2},{5,29},{6,0},{7,31},{8,14},{9,17},... | collective-permute-start | bytes 405512 | tf_op jit(solution)/shard_map/ppermute | solution.py:265
  20.5 0.6 %collective-permute-start.5 = (f32[264,128]{1,0:T(8,128)S(1)}, f32[264,128]{1,0:T(8,128)S(1)}, u32[]{:S(2)}, u32[]{:S(2)}) collective-permute-start(f32[264,128]{1,0:T(8,128)S(1)} %get-tuple-element.16.refs_0_), channel_id=1, source_target_pairs={{0,2},{1,9},{2,0},{3,11},{4,6},{5,13},{6,4},{7,15},{8,10},{9,1},{1... | collective-permute-start | bytes 405512 | tf_op jit(solution)/shard_map/ppermute | solution.py:265
  21.1 2.5 %collective-permute-done.7.refs_3_ = f32[264,128]{1,0:T(8,128)S(1)} collective-permute-done((f32[264,128]{1,0:T(8,128)S(1)}, f32[264,128]{1,0:T(8,128)S(1)}, u32[]{:S(2)}, u32[]{:S(2)}) %collective-permute-start.7) | collective-permute-done | bytes 135200 | tf_op jit(solution)/shard_map/ppermute | solution.py:265
  23.6 3.2 %collective-permute-done.6.refs_2_ = f32[264,128]{1,0:T(8,128)S(1)} collective-permute-done((f32[264,128]{1,0:T(8,128)S(1)}, f32[264,128]{1,0:T(8,128)S(1)}, u32[]{:S(2)}, u32[]{:S(2)}) %collective-permute-start.6) | collective-permute-done | bytes 135200 | tf_op jit(solution)/shard_map/ppermute | solution.py:265
  26.8 0.2 collective-permute-done.5.refs_1_
  26.9 0.2 shard_map.69
  27.2 1.3 %collective-permute-done.8.other_ref.peer_ref = f32[168,128]{1,0:T(8,128)S(1)} collective-permute-done((f32[168,128]{1,0:T(8,128)S(1)}, f32[168,128]{1,0:T(8,128)S(1)}, u32[]{:S(2)}, u32[]{:S(2)}) %collective-permute-start.8) | collective-permute-done | bytes 86048 | tf_op jit(solution)/shard_map/ppermute | solution.py:256
  28.5 1.1 %shard_map.70.refs_0_ = f32[136,128]{1,0:T(8,128)S(1)} custom-call(f32[168,128]{1,0:T(8,128)S(1)} %get-tuple-element.19.mine_ref.refs_4_.send_ref, f32[168,128]{1,0:T(8,128)S(1)} %collective-permute-done.8.other_ref.peer_ref, f32[256,128]{1,0:T(8,128)S(1)} %get-tuple-element.17.refs_4_.left_ref, f32[256,128]{1,0:T(8,128)S(1)} %get-tuple-element.20.right_ref, ...), custom_call_target="tpu_custom_call" | custom-call | tf_op jit(solution)/shard_map/pallas_call | solution.py:246
  29.6 2.4 %collective-permute-start.11 = (f32[136,128]{1,0:T(8,128)S(1)}, f32[136,128]{1,0:T(8,128)S(1)}, u32[]{:S(2)}, u32[]{:S(2)}) collective-permute-start(f32[136,128]{1,0:T(8,128)S(1)} %shard_map.70.refs_0_), channel_id=1, source_target_pairs={{0,6},{1,25},{2,4},{3,27},{4,2},{5,29},{6,0},{7,31},{8,14},{9,17},... | collective-permute-start | bytes 208904 | tf_op jit(solution)/shard_map/ppermute | solution.py:265
  32.0 0.6 %collective-permute-start.10 = (f32[136,128]{1,0:T(8,128)S(1)}, f32[136,128]{1,0:T(8,128)S(1)}, u32[]{:S(2)}, u32[]{:S(2)}) collective-permute-start(f32[136,128]{1,0:T(8,128)S(1)} %shard_map.70.refs_0_), channel_id=1, source_target_pairs={{0,4},{1,17},{2,6},{3,19},{4,0},{5,21},{6,2},{7,23},{8,12},{9,25},... | collective-permute-start | bytes 208904 | tf_op jit(solution)/shard_map/ppermute | solution.py:265
  32.6 1.4 %collective-permute-start.9 = (f32[136,128]{1,0:T(8,128)S(1)}, f32[136,128]{1,0:T(8,128)S(1)}, u32[]{:S(2)}, u32[]{:S(2)}) collective-permute-start(f32[136,128]{1,0:T(8,128)S(1)} %shard_map.70.refs_0_), channel_id=1, source_target_pairs={{0,2},{1,9},{2,0},{3,11},{4,6},{5,13},{6,4},{7,15},{8,10},{9,1},{1... | collective-permute-start | bytes 208904 | tf_op jit(solution)/shard_map/ppermute | solution.py:265
  34.0 1.7 %collective-permute-done.11.refs_3_ = f32[136,128]{1,0:T(8,128)S(1)} collective-permute-done((f32[136,128]{1,0:T(8,128)S(1)}, f32[136,128]{1,0:T(8,128)S(1)}, u32[]{:S(2)}, u32[]{:S(2)}) %collective-permute-start.11) | collective-permute-done | bytes 69664 | tf_op jit(solution)/shard_map/ppermute | solution.py:265
  35.8 1.6 %collective-permute-done.10.refs_2_ = f32[136,128]{1,0:T(8,128)S(1)} collective-permute-done((f32[136,128]{1,0:T(8,128)S(1)}, f32[136,128]{1,0:T(8,128)S(1)}, u32[]{:S(2)}, u32[]{:S(2)}) %collective-permute-start.10) | collective-permute-done | bytes 69664 | tf_op jit(solution)/shard_map/ppermute | solution.py:265
  37.4 0.3 collective-permute-done.9.refs_1_
  37.7 0.2 shard_map.71
  37.9 1.2 %collective-permute-done.12.other_ref.peer_second_ref = f32[136,128]{1,0:T(8,128)S(1)} collective-permute-done((f32[136,128]{1,0:T(8,128)S(1)}, f32[136,128]{1,0:T(8,128)S(1)}, u32[]{:S(2)}, u32[]{:S(2)}) %collective-permute-start.12) | collective-permute-done | bytes 69664 | tf_op jit(solution)/shard_map/ppermute | solution.py:256
  39.2 0.6 %shard_map.72 = f32[32,1,128]{2,1,0:T(1,128)S(1)} custom-call(f32[136,128]{1,0:T(8,128)S(1)} %get-tuple-element.23.mine_ref.second_ref, f32[136,128]{1,0:T(8,128)S(1)} %collective-permute-done.12.other_ref.peer_second_ref, f32[256,128]{1,0:T(8,128)S(1)} %get-tuple-element.17.refs_4_.left_ref, f32[256,128]{1,0:T(8,128)S(1)} %get-tuple-element.20.right_ref, ...), custom_call_target="tpu_custom_call" | custom-call | tf_op jit(solution)/shard_map/pallas_call | solution.py:246
  39.8 11.2 %all_to_all.5.dots_ref = f32[32,1,128]{2,1,0:T(1,128)S(1)} all-to-all(f32[32,1,128]{2,1,0:T(1,128)S(1)} %shard_map.72), channel_id=1, replica_groups=mesh['stu'=4,'que'=8] {'stu','que'}, dimensions={0} | all-to-all | bytes 32768 | tf_op jit(solution)/shard_map/all_to_all | solution.py:336
  50.9 0.8 %shard_map.73 = (f32[32,64]{1,0:T(8,128)}, f32[32,64]{1,0:T(8,128)}, f32[8,128]{1,0:T(8,128)S(1)}) custom-call(f32[32,1,128]{2,1,0:T(1,128)S(1)} %all_to_all.5.dots_ref, f32[168,128]{1,0:T(8,128)S(1)} %get-tuple-element.19.mine_ref.refs_4_.send_ref, f32[168,128]{1,0:T(8,128)S(1)} %collective-permute-done.8.other_ref.peer_ref, ...), custom_call_target="tpu_custom_call" | custom-call | tf_op jit(solution)/shard_map/pallas_call | solution.py:246
  51.8 0.5 slice_bitcast_fusion
  (19 shorter events, 0.4 us)
Async XLA Ops:
  0.6 0.7 %copy-start.3 = (f32[32]{0:T(128)S(1)}, f32[32]{0:T(128)}, u32[]{:S(2)}) copy-start(f32[32]{0:T(128)} %param.7) | copy-start | bytes 388
  0.6 0.7 %copy-start.2 = (f32[32,64]{1,0:T(8,128)S(1)}, f32[32,64]{1,0:T(8,128)}, u32[]{:S(2)}) copy-start(f32[32,64]{1,0:T(8,128)} %param.6) | copy-start | bytes 24580
  0.7 0.7 %copy-start.1 = (f32[32,64]{1,0:T(8,128)S(1)}, f32[32,64]{1,0:T(8,128)}, u32[]{:S(2)}) copy-start(f32[32,64]{1,0:T(8,128)} %param.5) | copy-start | bytes 24580
  1.4 9.2 %copy-start = (s32[256,128]{1,0:T(8,128)S(1)}, s32[256,128]{1,0:T(8,128)}, u32[]{:S(2)}) copy-start(s32[256,128]{1,0:T(8,128)} %own_ref.1) | copy-start | bytes 393220
  1.5 1.3 %collective-permute-start = (f32[32,128]{1,0:T(8,128)S(1)}, f32[32,128]{1,0:T(8,128)S(1)}, u32[]{:S(2)}, u32[]{:S(2)}) collective-permute-start(f32[32,128]{1,0:T(8,128)S(1)} %get-tuple-element.30), channel_id=1, source_target_pairs={{0,1},{1,0},{2,3},{3,2},{4,5},{5,4},{6,7},{7,6},{8,9},{9,8},{10,11... | collective-permute-start | bytes 49160 | tf_op jit(solution)/shard_map/ppermute | solution.py:256
  2.8 4.8 %collective-permute-start.1 = (f32[64,128]{1,0:T(8,128)S(1)}, f32[64,128]{1,0:T(8,128)S(1)}, u32[]{:S(2)}, u32[]{:S(2)}) collective-permute-start(f32[64,128]{1,0:T(8,128)S(1)} %pad_maximum_fusion.2), channel_id=1, source_target_pairs={{0,2},{1,9},{2,0},{3,11},{4,6},{5,13},{6,4},{7,15},{8,10},{9,1},{1... | collective-permute-start | bytes 98312 | tf_op jit(solution)/shard_map/ppermute | solution.py:265
  7.6 5.3 %collective-permute-start.2 = (f32[128,128]{1,0:T(8,128)S(1)}, f32[128,128]{1,0:T(8,128)S(1)}, u32[]{:S(2)}, u32[]{:S(2)}) collective-permute-start(f32[128,128]{1,0:T(8,128)S(1)} %pad_maximum_fusion.1), channel_id=1, source_target_pairs={{0,4},{1,17},{2,6},{3,19},{4,0},{5,21},{6,2},{7,23},{8,12},{9,25},... | collective-permute-start | bytes 196616 | tf_op jit(solution)/shard_map/ppermute | solution.py:265
  10.6 2.3 %collective-permute-start.4 = (s32[256,128]{1,0:T(8,128)S(1)}, s32[256,128]{1,0:T(8,128)S(1)}, u32[]{:S(2)}, u32[]{:S(2)}) collective-permute-start(s32[256,128]{1,0:T(8,128)S(1)} %copy-done), channel_id=1, source_target_pairs={{0,1},{1,0},{2,3},{3,2},{4,5},{5,4},{6,7},{7,6},{8,9},{9,8},{10,11... | collective-permute-start | bytes 393224 | tf_op jit(solution)/shard_map/ppermute | solution.py:256
  12.9 1.4 %collective-permute-start.3 = (f32[256,128]{1,0:T(8,128)S(1)}, f32[256,128]{1,0:T(8,128)S(1)}, u32[]{:S(2)}, u32[]{:S(2)}) collective-permute-start(f32[256,128]{1,0:T(8,128)S(1)} %pad_maximum_fusion.mine_ref), channel_id=1, source_target_pairs={{0,1},{1,0},{2,3},{3,2},{4,5},{5,4},{6,7},{7,6},{8,9},{9,8},{10,11... | collective-permute-start | bytes 393224 | tf_op jit(solution)/shard_map/ppermute | solution.py:256
  15.9 7.6 %collective-permute-start.7 = (f32[264,128]{1,0:T(8,128)S(1)}, f32[264,128]{1,0:T(8,128)S(1)}, u32[]{:S(2)}, u32[]{:S(2)}) collective-permute-start(f32[264,128]{1,0:T(8,128)S(1)} %get-tuple-element.16.refs_0_), channel_id=1, source_target_pairs={{0,6},{1,25},{2,4},{3,27},{4,2},{5,29},{6,0},{7,31},{8,14},{9,17},... | collective-permute-start | bytes 405512 | tf_op jit(solution)/shard_map/ppermute | solution.py:265
  20.5 6.3 %collective-permute-start.6 = (f32[264,128]{1,0:T(8,128)S(1)}, f32[264,128]{1,0:T(8,128)S(1)}, u32[]{:S(2)}, u32[]{:S(2)}) collective-permute-start(f32[264,128]{1,0:T(8,128)S(1)} %get-tuple-element.16.refs_0_), channel_id=1, source_target_pairs={{0,4},{1,17},{2,6},{3,19},{4,0},{5,21},{6,2},{7,23},{8,12},{9,25},... | collective-permute-start | bytes 405512 | tf_op jit(solution)/shard_map/ppermute | solution.py:265
  20.5 6.5 %collective-permute-start.5 = (f32[264,128]{1,0:T(8,128)S(1)}, f32[264,128]{1,0:T(8,128)S(1)}, u32[]{:S(2)}, u32[]{:S(2)}) collective-permute-start(f32[264,128]{1,0:T(8,128)S(1)} %get-tuple-element.16.refs_0_), channel_id=1, source_target_pairs={{0,2},{1,9},{2,0},{3,11},{4,6},{5,13},{6,4},{7,15},{8,10},{9,1},{1... | collective-permute-start | bytes 405512 | tf_op jit(solution)/shard_map/ppermute | solution.py:265
  27.1 1.3 %collective-permute-start.8 = (f32[168,128]{1,0:T(8,128)S(1)}, f32[168,128]{1,0:T(8,128)S(1)}, u32[]{:S(2)}, u32[]{:S(2)}) collective-permute-start(f32[168,128]{1,0:T(8,128)S(1)} %get-tuple-element.19.mine_ref.refs_4_.send_ref), channel_id=1, source_target_pairs={{0,1},{1,0},{2,3},{3,2},{4,5},{5,4},{6,7},{7,6},{8,9},{9,8},{10,11... | collective-permute-start | bytes 258056 | tf_op jit(solution)/shard_map/ppermute | solution.py:256
  29.6 6.2 %collective-permute-start.11 = (f32[136,128]{1,0:T(8,128)S(1)}, f32[136,128]{1,0:T(8,128)S(1)}, u32[]{:S(2)}, u32[]{:S(2)}) collective-permute-start(f32[136,128]{1,0:T(8,128)S(1)} %shard_map.70.refs_0_), channel_id=1, source_target_pairs={{0,6},{1,25},{2,4},{3,27},{4,2},{5,29},{6,0},{7,31},{8,14},{9,17},... | collective-permute-start | bytes 208904 | tf_op jit(solution)/shard_map/ppermute | solution.py:265
  32.0 5.3 %collective-permute-start.10 = (f32[136,128]{1,0:T(8,128)S(1)}, f32[136,128]{1,0:T(8,128)S(1)}, u32[]{:S(2)}, u32[]{:S(2)}) collective-permute-start(f32[136,128]{1,0:T(8,128)S(1)} %shard_map.70.refs_0_), channel_id=1, source_target_pairs={{0,4},{1,17},{2,6},{3,19},{4,0},{5,21},{6,2},{7,23},{8,12},{9,25},... | collective-permute-start | bytes 208904 | tf_op jit(solution)/shard_map/ppermute | solution.py:265
  32.6 5.1 %collective-permute-start.9 = (f32[136,128]{1,0:T(8,128)S(1)}, f32[136,128]{1,0:T(8,128)S(1)}, u32[]{:S(2)}, u32[]{:S(2)}) collective-permute-start(f32[136,128]{1,0:T(8,128)S(1)} %shard_map.70.refs_0_), channel_id=1, source_target_pairs={{0,2},{1,9},{2,0},{3,11},{4,6},{5,13},{6,4},{7,15},{8,10},{9,1},{1... | collective-permute-start | bytes 208904 | tf_op jit(solution)/shard_map/ppermute | solution.py:265
  37.8 1.3 %collective-permute-start.12 = (f32[136,128]{1,0:T(8,128)S(1)}, f32[136,128]{1,0:T(8,128)S(1)}, u32[]{:S(2)}, u32[]{:S(2)}) collective-permute-start(f32[136,128]{1,0:T(8,128)S(1)} %get-tuple-element.23.mine_ref.second_ref), channel_id=1, source_target_pairs={{0,1},{1,0},{2,3},{3,2},{4,5},{5,4},{6,7},{7,6},{8,9},{9,8},{10,11... | collective-permute-start | bytes 208904 | tf_op jit(solution)/shard_map/ppermute | solution.py:256

commit v2 on v1

--- a/solution.py
+++ b/solution.py
@@ -292,9 +292,7 @@
     given = jnp.where(core == 0, questions, students)
     mine = jnp.concatenate([kept, swap(given)], 0)
     for steps in stages(group):
-        for step in steps:
-            if step & (step - 1) == 0:
-                mine = jnp.concatenate([mine, send(mine, step)], 0)
+        mine = jnp.concatenate([mine] + [send(mine, step) for step in steps], 0)
     other = swap(mine)
 
     def totals(value):

time: 52.5 us -> 52 us (level)
  starting transfers between devices: 16.2 us -> 15.1 us
  waiting for transfers between devices: 18.3 us -> 17.5 us
  other arithmetic: 0.1 us -> 0.8 us
    ppermute x8 -> x9, starting transfers between devices: 15.5 us -> 14.4 us  [send_over(): return lax.ppermute(value, AXES, pairs)]
    unnamed x0 -> x1, other arithmetic: none -> 0.8 us
    broadcast_in_dim x1, local copies, waits for them, and re-layouts: 0.09 us -> 0.74 us  [shards(): questions = jnp.concatenate([disc, intercept[:, None], pad], 1)]
    ppermute x8 -> x9, waiting for transfers between devices: 13.6 us -> 13 us  [send_over(): return lax.ppermute(value, AXES, pairs)]
  transfers between devices with their start and end apart: 13 -> 14, of which waited for: 12 -> 10; matrix products, arithmetic and copies ran while one was open for 0% -> 0% of each run, Pallas kernels for 0% -> 0%
where the time goes in v2:
time: 52 us; the launch traced here: 51.8 us
  waiting for transfers between devices  17.5 us (34%)
  starting transfers between devices  15.1 us (29%)
  blocking collectives  11.6 us (22%)
  Pallas kernels  4.53 us (9%)
  local copies, waits for them, and re-layouts  1.42 us (3%)
  other arithmetic  0.8 us (2%)
  between operations  0.74 us (1%)
    ppermute x9, starting transfers between devices, send_over(): return lax.ppermute(value, AXES, pairs)  14.4 us
    ppermute x9, waiting for transfers between devices, send_over(): return lax.ppermute(value, AXES, pairs)  13 us
    all_to_all x1, blocking collectives, shards(): dots = lax.all_to_all(dots, AXES, 0, 0, tiled=True)  11.6 us
    ppermute x5, waiting for transfers between devices, swap_cores(): return lax.ppermute(value, AXES, [(i, i ^ 1) for i in range(n_stu * n_que)])  4.55 us
    pallas_call x7, Pallas kernels, call(): pl.pallas_call(kernel, out_shape=out, in_specs=[pl.BlockSpec(memory_space...  4.53 us
  transfers between devices with their start and end apart: 14, of which 10 were waited for; matrix products, arithmetic and copies ran while one was open for 0% of the time, Pallas kernels for 0%

profile of v2, /device:TPU:0, one launch (start us, length us, event | category | flops | bytes accessed | tf_op | source)
XLA Modules:
  0.0 51.8 jit_solution(15683315920818046761)
XLA Ops:
  0.7 0.1 pad.6.clone
  0.7 0.1 pad.7.clone
  0.8 0.7 %copy.7 = f32[32,1]{1,0:T(8,128)S(1)} copy(f32[32,1]{0,1:T(1,128)} %bitcast.4) | data formatting | bytes 256 | tf_op jit(solution)/shard_map/broadcast_in_dim | solution.py:289
  1.5 0.8 %constant_dynamic-update-slice_fusion.4 = (f32[256,128]{1,0:T(8,128)S(1)}, f32[32,128]{1,0:T(8,128)S(1)}, f32[32,128]{1,0:T(8,128)S(1)}) fusion(f32[32,1]{1,0:T(8,128)S(1)} %copy.7, f32[32,64]{1,0:T(8,128)S(1)} %copy-done.1, f32[128]{0:T(128)S(1)} %pad.7.clone, f32[128]{0:T(128)S(1)} %pad.6.clone, f32[32,64]{1,0:T(8,128)} %param.5, pred[]{:T(512)S(6)} %eq.4), kind=kLoop, calls=%fused_computation.9 | loop fusion | flops 24575 | bytes 66689
  2.3 0.5 collective-permute-start
  2.8 0.1 collective-permute-start.5
  2.9 0.8 %collective-permute-done = f32[32,128]{1,0:T(8,128)S(1)} collective-permute-done((f32[32,128]{1,0:T(8,128)S(1)}, f32[32,128]{1,0:T(8,128)S(1)}, u32[]{:S(2)}, u32[]{:S(2)}) %collective-permute-start) | collective-permute-done | bytes 16416 | tf_op jit(solution)/shard_map/ppermute | solution.py:256
  3.6 4.9 %collective-permute-start.3 = (f32[64,128]{1,0:T(8,128)S(1)}, f32[64,128]{1,0:T(8,128)S(1)}, u32[]{:S(2)}, u32[]{:S(2)}) collective-permute-start(f32[64,128]{1,0:T(8,128)S(1)} %pad_maximum_fusion), channel_id=1, source_target_pairs={{0,6},{1,25},{2,4},{3,27},{4,2},{5,29},{6,0},{7,31},{8,14},{9,17},... | collective-permute-start | bytes 98312 | tf_op jit(solution)/shard_map/ppermute | solution.py:265
  8.6 0.6 %collective-permute-start.1 = (f32[64,128]{1,0:T(8,128)S(1)}, f32[64,128]{1,0:T(8,128)S(1)}, u32[]{:S(2)}, u32[]{:S(2)}) collective-permute-start(f32[64,128]{1,0:T(8,128)S(1)} %pad_maximum_fusion), channel_id=1, source_target_pairs={{0,2},{1,9},{2,0},{3,11},{4,6},{5,13},{6,4},{7,15},{8,10},{9,1},{1... | collective-permute-start | bytes 98312 | tf_op jit(solution)/shard_map/ppermute | solution.py:265
  9.2 3.3 %collective-permute-done.1 = f32[64,128]{1,0:T(8,128)S(1)} collective-permute-done((f32[64,128]{1,0:T(8,128)S(1)}, f32[64,128]{1,0:T(8,128)S(1)}, u32[]{:S(2)}, u32[]{:S(2)}) %collective-permute-start.1) | collective-permute-done | bytes 32800 | tf_op jit(solution)/shard_map/ppermute | solution.py:265
  12.5 0.9 %collective-permute-done.2 = f32[64,128]{1,0:T(8,128)S(1)} collective-permute-done((f32[64,128]{1,0:T(8,128)S(1)}, f32[64,128]{1,0:T(8,128)S(1)}, u32[]{:S(2)}, u32[]{:S(2)}) %collective-permute-start.2) | collective-permute-done | bytes 32800 | tf_op jit(solution)/shard_map/ppermute | solution.py:265
  13.4 0.1 collective-permute-start.4
  13.6 1.3 %collective-permute-done.4.other_ref = f32[256,128]{1,0:T(8,128)S(1)} collective-permute-done((f32[256,128]{1,0:T(8,128)S(1)}, f32[256,128]{1,0:T(8,128)S(1)}, u32[]{:S(2)}, u32[]{:S(2)}) %collective-permute-start.4) | collective-permute-done | bytes 131104 | tf_op jit(solution)/shard_map/ppermute | solution.py:256
  14.8 1.6 %shard_map.68 = (f32[264,128]{1,0:T(8,128)S(1)}, f32[256,128]{1,0:T(8,128)S(1)}, f32[256,128]{1,0:T(8,128)S(1)}, f32[256,256]{1,0:T(8,128)S(1)}, f32[8,128]{1,0:T(8,128)S(1)}) custom-call(f32[256,128]{1,0:T(8,128)S(1)} %constant_dynamic-update-slice_fusion.mine_ref, f32[256,128]{1,0:T(8,128)S(1)} %collective-permute-done.4.other_ref, ...), custom_call_target="tpu_custom_call" | custom-call | tf_op jit(solution)/shard_map/pallas_call | solution.py:246
  16.5 1.5 %collective-permute-start.8 = (f32[264,128]{1,0:T(8,128)S(1)}, f32[264,128]{1,0:T(8,128)S(1)}, u32[]{:S(2)}, u32[]{:S(2)}) collective-permute-start(f32[264,128]{1,0:T(8,128)S(1)} %get-tuple-element.16.refs_0_), channel_id=1, source_target_pairs={{0,6},{1,25},{2,4},{3,27},{4,2},{5,29},{6,0},{7,31},{8,14},{9,17},... | collective-permute-start | bytes 405512 | tf_op jit(solution)/shard_map/ppermute | solution.py:265
  18.0 0.6 %collective-permute-start.7 = (f32[264,128]{1,0:T(8,128)S(1)}, f32[264,128]{1,0:T(8,128)S(1)}, u32[]{:S(2)}, u32[]{:S(2)}) collective-permute-start(f32[264,128]{1,0:T(8,128)S(1)} %get-tuple-element.16.refs_0_), channel_id=1, source_target_pairs={{0,4},{1,17},{2,6},{3,19},{4,0},{5,21},{6,2},{7,23},{8,12},{9,25},... | collective-permute-start | bytes 405512 | tf_op jit(solution)/shard_map/ppermute | solution.py:265
  18.6 2.3 %collective-permute-start.6 = (f32[264,128]{1,0:T(8,128)S(1)}, f32[264,128]{1,0:T(8,128)S(1)}, u32[]{:S(2)}, u32[]{:S(2)}) collective-permute-start(f32[264,128]{1,0:T(8,128)S(1)} %get-tuple-element.16.refs_0_), channel_id=1, source_target_pairs={{0,2},{1,9},{2,0},{3,11},{4,6},{5,13},{6,4},{7,15},{8,10},{9,1},{1... | collective-permute-start | bytes 405512 | tf_op jit(solution)/shard_map/ppermute | solution.py:265
  20.9 2.6 %collective-permute-done.8.refs_3_ = f32[264,128]{1,0:T(8,128)S(1)} collective-permute-done((f32[264,128]{1,0:T(8,128)S(1)}, f32[264,128]{1,0:T(8,128)S(1)}, u32[]{:S(2)}, u32[]{:S(2)}) %collective-permute-start.8) | collective-permute-done | bytes 135200 | tf_op jit(solution)/shard_map/ppermute | solution.py:265
  23.5 2.7 %collective-permute-done.7.refs_2_ = f32[264,128]{1,0:T(8,128)S(1)} collective-permute-done((f32[264,128]{1,0:T(8,128)S(1)}, f32[264,128]{1,0:T(8,128)S(1)}, u32[]{:S(2)}, u32[]{:S(2)}) %collective-permute-start.7) | collective-permute-done | bytes 135200 | tf_op jit(solution)/shard_map/ppermute | solution.py:265
  26.2 0.2 shard_map.69
  26.5 1.3 %collective-permute-done.9.other_ref.peer_ref = f32[168,128]{1,0:T(8,128)S(1)} collective-permute-done((f32[168,128]{1,0:T(8,128)S(1)}, f32[168,128]{1,0:T(8,128)S(1)}, u32[]{:S(2)}, u32[]{:S(2)}) %collective-permute-start.9) | collective-permute-done | bytes 86048 | tf_op jit(solution)/shard_map/ppermute | solution.py:256
  27.8 1.1 %shard_map.70.refs_0_ = f32[136,128]{1,0:T(8,128)S(1)} custom-call(f32[168,128]{1,0:T(8,128)S(1)} %get-tuple-element.19.mine_ref.refs_4_.send_ref, f32[168,128]{1,0:T(8,128)S(1)} %collective-permute-done.9.other_ref.peer_ref, f32[256,128]{1,0:T(8,128)S(1)} %get-tuple-element.17.refs_4_.left_ref, f32[256,128]{1,0:T(8,128)S(1)} %get-tuple-element.20.right_ref, ...), custom_call_target="tpu_custom_call" | custom-call | tf_op jit(solution)/shard_map/pallas_call | solution.py:246
  28.8 2.7 %collective-permute-start.12 = (f32[136,128]{1,0:T(8,128)S(1)}, f32[136,128]{1,0:T(8,128)S(1)}, u32[]{:S(2)}, u32[]{:S(2)}) collective-permute-start(f32[136,128]{1,0:T(8,128)S(1)} %shard_map.70.refs_0_), channel_id=1, source_target_pairs={{0,6},{1,25},{2,4},{3,27},{4,2},{5,29},{6,0},{7,31},{8,14},{9,17},... | collective-permute-start | bytes 208904 | tf_op jit(solution)/shard_map/ppermute | solution.py:265
  31.5 1.8 %collective-permute-start.10 = (f32[136,128]{1,0:T(8,128)S(1)}, f32[136,128]{1,0:T(8,128)S(1)}, u32[]{:S(2)}, u32[]{:S(2)}) collective-permute-start(f32[136,128]{1,0:T(8,128)S(1)} %shard_map.70.refs_0_), channel_id=1, source_target_pairs={{0,2},{1,9},{2,0},{3,11},{4,6},{5,13},{6,4},{7,15},{8,10},{9,1},{1... | collective-permute-start | bytes 208904 | tf_op jit(solution)/shard_map/ppermute | solution.py:265
  33.3 1.7 %collective-permute-done.12.refs_3_ = f32[136,128]{1,0:T(8,128)S(1)} collective-permute-done((f32[136,128]{1,0:T(8,128)S(1)}, f32[136,128]{1,0:T(8,128)S(1)}, u32[]{:S(2)}, u32[]{:S(2)}) %collective-permute-start.12) | collective-permute-done | bytes 69664 | tf_op jit(solution)/shard_map/ppermute | solution.py:265
  35.0 1.7 %collective-permute-done.11.refs_2_ = f32[136,128]{1,0:T(8,128)S(1)} collective-permute-done((f32[136,128]{1,0:T(8,128)S(1)}, f32[136,128]{1,0:T(8,128)S(1)}, u32[]{:S(2)}, u32[]{:S(2)}) %collective-permute-start.11) | collective-permute-done | bytes 69664 | tf_op jit(solution)/shard_map/ppermute | solution.py:265
  36.7 0.2 shard_map.71
  37.0 1.2 %collective-permute-done.13.other_ref.peer_second_ref = f32[136,128]{1,0:T(8,128)S(1)} collective-permute-done((f32[136,128]{1,0:T(8,128)S(1)}, f32[136,128]{1,0:T(8,128)S(1)}, u32[]{:S(2)}, u32[]{:S(2)}) %collective-permute-start.13) | collective-permute-done | bytes 69664 | tf_op jit(solution)/shard_map/ppermute | solution.py:256
  38.2 0.6 %shard_map.72 = f32[32,1,128]{2,1,0:T(1,128)S(1)} custom-call(f32[136,128]{1,0:T(8,128)S(1)} %get-tuple-element.23.mine_ref.second_ref, f32[136,128]{1,0:T(8,128)S(1)} %collective-permute-done.13.other_ref.peer_second_ref, f32[256,128]{1,0:T(8,128)S(1)} %get-tuple-element.17.refs_4_.left_ref, f32[256,128]{1,0:T(8,128)S(1)} %get-tuple-element.20.right_ref, ...), custom_call_target="tpu_custom_call" | custom-call | tf_op jit(solution)/shard_map/pallas_call | solution.py:246
  38.8 11.6 %all_to_all.5.dots_ref = f32[32,1,128]{2,1,0:T(1,128)S(1)} all-to-all(f32[32,1,128]{2,1,0:T(1,128)S(1)} %shard_map.72), channel_id=1, replica_groups=mesh['stu'=4,'que'=8] {'stu','que'}, dimensions={0} | all-to-all | bytes 32768 | tf_op jit(solution)/shard_map/all_to_all | solution.py:334
  50.4 0.8 %shard_map.73 = (f32[32,64]{1,0:T(8,128)}, f32[32,64]{1,0:T(8,128)}, f32[8,128]{1,0:T(8,128)S(1)}) custom-call(f32[32,1,128]{2,1,0:T(1,128)S(1)} %all_to_all.5.dots_ref, f32[168,128]{1,0:T(8,128)S(1)} %get-tuple-element.19.mine_ref.refs_4_.send_ref, f32[168,128]{1,0:T(8,128)S(1)} %collective-permute-done.9.other_ref.peer_ref, ...), custom_call_target="tpu_custom_call" | custom-call | tf_op jit(solution)/shard_map/pallas_call | solution.py:246
  51.3 0.5 slice_bitcast_fusion
  (19 shorter events, 0.2 us)
Async XLA Ops:
  0.6 0.9 %copy-start.1 = (f32[32,64]{1,0:T(8,128)S(1)}, f32[32,64]{1,0:T(8,128)}, u32[]{:S(2)}) copy-start(f32[32,64]{1,0:T(8,128)} %param.6) | copy-start | bytes 24580
  0.6 2.2 %copy-start = (s32[256,128]{1,0:T(8,128)S(1)}, s32[256,128]{1,0:T(8,128)}, u32[]{:S(2)}) copy-start(s32[256,128]{1,0:T(8,128)} %own_ref.1) | copy-start | bytes 393220
  2.3 1.3 %collective-permute-start = (f32[32,128]{1,0:T(8,128)S(1)}, f32[32,128]{1,0:T(8,128)S(1)}, u32[]{:S(2)}, u32[]{:S(2)}) collective-permute-start(f32[32,128]{1,0:T(8,128)S(1)} %get-tuple-element.31), channel_id=1, source_target_pairs={{0,1},{1,0},{2,3},{3,2},{4,5},{5,4},{6,7},{7,6},{8,9},{9,8},{10,11... | collective-permute-start | bytes 49160 | tf_op jit(solution)/shard_map/ppermute | solution.py:256
  2.8 10.7 %collective-permute-start.5 = (s32[256,128]{1,0:T(8,128)S(1)}, s32[256,128]{1,0:T(8,128)S(1)}, u32[]{:S(2)}, u32[]{:S(2)}) collective-permute-start(s32[256,128]{1,0:T(8,128)S(1)} %copy-done), channel_id=1, source_target_pairs={{0,1},{1,0},{2,3},{3,2},{4,5},{5,4},{6,7},{7,6},{8,9},{9,8},{10,11... | collective-permute-start | bytes 393224 | tf_op jit(solution)/shard_map/ppermute | solution.py:256
  3.6 9.8 %collective-permute-start.3 = (f32[64,128]{1,0:T(8,128)S(1)}, f32[64,128]{1,0:T(8,128)S(1)}, u32[]{:S(2)}, u32[]{:S(2)}) collective-permute-start(f32[64,128]{1,0:T(8,128)S(1)} %pad_maximum_fusion), channel_id=1, source_target_pairs={{0,6},{1,25},{2,4},{3,27},{4,2},{5,29},{6,0},{7,31},{8,14},{9,17},... | collective-permute-start | bytes 98312 | tf_op jit(solution)/shard_map/ppermute | solution.py:265
  8.6 4.8 %collective-permute-start.2 = (f32[64,128]{1,0:T(8,128)S(1)}, f32[64,128]{1,0:T(8,128)S(1)}, u32[]{:S(2)}, u32[]{:S(2)}) collective-permute-start(f32[64,128]{1,0:T(8,128)S(1)} %pad_maximum_fusion), channel_id=1, source_target_pairs={{0,4},{1,17},{2,6},{3,19},{4,0},{5,21},{6,2},{7,23},{8,12},{9,25},... | collective-permute-start | bytes 98312 | tf_op jit(solution)/shard_map/ppermute | solution.py:265
  8.6 3.9 %collective-permute-start.1 = (f32[64,128]{1,0:T(8,128)S(1)}, f32[64,128]{1,0:T(8,128)S(1)}, u32[]{:S(2)}, u32[]{:S(2)}) collective-permute-start(f32[64,128]{1,0:T(8,128)S(1)} %pad_maximum_fusion), channel_id=1, source_target_pairs={{0,2},{1,9},{2,0},{3,11},{4,6},{5,13},{6,4},{7,15},{8,10},{9,1},{1... | collective-permute-start | bytes 98312 | tf_op jit(solution)/shard_map/ppermute | solution.py:265
  13.4 1.4 %collective-permute-start.4 = (f32[256,128]{1,0:T(8,128)S(1)}, f32[256,128]{1,0:T(8,128)S(1)}, u32[]{:S(2)}, u32[]{:S(2)}) collective-permute-start(f32[256,128]{1,0:T(8,128)S(1)} %constant_dynamic-update-slice_fusion.mine_ref), channel_id=1, source_target_pairs={{0,1},{1,0},{2,3},{3,2},{4,5},{5,4},{6,7},{7,6},{8,9},{9,8},{10,11... | collective-permute-start | bytes 393224 | tf_op jit(solution)/shard_map/ppermute | solution.py:256
  16.5 7.0 %collective-permute-start.8 = (f32[264,128]{1,0:T(8,128)S(1)}, f32[264,128]{1,0:T(8,128)S(1)}, u32[]{:S(2)}, u32[]{:S(2)}) collective-permute-start(f32[264,128]{1,0:T(8,128)S(1)} %get-tuple-element.16.refs_0_), channel_id=1, source_target_pairs={{0,6},{1,25},{2,4},{3,27},{4,2},{5,29},{6,0},{7,31},{8,14},{9,17},... | collective-permute-start | bytes 405512 | tf_op jit(solution)/shard_map/ppermute | solution.py:265
  18.0 8.2 %collective-permute-start.7 = (f32[264,128]{1,0:T(8,128)S(1)}, f32[264,128]{1,0:T(8,128)S(1)}, u32[]{:S(2)}, u32[]{:S(2)}) collective-permute-start(f32[264,128]{1,0:T(8,128)S(1)} %get-tuple-element.16.refs_0_), channel_id=1, source_target_pairs={{0,4},{1,17},{2,6},{3,19},{4,0},{5,21},{6,2},{7,23},{8,12},{9,25},... | collective-permute-start | bytes 405512 | tf_op jit(solution)/shard_map/ppermute | solution.py:265
  18.6 7.6 %collective-permute-start.6 = (f32[264,128]{1,0:T(8,128)S(1)}, f32[264,128]{1,0:T(8,128)S(1)}, u32[]{:S(2)}, u32[]{:S(2)}) collective-permute-start(f32[264,128]{1,0:T(8,128)S(1)} %get-tuple-element.16.refs_0_), channel_id=1, source_target_pairs={{0,2},{1,9},{2,0},{3,11},{4,6},{5,13},{6,4},{7,15},{8,10},{9,1},{1... | collective-permute-start | bytes 405512 | tf_op jit(solution)/shard_map/ppermute | solution.py:265
  26.4 1.3 %collective-permute-start.9 = (f32[168,128]{1,0:T(8,128)S(1)}, f32[168,128]{1,0:T(8,128)S(1)}, u32[]{:S(2)}, u32[]{:S(2)}) collective-permute-start(f32[168,128]{1,0:T(8,128)S(1)} %get-tuple-element.19.mine_ref.refs_4_.send_ref), channel_id=1, source_target_pairs={{0,1},{1,0},{2,3},{3,2},{4,5},{5,4},{6,7},{7,6},{8,9},{9,8},{10,11... | collective-permute-start | bytes 258056 | tf_op jit(solution)/shard_map/ppermute | solution.py:256
  28.8 6.2 %collective-permute-start.12 = (f32[136,128]{1,0:T(8,128)S(1)}, f32[136,128]{1,0:T(8,128)S(1)}, u32[]{:S(2)}, u32[]{:S(2)}) collective-permute-start(f32[136,128]{1,0:T(8,128)S(1)} %shard_map.70.refs_0_), channel_id=1, source_target_pairs={{0,6},{1,25},{2,4},{3,27},{4,2},{5,29},{6,0},{7,31},{8,14},{9,17},... | collective-permute-start | bytes 208904 | tf_op jit(solution)/shard_map/ppermute | solution.py:265
  31.5 5.2 %collective-permute-start.11 = (f32[136,128]{1,0:T(8,128)S(1)}, f32[136,128]{1,0:T(8,128)S(1)}, u32[]{:S(2)}, u32[]{:S(2)}) collective-permute-start(f32[136,128]{1,0:T(8,128)S(1)} %shard_map.70.refs_0_), channel_id=1, source_target_pairs={{0,4},{1,17},{2,6},{3,19},{4,0},{5,21},{6,2},{7,23},{8,12},{9,25},... | collective-permute-start | bytes 208904 | tf_op jit(solution)/shard_map/ppermute | solution.py:265
  31.5 5.2 %collective-permute-start.10 = (f32[136,128]{1,0:T(8,128)S(1)}, f32[136,128]{1,0:T(8,128)S(1)}, u32[]{:S(2)}, u32[]{:S(2)}) collective-permute-start(f32[136,128]{1,0:T(8,128)S(1)} %shard_map.70.refs_0_), channel_id=1, source_target_pairs={{0,2},{1,9},{2,0},{3,11},{4,6},{5,13},{6,4},{7,15},{8,10},{9,1},{1... | collective-permute-start | bytes 208904 | tf_op jit(solution)/shard_map/ppermute | solution.py:265
  36.9 1.3 %collective-permute-start.13 = (f32[136,128]{1,0:T(8,128)S(1)}, f32[136,128]{1,0:T(8,128)S(1)}, u32[]{:S(2)}, u32[]{:S(2)}) collective-permute-start(f32[136,128]{1,0:T(8,128)S(1)} %get-tuple-element.23.mine_ref.second_ref), channel_id=1, source_target_pairs={{0,1},{1,0},{2,3},{3,2},{4,5},{5,4},{6,7},{7,6},{8,9},{9,8},{10,11... | collective-permute-start | bytes 208904 | tf_op jit(solution)/shard_map/ppermute | solution.py:256

commit v3 on v2

--- a/solution.py
+++ b/solution.py
@@ -7,20 +7,37 @@
 from jax.experimental.pallas import tpu as pltpu
 from jax.sharding import PartitionSpec as P
 
-HIGH = lax.Precision.HIGHEST
 AXES = ("stu", "que")
 LANES = 128
 BIAS = 8
 
 
+def halves(value):
+    high = value.astype(jnp.bfloat16)
+    return high, (value - high.astype(jnp.float32)).astype(jnp.bfloat16)
+
+
+def product(left, right, dims):
+    return lax.dot_general(left, right, (dims, ((), ())), preferred_element_type=jnp.float32)
+
+
 def dot_nt(left, right):
-    return lax.dot_general(
-        left, right, (((1,), (1,)), ((), ())), precision=HIGH, preferred_element_type=jnp.float32
-    )
+    left_high, left_low = halves(left)
+    right_high, right_low = halves(right)
+    dims = ((1,), (1,))
+    both = product(
+        jnp.concatenate([left_high, left_low], 1), jnp.concatenate([right_high, right_high], 1), dims
+    )
+    return both + product(left_high, right_low, dims)
 
 
 def dot_nn(left, right):
-    return jnp.dot(left, right, precision=HIGH, preferred_element_type=jnp.float32)
+    left_high, left_low = halves(left)
+    right_high, right_low = halves(right)
+    dims = ((1,), (0,))
+    both = product(left_high, jnp.concatenate([right_high, right_low], 1), dims)
+    width = right.shape[1]
+    return both[:, :width] + both[:, width:] + product(left_low, right_high, dims)
 
 
 def position():
@@ -47,7 +64,7 @@
 
 
 def bias_rows(lanes, mine):
-    return jnp.where(mine, jnp.concatenate([lanes[0:1, :LANES], lanes[0:1, LANES:]], 0), 0.0)
+    return jnp.where(mine, jnp.concatenate([lanes[:, :LANES], lanes[:, LANES:]], 0), 0.0)
 
 
 def column(rows):
@@ -56,6 +73,30 @@
     return jnp.concatenate([tall[:, 0:1], tall[:, 1:2]], 0)
 
 
+def block_kernel(theta_ref, disc_ref, icpt_ref, peer_theta_ref, peer_disc_ref, peer_icpt_ref, out_ref):
+    core, _, _ = position()
+    size, width = theta_ref.shape
+
+    def fill(students_ref, questions_ref, intercept_ref, first):
+        rows = slice(first, first + size)
+
+        @pl.when(core == 0)
+        def _():
+            out_ref[rows, :width] = students_ref[...]
+            lane = lax.broadcasted_iota(jnp.int32, (size, LANES - width), 1)
+            out_ref[rows, width:] = jnp.where(lane == 0, 1.0, 0.0)
+
+        @pl.when(core == 1)
+        def _():
+            out_ref[rows, :width] = questions_ref[...]
+            row = jnp.concatenate([intercept_ref[...], jnp.zeros((1, LANES - size), jnp.float32)], 1)
+            tall = jnp.concatenate([row, jnp.zeros((LANES - 1, LANES), jnp.float32)], 0).T
+            out_ref[rows, width:] = tall[:size, : LANES - width]
+
+    fill(theta_ref, disc_ref, icpt_ref, 0)
+    fill(peer_theta_ref, peer_disc_ref, peer_icpt_ref, size)
+
+
 def arrange_kernel(own_ref, peer_ref, out_ref):
     core, _, _ = position()
     cols = own_ref.shape[1]
@@ -71,19 +112,24 @@
         out_ref[cols:, :] = own_ref[...].astype(jnp.float32).T
 
 
-def place(src_ref, dst_ref, side, core, line, plane, group):
-    rows = src_ref.shape[0] // (2 * group)
-    for k in range(group):
-        for j in range(2):
-            at = block_of(side, core ^ j, line ^ k, plane ^ k, group) * rows
-            first = (k * 2 + j) * rows
-            dst_ref[pl.ds(pl.multiple_of(at, rows), rows), :] = src_ref[first : first + rows, :]
-
-
-def gradient_kernel(group, mine_ref, other_ref, code_ref, sums_ref, left_ref, right_ref, weight_ref, icpt_ref):
+def place(refs, dst_ref, side, core, line, plane, group):
+    size = dst_ref.shape[0] // (2 * group)
+    k = 0
+    for ref in refs:
+        for first in range(0, ref.shape[0], 2 * size):
+            for j in range(2):
+                at = block_of(side, core ^ j, line ^ k, plane ^ k, group) * size
+                rows = slice(first + j * size, first + (j + 1) * size)
+                dst_ref[pl.ds(pl.multiple_of(at, size), size), :] = ref[rows, :]
+            k += 1
+
+
+def gradient_kernel(group, parts, *refs):
+    mine_refs, other_refs = refs[:parts], refs[parts : 2 * parts]
+    code_ref, sums_ref, left_ref, right_ref, weight_ref, icpt_ref = refs[2 * parts :]
     core, line, plane = position()
-    place(mine_ref, left_ref, core, core, line, plane, group)
-    place(other_ref, right_ref, 1 - core, 1 - core, line, plane, group)
+    place(mine_refs, left_ref, core, core, line, plane, group)
+    place(other_refs, right_ref, 1 - core, 1 - core, line, plane, group)
     left = left_ref[...]
     right = right_ref[...]
     prob = 1.0 / (1.0 + jnp.exp(-dot_nt(left, right)))
@@ -96,18 +142,20 @@
     grad = dot_nn(resid, right)
     diag = dot_nn(weight, right * right)
     sums_ref[:rows, :] = jnp.where(low_lanes((rows, LANES)), grad, turn(diag))
-    ones = jnp.ones((8, rows), jnp.float32)
+    lane = lax.broadcasted_iota(jnp.int32, (rows, LANES), 1)
+    at = LANES // 2
+    extra = jnp.where(lane == at, grad, jnp.where(lane == at + 1, pltpu.roll(diag, 1, 1), pltpu.roll(left, 2, 1)))
+    lanes = extra.T
     mine = core == 1
     sums_ref[rows:, :] = jnp.concatenate(
         [
-            bias_rows(dot_nt(ones, resid), mine),
-            bias_rows(dot_nt(ones, weight), mine),
+            bias_rows(lanes[at : at + 1], mine),
+            bias_rows(lanes[at + 1 : at + 2], mine),
             jnp.zeros((BIAS - 4, LANES), jnp.float32),
         ],
         0,
     )
-    pick = (lax.broadcasted_iota(jnp.int32, (8, LANES), 1) == LANES // 2).astype(jnp.float32)
-    icpt = bias_rows(dot_nt(pick, left), mine)
+    icpt = bias_rows(lanes[at + 2 : at + 3], mine)
     icpt_ref[...] = jnp.concatenate([icpt, jnp.zeros((BIAS - 2, LANES), jnp.float32)], 0)
 
 
@@ -166,11 +214,11 @@
     half = rows // 2
     right = right_ref[...]
     scaled = weight_ref[...] * change_of(mine_ref, other_ref, left_ref[...], right, half)
-    sums_ref[:half, :] = pack(dot_nn(scaled, right))
-    ones = jnp.ones((8, rows), jnp.float32)
-    sums_ref[half:, :] = jnp.concatenate(
-        [bias_rows(dot_nt(ones, scaled), core == 1), jnp.zeros((BIAS - 2, LANES), jnp.float32)], 0
-    )
+    sums = dot_nn(scaled, right)
+    sums_ref[:half, :] = pack(sums)
+    at = LANES // 2
+    bias = bias_rows(sums.T[at : at + 1], core == 1)
+    sums_ref[half:, :] = jnp.concatenate([bias, jnp.zeros((BIAS - 2, LANES), jnp.float32)], 0)
 
 
 def second_kernel(group, parts, *refs):
@@ -238,7 +286,7 @@
     disc_at = jnp.where(core == 0, other_at, mine_at)
     row = jnp.where(disc_at // group == 1, bias[1:2], bias[0:1])
     back = lax.rem(LANES - lax.rem(disc_at, group) * size, LANES)
-    icpt_ref[...] = jnp.broadcast_to(pltpu.roll(row, back, 1), icpt_ref.shape)
+    icpt_ref[...] = pltpu.roll(row, back, 1)[:, :size]
 
 
 def call(kernel, shapes, *args):
@@ -283,17 +331,16 @@
     half = rows // 2
     assert width == LANES // 2 and rows == 2 * LANES
     assert disc.shape == theta.shape and codes.shape == (rows, half)
-    core = lax.rem(lax.axis_index("que"), 2)
-    pad = jnp.zeros((size, LANES - width - 1), jnp.float32)
-    students = jnp.concatenate([theta, jnp.ones((size, 1), jnp.float32), pad], 1)
-    questions = jnp.concatenate([disc, intercept[:, None], pad], 1)
+    icpt = intercept[None, :]
+    (mine,) = call(
+        block_kernel, [(2 * size, LANES)], theta, disc, icpt, swap(theta), swap(disc), swap(icpt)
+    )
     (code,) = call(arrange_kernel, [(rows, rows)], codes, swap(codes))
-    kept = jnp.where(core == 0, students, questions)
-    given = jnp.where(core == 0, questions, students)
-    mine = jnp.concatenate([kept, swap(given)], 0)
+    mine = [mine]
     for steps in stages(group):
-        mine = jnp.concatenate([mine] + [send(mine, step) for step in steps], 0)
-    other = swap(mine)
+        joined = jnp.concatenate(mine, 0)
+        mine = mine + [send(joined, step) for step in steps]
+    other = [swap(piece) for piece in mine]
 
     def totals(value):
         parts = [value]
@@ -304,10 +351,10 @@
         return parts
 
     sums, left, right, weight, icpt = call(
-        functools.partial(gradient_kernel, group),
+        functools.partial(gradient_kernel, group, len(mine)),
         [(rows + BIAS, LANES), (rows, LANES), (rows, LANES), (rows, rows), (BIAS, LANES)],
-        mine,
-        other,
+        *mine,
+        *other,
         code,
     )
     parts = totals(sums)
@@ -334,7 +381,7 @@
     dots = lax.all_to_all(dots, AXES, 0, 0, tiled=True)
     abilities, discs, icpts = call(
         functools.partial(finish_kernel, group),
-        [(size, width), (size, width), (8, LANES)],
+        [(size, width), (size, width), (1, size)],
         dots,
         first,
         peer,
@@ -342,7 +389,7 @@
         peer_second,
         root,
     )
-    return abilities, discs, icpts[0, :size]
+    return abilities, discs, icpts[0]
 
 
 def solution(mesh):

time: 52 us -> 50.7 us (0.975)
  Pallas kernels: 4.53 us -> 3.3 us
  waiting for transfers between devices: 17.5 us -> 16.3 us
  starting transfers between devices: 15.1 us -> 16.1 us
  local copies, waits for them, and re-layouts: 1.42 us -> 2.34 us
  other arithmetic: 0.8 us -> 0 us
    unnamed x7 -> x8, local copies, waits for them, and re-layouts: 0.02 us -> 2.34 us
    pallas_call x7 -> x8, Pallas kernels: 4.53 us -> 3.3 us  [call(): pl.pallas_call(kernel, out_shape=out, in_specs=[pl.BlockSpec(memory_space...]
    ppermute x5 -> x10, starting transfers between devices: 0.75 us -> 1.77 us  [swap_cores(): return lax.ppermute(value, AXES, [(i, i ^ 1) for i in range(n_stu * n_que)])]
    ppermute x5 -> x10, waiting for transfers between devices: 4.55 us -> 3.58 us  [swap_cores(): return lax.ppermute(value, AXES, [(i, i ^ 1) for i in range(n_stu * n_que)])]
    unnamed x1 -> x0, other arithmetic: 0.8 us -> none
    broadcast_in_dim x2 -> x0, local copies, waits for them, and re-layouts: 0.74 us -> none  [the longest x1 0.74 us: shards(): questions = jnp.concatenate([disc, intercept[:, None], pad], 1)]
  transfers between devices with their start and end apart: 14 -> 19, of which waited for: 10 -> 9; matrix products, arithmetic and copies ran while one was open for 0% -> 0% of each run, Pallas kernels for 0% -> 0%
where the time goes in v3:
time: 50.7 us; the launch traced here: 50.3 us
  waiting for transfers between devices  16.3 us (32%)
  starting transfers between devices  16.1 us (32%)
  blocking collectives  11.5 us (23%)
  Pallas kernels  3.3 us (7%)
  local copies, waits for them, and re-layouts  2.34 us (5%)
  between operations  0.75 us (1%)
    ppermute x9, starting transfers between devices, send_over(): return lax.ppermute(value, AXES, pairs)  14.3 us
    ppermute x9, waiting for transfers between devices, send_over(): return lax.ppermute(value, AXES, pairs)  12.8 us
    all_to_all x1, blocking collectives, shards(): dots = lax.all_to_all(dots, AXES, 0, 0, tiled=True)  11.5 us
    ppermute x10, waiting for transfers between devices, swap_cores(): return lax.ppermute(value, AXES, [(i, i ^ 1) for i in range(n_stu * n_que)])  3.58 us
    pallas_call x8, Pallas kernels, call(): pl.pallas_call(kernel, out_shape=out, in_specs=[pl.BlockSpec(memory_space...  3.3 us
    unnamed x8, local copies, waits for them, and re-layouts  2.34 us
    ppermute x10, starting transfers between devices, swap_cores(): return lax.ppermute(value, AXES, [(i, i ^ 1) for i in range(n_stu * n_que)])  1.77 us
  transfers between devices with their start and end apart: 19, of which 9 were waited for; matrix products, arithmetic and copies ran while one was open for 0% of the time, Pallas kernels for 0%

profile of v3, /device:TPU:0, one launch (start us, length us, event | category | flops | bytes accessed | tf_op | source)
XLA Modules:
  0.0 50.3 jit_solution(13832980732760534789)
XLA Ops:
  0.6 0.5 %collective-permute-start.10 = (s32[256,128]{1,0:T(8,128)}, s32[256,128]{1,0:T(8,128)S(1)}, u32[]{:S(2)}, u32[]{:S(2)}) collective-permute-start(s32[256,128]{1,0:T(8,128)} %own_ref.1), channel_id=1, source_target_pairs={{0,1},{1,0},{2,3},{3,2},{4,5},{5,4},{6,7},{7,6},{8,9},{9,8},{10,11... | collective-permute-start | bytes 393224 | tf_op jit(solution)/shard_map/ppermute | solution.py:304
  1.2 0.1 collective-permute-start
  1.2 0.4 collective-permute-start.1
  1.7 0.1 collective-permute-start.2
  1.8 1.0 %collective-permute-done.2.peer_icpt_ref = f32[1,32]{1,0:T(1,128)S(1)} collective-permute-done((f32[1,32]{1,0:T(1,128)S(1)}, f32[1,32]{1,0:T(1,128)S(1)}, u32[]{:S(2)}, u32[]{:S(2)}) %collective-permute-start.2) | collective-permute-done | bytes 160 | tf_op jit(solution)/shard_map/ppermute | solution.py:304
  2.8 0.7 %copy-done.1 = f32[32,64]{1,0:T(8,128)S(1)} copy-done((f32[32,64]{1,0:T(8,128)S(1)}, f32[32,64]{1,0:T(8,128)}, u32[]{:S(2)}) %copy-start.1) | copy-done | bytes 8216
  3.5 0.7 %copy-done.2 = f32[32,64]{1,0:T(8,128)S(1)} copy-done((f32[32,64]{1,0:T(8,128)S(1)}, f32[32,64]{1,0:T(8,128)}, u32[]{:S(2)}) %copy-start.2) | copy-done | bytes 8216
  4.2 0.1 shard_map.67.refs_0_
  4.4 4.9 %collective-permute-start.5 = (f32[64,128]{1,0:T(8,128)S(1)}, f32[64,128]{1,0:T(8,128)S(1)}, u32[]{:S(2)}, u32[]{:S(2)}) collective-permute-start(f32[64,128]{1,0:T(8,128)S(1)} %shard_map.67.refs_0_), channel_id=1, source_target_pairs={{0,6},{1,25},{2,4},{3,27},{4,2},{5,29},{6,0},{7,31},{8,14},{9,17},... | collective-permute-start | bytes 98312 | tf_op jit(solution)/shard_map/ppermute | solution.py:313
  9.2 0.6 %collective-permute-start.3 = (f32[64,128]{1,0:T(8,128)S(1)}, f32[64,128]{1,0:T(8,128)S(1)}, u32[]{:S(2)}, u32[]{:S(2)}) collective-permute-start(f32[64,128]{1,0:T(8,128)S(1)} %shard_map.67.refs_0_), channel_id=1, source_target_pairs={{0,2},{1,9},{2,0},{3,11},{4,6},{5,13},{6,4},{7,15},{8,10},{9,1},{1... | collective-permute-start | bytes 98312 | tf_op jit(solution)/shard_map/ppermute | solution.py:313
  9.8 1.3 %collective-permute-done.5.refs_3_ = f32[64,128]{1,0:T(8,128)S(1)} collective-permute-done((f32[64,128]{1,0:T(8,128)S(1)}, f32[64,128]{1,0:T(8,128)S(1)}, u32[]{:S(2)}, u32[]{:S(2)}) %collective-permute-start.5) | collective-permute-done | bytes 32800 | tf_op jit(solution)/shard_map/ppermute | solution.py:313
  11.1 2.9 %collective-permute-done.4.refs_2_ = f32[64,128]{1,0:T(8,128)S(1)} collective-permute-done((f32[64,128]{1,0:T(8,128)S(1)}, f32[64,128]{1,0:T(8,128)S(1)}, u32[]{:S(2)}, u32[]{:S(2)}) %collective-permute-start.4) | collective-permute-done | bytes 32800 | tf_op jit(solution)/shard_map/ppermute | solution.py:313
  14.1 0.5 %collective-permute-start.7 = (f32[64,128]{1,0:T(8,128)S(1)}, f32[64,128]{1,0:T(8,128)S(1)}, u32[]{:S(2)}, u32[]{:S(2)}) collective-permute-start(f32[64,128]{1,0:T(8,128)S(1)} %collective-permute-done.3.refs_1_), channel_id=1, source_target_pairs={{0,1},{1,0},{2,3},{3,2},{4,5},{5,4},{6,7},{7,6},{8,9},{9,8},{10,11... | collective-permute-start | bytes 98312 | tf_op jit(solution)/shard_map/ppermute | solution.py:304
  14.6 0.9 %copy-done = s32[256,128]{1,0:T(8,128)S(1)} copy-done((s32[256,128]{1,0:T(8,128)S(1)}, s32[256,128]{1,0:T(8,128)}, u32[]{:S(2)}) %copy-start) | copy-done | bytes 131096
  15.5 0.7 %shard_map.69 = (f32[264,128]{1,0:T(8,128)S(1)}, f32[256,128]{1,0:T(8,128)S(1)}, f32[256,128]{1,0:T(8,128)S(1)}, f32[256,256]{1,0:T(8,128)S(1)}, f32[8,128]{1,0:T(8,128)S(1)}) custom-call(f32[64,128]{1,0:T(8,128)S(1)} %shard_map.67.refs_0_, f32[64,128]{1,0:T(8,128)S(1)} %collective-permute-done.3.refs_1_, f32[64,128]{1,0:T(8,128)S(1)} %collective-permute-done.4.refs_2_, ...), custom_call_target="tpu_custom_call" | custom-call | tf_op jit(solution)/shard_map/pallas_call | solution.py:294
  16.3 1.2 %collective-permute-start.13 = (f32[264,128]{1,0:T(8,128)S(1)}, f32[264,128]{1,0:T(8,128)S(1)}, u32[]{:S(2)}, u32[]{:S(2)}) collective-permute-start(f32[264,128]{1,0:T(8,128)S(1)} %get-tuple-element.16.refs_0_), channel_id=1, source_target_pairs={{0,6},{1,25},{2,4},{3,27},{4,2},{5,29},{6,0},{7,31},{8,14},{9,17},... | collective-permute-start | bytes 405512 | tf_op jit(solution)/shard_map/ppermute | solution.py:313
  17.5 0.6 %collective-permute-start.12 = (f32[264,128]{1,0:T(8,128)S(1)}, f32[264,128]{1,0:T(8,128)S(1)}, u32[]{:S(2)}, u32[]{:S(2)}) collective-permute-start(f32[264,128]{1,0:T(8,128)S(1)} %get-tuple-element.16.refs_0_), channel_id=1, source_target_pairs={{0,4},{1,17},{2,6},{3,19},{4,0},{5,21},{6,2},{7,23},{8,12},{9,25},... | collective-permute-start | bytes 405512 | tf_op jit(solution)/shard_map/ppermute | solution.py:313
  18.2 2.6 %collective-permute-start.11 = (f32[264,128]{1,0:T(8,128)S(1)}, f32[264,128]{1,0:T(8,128)S(1)}, u32[]{:S(2)}, u32[]{:S(2)}) collective-permute-start(f32[264,128]{1,0:T(8,128)S(1)} %get-tuple-element.16.refs_0_), channel_id=1, source_target_pairs={{0,2},{1,9},{2,0},{3,11},{4,6},{5,13},{6,4},{7,15},{8,10},{9,1},{1... | collective-permute-start | bytes 405512 | tf_op jit(solution)/shard_map/ppermute | solution.py:313
  20.8 2.6 %collective-permute-done.13.refs_3_ = f32[264,128]{1,0:T(8,128)S(1)} collective-permute-done((f32[264,128]{1,0:T(8,128)S(1)}, f32[264,128]{1,0:T(8,128)S(1)}, u32[]{:S(2)}, u32[]{:S(2)}) %collective-permute-start.13) | collective-permute-done | bytes 135200 | tf_op jit(solution)/shard_map/ppermute | solution.py:313
  23.4 2.7 %collective-permute-done.12.refs_2_ = f32[264,128]{1,0:T(8,128)S(1)} collective-permute-done((f32[264,128]{1,0:T(8,128)S(1)}, f32[264,128]{1,0:T(8,128)S(1)}, u32[]{:S(2)}, u32[]{:S(2)}) %collective-permute-start.12) | collective-permute-done | bytes 135200 | tf_op jit(solution)/shard_map/ppermute | solution.py:313
  26.1 0.2 shard_map.70
  26.4 1.3 %collective-permute-done.14.other_ref.peer_ref = f32[168,128]{1,0:T(8,128)S(1)} collective-permute-done((f32[168,128]{1,0:T(8,128)S(1)}, f32[168,128]{1,0:T(8,128)S(1)}, u32[]{:S(2)}, u32[]{:S(2)}) %collective-permute-start.14) | collective-permute-done | bytes 86048 | tf_op jit(solution)/shard_map/ppermute | solution.py:304
  27.6 0.7 %shard_map.71.refs_0_ = f32[136,128]{1,0:T(8,128)S(1)} custom-call(f32[168,128]{1,0:T(8,128)S(1)} %get-tuple-element.19.mine_ref.refs_4_.send_ref, f32[168,128]{1,0:T(8,128)S(1)} %collective-permute-done.14.other_ref.peer_ref, f32[256,128]{1,0:T(8,128)S(1)} %get-tuple-element.17.refs_4_.left_ref, f32[256,128]{1,0:T(8,128)S(1)} %get-tuple-element.20.right_ref, ...), custom_call_target="tpu_custom_call" | custom-call | tf_op jit(solution)/shard_map/pallas_call | solution.py:294
  28.3 2.3 %collective-permute-start.17 = (f32[136,128]{1,0:T(8,128)S(1)}, f32[136,128]{1,0:T(8,128)S(1)}, u32[]{:S(2)}, u32[]{:S(2)}) collective-permute-start(f32[136,128]{1,0:T(8,128)S(1)} %shard_map.71.refs_0_), channel_id=1, source_target_pairs={{0,6},{1,25},{2,4},{3,27},{4,2},{5,29},{6,0},{7,31},{8,14},{9,17},... | collective-permute-start | bytes 208904 | tf_op jit(solution)/shard_map/ppermute | solution.py:313
  30.7 2.1 %collective-permute-start.15 = (f32[136,128]{1,0:T(8,128)S(1)}, f32[136,128]{1,0:T(8,128)S(1)}, u32[]{:S(2)}, u32[]{:S(2)}) collective-permute-start(f32[136,128]{1,0:T(8,128)S(1)} %shard_map.71.refs_0_), channel_id=1, source_target_pairs={{0,2},{1,9},{2,0},{3,11},{4,6},{5,13},{6,4},{7,15},{8,10},{9,1},{1... | collective-permute-start | bytes 208904 | tf_op jit(solution)/shard_map/ppermute | solution.py:313
  32.8 1.7 %collective-permute-done.17.refs_3_ = f32[136,128]{1,0:T(8,128)S(1)} collective-permute-done((f32[136,128]{1,0:T(8,128)S(1)}, f32[136,128]{1,0:T(8,128)S(1)}, u32[]{:S(2)}, u32[]{:S(2)}) %collective-permute-start.17) | collective-permute-done | bytes 69664 | tf_op jit(solution)/shard_map/ppermute | solution.py:313
  34.5 1.5 %collective-permute-done.16.refs_2_ = f32[136,128]{1,0:T(8,128)S(1)} collective-permute-done((f32[136,128]{1,0:T(8,128)S(1)}, f32[136,128]{1,0:T(8,128)S(1)}, u32[]{:S(2)}, u32[]{:S(2)}) %collective-permute-start.16) | collective-permute-done | bytes 69664 | tf_op jit(solution)/shard_map/ppermute | solution.py:313
  36.0 0.2 shard_map.72
  36.2 1.2 %collective-permute-done.18.other_ref.peer_second_ref = f32[136,128]{1,0:T(8,128)S(1)} collective-permute-done((f32[136,128]{1,0:T(8,128)S(1)}, f32[136,128]{1,0:T(8,128)S(1)}, u32[]{:S(2)}, u32[]{:S(2)}) %collective-permute-start.18) | collective-permute-done | bytes 69664 | tf_op jit(solution)/shard_map/ppermute | solution.py:304
  37.5 0.5 %shard_map.73 = f32[32,1,128]{2,1,0:T(1,128)S(1)} custom-call(f32[136,128]{1,0:T(8,128)S(1)} %get-tuple-element.23.mine_ref.second_ref, f32[136,128]{1,0:T(8,128)S(1)} %collective-permute-done.18.other_ref.peer_second_ref, f32[256,128]{1,0:T(8,128)S(1)} %get-tuple-element.17.refs_4_.left_ref, f32[256,128]{1,0:T(8,128)S(1)} %get-tuple-element.20.right_ref, ...), custom_call_target="tpu_custom_call" | custom-call | tf_op jit(solution)/shard_map/pallas_call | solution.py:294
  38.0 11.5 %all_to_all.5.dots_ref = f32[32,1,128]{2,1,0:T(1,128)S(1)} all-to-all(f32[32,1,128]{2,1,0:T(1,128)S(1)} %shard_map.73), channel_id=1, replica_groups=mesh['stu'=4,'que'=8] {'stu','que'}, dimensions={0} | all-to-all | bytes 32768 | tf_op jit(solution)/shard_map/all_to_all | solution.py:381
  49.5 0.8 %shard_map.74 = (f32[32,64]{1,0:T(8,128)}, f32[32,64]{1,0:T(8,128)}, f32[1,32]{1,0:T(1,128)}) custom-call(f32[32,1,128]{2,1,0:T(1,128)S(1)} %all_to_all.5.dots_ref, f32[168,128]{1,0:T(8,128)S(1)} %get-tuple-element.19.mine_ref.refs_4_.send_ref, f32[168,128]{1,0:T(8,128)S(1)} %collective-permute-done.14.other_ref.peer_ref, ...), custom_call_target="tpu_custom_call" | custom-call | tf_op jit(solution)/shard_map/pallas_call | solution.py:294
  (23 shorter events, 0.2 us)
Async XLA Ops:
  0.6 1.0 %copy-start.3 = (f32[32]{0:T(128)S(1)}, f32[32]{0:T(128)}, u32[]{:S(2)}) copy-start(f32[32]{0:T(128)} %param.7) | copy-start | bytes 388
  0.6 13.9 %collective-permute-start.10 = (s32[256,128]{1,0:T(8,128)}, s32[256,128]{1,0:T(8,128)S(1)}, u32[]{:S(2)}, u32[]{:S(2)}) collective-permute-start(s32[256,128]{1,0:T(8,128)} %own_ref.1), channel_id=1, source_target_pairs={{0,1},{1,0},{2,3},{3,2},{4,5},{5,4},{6,7},{7,6},{8,9},{9,8},{10,11... | collective-permute-start | bytes 393224 | tf_op jit(solution)/shard_map/ppermute | solution.py:304
  1.2 1.6 %collective-permute-start = (f32[32,64]{1,0:T(8,128)}, f32[32,64]{1,0:T(8,128)S(1)}, u32[]{:S(2)}, u32[]{:S(2)}) collective-permute-start(f32[32,64]{1,0:T(8,128)} %theta_ref.1), channel_id=1, source_target_pairs={{0,1},{1,0},{2,3},{3,2},{4,5},{5,4},{6,7},{7,6},{8,9},{9,8},{10,11... | collective-permute-start | bytes 24584 | tf_op jit(solution)/shard_map/ppermute | solution.py:304
  1.2 1.6 %collective-permute-start.1 = (f32[32,64]{1,0:T(8,128)}, f32[32,64]{1,0:T(8,128)S(1)}, u32[]{:S(2)}, u32[]{:S(2)}) collective-permute-start(f32[32,64]{1,0:T(8,128)} %disc_ref.1), channel_id=1, source_target_pairs={{0,1},{1,0},{2,3},{3,2},{4,5},{5,4},{6,7},{7,6},{8,9},{9,8},{10,11... | collective-permute-start | bytes 24584 | tf_op jit(solution)/shard_map/ppermute | solution.py:304
  1.7 1.1 %collective-permute-start.2 = (f32[1,32]{1,0:T(1,128)S(1)}, f32[1,32]{1,0:T(1,128)S(1)}, u32[]{:S(2)}, u32[]{:S(2)}) collective-permute-start(f32[1,32]{1,0:T(1,128)S(1)} %bitcast.2), channel_id=1, source_target_pairs={{0,1},{1,0},{2,3},{3,2},{4,5},{5,4},{6,7},{7,6},{8,9},{9,8},{10,11... | collective-permute-start | bytes 392 | tf_op jit(solution)/shard_map/ppermute | solution.py:304
  2.8 0.7 %copy-start.1 = (f32[32,64]{1,0:T(8,128)S(1)}, f32[32,64]{1,0:T(8,128)}, u32[]{:S(2)}) copy-start(f32[32,64]{1,0:T(8,128)} %theta_ref.1) | copy-start | bytes 24580
  3.5 0.7 %copy-start.2 = (f32[32,64]{1,0:T(8,128)S(1)}, f32[32,64]{1,0:T(8,128)}, u32[]{:S(2)}) copy-start(f32[32,64]{1,0:T(8,128)} %disc_ref.1) | copy-start | bytes 24580
  4.4 6.7 %collective-permute-start.5 = (f32[64,128]{1,0:T(8,128)S(1)}, f32[64,128]{1,0:T(8,128)S(1)}, u32[]{:S(2)}, u32[]{:S(2)}) collective-permute-start(f32[64,128]{1,0:T(8,128)S(1)} %shard_map.67.refs_0_), channel_id=1, source_target_pairs={{0,6},{1,25},{2,4},{3,27},{4,2},{5,29},{6,0},{7,31},{8,14},{9,17},... | collective-permute-start | bytes 98312 | tf_op jit(solution)/shard_map/ppermute | solution.py:313
  9.2 4.8 %collective-permute-start.4 = (f32[64,128]{1,0:T(8,128)S(1)}, f32[64,128]{1,0:T(8,128)S(1)}, u32[]{:S(2)}, u32[]{:S(2)}) collective-permute-start(f32[64,128]{1,0:T(8,128)S(1)} %shard_map.67.refs_0_), channel_id=1, source_target_pairs={{0,4},{1,17},{2,6},{3,19},{4,0},{5,21},{6,2},{7,23},{8,12},{9,25},... | collective-permute-start | bytes 98312 | tf_op jit(solution)/shard_map/ppermute | solution.py:313
  9.2 4.8 %collective-permute-start.3 = (f32[64,128]{1,0:T(8,128)S(1)}, f32[64,128]{1,0:T(8,128)S(1)}, u32[]{:S(2)}, u32[]{:S(2)}) collective-permute-start(f32[64,128]{1,0:T(8,128)S(1)} %shard_map.67.refs_0_), channel_id=1, source_target_pairs={{0,2},{1,9},{2,0},{3,11},{4,6},{5,13},{6,4},{7,15},{8,10},{9,1},{1... | collective-permute-start | bytes 98312 | tf_op jit(solution)/shard_map/ppermute | solution.py:313
  9.8 5.7 %collective-permute-start.6 = (f32[64,128]{1,0:T(8,128)S(1)}, f32[64,128]{1,0:T(8,128)S(1)}, u32[]{:S(2)}, u32[]{:S(2)}) collective-permute-start(f32[64,128]{1,0:T(8,128)S(1)} %shard_map.67.refs_0_), channel_id=1, source_target_pairs={{0,1},{1,0},{2,3},{3,2},{4,5},{5,4},{6,7},{7,6},{8,9},{9,8},{10,11... | collective-permute-start | bytes 98312 | tf_op jit(solution)/shard_map/ppermute | solution.py:304
  11.1 4.4 %collective-permute-start.9 = (f32[64,128]{1,0:T(8,128)S(1)}, f32[64,128]{1,0:T(8,128)S(1)}, u32[]{:S(2)}, u32[]{:S(2)}) collective-permute-start(f32[64,128]{1,0:T(8,128)S(1)} %collective-permute-done.5.refs_3_), channel_id=1, source_target_pairs={{0,1},{1,0},{2,3},{3,2},{4,5},{5,4},{6,7},{7,6},{8,9},{9,8},{10,11... | collective-permute-start | bytes 98312 | tf_op jit(solution)/shard_map/ppermute | solution.py:304
  14.1 1.5 %collective-permute-start.8 = (f32[64,128]{1,0:T(8,128)S(1)}, f32[64,128]{1,0:T(8,128)S(1)}, u32[]{:S(2)}, u32[]{:S(2)}) collective-permute-start(f32[64,128]{1,0:T(8,128)S(1)} %collective-permute-done.4.refs_2_), channel_id=1, source_target_pairs={{0,1},{1,0},{2,3},{3,2},{4,5},{5,4},{6,7},{7,6},{8,9},{9,8},{10,11... | collective-permute-start | bytes 98312 | tf_op jit(solution)/shard_map/ppermute | solution.py:304
  14.1 1.5 %collective-permute-start.7 = (f32[64,128]{1,0:T(8,128)S(1)}, f32[64,128]{1,0:T(8,128)S(1)}, u32[]{:S(2)}, u32[]{:S(2)}) collective-permute-start(f32[64,128]{1,0:T(8,128)S(1)} %collective-permute-done.3.refs_1_), channel_id=1, source_target_pairs={{0,1},{1,0},{2,3},{3,2},{4,5},{5,4},{6,7},{7,6},{8,9},{9,8},{10,11... | collective-permute-start | bytes 98312 | tf_op jit(solution)/shard_map/ppermute | solution.py:304
  14.6 0.9 %copy-start = (s32[256,128]{1,0:T(8,128)S(1)}, s32[256,128]{1,0:T(8,128)}, u32[]{:S(2)}) copy-start(s32[256,128]{1,0:T(8,128)} %own_ref.1) | copy-start | bytes 393220
  16.3 7.1 %collective-permute-start.13 = (f32[264,128]{1,0:T(8,128)S(1)}, f32[264,128]{1,0:T(8,128)S(1)}, u32[]{:S(2)}, u32[]{:S(2)}) collective-permute-start(f32[264,128]{1,0:T(8,128)S(1)} %get-tuple-element.16.refs_0_), channel_id=1, source_target_pairs={{0,6},{1,25},{2,4},{3,27},{4,2},{5,29},{6,0},{7,31},{8,14},{9,17},... | collective-permute-start | bytes 405512 | tf_op jit(solution)/shard_map/ppermute | solution.py:313
  17.5 8.6 %collective-permute-start.12 = (f32[264,128]{1,0:T(8,128)S(1)}, f32[264,128]{1,0:T(8,128)S(1)}, u32[]{:S(2)}, u32[]{:S(2)}) collective-permute-start(f32[264,128]{1,0:T(8,128)S(1)} %get-tuple-element.16.refs_0_), channel_id=1, source_target_pairs={{0,4},{1,17},{2,6},{3,19},{4,0},{5,21},{6,2},{7,23},{8,12},{9,25},... | collective-permute-start | bytes 405512 | tf_op jit(solution)/shard_map/ppermute | solution.py:313
  18.2 7.9 %collective-permute-start.11 = (f32[264,128]{1,0:T(8,128)S(1)}, f32[264,128]{1,0:T(8,128)S(1)}, u32[]{:S(2)}, u32[]{:S(2)}) collective-permute-start(f32[264,128]{1,0:T(8,128)S(1)} %get-tuple-element.16.refs_0_), channel_id=1, source_target_pairs={{0,2},{1,9},{2,0},{3,11},{4,6},{5,13},{6,4},{7,15},{8,10},{9,1},{1... | collective-permute-start | bytes 405512 | tf_op jit(solution)/shard_map/ppermute | solution.py:313
  26.3 1.3 %collective-permute-start.14 = (f32[168,128]{1,0:T(8,128)S(1)}, f32[168,128]{1,0:T(8,128)S(1)}, u32[]{:S(2)}, u32[]{:S(2)}) collective-permute-start(f32[168,128]{1,0:T(8,128)S(1)} %get-tuple-element.19.mine_ref.refs_4_.send_ref), channel_id=1, source_target_pairs={{0,1},{1,0},{2,3},{3,2},{4,5},{5,4},{6,7},{7,6},{8,9},{9,8},{10,11... | collective-permute-start | bytes 258056 | tf_op jit(solution)/shard_map/ppermute | solution.py:304
  28.3 6.2 %collective-permute-start.17 = (f32[136,128]{1,0:T(8,128)S(1)}, f32[136,128]{1,0:T(8,128)S(1)}, u32[]{:S(2)}, u32[]{:S(2)}) collective-permute-start(f32[136,128]{1,0:T(8,128)S(1)} %shard_map.71.refs_0_), channel_id=1, source_target_pairs={{0,6},{1,25},{2,4},{3,27},{4,2},{5,29},{6,0},{7,31},{8,14},{9,17},... | collective-permute-start | bytes 208904 | tf_op jit(solution)/shard_map/ppermute | solution.py:313
  30.7 5.3 %collective-permute-start.16 = (f32[136,128]{1,0:T(8,128)S(1)}, f32[136,128]{1,0:T(8,128)S(1)}, u32[]{:S(2)}, u32[]{:S(2)}) collective-permute-start(f32[136,128]{1,0:T(8,128)S(1)} %shard_map.71.refs_0_), channel_id=1, source_target_pairs={{0,4},{1,17},{2,6},{3,19},{4,0},{5,21},{6,2},{7,23},{8,12},{9,25},... | collective-permute-start | bytes 208904 | tf_op jit(solution)/shard_map/ppermute | solution.py:313
  30.7 5.3 %collective-permute-start.15 = (f32[136,128]{1,0:T(8,128)S(1)}, f32[136,128]{1,0:T(8,128)S(1)}, u32[]{:S(2)}, u32[]{:S(2)}) collective-permute-start(f32[136,128]{1,0:T(8,128)S(1)} %shard_map.71.refs_0_), channel_id=1, source_target_pairs={{0,2},{1,9},{2,0},{3,11},{4,6},{5,13},{6,4},{7,15},{8,10},{9,1},{1... | collective-permute-start | bytes 208904 | tf_op jit(solution)/shard_map/ppermute | solution.py:313
  36.2 1.3 %collective-permute-start.18 = (f32[136,128]{1,0:T(8,128)S(1)}, f32[136,128]{1,0:T(8,128)S(1)}, u32[]{:S(2)}, u32[]{:S(2)}) collective-permute-start(f32[136,128]{1,0:T(8,128)S(1)} %get-tuple-element.23.mine_ref.second_ref), channel_id=1, source_target_pairs={{0,1},{1,0},{2,3},{3,2},{4,5},{5,4},{6,7},{7,6},{8,9},{9,8},{10,11... | collective-permute-start | bytes 208904 | tf_op jit(solution)/shard_map/ppermute | solution.py:304

commit v4 on v3

--- a/solution.py
+++ b/solution.py
@@ -73,30 +73,6 @@
     return jnp.concatenate([tall[:, 0:1], tall[:, 1:2]], 0)
 
 
-def block_kernel(theta_ref, disc_ref, icpt_ref, peer_theta_ref, peer_disc_ref, peer_icpt_ref, out_ref):
-    core, _, _ = position()
-    size, width = theta_ref.shape
-
-    def fill(students_ref, questions_ref, intercept_ref, first):
-        rows = slice(first, first + size)
-
-        @pl.when(core == 0)
-        def _():
-            out_ref[rows, :width] = students_ref[...]
-            lane = lax.broadcasted_iota(jnp.int32, (size, LANES - width), 1)
-            out_ref[rows, width:] = jnp.where(lane == 0, 1.0, 0.0)
-
-        @pl.when(core == 1)
-        def _():
-            out_ref[rows, :width] = questions_ref[...]
-            row = jnp.concatenate([intercept_ref[...], jnp.zeros((1, LANES - size), jnp.float32)], 1)
-            tall = jnp.concatenate([row, jnp.zeros((LANES - 1, LANES), jnp.float32)], 0).T
-            out_ref[rows, width:] = tall[:size, : LANES - width]
-
-    fill(theta_ref, disc_ref, icpt_ref, 0)
-    fill(peer_theta_ref, peer_disc_ref, peer_icpt_ref, size)
-
-
 def arrange_kernel(own_ref, peer_ref, out_ref):
     core, _, _ = position()
     cols = own_ref.shape[1]
@@ -112,24 +88,35 @@
         out_ref[cols:, :] = own_ref[...].astype(jnp.float32).T
 
 
-def place(refs, dst_ref, side, core, line, plane, group):
+def pieces(refs, size):
+    step = size + BIAS
+    return [ref[first : first + step, :] for ref in refs for first in range(0, ref.shape[0], step)]
+
+
+def place(blocks, dst_ref, side, columns, core, line, plane, group):
     size = dst_ref.shape[0] // (2 * group)
-    k = 0
-    for ref in refs:
-        for first in range(0, ref.shape[0], 2 * size):
-            for j in range(2):
-                at = block_of(side, core ^ j, line ^ k, plane ^ k, group) * size
-                rows = slice(first + j * size, first + (j + 1) * size)
-                dst_ref[pl.ds(pl.multiple_of(at, size), size), :] = ref[rows, :]
-            k += 1
+    lane = lax.broadcasted_iota(jnp.int32, (size, LANES), 1)
+    half = LANES // 2
+    for k, block in enumerate(blocks):
+        for j in range(2):
+            value = turn(block[:size]) if j else block[:size]
+            last = jnp.where(side == 0, 1.0, columns[j * half : j * half + size, k : k + 1])
+            at = block_of(side, core ^ j, line ^ k, plane ^ k, group) * size
+            dst_ref[pl.ds(pl.multiple_of(at, size), size), :] = jnp.where(
+                lane < half, value, jnp.where(lane == half, last, 0.0)
+            )
 
 
 def gradient_kernel(group, parts, *refs):
-    mine_refs, other_refs = refs[:parts], refs[parts : 2 * parts]
     code_ref, sums_ref, left_ref, right_ref, weight_ref, icpt_ref = refs[2 * parts :]
     core, line, plane = position()
-    place(mine_refs, left_ref, core, core, line, plane, group)
-    place(other_refs, right_ref, 1 - core, 1 - core, line, plane, group)
+    size = left_ref.shape[0] // (2 * group)
+    mine = pieces(refs[:parts], size)
+    other = pieces(refs[parts : 2 * parts], size)
+    rows = [jnp.where(core == 0, there[size : size + 1], here[size : size + 1]) for here, there in zip(mine, other)]
+    columns = jnp.concatenate(rows + [jnp.zeros((LANES - group, LANES), jnp.float32)], 0).T
+    place(mine, left_ref, core, columns, core, line, plane, group)
+    place(other, right_ref, 1 - core, columns, 1 - core, line, plane, group)
     left = left_ref[...]
     right = right_ref[...]
     prob = 1.0 / (1.0 + jnp.exp(-dot_nt(left, right)))
@@ -331,9 +318,13 @@
     half = rows // 2
     assert width == LANES // 2 and rows == 2 * LANES
     assert disc.shape == theta.shape and codes.shape == (rows, half)
-    icpt = intercept[None, :]
-    (mine,) = call(
-        block_kernel, [(2 * size, LANES)], theta, disc, icpt, swap(theta), swap(disc), swap(icpt)
+    core = lax.rem(lax.axis_index("que"), 2)
+    peer_theta, peer_disc, peer_icpt = swap(theta), swap(disc), swap(intercept)
+    here = jnp.where(core == 0, theta, disc)
+    there = jnp.where(core == 0, peer_theta, peer_disc)
+    icpt = jnp.pad(jnp.stack([intercept, peer_icpt]), ((0, 0), (0, width - size))).reshape(1, LANES)
+    mine = jnp.concatenate(
+        [jnp.concatenate([here, there], 1), icpt, jnp.zeros((BIAS - 1, LANES), jnp.float32)], 0
     )
     (code,) = call(arrange_kernel, [(rows, rows)], codes, swap(codes))
     mine = [mine]

time: 50.7 us -> 49.2 us (0.970)
  local copies, waits for them, and re-layouts: 2.34 us -> 0.17 us
  other arithmetic: 0 us -> 0.75 us
    unnamed x8 -> x4, local copies, waits for them, and re-layouts: 2.34 us -> 0.01 us
    another operation x0 -> x1, other arithmetic: none -> 0.66 us  [shards(): jnp.stack([intercept, peer_icpt])]
    pallas_call x8 -> x7, Pallas kernels: 3.3 us -> 3.38 us  [call(): pl.pallas_call(kernel, out_shape=out, in_specs=[pl.BlockSpec(memory_space...]
  transfers between devices with their start and end apart: 19 -> 19, of which waited for: 9 -> 11; matrix products, arithmetic and copies ran while one was open for 0% -> 2% of each run, Pallas kernels for 0% -> 0%
where the time goes in v4:
time: 49.2 us; the launch traced here: 49 us
  starting transfers between devices  16.2 us (33%)
  waiting for transfers between devices  16.2 us (33%)
  blocking collectives  11.6 us (24%)
  Pallas kernels  3.38 us (7%)
  between operations  0.76 us (2%)
  other arithmetic  0.75 us (2%)
    ppermute x9, starting transfers between devices, send_over(): return lax.ppermute(value, AXES, pairs)  14.5 us
    ppermute x9, waiting for transfers between devices, send_over(): return lax.ppermute(value, AXES, pairs)  12.6 us
    all_to_all x1, blocking collectives, shards(): dots = lax.all_to_all(dots, AXES, 0, 0, tiled=True)  11.6 us
    ppermute x10, waiting for transfers between devices, swap_cores(): return lax.ppermute(value, AXES, [(i, i ^ 1) for i in range(n_stu * n_que)])  3.58 us
    pallas_call x7, Pallas kernels, call(): pl.pallas_call(kernel, out_shape=out, in_specs=[pl.BlockSpec(memory_space...  3.38 us
    ppermute x10, starting transfers between devices, swap_cores(): return lax.ppermute(value, AXES, [(i, i ^ 1) for i in range(n_stu * n_que)])  1.77 us
  transfers between devices with their start and end apart: 19, of which 11 were waited for; matrix products, arithmetic and copies ran while one was open for 2% of the time, Pallas kernels for 0%

profile of v4, /device:TPU:0, one launch (start us, length us, event | category | flops | bytes accessed | tf_op | source)
XLA Modules:
  0.0 49.0 jit_solution(16345902185974583461)
XLA Ops:
  0.7 0.5 %collective-permute-start.2 = (f32[32]{0:T(128)}, f32[32]{0:T(128)S(1)}, u32[]{:S(2)}, u32[]{:S(2)}) collective-permute-start(f32[32]{0:T(128)} %param.7), channel_id=1, source_target_pairs={{0,1},{1,0},{2,3},{3,2},{4,5},{5,4},{6,7},{7,6},{8,9},{9,8},{10,11... | collective-permute-start | bytes 392 | tf_op jit(solution)/shard_map/ppermute | solution.py:291
  1.2 0.1 collective-permute-start
  1.2 0.4 collective-permute-start.1
  1.7 0.1 collective-permute-start.10
  1.9 0.3 collective-permute-done.2
  2.1 0.7 %select_maximum_fusion = f32[2,64]{1,0:T(2,128)S(1)} fusion(f32[1,32]{1,0:T(1,128)S(1)} %bitcast.4, f32[1,32]{1,0:T(1,128)} %bitcast.3), kind=kLoop, calls=%fused_computation.3 | loop fusion | flops 512 | bytes 768 | tf_op jit(solution)/shard_map/stack | solution.py:325
  2.8 0.1 reshape.9
  3.0 4.9 %collective-permute-start.5 = (f32[40,128]{1,0:T(8,128)S(1)}, f32[40,128]{1,0:T(8,128)S(1)}, u32[]{:S(2)}, u32[]{:S(2)}) collective-permute-start(f32[40,128]{1,0:T(8,128)S(1)} %maximum_maximum_fusion.refs_0_), channel_id=1, source_target_pairs={{0,6},{1,25},{2,4},{3,27},{4,2},{5,29},{6,0},{7,31},{8,14},{9,17},... | collective-permute-start | bytes 61448 | tf_op jit(solution)/shard_map/ppermute | solution.py:300
  7.9 0.6 %collective-permute-start.3 = (f32[40,128]{1,0:T(8,128)S(1)}, f32[40,128]{1,0:T(8,128)S(1)}, u32[]{:S(2)}, u32[]{:S(2)}) collective-permute-start(f32[40,128]{1,0:T(8,128)S(1)} %maximum_maximum_fusion.refs_0_), channel_id=1, source_target_pairs={{0,2},{1,9},{2,0},{3,11},{4,6},{5,13},{6,4},{7,15},{8,10},{9,1},{1... | collective-permute-start | bytes 61448 | tf_op jit(solution)/shard_map/ppermute | solution.py:300
  8.5 1.1 %collective-permute-done.5.refs_3_ = f32[40,128]{1,0:T(8,128)S(1)} collective-permute-done((f32[40,128]{1,0:T(8,128)S(1)}, f32[40,128]{1,0:T(8,128)S(1)}, u32[]{:S(2)}, u32[]{:S(2)}) %collective-permute-start.5) | collective-permute-done | bytes 20512 | tf_op jit(solution)/shard_map/ppermute | solution.py:300
  9.6 2.9 %collective-permute-done.4.refs_2_ = f32[40,128]{1,0:T(8,128)S(1)} collective-permute-done((f32[40,128]{1,0:T(8,128)S(1)}, f32[40,128]{1,0:T(8,128)S(1)}, u32[]{:S(2)}, u32[]{:S(2)}) %collective-permute-start.4) | collective-permute-done | bytes 20512 | tf_op jit(solution)/shard_map/ppermute | solution.py:300
  12.6 0.5 %collective-permute-start.7 = (f32[40,128]{1,0:T(8,128)S(1)}, f32[40,128]{1,0:T(8,128)S(1)}, u32[]{:S(2)}, u32[]{:S(2)}) collective-permute-start(f32[40,128]{1,0:T(8,128)S(1)} %collective-permute-done.3.refs_1_), channel_id=1, source_target_pairs={{0,1},{1,0},{2,3},{3,2},{4,5},{5,4},{6,7},{7,6},{8,9},{9,8},{10,11... | collective-permute-start | bytes 61448 | tf_op jit(solution)/shard_map/ppermute | solution.py:291
  13.1 0.6 %collective-permute-done.8.refs_6_ = f32[40,128]{1,0:T(8,128)S(1)} collective-permute-done((f32[40,128]{1,0:T(8,128)S(1)}, f32[40,128]{1,0:T(8,128)S(1)}, u32[]{:S(2)}, u32[]{:S(2)}) %collective-permute-start.8) | collective-permute-done | bytes 20512 | tf_op jit(solution)/shard_map/ppermute | solution.py:291
  13.7 0.2 collective-permute-done.7.refs_5_
  13.9 1.0 %shard_map.68 = (f32[264,128]{1,0:T(8,128)S(1)}, f32[256,128]{1,0:T(8,128)S(1)}, f32[256,128]{1,0:T(8,128)S(1)}, f32[256,256]{1,0:T(8,128)S(1)}, f32[8,128]{1,0:T(8,128)S(1)}) custom-call(f32[40,128]{1,0:T(8,128)S(1)} %maximum_maximum_fusion.refs_0_, f32[40,128]{1,0:T(8,128)S(1)} %collective-permute-done.3.refs_1_, ...), custom_call_target="tpu_custom_call" | custom-call | tf_op jit(solution)/shard_map/pallas_call | solution.py:281
  14.9 1.4 %collective-permute-start.13 = (f32[264,128]{1,0:T(8,128)S(1)}, f32[264,128]{1,0:T(8,128)S(1)}, u32[]{:S(2)}, u32[]{:S(2)}) collective-permute-start(f32[264,128]{1,0:T(8,128)S(1)} %get-tuple-element.16.refs_0_), channel_id=1, source_target_pairs={{0,6},{1,25},{2,4},{3,27},{4,2},{5,29},{6,0},{7,31},{8,14},{9,17},... | collective-permute-start | bytes 405512 | tf_op jit(solution)/shard_map/ppermute | solution.py:300
  16.2 0.6 %collective-permute-start.12 = (f32[264,128]{1,0:T(8,128)S(1)}, f32[264,128]{1,0:T(8,128)S(1)}, u32[]{:S(2)}, u32[]{:S(2)}) collective-permute-start(f32[264,128]{1,0:T(8,128)S(1)} %get-tuple-element.16.refs_0_), channel_id=1, source_target_pairs={{0,4},{1,17},{2,6},{3,19},{4,0},{5,21},{6,2},{7,23},{8,12},{9,25},... | collective-permute-start | bytes 405512 | tf_op jit(solution)/shard_map/ppermute | solution.py:300
  16.9 2.5 %collective-permute-start.11 = (f32[264,128]{1,0:T(8,128)S(1)}, f32[264,128]{1,0:T(8,128)S(1)}, u32[]{:S(2)}, u32[]{:S(2)}) collective-permute-start(f32[264,128]{1,0:T(8,128)S(1)} %get-tuple-element.16.refs_0_), channel_id=1, source_target_pairs={{0,2},{1,9},{2,0},{3,11},{4,6},{5,13},{6,4},{7,15},{8,10},{9,1},{1... | collective-permute-start | bytes 405512 | tf_op jit(solution)/shard_map/ppermute | solution.py:300
  19.3 2.6 %collective-permute-done.13.refs_3_ = f32[264,128]{1,0:T(8,128)S(1)} collective-permute-done((f32[264,128]{1,0:T(8,128)S(1)}, f32[264,128]{1,0:T(8,128)S(1)}, u32[]{:S(2)}, u32[]{:S(2)}) %collective-permute-start.13) | collective-permute-done | bytes 135200 | tf_op jit(solution)/shard_map/ppermute | solution.py:300
  22.0 2.7 %collective-permute-done.12.refs_2_ = f32[264,128]{1,0:T(8,128)S(1)} collective-permute-done((f32[264,128]{1,0:T(8,128)S(1)}, f32[264,128]{1,0:T(8,128)S(1)}, u32[]{:S(2)}, u32[]{:S(2)}) %collective-permute-start.12) | collective-permute-done | bytes 135200 | tf_op jit(solution)/shard_map/ppermute | solution.py:300
  24.7 0.2 shard_map.69
  24.9 1.3 %collective-permute-done.14.other_ref.peer_ref = f32[168,128]{1,0:T(8,128)S(1)} collective-permute-done((f32[168,128]{1,0:T(8,128)S(1)}, f32[168,128]{1,0:T(8,128)S(1)}, u32[]{:S(2)}, u32[]{:S(2)}) %collective-permute-start.14) | collective-permute-done | bytes 86048 | tf_op jit(solution)/shard_map/ppermute | solution.py:291
  26.2 0.7 %shard_map.70.refs_0_ = f32[136,128]{1,0:T(8,128)S(1)} custom-call(f32[168,128]{1,0:T(8,128)S(1)} %get-tuple-element.19.mine_ref.refs_4_.send_ref, f32[168,128]{1,0:T(8,128)S(1)} %collective-permute-done.14.other_ref.peer_ref, f32[256,128]{1,0:T(8,128)S(1)} %get-tuple-element.17.refs_4_.left_ref, f32[256,128]{1,0:T(8,128)S(1)} %get-tuple-element.20.right_ref, ...), custom_call_target="tpu_custom_call" | custom-call | tf_op jit(solution)/shard_map/pallas_call | solution.py:281
  26.9 2.5 %collective-permute-start.17 = (f32[136,128]{1,0:T(8,128)S(1)}, f32[136,128]{1,0:T(8,128)S(1)}, u32[]{:S(2)}, u32[]{:S(2)}) collective-permute-start(f32[136,128]{1,0:T(8,128)S(1)} %shard_map.70.refs_0_), channel_id=1, source_target_pairs={{0,6},{1,25},{2,4},{3,27},{4,2},{5,29},{6,0},{7,31},{8,14},{9,17},... | collective-permute-start | bytes 208904 | tf_op jit(solution)/shard_map/ppermute | solution.py:300
  29.4 2.0 %collective-permute-start.15 = (f32[136,128]{1,0:T(8,128)S(1)}, f32[136,128]{1,0:T(8,128)S(1)}, u32[]{:S(2)}, u32[]{:S(2)}) collective-permute-start(f32[136,128]{1,0:T(8,128)S(1)} %shard_map.70.refs_0_), channel_id=1, source_target_pairs={{0,2},{1,9},{2,0},{3,11},{4,6},{5,13},{6,4},{7,15},{8,10},{9,1},{1... | collective-permute-start | bytes 208904 | tf_op jit(solution)/shard_map/ppermute | solution.py:300
  31.4 1.7 %collective-permute-done.17.refs_3_ = f32[136,128]{1,0:T(8,128)S(1)} collective-permute-done((f32[136,128]{1,0:T(8,128)S(1)}, f32[136,128]{1,0:T(8,128)S(1)}, u32[]{:S(2)}, u32[]{:S(2)}) %collective-permute-start.17) | collective-permute-done | bytes 69664 | tf_op jit(solution)/shard_map/ppermute | solution.py:300
  33.1 1.5 %collective-permute-done.16.refs_2_ = f32[136,128]{1,0:T(8,128)S(1)} collective-permute-done((f32[136,128]{1,0:T(8,128)S(1)}, f32[136,128]{1,0:T(8,128)S(1)}, u32[]{:S(2)}, u32[]{:S(2)}) %collective-permute-start.16) | collective-permute-done | bytes 69664 | tf_op jit(solution)/shard_map/ppermute | solution.py:300
  34.6 0.2 shard_map.71
  34.8 1.2 %collective-permute-done.18.other_ref.peer_second_ref = f32[136,128]{1,0:T(8,128)S(1)} collective-permute-done((f32[136,128]{1,0:T(8,128)S(1)}, f32[136,128]{1,0:T(8,128)S(1)}, u32[]{:S(2)}, u32[]{:S(2)}) %collective-permute-start.18) | collective-permute-done | bytes 69664 | tf_op jit(solution)/shard_map/ppermute | solution.py:291
  36.1 0.5 %shard_map.72 = f32[32,1,128]{2,1,0:T(1,128)S(1)} custom-call(f32[136,128]{1,0:T(8,128)S(1)} %get-tuple-element.23.mine_ref.second_ref, f32[136,128]{1,0:T(8,128)S(1)} %collective-permute-done.18.other_ref.peer_second_ref, f32[256,128]{1,0:T(8,128)S(1)} %get-tuple-element.17.refs_4_.left_ref, f32[256,128]{1,0:T(8,128)S(1)} %get-tuple-element.20.right_ref, ...), custom_call_target="tpu_custom_call" | custom-call | tf_op jit(solution)/shard_map/pallas_call | solution.py:281
  36.6 11.6 %all_to_all.5.dots_ref = f32[32,1,128]{2,1,0:T(1,128)S(1)} all-to-all(f32[32,1,128]{2,1,0:T(1,128)S(1)} %shard_map.72), channel_id=1, replica_groups=mesh['stu'=4,'que'=8] {'stu','que'}, dimensions={0} | all-to-all | bytes 32768 | tf_op jit(solution)/shard_map/all_to_all | solution.py:372
  48.2 0.8 %shard_map.73 = (f32[32,64]{1,0:T(8,128)}, f32[32,64]{1,0:T(8,128)}, f32[1,32]{1,0:T(1,128)}) custom-call(f32[32,1,128]{2,1,0:T(1,128)S(1)} %all_to_all.5.dots_ref, f32[168,128]{1,0:T(8,128)S(1)} %get-tuple-element.19.mine_ref.refs_4_.send_ref, f32[168,128]{1,0:T(8,128)S(1)} %collective-permute-done.14.other_ref.peer_ref, ...), custom_call_target="tpu_custom_call" | custom-call | tf_op jit(solution)/shard_map/pallas_call | solution.py:281
  (25 shorter events, 0.4 us)
Async XLA Ops:
  0.6 1.1 %copy-start.1 = (f32[32,64]{1,0:T(8,128)S(1)}, f32[32,64]{1,0:T(8,128)}, u32[]{:S(2)}) copy-start(f32[32,64]{1,0:T(8,128)} %param.5) | copy-start | bytes 24580
  0.6 12.4 %copy-start = (s32[256,128]{1,0:T(8,128)S(1)}, s32[256,128]{1,0:T(8,128)}, u32[]{:S(2)}) copy-start(s32[256,128]{1,0:T(8,128)} %own_ref.1) | copy-start | bytes 393220
  0.7 1.5 %collective-permute-start.2 = (f32[32]{0:T(128)}, f32[32]{0:T(128)S(1)}, u32[]{:S(2)}, u32[]{:S(2)}) collective-permute-start(f32[32]{0:T(128)} %param.7), channel_id=1, source_target_pairs={{0,1},{1,0},{2,3},{3,2},{4,5},{5,4},{6,7},{7,6},{8,9},{9,8},{10,11... | collective-permute-start | bytes 392 | tf_op jit(solution)/shard_map/ppermute | solution.py:291
  1.2 1.7 %collective-permute-start = (f32[32,64]{1,0:T(8,128)}, f32[32,64]{1,0:T(8,128)S(1)}, u32[]{:S(2)}, u32[]{:S(2)}) collective-permute-start(f32[32,64]{1,0:T(8,128)} %param.5), channel_id=1, source_target_pairs={{0,1},{1,0},{2,3},{3,2},{4,5},{5,4},{6,7},{7,6},{8,9},{9,8},{10,11... | collective-permute-start | bytes 24584 | tf_op jit(solution)/shard_map/ppermute | solution.py:291
  1.2 1.6 %collective-permute-start.1 = (f32[32,64]{1,0:T(8,128)}, f32[32,64]{1,0:T(8,128)S(1)}, u32[]{:S(2)}, u32[]{:S(2)}) collective-permute-start(f32[32,64]{1,0:T(8,128)} %param.6), channel_id=1, source_target_pairs={{0,1},{1,0},{2,3},{3,2},{4,5},{5,4},{6,7},{7,6},{8,9},{9,8},{10,11... | collective-permute-start | bytes 24584 | tf_op jit(solution)/shard_map/ppermute | solution.py:291
  1.7 11.4 %collective-permute-start.10 = (s32[256,128]{1,0:T(8,128)}, s32[256,128]{1,0:T(8,128)S(1)}, u32[]{:S(2)}, u32[]{:S(2)}) collective-permute-start(s32[256,128]{1,0:T(8,128)} %own_ref.1), channel_id=1, source_target_pairs={{0,1},{1,0},{2,3},{3,2},{4,5},{5,4},{6,7},{7,6},{8,9},{9,8},{10,11... | collective-permute-start | bytes 393224 | tf_op jit(solution)/shard_map/ppermute | solution.py:291
  3.0 6.7 %collective-permute-start.5 = (f32[40,128]{1,0:T(8,128)S(1)}, f32[40,128]{1,0:T(8,128)S(1)}, u32[]{:S(2)}, u32[]{:S(2)}) collective-permute-start(f32[40,128]{1,0:T(8,128)S(1)} %maximum_maximum_fusion.refs_0_), channel_id=1, source_target_pairs={{0,6},{1,25},{2,4},{3,27},{4,2},{5,29},{6,0},{7,31},{8,14},{9,17},... | collective-permute-start | bytes 61448 | tf_op jit(solution)/shard_map/ppermute | solution.py:300
  7.9 4.7 %collective-permute-start.4 = (f32[40,128]{1,0:T(8,128)S(1)}, f32[40,128]{1,0:T(8,128)S(1)}, u32[]{:S(2)}, u32[]{:S(2)}) collective-permute-start(f32[40,128]{1,0:T(8,128)S(1)} %maximum_maximum_fusion.refs_0_), channel_id=1, source_target_pairs={{0,4},{1,17},{2,6},{3,19},{4,0},{5,21},{6,2},{7,23},{8,12},{9,25},... | collective-permute-start | bytes 61448 | tf_op jit(solution)/shard_map/ppermute | solution.py:300
  7.9 4.7 %collective-permute-start.3 = (f32[40,128]{1,0:T(8,128)S(1)}, f32[40,128]{1,0:T(8,128)S(1)}, u32[]{:S(2)}, u32[]{:S(2)}) collective-permute-start(f32[40,128]{1,0:T(8,128)S(1)} %maximum_maximum_fusion.refs_0_), channel_id=1, source_target_pairs={{0,2},{1,9},{2,0},{3,11},{4,6},{5,13},{6,4},{7,15},{8,10},{9,1},{1... | collective-permute-start | bytes 61448 | tf_op jit(solution)/shard_map/ppermute | solution.py:300
  8.5 4.6 %collective-permute-start.6 = (f32[40,128]{1,0:T(8,128)S(1)}, f32[40,128]{1,0:T(8,128)S(1)}, u32[]{:S(2)}, u32[]{:S(2)}) collective-permute-start(f32[40,128]{1,0:T(8,128)S(1)} %maximum_maximum_fusion.refs_0_), channel_id=1, source_target_pairs={{0,1},{1,0},{2,3},{3,2},{4,5},{5,4},{6,7},{7,6},{8,9},{9,8},{10,11... | collective-permute-start | bytes 61448 | tf_op jit(solution)/shard_map/ppermute | solution.py:291
  9.6 3.5 %collective-permute-start.9 = (f32[40,128]{1,0:T(8,128)S(1)}, f32[40,128]{1,0:T(8,128)S(1)}, u32[]{:S(2)}, u32[]{:S(2)}) collective-permute-start(f32[40,128]{1,0:T(8,128)S(1)} %collective-permute-done.5.refs_3_), channel_id=1, source_target_pairs={{0,1},{1,0},{2,3},{3,2},{4,5},{5,4},{6,7},{7,6},{8,9},{9,8},{10,11... | collective-permute-start | bytes 61448 | tf_op jit(solution)/shard_map/ppermute | solution.py:291
  12.6 1.2 %collective-permute-start.8 = (f32[40,128]{1,0:T(8,128)S(1)}, f32[40,128]{1,0:T(8,128)S(1)}, u32[]{:S(2)}, u32[]{:S(2)}) collective-permute-start(f32[40,128]{1,0:T(8,128)S(1)} %collective-permute-done.4.refs_2_), channel_id=1, source_target_pairs={{0,1},{1,0},{2,3},{3,2},{4,5},{5,4},{6,7},{7,6},{8,9},{9,8},{10,11... | collective-permute-start | bytes 61448 | tf_op jit(solution)/shard_map/ppermute | solution.py:291
  12.6 1.4 %collective-permute-start.7 = (f32[40,128]{1,0:T(8,128)S(1)}, f32[40,128]{1,0:T(8,128)S(1)}, u32[]{:S(2)}, u32[]{:S(2)}) collective-permute-start(f32[40,128]{1,0:T(8,128)S(1)} %collective-permute-done.3.refs_1_), channel_id=1, source_target_pairs={{0,1},{1,0},{2,3},{3,2},{4,5},{5,4},{6,7},{7,6},{8,9},{9,8},{10,11... | collective-permute-start | bytes 61448 | tf_op jit(solution)/shard_map/ppermute | solution.py:291
  14.9 7.1 %collective-permute-start.13 = (f32[264,128]{1,0:T(8,128)S(1)}, f32[264,128]{1,0:T(8,128)S(1)}, u32[]{:S(2)}, u32[]{:S(2)}) collective-permute-start(f32[264,128]{1,0:T(8,128)S(1)} %get-tuple-element.16.refs_0_), channel_id=1, source_target_pairs={{0,6},{1,25},{2,4},{3,27},{4,2},{5,29},{6,0},{7,31},{8,14},{9,17},... | collective-permute-start | bytes 405512 | tf_op jit(solution)/shard_map/ppermute | solution.py:300
  16.2 8.4 %collective-permute-start.12 = (f32[264,128]{1,0:T(8,128)S(1)}, f32[264,128]{1,0:T(8,128)S(1)}, u32[]{:S(2)}, u32[]{:S(2)}) collective-permute-start(f32[264,128]{1,0:T(8,128)S(1)} %get-tuple-element.16.refs_0_), channel_id=1, source_target_pairs={{0,4},{1,17},{2,6},{3,19},{4,0},{5,21},{6,2},{7,23},{8,12},{9,25},... | collective-permute-start | bytes 405512 | tf_op jit(solution)/shard_map/ppermute | solution.py:300
  16.9 7.8 %collective-permute-start.11 = (f32[264,128]{1,0:T(8,128)S(1)}, f32[264,128]{1,0:T(8,128)S(1)}, u32[]{:S(2)}, u32[]{:S(2)}) collective-permute-start(f32[264,128]{1,0:T(8,128)S(1)} %get-tuple-element.16.refs_0_), channel_id=1, source_target_pairs={{0,2},{1,9},{2,0},{3,11},{4,6},{5,13},{6,4},{7,15},{8,10},{9,1},{1... | collective-permute-start | bytes 405512 | tf_op jit(solution)/shard_map/ppermute | solution.py:300
  24.9 1.3 %collective-permute-start.14 = (f32[168,128]{1,0:T(8,128)S(1)}, f32[168,128]{1,0:T(8,128)S(1)}, u32[]{:S(2)}, u32[]{:S(2)}) collective-permute-start(f32[168,128]{1,0:T(8,128)S(1)} %get-tuple-element.19.mine_ref.refs_4_.send_ref), channel_id=1, source_target_pairs={{0,1},{1,0},{2,3},{3,2},{4,5},{5,4},{6,7},{7,6},{8,9},{9,8},{10,11... | collective-permute-start | bytes 258056 | tf_op jit(solution)/shard_map/ppermute | solution.py:291
  26.9 6.2 %collective-permute-start.17 = (f32[136,128]{1,0:T(8,128)S(1)}, f32[136,128]{1,0:T(8,128)S(1)}, u32[]{:S(2)}, u32[]{:S(2)}) collective-permute-start(f32[136,128]{1,0:T(8,128)S(1)} %shard_map.70.refs_0_), channel_id=1, source_target_pairs={{0,6},{1,25},{2,4},{3,27},{4,2},{5,29},{6,0},{7,31},{8,14},{9,17},... | collective-permute-start | bytes 208904 | tf_op jit(solution)/shard_map/ppermute | solution.py:300
  29.4 5.2 %collective-permute-start.16 = (f32[136,128]{1,0:T(8,128)S(1)}, f32[136,128]{1,0:T(8,128)S(1)}, u32[]{:S(2)}, u32[]{:S(2)}) collective-permute-start(f32[136,128]{1,0:T(8,128)S(1)} %shard_map.70.refs_0_), channel_id=1, source_target_pairs={{0,4},{1,17},{2,6},{3,19},{4,0},{5,21},{6,2},{7,23},{8,12},{9,25},... | collective-permute-start | bytes 208904 | tf_op jit(solution)/shard_map/ppermute | solution.py:300
  29.4 5.2 %collective-permute-start.15 = (f32[136,128]{1,0:T(8,128)S(1)}, f32[136,128]{1,0:T(8,128)S(1)}, u32[]{:S(2)}, u32[]{:S(2)}) collective-permute-start(f32[136,128]{1,0:T(8,128)S(1)} %shard_map.70.refs_0_), channel_id=1, source_target_pairs={{0,2},{1,9},{2,0},{3,11},{4,6},{5,13},{6,4},{7,15},{8,10},{9,1},{1... | collective-permute-start | bytes 208904 | tf_op jit(solution)/shard_map/ppermute | solution.py:300
  34.8 1.3 %collective-permute-start.18 = (f32[136,128]{1,0:T(8,128)S(1)}, f32[136,128]{1,0:T(8,128)S(1)}, u32[]{:S(2)}, u32[]{:S(2)}) collective-permute-start(f32[136,128]{1,0:T(8,128)S(1)} %get-tuple-element.23.mine_ref.second_ref), channel_id=1, source_target_pairs={{0,1},{1,0},{2,3},{3,2},{4,5},{5,4},{6,7},{7,6},{8,9},{9,8},{10,11... | collective-permute-start | bytes 208904 | tf_op jit(solution)/shard_map/ppermute | solution.py:291

commit v5 on v4

--- a/solution.py
+++ b/solution.py
@@ -9,6 +9,9 @@
 
 AXES = ("stu", "que")
 LANES = 128
+GATHER_ORDER = (1, 3, 2)
+FIRST_ORDER = (1, 3, 2)
+SECOND_ORDER = (2, 1, 3)
 BIAS = 8
 
 
@@ -63,8 +66,12 @@
     return jnp.where(low, value[:half], turn(value[half:]))
 
 
-def bias_rows(lanes, mine):
-    return jnp.where(mine, jnp.concatenate([lanes[:, :LANES], lanes[:, LANES:]], 0), 0.0)
+def bias_rows(lanes):
+    return jnp.concatenate([lanes[:, :LANES], lanes[:, LANES:]], 0)
+
+
+def bias_lanes(rows):
+    return jnp.concatenate([rows[0:1], rows[1:2]], 1)
 
 
 def column(rows):
@@ -97,17 +104,17 @@
     size = dst_ref.shape[0] // (2 * group)
     lane = lax.broadcasted_iota(jnp.int32, (size, LANES), 1)
     half = LANES // 2
-    for k, block in enumerate(blocks):
+    for at, (k, block) in enumerate(blocks):
         for j in range(2):
             value = turn(block[:size]) if j else block[:size]
-            last = jnp.where(side == 0, 1.0, columns[j * half : j * half + size, k : k + 1])
-            at = block_of(side, core ^ j, line ^ k, plane ^ k, group) * size
-            dst_ref[pl.ds(pl.multiple_of(at, size), size), :] = jnp.where(
+            last = jnp.where(side == 0, 1.0, columns[j * half : j * half + size, at : at + 1])
+            row = block_of(side, core ^ j, line ^ k, plane ^ k, group) * size
+            dst_ref[pl.ds(pl.multiple_of(row, size), size), :] = jnp.where(
                 lane < half, value, jnp.where(lane == half, last, 0.0)
             )
 
 
-def gradient_kernel(group, parts, *refs):
+def gradient_kernel(group, places, parts, *refs):
     code_ref, sums_ref, left_ref, right_ref, weight_ref, icpt_ref = refs[2 * parts :]
     core, line, plane = position()
     size = left_ref.shape[0] // (2 * group)
@@ -115,8 +122,8 @@
     other = pieces(refs[parts : 2 * parts], size)
     rows = [jnp.where(core == 0, there[size : size + 1], here[size : size + 1]) for here, there in zip(mine, other)]
     columns = jnp.concatenate(rows + [jnp.zeros((LANES - group, LANES), jnp.float32)], 0).T
-    place(mine, left_ref, core, columns, core, line, plane, group)
-    place(other, right_ref, 1 - core, columns, 1 - core, line, plane, group)
+    place(list(zip(places, mine)), left_ref, core, columns, core, line, plane, group)
+    place(list(zip(places, other)), right_ref, 1 - core, columns, 1 - core, line, plane, group)
     left = left_ref[...]
     right = right_ref[...]
     prob = 1.0 / (1.0 + jnp.exp(-dot_nt(left, right)))
@@ -129,21 +136,22 @@
     grad = dot_nn(resid, right)
     diag = dot_nn(weight, right * right)
     sums_ref[:rows, :] = jnp.where(low_lanes((rows, LANES)), grad, turn(diag))
-    lane = lax.broadcasted_iota(jnp.int32, (rows, LANES), 1)
     at = LANES // 2
-    extra = jnp.where(lane == at, grad, jnp.where(lane == at + 1, pltpu.roll(diag, 1, 1), pltpu.roll(left, 2, 1)))
-    lanes = extra.T
-    mine = core == 1
-    sums_ref[rows:, :] = jnp.concatenate(
-        [
-            bias_rows(lanes[at : at + 1], mine),
-            bias_rows(lanes[at + 1 : at + 2], mine),
-            jnp.zeros((BIAS - 4, LANES), jnp.float32),
-        ],
-        0,
-    )
-    icpt = bias_rows(lanes[at + 2 : at + 3], mine)
-    icpt_ref[...] = jnp.concatenate([icpt, jnp.zeros((BIAS - 2, LANES), jnp.float32)], 0)
+
+    @pl.when(core == 0)
+    def _():
+        sums_ref[rows:, :] = jnp.zeros((BIAS, LANES), jnp.float32)
+        icpt_ref[...] = jnp.zeros((BIAS, LANES), jnp.float32)
+
+    @pl.when(core == 1)
+    def _():
+        lane = lax.broadcasted_iota(jnp.int32, (rows, LANES), 1)
+        moved = jnp.where(lane == at + 1, pltpu.roll(diag, 1, 1), pltpu.roll(left, 2, 1))
+        lanes = jnp.where(lane == at, grad, moved).T
+        spare = jnp.zeros((BIAS - 4, LANES), jnp.float32)
+        sums_ref[rows:, :] = jnp.concatenate([bias_rows(lanes[at : at + 1]), bias_rows(lanes[at + 1 : at + 2]), spare], 0)
+        spare = jnp.zeros((BIAS - 2, LANES), jnp.float32)
+        icpt_ref[...] = jnp.concatenate([bias_rows(lanes[at + 2 : at + 3]), spare], 0)
 
 
 def start_kernel(group, parts, *refs):
@@ -191,21 +199,38 @@
         ],
         0,
     )
-    lanes = jnp.concatenate([other_ref[half : half + 1, :], other_ref[half + 1 : half + 2, :]], 1)
-    return dot_nt(lhs, rhs) + lanes + column(mine_ref[half : half + 2, :])
+    return dot_nt(lhs, rhs)
+
+
+def with_bias(change, mine_ref, other_ref, half, use):
+    core, _, _ = position()
+
+    @pl.when(core == 0)
+    def _():
+        use(change + bias_lanes(other_ref[half : half + 2, :]))
+
+    @pl.when(core == 1)
+    def _():
+        use(change + column(mine_ref[half : half + 2, :]))
 
 
 def image_kernel(mine_ref, other_ref, left_ref, right_ref, weight_ref, sums_ref):
     core, _, _ = position()
-    rows = left_ref.shape[0]
-    half = rows // 2
+    half = left_ref.shape[0] // 2
     right = right_ref[...]
-    scaled = weight_ref[...] * change_of(mine_ref, other_ref, left_ref[...], right, half)
-    sums = dot_nn(scaled, right)
-    sums_ref[:half, :] = pack(sums)
+    change = change_of(mine_ref, other_ref, left_ref[...], right, half)
     at = LANES // 2
-    bias = bias_rows(sums.T[at : at + 1], core == 1)
-    sums_ref[half:, :] = jnp.concatenate([bias, jnp.zeros((BIAS - 2, LANES), jnp.float32)], 0)
+
+    def use(value):
+        sums = dot_nn(weight_ref[...] * value, right)
+        sums_ref[:half, :] = pack(sums)
+        sums_ref[half:, :] = jnp.zeros((BIAS, LANES), jnp.float32)
+
+        @pl.when(core == 1)
+        def _():
+            sums_ref[half : half + 2, :] = bias_rows(sums.T[at : at + 1])
+
+    with_bias(change, mine_ref, other_ref, half, use)
 
 
 def second_kernel(group, parts, *refs):
@@ -232,10 +257,14 @@
 def form_kernel(mine_ref, other_ref, left_ref, right_ref, weight_ref, dots_ref, out_ref):
     half = left_ref.shape[0] // 2
     change = change_of(mine_ref, other_ref, left_ref[...], right_ref[...], half)
-    form = 0.5 * jnp.sum(weight_ref[...] * change * change)
-    lane = lax.broadcasted_iota(jnp.int32, (1, LANES), 1)
-    value = dots_ref[0:1, :] + jnp.where(lane == 3, form, 0.0)
-    out_ref[...] = jnp.broadcast_to(value[None], out_ref.shape)
+
+    def use(value):
+        form = 0.5 * jnp.sum(weight_ref[...] * value * value)
+        lane = lax.broadcasted_iota(jnp.int32, (1, LANES), 1)
+        dots = dots_ref[0:1, :] + jnp.where(lane == 3, form, 0.0)
+        out_ref[...] = jnp.broadcast_to(dots[None], out_ref.shape)
+
+    with_bias(change, mine_ref, other_ref, half, use)
 
 
 def finish_kernel(
@@ -300,11 +329,11 @@
     return lax.ppermute(value, AXES, pairs)
 
 
-def stages(group):
+def stages(group, order):
     base = 1
     while base < group:
         width = min(4, group // base)
-        yield [base * k for k in range(1, width)]
+        yield [base * k for k in order if k < width]
         base *= width
 
 
@@ -328,27 +357,29 @@
     )
     (code,) = call(arrange_kernel, [(rows, rows)], codes, swap(codes))
     mine = [mine]
-    for steps in stages(group):
+    places = [0]
+    for steps in stages(group, GATHER_ORDER):
         joined = jnp.concatenate(mine, 0)
         mine = mine + [send(joined, step) for step in steps]
+        places = places + [step + place for step in steps for place in places]
     other = [swap(piece) for piece in mine]
 
-    def totals(value):
+    def totals(value, order):
         parts = [value]
-        for number, steps in enumerate(stages(group)):
+        for number, steps in enumerate(stages(group, order)):
             if number:
                 parts = [functools.reduce(jnp.add, parts)]
             parts = parts + [send(parts[0], step) for step in steps]
         return parts
 
     sums, left, right, weight, icpt = call(
-        functools.partial(gradient_kernel, group, len(mine)),
+        functools.partial(gradient_kernel, group, tuple(places), len(mine)),
         [(rows + BIAS, LANES), (rows, LANES), (rows, LANES), (rows, rows), (BIAS, LANES)],
         *mine,
         *other,
         code,
     )
-    parts = totals(sums)
+    parts = totals(sums, FIRST_ORDER)
     first, diag, root = call(
         functools.partial(start_kernel, group, len(parts)),
         [(half + BIAS + size, LANES), (half + BIAS, LANES), (rows, LANES)],
@@ -358,7 +389,7 @@
     )
     peer = swap(first)
     (sums,) = call(image_kernel, [(half + BIAS, LANES)], first, peer, left, right, weight)
-    parts = totals(sums)
+    parts = totals(sums, SECOND_ORDER)
     second, dots = call(
         functools.partial(second_kernel, group, len(parts)),
         [(half + BIAS, LANES), (8, LANES)],

time: 49.2 us -> 48.6 us (0.988)
  starting transfers between devices: 16.2 us -> 15.6 us
  waiting for transfers between devices: 16.2 us -> 16.7 us
    ppermute x9, starting transfers between devices: 14.5 us -> 13.5 us  [send_over(): return lax.ppermute(value, AXES, pairs)]
    ppermute x9, waiting for transfers between devices: 12.6 us -> 13.1 us  [send_over(): return lax.ppermute(value, AXES, pairs)]
  transfers between devices with their start and end apart: 19 -> 19, of which waited for: 11 -> 12; matrix products, arithmetic and copies ran while one was open for 2% -> 2% of each run, Pallas kernels for 0% -> 0%
where the time goes in v5:
time: 48.6 us; the launch traced here: 48.4 us
  waiting for transfers between devices  16.7 us (34%)
  starting transfers between devices  15.6 us (32%)
  blocking collectives  11.2 us (23%)
  Pallas kernels  3.25 us (7%)
  other arithmetic  0.75 us (2%)
  between operations  0.75 us (2%)
    ppermute x9, starting transfers between devices, send_over(): return lax.ppermute(value, AXES, pairs)  13.5 us
    ppermute x9, waiting for transfers between devices, send_over(): return lax.ppermute(value, AXES, pairs)  13.1 us
    all_to_all x1, blocking collectives, shards(): dots = lax.all_to_all(dots, AXES, 0, 0, tiled=True)  11.2 us
    ppermute x10, waiting for transfers between devices, swap_cores(): return lax.ppermute(value, AXES, [(i, i ^ 1) for i in range(n_stu * n_que)])  3.58 us
    pallas_call x7, Pallas kernels, call(): pl.pallas_call(kernel, out_shape=out, in_specs=[pl.BlockSpec(memory_space...  3.25 us
    ppermute x10, starting transfers between devices, swap_cores(): return lax.ppermute(value, AXES, [(i, i ^ 1) for i in range(n_stu * n_que)])  2.1 us
  transfers between devices with their start and end apart: 19, of which 12 were waited for; matrix products, arithmetic and copies ran while one was open for 2% of the time, Pallas kernels for 0%

profile of v5, /device:TPU:0, one launch (start us, length us, event | category | flops | bytes accessed | tf_op | source)
XLA Modules:
  0.0 48.4 jit_solution(14613446719949899740)
XLA Ops:
  0.7 0.5 %collective-permute-start.2 = (f32[32]{0:T(128)}, f32[32]{0:T(128)S(1)}, u32[]{:S(2)}, u32[]{:S(2)}) collective-permute-start(f32[32]{0:T(128)} %param.7), channel_id=1, source_target_pairs={{0,1},{1,0},{2,3},{3,2},{4,5},{5,4},{6,7},{7,6},{8,9},{9,8},{10,11... | collective-permute-start | bytes 392 | tf_op jit(solution)/shard_map/ppermute | solution.py:320
  1.2 0.4 collective-permute-start.1
  1.9 0.3 collective-permute-done.2
  2.1 0.7 %select_maximum_fusion = f32[2,64]{1,0:T(2,128)S(1)} fusion(f32[1,32]{1,0:T(1,128)S(1)} %bitcast.4, f32[1,32]{1,0:T(1,128)} %bitcast.3), kind=kLoop, calls=%fused_computation.3 | loop fusion | flops 512 | bytes 768 | tf_op jit(solution)/shard_map/stack | solution.py:354
  3.0 3.9 %collective-permute-start.5 = (f32[40,128]{1,0:T(8,128)S(1)}, f32[40,128]{1,0:T(8,128)S(1)}, u32[]{:S(2)}, u32[]{:S(2)}) collective-permute-start(f32[40,128]{1,0:T(8,128)S(1)} %maximum_maximum_fusion.refs_0_), channel_id=1, source_target_pairs={{0,4},{1,17},{2,6},{3,19},{4,0},{5,21},{6,2},{7,23},{8,12},{9,25},... | collective-permute-start | bytes 61448 | tf_op jit(solution)/shard_map/ppermute | solution.py:329
  6.9 1.3 %collective-permute-start.4 = (f32[40,128]{1,0:T(8,128)S(1)}, f32[40,128]{1,0:T(8,128)S(1)}, u32[]{:S(2)}, u32[]{:S(2)}) collective-permute-start(f32[40,128]{1,0:T(8,128)S(1)} %maximum_maximum_fusion.refs_0_), channel_id=1, source_target_pairs={{0,6},{1,25},{2,4},{3,27},{4,2},{5,29},{6,0},{7,31},{8,14},{9,17},... | collective-permute-start | bytes 61448 | tf_op jit(solution)/shard_map/ppermute | solution.py:329
  8.2 0.2 collective-permute-start.3
  8.4 0.2 collective-permute-done.5.refs_3_
  8.6 0.3 collective-permute-start.9
  9.0 3.5 %collective-permute-done.4.refs_2_ = f32[40,128]{1,0:T(8,128)S(1)} collective-permute-done((f32[40,128]{1,0:T(8,128)S(1)}, f32[40,128]{1,0:T(8,128)S(1)}, u32[]{:S(2)}, u32[]{:S(2)}) %collective-permute-start.4) | collective-permute-done | bytes 20512 | tf_op jit(solution)/shard_map/ppermute | solution.py:329
  12.4 0.5 %collective-permute-start.7 = (f32[40,128]{1,0:T(8,128)S(1)}, f32[40,128]{1,0:T(8,128)S(1)}, u32[]{:S(2)}, u32[]{:S(2)}) collective-permute-start(f32[40,128]{1,0:T(8,128)S(1)} %collective-permute-done.3.refs_1_), channel_id=1, source_target_pairs={{0,1},{1,0},{2,3},{3,2},{4,5},{5,4},{6,7},{7,6},{8,9},{9,8},{10,11... | collective-permute-start | bytes 61448 | tf_op jit(solution)/shard_map/ppermute | solution.py:320
  13.0 0.6 %collective-permute-done.8.refs_6_ = f32[40,128]{1,0:T(8,128)S(1)} collective-permute-done((f32[40,128]{1,0:T(8,128)S(1)}, f32[40,128]{1,0:T(8,128)S(1)}, u32[]{:S(2)}, u32[]{:S(2)}) %collective-permute-start.8) | collective-permute-done | bytes 20512 | tf_op jit(solution)/shard_map/ppermute | solution.py:320
  13.6 0.2 collective-permute-done.7.refs_5_
  13.8 0.9 %shard_map.68 = (f32[264,128]{1,0:T(8,128)S(1)}, f32[256,128]{1,0:T(8,128)S(1)}, f32[256,128]{1,0:T(8,128)S(1)}, f32[256,256]{1,0:T(8,128)S(1)}, f32[8,128]{1,0:T(8,128)S(1)}) custom-call(f32[40,128]{1,0:T(8,128)S(1)} %maximum_maximum_fusion.refs_0_, f32[40,128]{1,0:T(8,128)S(1)} %collective-permute-done.3.refs_1_, ...), custom_call_target="tpu_custom_call" | custom-call | tf_op jit(solution)/shard_map/pallas_call | solution.py:310
  14.7 1.1 %collective-permute-start.13 = (f32[264,128]{1,0:T(8,128)S(1)}, f32[264,128]{1,0:T(8,128)S(1)}, u32[]{:S(2)}, u32[]{:S(2)}) collective-permute-start(f32[264,128]{1,0:T(8,128)S(1)} %get-tuple-element.16.refs_0_), channel_id=1, source_target_pairs={{0,4},{1,17},{2,6},{3,19},{4,0},{5,21},{6,2},{7,23},{8,12},{9,25},... | collective-permute-start | bytes 405512 | tf_op jit(solution)/shard_map/ppermute | solution.py:329
  15.9 1.1 %collective-permute-start.12 = (f32[264,128]{1,0:T(8,128)S(1)}, f32[264,128]{1,0:T(8,128)S(1)}, u32[]{:S(2)}, u32[]{:S(2)}) collective-permute-start(f32[264,128]{1,0:T(8,128)S(1)} %get-tuple-element.16.refs_0_), channel_id=1, source_target_pairs={{0,6},{1,25},{2,4},{3,27},{4,2},{5,29},{6,0},{7,31},{8,14},{9,17},... | collective-permute-start | bytes 405512 | tf_op jit(solution)/shard_map/ppermute | solution.py:329
  16.9 1.3 %collective-permute-start.11 = (f32[264,128]{1,0:T(8,128)S(1)}, f32[264,128]{1,0:T(8,128)S(1)}, u32[]{:S(2)}, u32[]{:S(2)}) collective-permute-start(f32[264,128]{1,0:T(8,128)S(1)} %get-tuple-element.16.refs_0_), channel_id=1, source_target_pairs={{0,2},{1,9},{2,0},{3,11},{4,6},{5,13},{6,4},{7,15},{8,10},{9,1},{1... | collective-permute-start | bytes 405512 | tf_op jit(solution)/shard_map/ppermute | solution.py:329
  18.3 4.6 %collective-permute-done.13.refs_3_ = f32[264,128]{1,0:T(8,128)S(1)} collective-permute-done((f32[264,128]{1,0:T(8,128)S(1)}, f32[264,128]{1,0:T(8,128)S(1)}, u32[]{:S(2)}, u32[]{:S(2)}) %collective-permute-start.13) | collective-permute-done | bytes 135200 | tf_op jit(solution)/shard_map/ppermute | solution.py:329
  22.9 1.3 %collective-permute-done.11.refs_1_ = f32[264,128]{1,0:T(8,128)S(1)} collective-permute-done((f32[264,128]{1,0:T(8,128)S(1)}, f32[264,128]{1,0:T(8,128)S(1)}, u32[]{:S(2)}, u32[]{:S(2)}) %collective-permute-start.11) | collective-permute-done | bytes 135200 | tf_op jit(solution)/shard_map/ppermute | solution.py:329
  24.3 0.2 shard_map.69
  24.5 1.3 %collective-permute-done.14.other_ref.peer_ref = f32[168,128]{1,0:T(8,128)S(1)} collective-permute-done((f32[168,128]{1,0:T(8,128)S(1)}, f32[168,128]{1,0:T(8,128)S(1)}, u32[]{:S(2)}, u32[]{:S(2)}) %collective-permute-start.14) | collective-permute-done | bytes 86048 | tf_op jit(solution)/shard_map/ppermute | solution.py:320
  25.8 0.6 %shard_map.70.refs_0_ = f32[136,128]{1,0:T(8,128)S(1)} custom-call(f32[168,128]{1,0:T(8,128)S(1)} %get-tuple-element.19.mine_ref.refs_4_.send_ref, f32[168,128]{1,0:T(8,128)S(1)} %collective-permute-done.14.other_ref.peer_ref, f32[256,128]{1,0:T(8,128)S(1)} %get-tuple-element.17.refs_4_.left_ref, f32[256,128]{1,0:T(8,128)S(1)} %get-tuple-element.20.right_ref, ...), custom_call_target="tpu_custom_call" | custom-call | tf_op jit(solution)/shard_map/pallas_call | solution.py:310
  26.4 2.7 %collective-permute-start.17 = (f32[136,128]{1,0:T(8,128)S(1)}, f32[136,128]{1,0:T(8,128)S(1)}, u32[]{:S(2)}, u32[]{:S(2)}) collective-permute-start(f32[136,128]{1,0:T(8,128)S(1)} %shard_map.70.refs_0_), channel_id=1, source_target_pairs={{0,6},{1,25},{2,4},{3,27},{4,2},{5,29},{6,0},{7,31},{8,14},{9,17},... | collective-permute-start | bytes 208904 | tf_op jit(solution)/shard_map/ppermute | solution.py:329
  29.1 1.7 %collective-permute-start.15 = (f32[136,128]{1,0:T(8,128)S(1)}, f32[136,128]{1,0:T(8,128)S(1)}, u32[]{:S(2)}, u32[]{:S(2)}) collective-permute-start(f32[136,128]{1,0:T(8,128)S(1)} %shard_map.70.refs_0_), channel_id=1, source_target_pairs={{0,4},{1,17},{2,6},{3,19},{4,0},{5,21},{6,2},{7,23},{8,12},{9,25},... | collective-permute-start | bytes 208904 | tf_op jit(solution)/shard_map/ppermute | solution.py:329
  30.9 1.7 %collective-permute-done.17.refs_3_ = f32[136,128]{1,0:T(8,128)S(1)} collective-permute-done((f32[136,128]{1,0:T(8,128)S(1)}, f32[136,128]{1,0:T(8,128)S(1)}, u32[]{:S(2)}, u32[]{:S(2)}) %collective-permute-start.17) | collective-permute-done | bytes 69664 | tf_op jit(solution)/shard_map/ppermute | solution.py:329
  32.6 0.8 %collective-permute-done.16.refs_2_ = f32[136,128]{1,0:T(8,128)S(1)} collective-permute-done((f32[136,128]{1,0:T(8,128)S(1)}, f32[136,128]{1,0:T(8,128)S(1)}, u32[]{:S(2)}, u32[]{:S(2)}) %collective-permute-start.16) | collective-permute-done | bytes 69664 | tf_op jit(solution)/shard_map/ppermute | solution.py:329
  33.5 0.9 %collective-permute-done.15.refs_1_ = f32[136,128]{1,0:T(8,128)S(1)} collective-permute-done((f32[136,128]{1,0:T(8,128)S(1)}, f32[136,128]{1,0:T(8,128)S(1)}, u32[]{:S(2)}, u32[]{:S(2)}) %collective-permute-start.15) | collective-permute-done | bytes 69664 | tf_op jit(solution)/shard_map/ppermute | solution.py:329
  34.4 0.2 shard_map.71
  34.6 1.2 %collective-permute-done.18.other_ref.peer_second_ref = f32[136,128]{1,0:T(8,128)S(1)} collective-permute-done((f32[136,128]{1,0:T(8,128)S(1)}, f32[136,128]{1,0:T(8,128)S(1)}, u32[]{:S(2)}, u32[]{:S(2)}) %collective-permute-start.18) | collective-permute-done | bytes 69664 | tf_op jit(solution)/shard_map/ppermute | solution.py:320
  35.9 0.5 %shard_map.72 = f32[32,1,128]{2,1,0:T(1,128)S(1)} custom-call(f32[136,128]{1,0:T(8,128)S(1)} %get-tuple-element.23.mine_ref.second_ref, f32[136,128]{1,0:T(8,128)S(1)} %collective-permute-done.18.other_ref.peer_second_ref, f32[256,128]{1,0:T(8,128)S(1)} %get-tuple-element.17.refs_4_.left_ref, f32[256,128]{1,0:T(8,128)S(1)} %get-tuple-element.20.right_ref, ...), custom_call_target="tpu_custom_call" | custom-call | tf_op jit(solution)/shard_map/pallas_call | solution.py:310
  36.4 11.2 %all_to_all.5.dots_ref = f32[32,1,128]{2,1,0:T(1,128)S(1)} all-to-all(f32[32,1,128]{2,1,0:T(1,128)S(1)} %shard_map.72), channel_id=1, replica_groups=mesh['stu'=4,'que'=8] {'stu','que'}, dimensions={0} | all-to-all | bytes 32768 | tf_op jit(solution)/shard_map/all_to_all | solution.py:403
  47.6 0.8 %shard_map.73 = (f32[32,64]{1,0:T(8,128)}, f32[32,64]{1,0:T(8,128)}, f32[1,32]{1,0:T(1,128)}) custom-call(f32[32,1,128]{2,1,0:T(1,128)S(1)} %all_to_all.5.dots_ref, f32[168,128]{1,0:T(8,128)S(1)} %get-tuple-element.19.mine_ref.refs_4_.send_ref, f32[168,128]{1,0:T(8,128)S(1)} %collective-permute-done.14.other_ref.peer_ref, ...), custom_call_target="tpu_custom_call" | custom-call | tf_op jit(solution)/shard_map/pallas_call | solution.py:310
  (25 shorter events, 0.6 us)
Async XLA Ops:
  0.6 1.1 %copy-start.1 = (f32[32,64]{1,0:T(8,128)S(1)}, f32[32,64]{1,0:T(8,128)}, u32[]{:S(2)}) copy-start(f32[32,64]{1,0:T(8,128)} %param.5) | copy-start | bytes 24580
  0.6 12.3 %copy-start = (s32[256,128]{1,0:T(8,128)S(1)}, s32[256,128]{1,0:T(8,128)}, u32[]{:S(2)}) copy-start(s32[256,128]{1,0:T(8,128)} %own_ref.1) | copy-start | bytes 393220
  0.7 1.5 %collective-permute-start.2 = (f32[32]{0:T(128)}, f32[32]{0:T(128)S(1)}, u32[]{:S(2)}, u32[]{:S(2)}) collective-permute-start(f32[32]{0:T(128)} %param.7), channel_id=1, source_target_pairs={{0,1},{1,0},{2,3},{3,2},{4,5},{5,4},{6,7},{7,6},{8,9},{9,8},{10,11... | collective-permute-start | bytes 392 | tf_op jit(solution)/shard_map/ppermute | solution.py:320
  1.2 1.7 %collective-permute-start = (f32[32,64]{1,0:T(8,128)}, f32[32,64]{1,0:T(8,128)S(1)}, u32[]{:S(2)}, u32[]{:S(2)}) collective-permute-start(f32[32,64]{1,0:T(8,128)} %param.5), channel_id=1, source_target_pairs={{0,1},{1,0},{2,3},{3,2},{4,5},{5,4},{6,7},{7,6},{8,9},{9,8},{10,11... | collective-permute-start | bytes 24584 | tf_op jit(solution)/shard_map/ppermute | solution.py:320
  1.2 1.6 %collective-permute-start.1 = (f32[32,64]{1,0:T(8,128)}, f32[32,64]{1,0:T(8,128)S(1)}, u32[]{:S(2)}, u32[]{:S(2)}) collective-permute-start(f32[32,64]{1,0:T(8,128)} %param.6), channel_id=1, source_target_pairs={{0,1},{1,0},{2,3},{3,2},{4,5},{5,4},{6,7},{7,6},{8,9},{9,8},{10,11... | collective-permute-start | bytes 24584 | tf_op jit(solution)/shard_map/ppermute | solution.py:320
  1.7 11.3 %collective-permute-start.10 = (s32[256,128]{1,0:T(8,128)}, s32[256,128]{1,0:T(8,128)S(1)}, u32[]{:S(2)}, u32[]{:S(2)}) collective-permute-start(s32[256,128]{1,0:T(8,128)} %own_ref.1), channel_id=1, source_target_pairs={{0,1},{1,0},{2,3},{3,2},{4,5},{5,4},{6,7},{7,6},{8,9},{9,8},{10,11... | collective-permute-start | bytes 393224 | tf_op jit(solution)/shard_map/ppermute | solution.py:320
  3.0 5.7 %collective-permute-start.5 = (f32[40,128]{1,0:T(8,128)S(1)}, f32[40,128]{1,0:T(8,128)S(1)}, u32[]{:S(2)}, u32[]{:S(2)}) collective-permute-start(f32[40,128]{1,0:T(8,128)S(1)} %maximum_maximum_fusion.refs_0_), channel_id=1, source_target_pairs={{0,4},{1,17},{2,6},{3,19},{4,0},{5,21},{6,2},{7,23},{8,12},{9,25},... | collective-permute-start | bytes 61448 | tf_op jit(solution)/shard_map/ppermute | solution.py:329
  6.9 5.6 %collective-permute-start.4 = (f32[40,128]{1,0:T(8,128)S(1)}, f32[40,128]{1,0:T(8,128)S(1)}, u32[]{:S(2)}, u32[]{:S(2)}) collective-permute-start(f32[40,128]{1,0:T(8,128)S(1)} %maximum_maximum_fusion.refs_0_), channel_id=1, source_target_pairs={{0,6},{1,25},{2,4},{3,27},{4,2},{5,29},{6,0},{7,31},{8,14},{9,17},... | collective-permute-start | bytes 61448 | tf_op jit(solution)/shard_map/ppermute | solution.py:329
  8.2 4.2 %collective-permute-start.3 = (f32[40,128]{1,0:T(8,128)S(1)}, f32[40,128]{1,0:T(8,128)S(1)}, u32[]{:S(2)}, u32[]{:S(2)}) collective-permute-start(f32[40,128]{1,0:T(8,128)S(1)} %maximum_maximum_fusion.refs_0_), channel_id=1, source_target_pairs={{0,2},{1,9},{2,0},{3,11},{4,6},{5,13},{6,4},{7,15},{8,10},{9,1},{1... | collective-permute-start | bytes 61448 | tf_op jit(solution)/shard_map/ppermute | solution.py:329
  8.4 4.6 %collective-permute-start.6 = (f32[40,128]{1,0:T(8,128)S(1)}, f32[40,128]{1,0:T(8,128)S(1)}, u32[]{:S(2)}, u32[]{:S(2)}) collective-permute-start(f32[40,128]{1,0:T(8,128)S(1)} %maximum_maximum_fusion.refs_0_), channel_id=1, source_target_pairs={{0,1},{1,0},{2,3},{3,2},{4,5},{5,4},{6,7},{7,6},{8,9},{9,8},{10,11... | collective-permute-start | bytes 61448 | tf_op jit(solution)/shard_map/ppermute | solution.py:320
  8.6 4.4 %collective-permute-start.9 = (f32[40,128]{1,0:T(8,128)S(1)}, f32[40,128]{1,0:T(8,128)S(1)}, u32[]{:S(2)}, u32[]{:S(2)}) collective-permute-start(f32[40,128]{1,0:T(8,128)S(1)} %collective-permute-done.5.refs_3_), channel_id=1, source_target_pairs={{0,1},{1,0},{2,3},{3,2},{4,5},{5,4},{6,7},{7,6},{8,9},{9,8},{10,11... | collective-permute-start | bytes 61448 | tf_op jit(solution)/shard_map/ppermute | solution.py:320
  12.4 1.2 %collective-permute-start.8 = (f32[40,128]{1,0:T(8,128)S(1)}, f32[40,128]{1,0:T(8,128)S(1)}, u32[]{:S(2)}, u32[]{:S(2)}) collective-permute-start(f32[40,128]{1,0:T(8,128)S(1)} %collective-permute-done.4.refs_2_), channel_id=1, source_target_pairs={{0,1},{1,0},{2,3},{3,2},{4,5},{5,4},{6,7},{7,6},{8,9},{9,8},{10,11... | collective-permute-start | bytes 61448 | tf_op jit(solution)/shard_map/ppermute | solution.py:320
  12.4 1.4 %collective-permute-start.7 = (f32[40,128]{1,0:T(8,128)S(1)}, f32[40,128]{1,0:T(8,128)S(1)}, u32[]{:S(2)}, u32[]{:S(2)}) collective-permute-start(f32[40,128]{1,0:T(8,128)S(1)} %collective-permute-done.3.refs_1_), channel_id=1, source_target_pairs={{0,1},{1,0},{2,3},{3,2},{4,5},{5,4},{6,7},{7,6},{8,9},{9,8},{10,11... | collective-permute-start | bytes 61448 | tf_op jit(solution)/shard_map/ppermute | solution.py:320
  14.7 8.2 %collective-permute-start.13 = (f32[264,128]{1,0:T(8,128)S(1)}, f32[264,128]{1,0:T(8,128)S(1)}, u32[]{:S(2)}, u32[]{:S(2)}) collective-permute-start(f32[264,128]{1,0:T(8,128)S(1)} %get-tuple-element.16.refs_0_), channel_id=1, source_target_pairs={{0,4},{1,17},{2,6},{3,19},{4,0},{5,21},{6,2},{7,23},{8,12},{9,25},... | collective-permute-start | bytes 405512 | tf_op jit(solution)/shard_map/ppermute | solution.py:329
  15.9 7.1 %collective-permute-start.12 = (f32[264,128]{1,0:T(8,128)S(1)}, f32[264,128]{1,0:T(8,128)S(1)}, u32[]{:S(2)}, u32[]{:S(2)}) collective-permute-start(f32[264,128]{1,0:T(8,128)S(1)} %get-tuple-element.16.refs_0_), channel_id=1, source_target_pairs={{0,6},{1,25},{2,4},{3,27},{4,2},{5,29},{6,0},{7,31},{8,14},{9,17},... | collective-permute-start | bytes 405512 | tf_op jit(solution)/shard_map/ppermute | solution.py:329
  16.9 7.3 %collective-permute-start.11 = (f32[264,128]{1,0:T(8,128)S(1)}, f32[264,128]{1,0:T(8,128)S(1)}, u32[]{:S(2)}, u32[]{:S(2)}) collective-permute-start(f32[264,128]{1,0:T(8,128)S(1)} %get-tuple-element.16.refs_0_), channel_id=1, source_target_pairs={{0,2},{1,9},{2,0},{3,11},{4,6},{5,13},{6,4},{7,15},{8,10},{9,1},{1... | collective-permute-start | bytes 405512 | tf_op jit(solution)/shard_map/ppermute | solution.py:329
  24.5 1.3 %collective-permute-start.14 = (f32[168,128]{1,0:T(8,128)S(1)}, f32[168,128]{1,0:T(8,128)S(1)}, u32[]{:S(2)}, u32[]{:S(2)}) collective-permute-start(f32[168,128]{1,0:T(8,128)S(1)} %get-tuple-element.19.mine_ref.refs_4_.send_ref), channel_id=1, source_target_pairs={{0,1},{1,0},{2,3},{3,2},{4,5},{5,4},{6,7},{7,6},{8,9},{9,8},{10,11... | collective-permute-start | bytes 258056 | tf_op jit(solution)/shard_map/ppermute | solution.py:320
  26.4 6.2 %collective-permute-start.17 = (f32[136,128]{1,0:T(8,128)S(1)}, f32[136,128]{1,0:T(8,128)S(1)}, u32[]{:S(2)}, u32[]{:S(2)}) collective-permute-start(f32[136,128]{1,0:T(8,128)S(1)} %shard_map.70.refs_0_), channel_id=1, source_target_pairs={{0,6},{1,25},{2,4},{3,27},{4,2},{5,29},{6,0},{7,31},{8,14},{9,17},... | collective-permute-start | bytes 208904 | tf_op jit(solution)/shard_map/ppermute | solution.py:329
  29.1 4.3 %collective-permute-start.16 = (f32[136,128]{1,0:T(8,128)S(1)}, f32[136,128]{1,0:T(8,128)S(1)}, u32[]{:S(2)}, u32[]{:S(2)}) collective-permute-start(f32[136,128]{1,0:T(8,128)S(1)} %shard_map.70.refs_0_), channel_id=1, source_target_pairs={{0,2},{1,9},{2,0},{3,11},{4,6},{5,13},{6,4},{7,15},{8,10},{9,1},{1... | collective-permute-start | bytes 208904 | tf_op jit(solution)/shard_map/ppermute | solution.py:329
  29.1 5.2 %collective-permute-start.15 = (f32[136,128]{1,0:T(8,128)S(1)}, f32[136,128]{1,0:T(8,128)S(1)}, u32[]{:S(2)}, u32[]{:S(2)}) collective-permute-start(f32[136,128]{1,0:T(8,128)S(1)} %shard_map.70.refs_0_), channel_id=1, source_target_pairs={{0,4},{1,17},{2,6},{3,19},{4,0},{5,21},{6,2},{7,23},{8,12},{9,25},... | collective-permute-start | bytes 208904 | tf_op jit(solution)/shard_map/ppermute | solution.py:329
  34.5 1.3 %collective-permute-start.18 = (f32[136,128]{1,0:T(8,128)S(1)}, f32[136,128]{1,0:T(8,128)S(1)}, u32[]{:S(2)}, u32[]{:S(2)}) collective-permute-start(f32[136,128]{1,0:T(8,128)S(1)} %get-tuple-element.23.mine_ref.second_ref), channel_id=1, source_target_pairs={{0,1},{1,0},{2,3},{3,2},{4,5},{5,4},{6,7},{7,6},{8,9},{9,8},{10,11... | collective-permute-start | bytes 208904 | tf_op jit(solution)/shard_map/ppermute | solution.py:320

commit v6 on v5

--- a/solution.py
+++ b/solution.py
@@ -320,11 +320,11 @@
     return lax.ppermute(value, AXES, [(i, i ^ 1) for i in range(n_stu * n_que)])
 
 
-def send_over(value, step, n_stu, n_que):
+def send_over(value, step, n_stu, n_que, crossed=False):
     pairs = []
     for stu in range(n_stu):
         for que in range(n_que):
-            there = (stu, que ^ (2 * step)) if que % 2 == 0 else (stu ^ step, que)
+            there = (stu, que ^ (2 * step)) if (que % 2 == 0) != crossed else (stu ^ step, que)
             pairs.append((stu * n_que + que, there[0] * n_que + there[1]))
     return lax.ppermute(value, AXES, pairs)
 
@@ -349,20 +349,28 @@
     assert disc.shape == theta.shape and codes.shape == (rows, half)
     core = lax.rem(lax.axis_index("que"), 2)
     peer_theta, peer_disc, peer_icpt = swap(theta), swap(disc), swap(intercept)
-    here = jnp.where(core == 0, theta, disc)
-    there = jnp.where(core == 0, peer_theta, peer_disc)
-    icpt = jnp.pad(jnp.stack([intercept, peer_icpt]), ((0, 0), (0, width - size))).reshape(1, LANES)
-    mine = jnp.concatenate(
-        [jnp.concatenate([here, there], 1), icpt, jnp.zeros((BIAS - 1, LANES), jnp.float32)], 0
-    )
+
+    def block(own, own_icpt, peers, peers_icpt):
+        icpt = jnp.pad(jnp.stack([own_icpt, peers_icpt]), ((0, 0), (0, width - size))).reshape(1, LANES)
+        spare = jnp.zeros((BIAS - 1, LANES), jnp.float32)
+        return jnp.concatenate([jnp.concatenate([own, peers], 1), icpt, spare], 0)
+
+    def side(students, questions):
+        return jnp.where(core == 0, students, questions)
+
+    mine = [block(side(theta, disc), intercept, side(peer_theta, peer_disc), peer_icpt)]
+    other = [block(side(peer_disc, peer_theta), peer_icpt, side(disc, theta), intercept)]
     (code,) = call(arrange_kernel, [(rows, rows)], codes, swap(codes))
-    mine = [mine]
     places = [0]
     for steps in stages(group, GATHER_ORDER):
-        joined = jnp.concatenate(mine, 0)
-        mine = mine + [send(joined, step) for step in steps]
+        ours, theirs = jnp.concatenate(mine, 0), jnp.concatenate(other, 0)
+        for step in steps:
+            crossed = step == max(steps)
+            piece = send(theirs if crossed else ours, step, crossed=crossed)
+            back = swap(piece)
+            mine.append(back if crossed else piece)
+            other.append(piece if crossed else back)
         places = places + [step + place for step in steps for place in places]
-    other = [swap(piece) for piece in mine]
 
     def totals(value, order):
         parts = [value]

time: 48.6 us -> 47.9 us (0.986)
  starting transfers between devices: 15.6 us -> 17.8 us
  blocking collectives: 11.2 us -> 9.31 us
  waiting for transfers between devices: 16.7 us -> 15.4 us
    ppermute x9, starting transfers between devices: 13.5 us -> 16.5 us  [send_over(): return lax.ppermute(value, AXES, pairs)]
    all_to_all x1, blocking collectives: 11.2 us -> 9.31 us  [shards(): dots = lax.all_to_all(dots, AXES, 0, 0, tiled=True)]
    ppermute x9, waiting for transfers between devices: 13.1 us -> 11.7 us  [send_over(): return lax.ppermute(value, AXES, pairs)]
    ppermute x10 -> x9, starting transfers between devices: 2.1 us -> 1.26 us  [swap_cores(): return lax.ppermute(value, AXES, [(i, i ^ 1) for i in range(n_stu * n_que)])]
    select_n x2, other arithmetic: 0.01 us -> 0.76 us  [side(): return jnp.where(core == 0, students, questions)]
    another operation x1, other arithmetic: 0.66 us -> 0.01 us  [block(): jnp.stack([own_icpt, peers_icpt])]
    ppermute x10 -> x9, waiting for transfers between devices: 3.58 us -> 3.65 us  [swap_cores(): return lax.ppermute(value, AXES, [(i, i ^ 1) for i in range(n_stu * n_que)])]
  transfers between devices with their start and end apart: 19 -> 18, of which waited for: 12 -> 9; matrix products, arithmetic and copies ran while one was open for 2% -> 2% of each run, Pallas kernels for 0% -> 0%
where the time goes in v6:
time: 47.9 us; the launch traced here: 47.6 us
  starting transfers between devices  17.8 us (37%)
  waiting for transfers between devices  15.4 us (32%)
  blocking collectives  9.31 us (19%)
  Pallas kernels  3.27 us (7%)
  other arithmetic  0.85 us (2%)
  between operations  0.75 us (2%)
    ppermute x9, starting transfers between devices, send_over(): return lax.ppermute(value, AXES, pairs)  16.5 us
    ppermute x9, waiting for transfers between devices, send_over(): return lax.ppermute(value, AXES, pairs)  11.7 us
    all_to_all x1, blocking collectives, shards(): dots = lax.all_to_all(dots, AXES, 0, 0, tiled=True)  9.31 us
    ppermute x9, waiting for transfers between devices, swap_cores(): return lax.ppermute(value, AXES, [(i, i ^ 1) for i in range(n_stu * n_que)])  3.65 us
    pallas_call x7, Pallas kernels, call(): pl.pallas_call(kernel, out_shape=out, in_specs=[pl.BlockSpec(memory_space...  3.27 us
    ppermute x9, starting transfers between devices, swap_cores(): return lax.ppermute(value, AXES, [(i, i ^ 1) for i in range(n_stu * n_que)])  1.26 us
  transfers between devices with their start and end apart: 18, of which 9 were waited for; matrix products, arithmetic and copies ran while one was open for 2% of the time, Pallas kernels for 0%

profile of v6, /device:TPU:0, one launch (start us, length us, event | category | flops | bytes accessed | tf_op | source)
XLA Modules:
  0.0 47.6 jit_solution(14053883328825944195)
XLA Ops:
  0.6 0.5 %collective-permute-start.2 = (f32[32]{0:T(128)}, f32[32]{0:T(128)S(1)}, u32[]{:S(2)}, u32[]{:S(2)}) collective-permute-start(f32[32]{0:T(128)} %param.7), channel_id=1, source_target_pairs={{0,1},{1,0},{2,3},{3,2},{4,5},{5,4},{6,7},{7,6},{8,9},{9,8},{10,11... | collective-permute-start | bytes 392 | tf_op jit(solution)/shard_map/ppermute | solution.py:320
  1.2 0.1 collective-permute-start
  1.2 0.4 collective-permute-start.1
  1.7 0.1 collective-permute-start.9
  1.8 0.8 %broadcast_select_fusion = (f32[32,64]{1,0:T(8,128)S(1)}, f32[32,64]{1,0:T(8,128)S(1)}) fusion(f32[32,64]{1,0:T(8,128)} %param.6, f32[32,64]{1,0:T(8,128)S(1)} %copy-done.1, pred[]{:T(512)S(6)} %eq.2), kind=kLoop, calls=%fused_computation.2 | loop fusion | flops 4096 | bytes 32769 | tf_op jit(solution)/shard_map/jit(_where)/select_n | solution.py:359
  2.5 0.1 pad.18.clone
  2.6 0.1 reshape.13
  2.7 0.1 reshape.12
  2.8 0.1 maximum_maximum_fusion.1
  2.9 3.9 %collective-permute-start.4 = (f32[40,128]{1,0:T(8,128)S(1)}, f32[40,128]{1,0:T(8,128)S(1)}, u32[]{:S(2)}, u32[]{:S(2)}) collective-permute-start(f32[40,128]{1,0:T(8,128)S(1)} %get-tuple-element.35.refs_4_), channel_id=1, source_target_pairs={{0,24},{1,7},{2,26},{3,5},{4,28},{5,3},{6,30},{7,1},{8,16},{9,15},... | collective-permute-start | bytes 61448 | tf_op jit(solution)/shard_map/ppermute | solution.py:329
  6.8 2.6 %collective-permute-start.6 = (f32[40,128]{1,0:T(8,128)S(1)}, f32[40,128]{1,0:T(8,128)S(1)}, u32[]{:S(2)}, u32[]{:S(2)}) collective-permute-start(f32[40,128]{1,0:T(8,128)S(1)} %get-tuple-element.36.refs_0_), channel_id=1, source_target_pairs={{0,4},{1,17},{2,6},{3,19},{4,0},{5,21},{6,2},{7,23},{8,12},{9,25},... | collective-permute-start | bytes 61448 | tf_op jit(solution)/shard_map/ppermute | solution.py:329
  9.4 1.6 %collective-permute-start.3 = (f32[40,128]{1,0:T(8,128)S(1)}, f32[40,128]{1,0:T(8,128)S(1)}, u32[]{:S(2)}, u32[]{:S(2)}) collective-permute-start(f32[40,128]{1,0:T(8,128)S(1)} %get-tuple-element.36.refs_0_), channel_id=1, source_target_pairs={{0,2},{1,9},{2,0},{3,11},{4,6},{5,13},{6,4},{7,15},{8,10},{9,1},{1... | collective-permute-start | bytes 61448 | tf_op jit(solution)/shard_map/ppermute | solution.py:329
  11.0 0.5 %collective-permute-done.6.refs_3_ = f32[40,128]{1,0:T(8,128)S(1)} collective-permute-done((f32[40,128]{1,0:T(8,128)S(1)}, f32[40,128]{1,0:T(8,128)S(1)}, u32[]{:S(2)}, u32[]{:S(2)}) %collective-permute-start.6) | collective-permute-done | bytes 20512 | tf_op jit(solution)/shard_map/ppermute | solution.py:329
  11.5 1.7 %collective-permute-done.3.refs_1_ = f32[40,128]{1,0:T(8,128)S(1)} collective-permute-done((f32[40,128]{1,0:T(8,128)S(1)}, f32[40,128]{1,0:T(8,128)S(1)}, u32[]{:S(2)}, u32[]{:S(2)}) %collective-permute-start.3) | collective-permute-done | bytes 20512 | tf_op jit(solution)/shard_map/ppermute | solution.py:329
  13.2 1.1 %collective-permute-done.7.refs_5_ = f32[40,128]{1,0:T(8,128)S(1)} collective-permute-done((f32[40,128]{1,0:T(8,128)S(1)}, f32[40,128]{1,0:T(8,128)S(1)}, u32[]{:S(2)}, u32[]{:S(2)}) %collective-permute-start.7) | collective-permute-done | bytes 20512 | tf_op jit(solution)/shard_map/ppermute | solution.py:320
  14.4 0.9 %shard_map.68 = (f32[264,128]{1,0:T(8,128)S(1)}, f32[256,128]{1,0:T(8,128)S(1)}, f32[256,128]{1,0:T(8,128)S(1)}, f32[256,256]{1,0:T(8,128)S(1)}, f32[8,128]{1,0:T(8,128)S(1)}) custom-call(f32[40,128]{1,0:T(8,128)S(1)} %get-tuple-element.36.refs_0_, f32[40,128]{1,0:T(8,128)S(1)} %collective-permute-done.3.refs_1_, ...), custom_call_target="tpu_custom_call" | custom-call | tf_op jit(solution)/shard_map/pallas_call | solution.py:310
  15.3 1.1 %collective-permute-start.12 = (f32[264,128]{1,0:T(8,128)S(1)}, f32[264,128]{1,0:T(8,128)S(1)}, u32[]{:S(2)}, u32[]{:S(2)}) collective-permute-start(f32[264,128]{1,0:T(8,128)S(1)} %get-tuple-element.16.refs_0_), channel_id=1, source_target_pairs={{0,4},{1,17},{2,6},{3,19},{4,0},{5,21},{6,2},{7,23},{8,12},{9,25},... | collective-permute-start | bytes 405512 | tf_op jit(solution)/shard_map/ppermute | solution.py:329
  16.4 2.9 %collective-permute-start.11 = (f32[264,128]{1,0:T(8,128)S(1)}, f32[264,128]{1,0:T(8,128)S(1)}, u32[]{:S(2)}, u32[]{:S(2)}) collective-permute-start(f32[264,128]{1,0:T(8,128)S(1)} %get-tuple-element.16.refs_0_), channel_id=1, source_target_pairs={{0,6},{1,25},{2,4},{3,27},{4,2},{5,29},{6,0},{7,31},{8,14},{9,17},... | collective-permute-start | bytes 405512 | tf_op jit(solution)/shard_map/ppermute | solution.py:329
  19.3 5.0 %collective-permute-done.12.refs_3_ = f32[264,128]{1,0:T(8,128)S(1)} collective-permute-done((f32[264,128]{1,0:T(8,128)S(1)}, f32[264,128]{1,0:T(8,128)S(1)}, u32[]{:S(2)}, u32[]{:S(2)}) %collective-permute-start.12) | collective-permute-done | bytes 135200 | tf_op jit(solution)/shard_map/ppermute | solution.py:329
  24.3 1.3 %collective-permute-done.10.refs_1_ = f32[264,128]{1,0:T(8,128)S(1)} collective-permute-done((f32[264,128]{1,0:T(8,128)S(1)}, f32[264,128]{1,0:T(8,128)S(1)}, u32[]{:S(2)}, u32[]{:S(2)}) %collective-permute-start.10) | collective-permute-done | bytes 135200 | tf_op jit(solution)/shard_map/ppermute | solution.py:329
  25.6 0.2 shard_map.69
  25.9 1.3 %collective-permute-done.13.other_ref.peer_ref = f32[168,128]{1,0:T(8,128)S(1)} collective-permute-done((f32[168,128]{1,0:T(8,128)S(1)}, f32[168,128]{1,0:T(8,128)S(1)}, u32[]{:S(2)}, u32[]{:S(2)}) %collective-permute-start.13) | collective-permute-done | bytes 86048 | tf_op jit(solution)/shard_map/ppermute | solution.py:320
  27.2 0.6 %shard_map.70.refs_0_ = f32[136,128]{1,0:T(8,128)S(1)} custom-call(f32[168,128]{1,0:T(8,128)S(1)} %get-tuple-element.19.mine_ref.refs_4_.send_ref, f32[168,128]{1,0:T(8,128)S(1)} %collective-permute-done.13.other_ref.peer_ref, f32[256,128]{1,0:T(8,128)S(1)} %get-tuple-element.17.refs_4_.left_ref, f32[256,128]{1,0:T(8,128)S(1)} %get-tuple-element.20.right_ref, ...), custom_call_target="tpu_custom_call" | custom-call | tf_op jit(solution)/shard_map/pallas_call | solution.py:310
  27.8 2.0 %collective-permute-start.16 = (f32[136,128]{1,0:T(8,128)S(1)}, f32[136,128]{1,0:T(8,128)S(1)}, u32[]{:S(2)}, u32[]{:S(2)}) collective-permute-start(f32[136,128]{1,0:T(8,128)S(1)} %shard_map.70.refs_0_), channel_id=1, source_target_pairs={{0,6},{1,25},{2,4},{3,27},{4,2},{5,29},{6,0},{7,31},{8,14},{9,17},... | collective-permute-start | bytes 208904 | tf_op jit(solution)/shard_map/ppermute | solution.py:329
  29.8 2.4 %collective-permute-start.14 = (f32[136,128]{1,0:T(8,128)S(1)}, f32[136,128]{1,0:T(8,128)S(1)}, u32[]{:S(2)}, u32[]{:S(2)}) collective-permute-start(f32[136,128]{1,0:T(8,128)S(1)} %shard_map.70.refs_0_), channel_id=1, source_target_pairs={{0,4},{1,17},{2,6},{3,19},{4,0},{5,21},{6,2},{7,23},{8,12},{9,25},... | collective-permute-start | bytes 208904 | tf_op jit(solution)/shard_map/ppermute | solution.py:329
  32.2 1.8 %collective-permute-done.16.refs_3_ = f32[136,128]{1,0:T(8,128)S(1)} collective-permute-done((f32[136,128]{1,0:T(8,128)S(1)}, f32[136,128]{1,0:T(8,128)S(1)}, u32[]{:S(2)}, u32[]{:S(2)}) %collective-permute-start.16) | collective-permute-done | bytes 69664 | tf_op jit(solution)/shard_map/ppermute | solution.py:329
  34.0 1.4 %collective-permute-done.15.refs_2_ = f32[136,128]{1,0:T(8,128)S(1)} collective-permute-done((f32[136,128]{1,0:T(8,128)S(1)}, f32[136,128]{1,0:T(8,128)S(1)}, u32[]{:S(2)}, u32[]{:S(2)}) %collective-permute-start.15) | collective-permute-done | bytes 69664 | tf_op jit(solution)/shard_map/ppermute | solution.py:329
  35.5 0.2 shard_map.71
  35.7 1.2 %collective-permute-done.17.other_ref.peer_second_ref = f32[136,128]{1,0:T(8,128)S(1)} collective-permute-done((f32[136,128]{1,0:T(8,128)S(1)}, f32[136,128]{1,0:T(8,128)S(1)}, u32[]{:S(2)}, u32[]{:S(2)}) %collective-permute-start.17) | collective-permute-done | bytes 69664 | tf_op jit(solution)/shard_map/ppermute | solution.py:320
  37.0 0.5 %shard_map.72 = f32[32,1,128]{2,1,0:T(1,128)S(1)} custom-call(f32[136,128]{1,0:T(8,128)S(1)} %get-tuple-element.23.mine_ref.second_ref, f32[136,128]{1,0:T(8,128)S(1)} %collective-permute-done.17.other_ref.peer_second_ref, f32[256,128]{1,0:T(8,128)S(1)} %get-tuple-element.17.refs_4_.left_ref, f32[256,128]{1,0:T(8,128)S(1)} %get-tuple-element.20.right_ref, ...), custom_call_target="tpu_custom_call" | custom-call | tf_op jit(solution)/shard_map/pallas_call | solution.py:310
  37.5 9.3 %all_to_all.5.dots_ref = f32[32,1,128]{2,1,0:T(1,128)S(1)} all-to-all(f32[32,1,128]{2,1,0:T(1,128)S(1)} %shard_map.72), channel_id=1, replica_groups=mesh['stu'=4,'que'=8] {'stu','que'}, dimensions={0} | all-to-all | bytes 32768 | tf_op jit(solution)/shard_map/all_to_all | solution.py:411
  46.8 0.8 %shard_map.73 = (f32[32,64]{1,0:T(8,128)}, f32[32,64]{1,0:T(8,128)}, f32[1,32]{1,0:T(1,128)}) custom-call(f32[32,1,128]{2,1,0:T(1,128)S(1)} %all_to_all.5.dots_ref, f32[168,128]{1,0:T(8,128)S(1)} %get-tuple-element.19.mine_ref.refs_4_.send_ref, f32[168,128]{1,0:T(8,128)S(1)} %collective-permute-done.13.other_ref.peer_ref, ...), custom_call_target="tpu_custom_call" | custom-call | tf_op jit(solution)/shard_map/pallas_call | solution.py:310
  (26 shorter events, 0.2 us)
Async XLA Ops:
  0.6 1.1 %copy-start.1 = (f32[32,64]{1,0:T(8,128)S(1)}, f32[32,64]{1,0:T(8,128)}, u32[]{:S(2)}) copy-start(f32[32,64]{1,0:T(8,128)} %param.5) | copy-start | bytes 24580
  0.6 2.0 %collective-permute-start.2 = (f32[32]{0:T(128)}, f32[32]{0:T(128)S(1)}, u32[]{:S(2)}, u32[]{:S(2)}) collective-permute-start(f32[32]{0:T(128)} %param.7), channel_id=1, source_target_pairs={{0,1},{1,0},{2,3},{3,2},{4,5},{5,4},{6,7},{7,6},{8,9},{9,8},{10,11... | collective-permute-start | bytes 392 | tf_op jit(solution)/shard_map/ppermute | solution.py:320
  1.2 1.6 %collective-permute-start = (f32[32,64]{1,0:T(8,128)}, f32[32,64]{1,0:T(8,128)S(1)}, u32[]{:S(2)}, u32[]{:S(2)}) collective-permute-start(f32[32,64]{1,0:T(8,128)} %param.5), channel_id=1, source_target_pairs={{0,1},{1,0},{2,3},{3,2},{4,5},{5,4},{6,7},{7,6},{8,9},{9,8},{10,11... | collective-permute-start | bytes 24584 | tf_op jit(solution)/shard_map/ppermute | solution.py:320
  1.2 1.5 %collective-permute-start.1 = (f32[32,64]{1,0:T(8,128)}, f32[32,64]{1,0:T(8,128)S(1)}, u32[]{:S(2)}, u32[]{:S(2)}) collective-permute-start(f32[32,64]{1,0:T(8,128)} %param.6), channel_id=1, source_target_pairs={{0,1},{1,0},{2,3},{3,2},{4,5},{5,4},{6,7},{7,6},{8,9},{9,8},{10,11... | collective-permute-start | bytes 24584 | tf_op jit(solution)/shard_map/ppermute | solution.py:320
  1.7 11.5 %collective-permute-start.9 = (s32[256,128]{1,0:T(8,128)}, s32[256,128]{1,0:T(8,128)S(1)}, u32[]{:S(2)}, u32[]{:S(2)}) collective-permute-start(s32[256,128]{1,0:T(8,128)} %own_ref.1), channel_id=1, source_target_pairs={{0,1},{1,0},{2,3},{3,2},{4,5},{5,4},{6,7},{7,6},{8,9},{9,8},{10,11... | collective-permute-start | bytes 393224 | tf_op jit(solution)/shard_map/ppermute | solution.py:320
  1.7 0.9 %copy-start.2 = (f32[32]{0:T(128)S(1)}, f32[32]{0:T(128)}, u32[]{:S(2)}) copy-start(f32[32]{0:T(128)} %param.7) | copy-start | bytes 388
  1.8 11.4 %copy-start = (s32[256,128]{1,0:T(8,128)S(1)}, s32[256,128]{1,0:T(8,128)}, u32[]{:S(2)}) copy-start(s32[256,128]{1,0:T(8,128)} %own_ref.1) | copy-start | bytes 393220
  2.9 8.1 %collective-permute-start.4 = (f32[40,128]{1,0:T(8,128)S(1)}, f32[40,128]{1,0:T(8,128)S(1)}, u32[]{:S(2)}, u32[]{:S(2)}) collective-permute-start(f32[40,128]{1,0:T(8,128)S(1)} %get-tuple-element.35.refs_4_), channel_id=1, source_target_pairs={{0,24},{1,7},{2,26},{3,5},{4,28},{5,3},{6,30},{7,1},{8,16},{9,15},... | collective-permute-start | bytes 61448 | tf_op jit(solution)/shard_map/ppermute | solution.py:329
  6.8 4.7 %collective-permute-start.6 = (f32[40,128]{1,0:T(8,128)S(1)}, f32[40,128]{1,0:T(8,128)S(1)}, u32[]{:S(2)}, u32[]{:S(2)}) collective-permute-start(f32[40,128]{1,0:T(8,128)S(1)} %get-tuple-element.36.refs_0_), channel_id=1, source_target_pairs={{0,4},{1,17},{2,6},{3,19},{4,0},{5,21},{6,2},{7,23},{8,12},{9,25},... | collective-permute-start | bytes 61448 | tf_op jit(solution)/shard_map/ppermute | solution.py:329
  9.4 3.8 %collective-permute-start.3 = (f32[40,128]{1,0:T(8,128)S(1)}, f32[40,128]{1,0:T(8,128)S(1)}, u32[]{:S(2)}, u32[]{:S(2)}) collective-permute-start(f32[40,128]{1,0:T(8,128)S(1)} %get-tuple-element.36.refs_0_), channel_id=1, source_target_pairs={{0,2},{1,9},{2,0},{3,11},{4,6},{5,13},{6,4},{7,15},{8,10},{9,1},{1... | collective-permute-start | bytes 61448 | tf_op jit(solution)/shard_map/ppermute | solution.py:329
  11.0 2.3 %collective-permute-start.5 = (f32[40,128]{1,0:T(8,128)S(1)}, f32[40,128]{1,0:T(8,128)S(1)}, u32[]{:S(2)}, u32[]{:S(2)}) collective-permute-start(f32[40,128]{1,0:T(8,128)S(1)} %collective-permute-done.4.refs_6_), channel_id=1, source_target_pairs={{0,1},{1,0},{2,3},{3,2},{4,5},{5,4},{6,7},{7,6},{8,9},{9,8},{10,11... | collective-permute-start | bytes 61448 | tf_op jit(solution)/shard_map/ppermute | solution.py:320
  11.5 1.8 %collective-permute-start.8 = (f32[40,128]{1,0:T(8,128)S(1)}, f32[40,128]{1,0:T(8,128)S(1)}, u32[]{:S(2)}, u32[]{:S(2)}) collective-permute-start(f32[40,128]{1,0:T(8,128)S(1)} %collective-permute-done.6.refs_3_), channel_id=1, source_target_pairs={{0,1},{1,0},{2,3},{3,2},{4,5},{5,4},{6,7},{7,6},{8,9},{9,8},{10,11... | collective-permute-start | bytes 61448 | tf_op jit(solution)/shard_map/ppermute | solution.py:320
  13.2 1.2 %collective-permute-start.7 = (f32[40,128]{1,0:T(8,128)S(1)}, f32[40,128]{1,0:T(8,128)S(1)}, u32[]{:S(2)}, u32[]{:S(2)}) collective-permute-start(f32[40,128]{1,0:T(8,128)S(1)} %collective-permute-done.3.refs_1_), channel_id=1, source_target_pairs={{0,1},{1,0},{2,3},{3,2},{4,5},{5,4},{6,7},{7,6},{8,9},{9,8},{10,11... | collective-permute-start | bytes 61448 | tf_op jit(solution)/shard_map/ppermute | solution.py:320
  15.3 9.0 %collective-permute-start.12 = (f32[264,128]{1,0:T(8,128)S(1)}, f32[264,128]{1,0:T(8,128)S(1)}, u32[]{:S(2)}, u32[]{:S(2)}) collective-permute-start(f32[264,128]{1,0:T(8,128)S(1)} %get-tuple-element.16.refs_0_), channel_id=1, source_target_pairs={{0,4},{1,17},{2,6},{3,19},{4,0},{5,21},{6,2},{7,23},{8,12},{9,25},... | collective-permute-start | bytes 405512 | tf_op jit(solution)/shard_map/ppermute | solution.py:329
  16.4 7.8 %collective-permute-start.11 = (f32[264,128]{1,0:T(8,128)S(1)}, f32[264,128]{1,0:T(8,128)S(1)}, u32[]{:S(2)}, u32[]{:S(2)}) collective-permute-start(f32[264,128]{1,0:T(8,128)S(1)} %get-tuple-element.16.refs_0_), channel_id=1, source_target_pairs={{0,6},{1,25},{2,4},{3,27},{4,2},{5,29},{6,0},{7,31},{8,14},{9,17},... | collective-permute-start | bytes 405512 | tf_op jit(solution)/shard_map/ppermute | solution.py:329
  19.3 6.3 %collective-permute-start.10 = (f32[264,128]{1,0:T(8,128)S(1)}, f32[264,128]{1,0:T(8,128)S(1)}, u32[]{:S(2)}, u32[]{:S(2)}) collective-permute-start(f32[264,128]{1,0:T(8,128)S(1)} %get-tuple-element.16.refs_0_), channel_id=1, source_target_pairs={{0,2},{1,9},{2,0},{3,11},{4,6},{5,13},{6,4},{7,15},{8,10},{9,1},{1... | collective-permute-start | bytes 405512 | tf_op jit(solution)/shard_map/ppermute | solution.py:329
  25.8 1.3 %collective-permute-start.13 = (f32[168,128]{1,0:T(8,128)S(1)}, f32[168,128]{1,0:T(8,128)S(1)}, u32[]{:S(2)}, u32[]{:S(2)}) collective-permute-start(f32[168,128]{1,0:T(8,128)S(1)} %get-tuple-element.19.mine_ref.refs_4_.send_ref), channel_id=1, source_target_pairs={{0,1},{1,0},{2,3},{3,2},{4,5},{5,4},{6,7},{7,6},{8,9},{9,8},{10,11... | collective-permute-start | bytes 258056 | tf_op jit(solution)/shard_map/ppermute | solution.py:320
  27.8 6.2 %collective-permute-start.16 = (f32[136,128]{1,0:T(8,128)S(1)}, f32[136,128]{1,0:T(8,128)S(1)}, u32[]{:S(2)}, u32[]{:S(2)}) collective-permute-start(f32[136,128]{1,0:T(8,128)S(1)} %shard_map.70.refs_0_), channel_id=1, source_target_pairs={{0,6},{1,25},{2,4},{3,27},{4,2},{5,29},{6,0},{7,31},{8,14},{9,17},... | collective-permute-start | bytes 208904 | tf_op jit(solution)/shard_map/ppermute | solution.py:329
  29.8 5.6 %collective-permute-start.15 = (f32[136,128]{1,0:T(8,128)S(1)}, f32[136,128]{1,0:T(8,128)S(1)}, u32[]{:S(2)}, u32[]{:S(2)}) collective-permute-start(f32[136,128]{1,0:T(8,128)S(1)} %shard_map.70.refs_0_), channel_id=1, source_target_pairs={{0,2},{1,9},{2,0},{3,11},{4,6},{5,13},{6,4},{7,15},{8,10},{9,1},{1... | collective-permute-start | bytes 208904 | tf_op jit(solution)/shard_map/ppermute | solution.py:329
  29.8 5.6 %collective-permute-start.14 = (f32[136,128]{1,0:T(8,128)S(1)}, f32[136,128]{1,0:T(8,128)S(1)}, u32[]{:S(2)}, u32[]{:S(2)}) collective-permute-start(f32[136,128]{1,0:T(8,128)S(1)} %shard_map.70.refs_0_), channel_id=1, source_target_pairs={{0,4},{1,17},{2,6},{3,19},{4,0},{5,21},{6,2},{7,23},{8,12},{9,25},... | collective-permute-start | bytes 208904 | tf_op jit(solution)/shard_map/ppermute | solution.py:329
  35.6 1.3 %collective-permute-start.17 = (f32[136,128]{1,0:T(8,128)S(1)}, f32[136,128]{1,0:T(8,128)S(1)}, u32[]{:S(2)}, u32[]{:S(2)}) collective-permute-start(f32[136,128]{1,0:T(8,128)S(1)} %get-tuple-element.23.mine_ref.second_ref), channel_id=1, source_target_pairs={{0,1},{1,0},{2,3},{3,2},{4,5},{5,4},{6,7},{7,6},{8,9},{9,8},{10,11... | collective-permute-start | bytes 208904 | tf_op jit(solution)/shard_map/ppermute | solution.py:320

commit v7 on v6

--- a/solution.py
+++ b/solution.py
@@ -10,7 +10,7 @@
 AXES = ("stu", "que")
 LANES = 128
 GATHER_ORDER = (1, 3, 2)
-FIRST_ORDER = (1, 3, 2)
+FIRST_ORDER = (3, 1, 2)
 SECOND_ORDER = (2, 1, 3)
 BIAS = 8
 
@@ -246,12 +246,10 @@
     lift = jnp.where(used, total + first - diag * first, 0.0)
     second = lift / diag
     second_ref[...] = second
-    scale = 1.0 / group
-    lane = lax.broadcasted_iota(jnp.int32, (8, LANES), 1)
-    dots = jnp.zeros((8, LANES), jnp.float32)
-    for at, value in enumerate((first * first * diag, first * lift, second * lift, second * second)):
-        dots = jnp.where(lane == at, jnp.sum(value) * scale, dots)
-    dots_ref[...] = dots
+    terms = (first * first * diag, first * lift, second * lift, second * second)
+    dots_ref[...] = jnp.concatenate(
+        [jnp.sum(term, axis=0, keepdims=True) for term in terms] + [jnp.zeros((8 - len(terms), LANES), jnp.float32)], 0
+    ) * (1.0 / group)
 
 
 def form_kernel(mine_ref, other_ref, left_ref, right_ref, weight_ref, dots_ref, out_ref):
@@ -259,9 +257,12 @@
     change = change_of(mine_ref, other_ref, left_ref[...], right_ref[...], half)
 
     def use(value):
-        form = 0.5 * jnp.sum(weight_ref[...] * value * value)
-        lane = lax.broadcasted_iota(jnp.int32, (1, LANES), 1)
-        dots = dots_ref[0:1, :] + jnp.where(lane == 3, form, 0.0)
+        form = 0.5 * jnp.sum(weight_ref[...] * value * value, axis=0, keepdims=True)
+        row = lax.broadcasted_iota(jnp.int32, (8, LANES), 0)
+        terms = dots_ref[...] + jnp.where(row == 3, form[:, :LANES] + form[:, LANES:], 0.0)
+        sums = jnp.sum(terms, axis=1, keepdims=True)
+        lane = lax.broadcasted_iota(jnp.int32, (8, LANES), 1)
+        dots = jnp.sum(jnp.where(lane == row, sums, 0.0), axis=0, keepdims=True)
         out_ref[...] = jnp.broadcast_to(dots[None], out_ref.shape)
 
     with_bias(change, mine_ref, other_ref, half, use)
@@ -272,8 +273,10 @@
 ):
     core, line, plane = position()
     dots = jnp.sum(dots_ref[...], axis=0)
-    lane = lax.broadcasted_iota(jnp.int32, (1, LANES), 1)
-    a, f, h, d = [jnp.sum(jnp.where(lane == at, dots, 0.0), axis=1, keepdims=True) for at in range(4)]
+    lane = lax.broadcasted_iota(jnp.int32, (8, LANES), 1)
+    row = lax.broadcasted_iota(jnp.int32, (8, LANES), 0)
+    sums = jnp.sum(jnp.where(lane == row, dots, 0.0), axis=1, keepdims=True)
+    a, f, h, d = [sums[at : at + 1] for at in range(4)]
     b = a + f
     e = f + h
     det = b * d - e * e

time: 47.9 us -> 47.4 us (0.990)
  waiting for transfers between devices: 15.4 us -> 14.6 us
  starting transfers between devices: 17.8 us -> 18.3 us
    ppermute x9, waiting for transfers between devices: 11.7 us -> 11 us  [send_over(): return lax.ppermute(value, AXES, pairs)]
where the time goes in v7:
time: 47.4 us; the launch traced here: 47.2 us
  starting transfers between devices  18.3 us (39%)
  waiting for transfers between devices  14.6 us (31%)
  blocking collectives  9.33 us (20%)
  Pallas kernels  3.14 us (7%)
  other arithmetic  0.85 us (2%)
  between operations  0.74 us (2%)
    ppermute x9, starting transfers between devices, send_over(): return lax.ppermute(value, AXES, pairs)  17 us
    ppermute x9, waiting for transfers between devices, send_over(): return lax.ppermute(value, AXES, pairs)  11 us
    all_to_all x1, blocking collectives, shards(): dots = lax.all_to_all(dots, AXES, 0, 0, tiled=True)  9.33 us
    ppermute x9, waiting for transfers between devices, swap_cores(): return lax.ppermute(value, AXES, [(i, i ^ 1) for i in range(n_stu * n_que)])  3.65 us
    pallas_call x7, Pallas kernels, call(): pl.pallas_call(kernel, out_shape=out, in_specs=[pl.BlockSpec(memory_space...  3.14 us
    ppermute x9, starting transfers between devices, swap_cores(): return lax.ppermute(value, AXES, [(i, i ^ 1) for i in range(n_stu * n_que)])  1.26 us
  transfers between devices with their start and end apart: 18, of which 9 were waited for; matrix products, arithmetic and copies ran while one was open for 2% of the time, Pallas kernels for 0%

profile of v7, /device:TPU:0, one launch (start us, length us, event | category | flops | bytes accessed | tf_op | source)
XLA Modules:
  0.0 47.2 jit_solution(1978765275952276816)
XLA Ops:
  0.6 0.5 %collective-permute-start.2 = (f32[32]{0:T(128)}, f32[32]{0:T(128)S(1)}, u32[]{:S(2)}, u32[]{:S(2)}) collective-permute-start(f32[32]{0:T(128)} %param.7), channel_id=1, source_target_pairs={{0,1},{1,0},{2,3},{3,2},{4,5},{5,4},{6,7},{7,6},{8,9},{9,8},{10,11... | collective-permute-start | bytes 392 | tf_op jit(solution)/shard_map/ppermute | solution.py:323
  1.2 0.1 collective-permute-start
  1.2 0.4 collective-permute-start.1
  1.7 0.1 collective-permute-start.9
  1.8 0.8 %broadcast_select_fusion = (f32[32,64]{1,0:T(8,128)S(1)}, f32[32,64]{1,0:T(8,128)S(1)}) fusion(f32[32,64]{1,0:T(8,128)} %param.6, f32[32,64]{1,0:T(8,128)S(1)} %copy-done.1, pred[]{:T(512)S(6)} %eq.2), kind=kLoop, calls=%fused_computation.2 | loop fusion | flops 4096 | bytes 32769 | tf_op jit(solution)/shard_map/jit(_where)/select_n | solution.py:362
  2.6 0.1 reshape.13
  2.7 0.1 reshape.12
  2.8 0.1 maximum_maximum_fusion.1
  2.9 3.9 %collective-permute-start.4 = (f32[40,128]{1,0:T(8,128)S(1)}, f32[40,128]{1,0:T(8,128)S(1)}, u32[]{:S(2)}, u32[]{:S(2)}) collective-permute-start(f32[40,128]{1,0:T(8,128)S(1)} %get-tuple-element.35.refs_4_), channel_id=1, source_target_pairs={{0,24},{1,7},{2,26},{3,5},{4,28},{5,3},{6,30},{7,1},{8,16},{9,15},... | collective-permute-start | bytes 61448 | tf_op jit(solution)/shard_map/ppermute | solution.py:332
  6.8 2.6 %collective-permute-start.6 = (f32[40,128]{1,0:T(8,128)S(1)}, f32[40,128]{1,0:T(8,128)S(1)}, u32[]{:S(2)}, u32[]{:S(2)}) collective-permute-start(f32[40,128]{1,0:T(8,128)S(1)} %get-tuple-element.36.refs_0_), channel_id=1, source_target_pairs={{0,4},{1,17},{2,6},{3,19},{4,0},{5,21},{6,2},{7,23},{8,12},{9,25},... | collective-permute-start | bytes 61448 | tf_op jit(solution)/shard_map/ppermute | solution.py:332
  9.4 1.6 %collective-permute-start.3 = (f32[40,128]{1,0:T(8,128)S(1)}, f32[40,128]{1,0:T(8,128)S(1)}, u32[]{:S(2)}, u32[]{:S(2)}) collective-permute-start(f32[40,128]{1,0:T(8,128)S(1)} %get-tuple-element.36.refs_0_), channel_id=1, source_target_pairs={{0,2},{1,9},{2,0},{3,11},{4,6},{5,13},{6,4},{7,15},{8,10},{9,1},{1... | collective-permute-start | bytes 61448 | tf_op jit(solution)/shard_map/ppermute | solution.py:332
  11.0 0.5 %collective-permute-done.6.refs_3_ = f32[40,128]{1,0:T(8,128)S(1)} collective-permute-done((f32[40,128]{1,0:T(8,128)S(1)}, f32[40,128]{1,0:T(8,128)S(1)}, u32[]{:S(2)}, u32[]{:S(2)}) %collective-permute-start.6) | collective-permute-done | bytes 20512 | tf_op jit(solution)/shard_map/ppermute | solution.py:332
  11.5 1.7 %collective-permute-done.3.refs_1_ = f32[40,128]{1,0:T(8,128)S(1)} collective-permute-done((f32[40,128]{1,0:T(8,128)S(1)}, f32[40,128]{1,0:T(8,128)S(1)}, u32[]{:S(2)}, u32[]{:S(2)}) %collective-permute-start.3) | collective-permute-done | bytes 20512 | tf_op jit(solution)/shard_map/ppermute | solution.py:332
  13.2 1.1 %collective-permute-done.7.refs_5_ = f32[40,128]{1,0:T(8,128)S(1)} collective-permute-done((f32[40,128]{1,0:T(8,128)S(1)}, f32[40,128]{1,0:T(8,128)S(1)}, u32[]{:S(2)}, u32[]{:S(2)}) %collective-permute-start.7) | collective-permute-done | bytes 20512 | tf_op jit(solution)/shard_map/ppermute | solution.py:323
  14.4 0.9 %shard_map.68 = (f32[264,128]{1,0:T(8,128)S(1)}, f32[256,128]{1,0:T(8,128)S(1)}, f32[256,128]{1,0:T(8,128)S(1)}, f32[256,256]{1,0:T(8,128)S(1)}, f32[8,128]{1,0:T(8,128)S(1)}) custom-call(f32[40,128]{1,0:T(8,128)S(1)} %get-tuple-element.36.refs_0_, f32[40,128]{1,0:T(8,128)S(1)} %collective-permute-done.3.refs_1_, ...), custom_call_target="tpu_custom_call" | custom-call | tf_op jit(solution)/shard_map/pallas_call | solution.py:313
  15.3 1.1 %collective-permute-start.12 = (f32[264,128]{1,0:T(8,128)S(1)}, f32[264,128]{1,0:T(8,128)S(1)}, u32[]{:S(2)}, u32[]{:S(2)}) collective-permute-start(f32[264,128]{1,0:T(8,128)S(1)} %get-tuple-element.16.refs_0_), channel_id=1, source_target_pairs={{0,4},{1,17},{2,6},{3,19},{4,0},{5,21},{6,2},{7,23},{8,12},{9,25},... | collective-permute-start | bytes 405512 | tf_op jit(solution)/shard_map/ppermute | solution.py:332
  16.4 1.7 %collective-permute-start.11 = (f32[264,128]{1,0:T(8,128)S(1)}, f32[264,128]{1,0:T(8,128)S(1)}, u32[]{:S(2)}, u32[]{:S(2)}) collective-permute-start(f32[264,128]{1,0:T(8,128)S(1)} %get-tuple-element.16.refs_0_), channel_id=1, source_target_pairs={{0,2},{1,9},{2,0},{3,11},{4,6},{5,13},{6,4},{7,15},{8,10},{9,1},{1... | collective-permute-start | bytes 405512 | tf_op jit(solution)/shard_map/ppermute | solution.py:332
  18.1 1.6 %collective-permute-start.10 = (f32[264,128]{1,0:T(8,128)S(1)}, f32[264,128]{1,0:T(8,128)S(1)}, u32[]{:S(2)}, u32[]{:S(2)}) collective-permute-start(f32[264,128]{1,0:T(8,128)S(1)} %get-tuple-element.16.refs_0_), channel_id=1, source_target_pairs={{0,6},{1,25},{2,4},{3,27},{4,2},{5,29},{6,0},{7,31},{8,14},{9,17},... | collective-permute-start | bytes 405512 | tf_op jit(solution)/shard_map/ppermute | solution.py:332
  19.7 3.0 %collective-permute-done.12.refs_3_ = f32[264,128]{1,0:T(8,128)S(1)} collective-permute-done((f32[264,128]{1,0:T(8,128)S(1)}, f32[264,128]{1,0:T(8,128)S(1)}, u32[]{:S(2)}, u32[]{:S(2)}) %collective-permute-start.12) | collective-permute-done | bytes 135200 | tf_op jit(solution)/shard_map/ppermute | solution.py:332
  22.7 2.6 %collective-permute-done.10.refs_1_ = f32[264,128]{1,0:T(8,128)S(1)} collective-permute-done((f32[264,128]{1,0:T(8,128)S(1)}, f32[264,128]{1,0:T(8,128)S(1)}, u32[]{:S(2)}, u32[]{:S(2)}) %collective-permute-start.10) | collective-permute-done | bytes 135200 | tf_op jit(solution)/shard_map/ppermute | solution.py:332
  25.3 0.2 shard_map.69
  25.6 1.3 %collective-permute-done.13.other_ref.peer_ref = f32[168,128]{1,0:T(8,128)S(1)} collective-permute-done((f32[168,128]{1,0:T(8,128)S(1)}, f32[168,128]{1,0:T(8,128)S(1)}, u32[]{:S(2)}, u32[]{:S(2)}) %collective-permute-start.13) | collective-permute-done | bytes 86048 | tf_op jit(solution)/shard_map/ppermute | solution.py:323
  26.9 0.6 %shard_map.70.refs_0_ = f32[136,128]{1,0:T(8,128)S(1)} custom-call(f32[168,128]{1,0:T(8,128)S(1)} %get-tuple-element.19.mine_ref.refs_4_.send_ref, f32[168,128]{1,0:T(8,128)S(1)} %collective-permute-done.13.other_ref.peer_ref, f32[256,128]{1,0:T(8,128)S(1)} %get-tuple-element.17.refs_4_.left_ref, f32[256,128]{1,0:T(8,128)S(1)} %get-tuple-element.20.right_ref, ...), custom_call_target="tpu_custom_call" | custom-call | tf_op jit(solution)/shard_map/pallas_call | solution.py:313
  27.5 1.9 %collective-permute-start.16 = (f32[136,128]{1,0:T(8,128)S(1)}, f32[136,128]{1,0:T(8,128)S(1)}, u32[]{:S(2)}, u32[]{:S(2)}) collective-permute-start(f32[136,128]{1,0:T(8,128)S(1)} %shard_map.70.refs_0_), channel_id=1, source_target_pairs={{0,6},{1,25},{2,4},{3,27},{4,2},{5,29},{6,0},{7,31},{8,14},{9,17},... | collective-permute-start | bytes 208904 | tf_op jit(solution)/shard_map/ppermute | solution.py:332
  29.4 0.2 collective-permute-start.15
  29.5 2.4 %collective-permute-start.14 = (f32[136,128]{1,0:T(8,128)S(1)}, f32[136,128]{1,0:T(8,128)S(1)}, u32[]{:S(2)}, u32[]{:S(2)}) collective-permute-start(f32[136,128]{1,0:T(8,128)S(1)} %shard_map.70.refs_0_), channel_id=1, source_target_pairs={{0,4},{1,17},{2,6},{3,19},{4,0},{5,21},{6,2},{7,23},{8,12},{9,25},... | collective-permute-start | bytes 208904 | tf_op jit(solution)/shard_map/ppermute | solution.py:332
  32.0 1.8 %collective-permute-done.16.refs_3_ = f32[136,128]{1,0:T(8,128)S(1)} collective-permute-done((f32[136,128]{1,0:T(8,128)S(1)}, f32[136,128]{1,0:T(8,128)S(1)}, u32[]{:S(2)}, u32[]{:S(2)}) %collective-permute-start.16) | collective-permute-done | bytes 69664 | tf_op jit(solution)/shard_map/ppermute | solution.py:332
  33.8 1.4 %collective-permute-done.15.refs_2_ = f32[136,128]{1,0:T(8,128)S(1)} collective-permute-done((f32[136,128]{1,0:T(8,128)S(1)}, f32[136,128]{1,0:T(8,128)S(1)}, u32[]{:S(2)}, u32[]{:S(2)}) %collective-permute-start.15) | collective-permute-done | bytes 69664 | tf_op jit(solution)/shard_map/ppermute | solution.py:332
  35.3 1.2 %collective-permute-done.17.other_ref.peer_second_ref = f32[136,128]{1,0:T(8,128)S(1)} collective-permute-done((f32[136,128]{1,0:T(8,128)S(1)}, f32[136,128]{1,0:T(8,128)S(1)}, u32[]{:S(2)}, u32[]{:S(2)}) %collective-permute-start.17) | collective-permute-done | bytes 69664 | tf_op jit(solution)/shard_map/ppermute | solution.py:323
  36.6 0.5 shard_map.72
  37.0 9.3 %all_to_all.5.dots_ref = f32[32,1,128]{2,1,0:T(1,128)S(1)} all-to-all(f32[32,1,128]{2,1,0:T(1,128)S(1)} %shard_map.72), channel_id=1, replica_groups=mesh['stu'=4,'que'=8] {'stu','que'}, dimensions={0} | all-to-all | bytes 32768 | tf_op jit(solution)/shard_map/all_to_all | solution.py:414
  46.3 0.9 %shard_map.73 = (f32[32,64]{1,0:T(8,128)}, f32[32,64]{1,0:T(8,128)}, f32[1,32]{1,0:T(1,128)}) custom-call(f32[32,1,128]{2,1,0:T(1,128)S(1)} %all_to_all.5.dots_ref, f32[168,128]{1,0:T(8,128)S(1)} %get-tuple-element.19.mine_ref.refs_4_.send_ref, f32[168,128]{1,0:T(8,128)S(1)} %collective-permute-done.13.other_ref.peer_ref, ...), custom_call_target="tpu_custom_call" | custom-call | tf_op jit(solution)/shard_map/pallas_call | solution.py:313
  (26 shorter events, 0.4 us)
Async XLA Ops:
  0.6 1.1 %copy-start.1 = (f32[32,64]{1,0:T(8,128)S(1)}, f32[32,64]{1,0:T(8,128)}, u32[]{:S(2)}) copy-start(f32[32,64]{1,0:T(8,128)} %param.5) | copy-start | bytes 24580
  0.6 2.0 %collective-permute-start.2 = (f32[32]{0:T(128)}, f32[32]{0:T(128)S(1)}, u32[]{:S(2)}, u32[]{:S(2)}) collective-permute-start(f32[32]{0:T(128)} %param.7), channel_id=1, source_target_pairs={{0,1},{1,0},{2,3},{3,2},{4,5},{5,4},{6,7},{7,6},{8,9},{9,8},{10,11... | collective-permute-start | bytes 392 | tf_op jit(solution)/shard_map/ppermute | solution.py:323
  1.2 1.6 %collective-permute-start = (f32[32,64]{1,0:T(8,128)}, f32[32,64]{1,0:T(8,128)S(1)}, u32[]{:S(2)}, u32[]{:S(2)}) collective-permute-start(f32[32,64]{1,0:T(8,128)} %param.5), channel_id=1, source_target_pairs={{0,1},{1,0},{2,3},{3,2},{4,5},{5,4},{6,7},{7,6},{8,9},{9,8},{10,11... | collective-permute-start | bytes 24584 | tf_op jit(solution)/shard_map/ppermute | solution.py:323
  1.2 1.5 %collective-permute-start.1 = (f32[32,64]{1,0:T(8,128)}, f32[32,64]{1,0:T(8,128)S(1)}, u32[]{:S(2)}, u32[]{:S(2)}) collective-permute-start(f32[32,64]{1,0:T(8,128)} %param.6), channel_id=1, source_target_pairs={{0,1},{1,0},{2,3},{3,2},{4,5},{5,4},{6,7},{7,6},{8,9},{9,8},{10,11... | collective-permute-start | bytes 24584 | tf_op jit(solution)/shard_map/ppermute | solution.py:323
  1.7 11.5 %collective-permute-start.9 = (s32[256,128]{1,0:T(8,128)}, s32[256,128]{1,0:T(8,128)S(1)}, u32[]{:S(2)}, u32[]{:S(2)}) collective-permute-start(s32[256,128]{1,0:T(8,128)} %own_ref.1), channel_id=1, source_target_pairs={{0,1},{1,0},{2,3},{3,2},{4,5},{5,4},{6,7},{7,6},{8,9},{9,8},{10,11... | collective-permute-start | bytes 393224 | tf_op jit(solution)/shard_map/ppermute | solution.py:323
  1.7 0.9 %copy-start.2 = (f32[32]{0:T(128)S(1)}, f32[32]{0:T(128)}, u32[]{:S(2)}) copy-start(f32[32]{0:T(128)} %param.7) | copy-start | bytes 388
  1.8 11.4 %copy-start = (s32[256,128]{1,0:T(8,128)S(1)}, s32[256,128]{1,0:T(8,128)}, u32[]{:S(2)}) copy-start(s32[256,128]{1,0:T(8,128)} %own_ref.1) | copy-start | bytes 393220
  2.9 8.1 %collective-permute-start.4 = (f32[40,128]{1,0:T(8,128)S(1)}, f32[40,128]{1,0:T(8,128)S(1)}, u32[]{:S(2)}, u32[]{:S(2)}) collective-permute-start(f32[40,128]{1,0:T(8,128)S(1)} %get-tuple-element.35.refs_4_), channel_id=1, source_target_pairs={{0,24},{1,7},{2,26},{3,5},{4,28},{5,3},{6,30},{7,1},{8,16},{9,15},... | collective-permute-start | bytes 61448 | tf_op jit(solution)/shard_map/ppermute | solution.py:332
  6.8 4.7 %collective-permute-start.6 = (f32[40,128]{1,0:T(8,128)S(1)}, f32[40,128]{1,0:T(8,128)S(1)}, u32[]{:S(2)}, u32[]{:S(2)}) collective-permute-start(f32[40,128]{1,0:T(8,128)S(1)} %get-tuple-element.36.refs_0_), channel_id=1, source_target_pairs={{0,4},{1,17},{2,6},{3,19},{4,0},{5,21},{6,2},{7,23},{8,12},{9,25},... | collective-permute-start | bytes 61448 | tf_op jit(solution)/shard_map/ppermute | solution.py:332
  9.4 3.8 %collective-permute-start.3 = (f32[40,128]{1,0:T(8,128)S(1)}, f32[40,128]{1,0:T(8,128)S(1)}, u32[]{:S(2)}, u32[]{:S(2)}) collective-permute-start(f32[40,128]{1,0:T(8,128)S(1)} %get-tuple-element.36.refs_0_), channel_id=1, source_target_pairs={{0,2},{1,9},{2,0},{3,11},{4,6},{5,13},{6,4},{7,15},{8,10},{9,1},{1... | collective-permute-start | bytes 61448 | tf_op jit(solution)/shard_map/ppermute | solution.py:332
  11.0 2.3 %collective-permute-start.5 = (f32[40,128]{1,0:T(8,128)S(1)}, f32[40,128]{1,0:T(8,128)S(1)}, u32[]{:S(2)}, u32[]{:S(2)}) collective-permute-start(f32[40,128]{1,0:T(8,128)S(1)} %collective-permute-done.4.refs_6_), channel_id=1, source_target_pairs={{0,1},{1,0},{2,3},{3,2},{4,5},{5,4},{6,7},{7,6},{8,9},{9,8},{10,11... | collective-permute-start | bytes 61448 | tf_op jit(solution)/shard_map/ppermute | solution.py:323
  11.5 1.8 %collective-permute-start.8 = (f32[40,128]{1,0:T(8,128)S(1)}, f32[40,128]{1,0:T(8,128)S(1)}, u32[]{:S(2)}, u32[]{:S(2)}) collective-permute-start(f32[40,128]{1,0:T(8,128)S(1)} %collective-permute-done.6.refs_3_), channel_id=1, source_target_pairs={{0,1},{1,0},{2,3},{3,2},{4,5},{5,4},{6,7},{7,6},{8,9},{9,8},{10,11... | collective-permute-start | bytes 61448 | tf_op jit(solution)/shard_map/ppermute | solution.py:323
  13.2 1.2 %collective-permute-start.7 = (f32[40,128]{1,0:T(8,128)S(1)}, f32[40,128]{1,0:T(8,128)S(1)}, u32[]{:S(2)}, u32[]{:S(2)}) collective-permute-start(f32[40,128]{1,0:T(8,128)S(1)} %collective-permute-done.3.refs_1_), channel_id=1, source_target_pairs={{0,1},{1,0},{2,3},{3,2},{4,5},{5,4},{6,7},{7,6},{8,9},{9,8},{10,11... | collective-permute-start | bytes 61448 | tf_op jit(solution)/shard_map/ppermute | solution.py:323
  15.3 7.4 %collective-permute-start.12 = (f32[264,128]{1,0:T(8,128)S(1)}, f32[264,128]{1,0:T(8,128)S(1)}, u32[]{:S(2)}, u32[]{:S(2)}) collective-permute-start(f32[264,128]{1,0:T(8,128)S(1)} %get-tuple-element.16.refs_0_), channel_id=1, source_target_pairs={{0,4},{1,17},{2,6},{3,19},{4,0},{5,21},{6,2},{7,23},{8,12},{9,25},... | collective-permute-start | bytes 405512 | tf_op jit(solution)/shard_map/ppermute | solution.py:332
  16.4 6.3 %collective-permute-start.11 = (f32[264,128]{1,0:T(8,128)S(1)}, f32[264,128]{1,0:T(8,128)S(1)}, u32[]{:S(2)}, u32[]{:S(2)}) collective-permute-start(f32[264,128]{1,0:T(8,128)S(1)} %get-tuple-element.16.refs_0_), channel_id=1, source_target_pairs={{0,2},{1,9},{2,0},{3,11},{4,6},{5,13},{6,4},{7,15},{8,10},{9,1},{1... | collective-permute-start | bytes 405512 | tf_op jit(solution)/shard_map/ppermute | solution.py:332
  18.1 7.2 %collective-permute-start.10 = (f32[264,128]{1,0:T(8,128)S(1)}, f32[264,128]{1,0:T(8,128)S(1)}, u32[]{:S(2)}, u32[]{:S(2)}) collective-permute-start(f32[264,128]{1,0:T(8,128)S(1)} %get-tuple-element.16.refs_0_), channel_id=1, source_target_pairs={{0,6},{1,25},{2,4},{3,27},{4,2},{5,29},{6,0},{7,31},{8,14},{9,17},... | collective-permute-start | bytes 405512 | tf_op jit(solution)/shard_map/ppermute | solution.py:332
  25.5 1.3 %collective-permute-start.13 = (f32[168,128]{1,0:T(8,128)S(1)}, f32[168,128]{1,0:T(8,128)S(1)}, u32[]{:S(2)}, u32[]{:S(2)}) collective-permute-start(f32[168,128]{1,0:T(8,128)S(1)} %get-tuple-element.19.mine_ref.refs_4_.send_ref), channel_id=1, source_target_pairs={{0,1},{1,0},{2,3},{3,2},{4,5},{5,4},{6,7},{7,6},{8,9},{9,8},{10,11... | collective-permute-start | bytes 258056 | tf_op jit(solution)/shard_map/ppermute | solution.py:323
  27.5 6.3 %collective-permute-start.16 = (f32[136,128]{1,0:T(8,128)S(1)}, f32[136,128]{1,0:T(8,128)S(1)}, u32[]{:S(2)}, u32[]{:S(2)}) collective-permute-start(f32[136,128]{1,0:T(8,128)S(1)} %shard_map.70.refs_0_), channel_id=1, source_target_pairs={{0,6},{1,25},{2,4},{3,27},{4,2},{5,29},{6,0},{7,31},{8,14},{9,17},... | collective-permute-start | bytes 208904 | tf_op jit(solution)/shard_map/ppermute | solution.py:332
  29.4 5.8 %collective-permute-start.15 = (f32[136,128]{1,0:T(8,128)S(1)}, f32[136,128]{1,0:T(8,128)S(1)}, u32[]{:S(2)}, u32[]{:S(2)}) collective-permute-start(f32[136,128]{1,0:T(8,128)S(1)} %shard_map.70.refs_0_), channel_id=1, source_target_pairs={{0,2},{1,9},{2,0},{3,11},{4,6},{5,13},{6,4},{7,15},{8,10},{9,1},{1... | collective-permute-start | bytes 208904 | tf_op jit(solution)/shard_map/ppermute | solution.py:332
  29.5 5.6 %collective-permute-start.14 = (f32[136,128]{1,0:T(8,128)S(1)}, f32[136,128]{1,0:T(8,128)S(1)}, u32[]{:S(2)}, u32[]{:S(2)}) collective-permute-start(f32[136,128]{1,0:T(8,128)S(1)} %shard_map.70.refs_0_), channel_id=1, source_target_pairs={{0,4},{1,17},{2,6},{3,19},{4,0},{5,21},{6,2},{7,23},{8,12},{9,25},... | collective-permute-start | bytes 208904 | tf_op jit(solution)/shard_map/ppermute | solution.py:332
  35.2 1.3 %collective-permute-start.17 = (f32[136,128]{1,0:T(8,128)S(1)}, f32[136,128]{1,0:T(8,128)S(1)}, u32[]{:S(2)}, u32[]{:S(2)}) collective-permute-start(f32[136,128]{1,0:T(8,128)S(1)} %get-tuple-element.23.mine_ref.second_ref), channel_id=1, source_target_pairs={{0,1},{1,0},{2,3},{3,2},{4,5},{5,4},{6,7},{7,6},{8,9},{9,8},{10,11... | collective-permute-start | bytes 208904 | tf_op jit(solution)/shard_map/ppermute | solution.py:323

commit v8 on v7

--- a/solution.py
+++ b/solution.py
@@ -11,7 +11,7 @@
 LANES = 128
 GATHER_ORDER = (1, 3, 2)
 FIRST_ORDER = (3, 1, 2)
-SECOND_ORDER = (2, 1, 3)
+SECOND_ORDER = (1, 2, 3)
 BIAS = 8
 
 

time: 47.4 us -> 47.2 us (level)
  no operation moved by 1% of the time
where the time goes in v8:
time: 47.2 us; the launch traced here: 47 us
  starting transfers between devices  18.2 us (39%)
  waiting for transfers between devices  14.6 us (31%)
  blocking collectives  9.13 us (19%)
  Pallas kernels  3.14 us (7%)
  other arithmetic  0.85 us (2%)
  between operations  0.74 us (2%)
    ppermute x9, starting transfers between devices, send_over(): return lax.ppermute(value, AXES, pairs)  17 us
    ppermute x9, waiting for transfers between devices, send_over(): return lax.ppermute(value, AXES, pairs)  11 us
    all_to_all x1, blocking collectives, shards(): dots = lax.all_to_all(dots, AXES, 0, 0, tiled=True)  9.13 us
    ppermute x9, waiting for transfers between devices, swap_cores(): return lax.ppermute(value, AXES, [(i, i ^ 1) for i in range(n_stu * n_que)])  3.65 us
    pallas_call x7, Pallas kernels, call(): pl.pallas_call(kernel, out_shape=out, in_specs=[pl.BlockSpec(memory_space...  3.14 us
    ppermute x9, starting transfers between devices, swap_cores(): return lax.ppermute(value, AXES, [(i, i ^ 1) for i in range(n_stu * n_que)])  1.26 us
  transfers between devices with their start and end apart: 18, of which 9 were waited for; matrix products, arithmetic and copies ran while one was open for 2% of the time, Pallas kernels for 0%

profile of v8, /device:TPU:0, one launch (start us, length us, event | category | flops | bytes accessed | tf_op | source)
XLA Modules:
  0.0 47.0 jit_solution(16920127112387549561)
XLA Ops:
  0.6 0.5 %collective-permute-start.2 = (f32[32]{0:T(128)}, f32[32]{0:T(128)S(1)}, u32[]{:S(2)}, u32[]{:S(2)}) collective-permute-start(f32[32]{0:T(128)} %param.7), channel_id=1, source_target_pairs={{0,1},{1,0},{2,3},{3,2},{4,5},{5,4},{6,7},{7,6},{8,9},{9,8},{10,11... | collective-permute-start | bytes 392 | tf_op jit(solution)/shard_map/ppermute | solution.py:323
  1.2 0.1 collective-permute-start
  1.2 0.4 collective-permute-start.1
  1.7 0.1 collective-permute-start.9
  1.8 0.8 %broadcast_select_fusion = (f32[32,64]{1,0:T(8,128)S(1)}, f32[32,64]{1,0:T(8,128)S(1)}) fusion(f32[32,64]{1,0:T(8,128)} %param.6, f32[32,64]{1,0:T(8,128)S(1)} %copy-done.1, pred[]{:T(512)S(6)} %eq.2), kind=kLoop, calls=%fused_computation.2 | loop fusion | flops 4096 | bytes 32769 | tf_op jit(solution)/shard_map/jit(_where)/select_n | solution.py:362
  2.6 0.1 reshape.13
  2.7 0.1 reshape.12
  2.8 0.1 maximum_maximum_fusion.1
  2.9 3.9 %collective-permute-start.4 = (f32[40,128]{1,0:T(8,128)S(1)}, f32[40,128]{1,0:T(8,128)S(1)}, u32[]{:S(2)}, u32[]{:S(2)}) collective-permute-start(f32[40,128]{1,0:T(8,128)S(1)} %get-tuple-element.35.refs_4_), channel_id=1, source_target_pairs={{0,24},{1,7},{2,26},{3,5},{4,28},{5,3},{6,30},{7,1},{8,16},{9,15},... | collective-permute-start | bytes 61448 | tf_op jit(solution)/shard_map/ppermute | solution.py:332
  6.8 2.6 %collective-permute-start.6 = (f32[40,128]{1,0:T(8,128)S(1)}, f32[40,128]{1,0:T(8,128)S(1)}, u32[]{:S(2)}, u32[]{:S(2)}) collective-permute-start(f32[40,128]{1,0:T(8,128)S(1)} %get-tuple-element.36.refs_0_), channel_id=1, source_target_pairs={{0,4},{1,17},{2,6},{3,19},{4,0},{5,21},{6,2},{7,23},{8,12},{9,25},... | collective-permute-start | bytes 61448 | tf_op jit(solution)/shard_map/ppermute | solution.py:332
  9.4 1.6 %collective-permute-start.3 = (f32[40,128]{1,0:T(8,128)S(1)}, f32[40,128]{1,0:T(8,128)S(1)}, u32[]{:S(2)}, u32[]{:S(2)}) collective-permute-start(f32[40,128]{1,0:T(8,128)S(1)} %get-tuple-element.36.refs_0_), channel_id=1, source_target_pairs={{0,2},{1,9},{2,0},{3,11},{4,6},{5,13},{6,4},{7,15},{8,10},{9,1},{1... | collective-permute-start | bytes 61448 | tf_op jit(solution)/shard_map/ppermute | solution.py:332
  11.0 0.5 %collective-permute-done.6.refs_3_ = f32[40,128]{1,0:T(8,128)S(1)} collective-permute-done((f32[40,128]{1,0:T(8,128)S(1)}, f32[40,128]{1,0:T(8,128)S(1)}, u32[]{:S(2)}, u32[]{:S(2)}) %collective-permute-start.6) | collective-permute-done | bytes 20512 | tf_op jit(solution)/shard_map/ppermute | solution.py:332
  11.5 1.7 %collective-permute-done.3.refs_1_ = f32[40,128]{1,0:T(8,128)S(1)} collective-permute-done((f32[40,128]{1,0:T(8,128)S(1)}, f32[40,128]{1,0:T(8,128)S(1)}, u32[]{:S(2)}, u32[]{:S(2)}) %collective-permute-start.3) | collective-permute-done | bytes 20512 | tf_op jit(solution)/shard_map/ppermute | solution.py:332
  13.2 1.1 %collective-permute-done.7.refs_5_ = f32[40,128]{1,0:T(8,128)S(1)} collective-permute-done((f32[40,128]{1,0:T(8,128)S(1)}, f32[40,128]{1,0:T(8,128)S(1)}, u32[]{:S(2)}, u32[]{:S(2)}) %collective-permute-start.7) | collective-permute-done | bytes 20512 | tf_op jit(solution)/shard_map/ppermute | solution.py:323
  14.4 0.9 %shard_map.68 = (f32[264,128]{1,0:T(8,128)S(1)}, f32[256,128]{1,0:T(8,128)S(1)}, f32[256,128]{1,0:T(8,128)S(1)}, f32[256,256]{1,0:T(8,128)S(1)}, f32[8,128]{1,0:T(8,128)S(1)}) custom-call(f32[40,128]{1,0:T(8,128)S(1)} %get-tuple-element.36.refs_0_, f32[40,128]{1,0:T(8,128)S(1)} %collective-permute-done.3.refs_1_, ...), custom_call_target="tpu_custom_call" | custom-call | tf_op jit(solution)/shard_map/pallas_call | solution.py:313
  15.3 1.1 %collective-permute-start.12 = (f32[264,128]{1,0:T(8,128)S(1)}, f32[264,128]{1,0:T(8,128)S(1)}, u32[]{:S(2)}, u32[]{:S(2)}) collective-permute-start(f32[264,128]{1,0:T(8,128)S(1)} %get-tuple-element.16.refs_0_), channel_id=1, source_target_pairs={{0,4},{1,17},{2,6},{3,19},{4,0},{5,21},{6,2},{7,23},{8,12},{9,25},... | collective-permute-start | bytes 405512 | tf_op jit(solution)/shard_map/ppermute | solution.py:332
  16.4 1.7 %collective-permute-start.11 = (f32[264,128]{1,0:T(8,128)S(1)}, f32[264,128]{1,0:T(8,128)S(1)}, u32[]{:S(2)}, u32[]{:S(2)}) collective-permute-start(f32[264,128]{1,0:T(8,128)S(1)} %get-tuple-element.16.refs_0_), channel_id=1, source_target_pairs={{0,2},{1,9},{2,0},{3,11},{4,6},{5,13},{6,4},{7,15},{8,10},{9,1},{1... | collective-permute-start | bytes 405512 | tf_op jit(solution)/shard_map/ppermute | solution.py:332
  18.1 1.6 %collective-permute-start.10 = (f32[264,128]{1,0:T(8,128)S(1)}, f32[264,128]{1,0:T(8,128)S(1)}, u32[]{:S(2)}, u32[]{:S(2)}) collective-permute-start(f32[264,128]{1,0:T(8,128)S(1)} %get-tuple-element.16.refs_0_), channel_id=1, source_target_pairs={{0,6},{1,25},{2,4},{3,27},{4,2},{5,29},{6,0},{7,31},{8,14},{9,17},... | collective-permute-start | bytes 405512 | tf_op jit(solution)/shard_map/ppermute | solution.py:332
  19.7 3.0 %collective-permute-done.12.refs_3_ = f32[264,128]{1,0:T(8,128)S(1)} collective-permute-done((f32[264,128]{1,0:T(8,128)S(1)}, f32[264,128]{1,0:T(8,128)S(1)}, u32[]{:S(2)}, u32[]{:S(2)}) %collective-permute-start.12) | collective-permute-done | bytes 135200 | tf_op jit(solution)/shard_map/ppermute | solution.py:332
  22.7 2.6 %collective-permute-done.10.refs_1_ = f32[264,128]{1,0:T(8,128)S(1)} collective-permute-done((f32[264,128]{1,0:T(8,128)S(1)}, f32[264,128]{1,0:T(8,128)S(1)}, u32[]{:S(2)}, u32[]{:S(2)}) %collective-permute-start.10) | collective-permute-done | bytes 135200 | tf_op jit(solution)/shard_map/ppermute | solution.py:332
  25.3 0.2 shard_map.69
  25.6 1.3 %collective-permute-done.13.other_ref.peer_ref = f32[168,128]{1,0:T(8,128)S(1)} collective-permute-done((f32[168,128]{1,0:T(8,128)S(1)}, f32[168,128]{1,0:T(8,128)S(1)}, u32[]{:S(2)}, u32[]{:S(2)}) %collective-permute-start.13) | collective-permute-done | bytes 86048 | tf_op jit(solution)/shard_map/ppermute | solution.py:323
  26.9 0.6 %shard_map.70.refs_0_ = f32[136,128]{1,0:T(8,128)S(1)} custom-call(f32[168,128]{1,0:T(8,128)S(1)} %get-tuple-element.19.mine_ref.refs_4_.send_ref, f32[168,128]{1,0:T(8,128)S(1)} %collective-permute-done.13.other_ref.peer_ref, f32[256,128]{1,0:T(8,128)S(1)} %get-tuple-element.17.refs_4_.left_ref, f32[256,128]{1,0:T(8,128)S(1)} %get-tuple-element.20.right_ref, ...), custom_call_target="tpu_custom_call" | custom-call | tf_op jit(solution)/shard_map/pallas_call | solution.py:313
  27.5 1.9 %collective-permute-start.16 = (f32[136,128]{1,0:T(8,128)S(1)}, f32[136,128]{1,0:T(8,128)S(1)}, u32[]{:S(2)}, u32[]{:S(2)}) collective-permute-start(f32[136,128]{1,0:T(8,128)S(1)} %shard_map.70.refs_0_), channel_id=1, source_target_pairs={{0,6},{1,25},{2,4},{3,27},{4,2},{5,29},{6,0},{7,31},{8,14},{9,17},... | collective-permute-start | bytes 208904 | tf_op jit(solution)/shard_map/ppermute | solution.py:332
  29.4 0.5 %collective-permute-start.15 = (f32[136,128]{1,0:T(8,128)S(1)}, f32[136,128]{1,0:T(8,128)S(1)}, u32[]{:S(2)}, u32[]{:S(2)}) collective-permute-start(f32[136,128]{1,0:T(8,128)S(1)} %shard_map.70.refs_0_), channel_id=1, source_target_pairs={{0,4},{1,17},{2,6},{3,19},{4,0},{5,21},{6,2},{7,23},{8,12},{9,25},... | collective-permute-start | bytes 208904 | tf_op jit(solution)/shard_map/ppermute | solution.py:332
  29.9 2.1 %collective-permute-start.14 = (f32[136,128]{1,0:T(8,128)S(1)}, f32[136,128]{1,0:T(8,128)S(1)}, u32[]{:S(2)}, u32[]{:S(2)}) collective-permute-start(f32[136,128]{1,0:T(8,128)S(1)} %shard_map.70.refs_0_), channel_id=1, source_target_pairs={{0,2},{1,9},{2,0},{3,11},{4,6},{5,13},{6,4},{7,15},{8,10},{9,1},{1... | collective-permute-start | bytes 208904 | tf_op jit(solution)/shard_map/ppermute | solution.py:332
  32.0 1.7 %collective-permute-done.16.refs_3_ = f32[136,128]{1,0:T(8,128)S(1)} collective-permute-done((f32[136,128]{1,0:T(8,128)S(1)}, f32[136,128]{1,0:T(8,128)S(1)}, u32[]{:S(2)}, u32[]{:S(2)}) %collective-permute-start.16) | collective-permute-done | bytes 69664 | tf_op jit(solution)/shard_map/ppermute | solution.py:332
  33.7 1.5 %collective-permute-done.15.refs_2_ = f32[136,128]{1,0:T(8,128)S(1)} collective-permute-done((f32[136,128]{1,0:T(8,128)S(1)}, f32[136,128]{1,0:T(8,128)S(1)}, u32[]{:S(2)}, u32[]{:S(2)}) %collective-permute-start.15) | collective-permute-done | bytes 69664 | tf_op jit(solution)/shard_map/ppermute | solution.py:332
  35.3 1.2 %collective-permute-done.17.other_ref.peer_second_ref = f32[136,128]{1,0:T(8,128)S(1)} collective-permute-done((f32[136,128]{1,0:T(8,128)S(1)}, f32[136,128]{1,0:T(8,128)S(1)}, u32[]{:S(2)}, u32[]{:S(2)}) %collective-permute-start.17) | collective-permute-done | bytes 69664 | tf_op jit(solution)/shard_map/ppermute | solution.py:323
  36.6 0.5 shard_map.72
  37.0 9.1 %all_to_all.5.dots_ref = f32[32,1,128]{2,1,0:T(1,128)S(1)} all-to-all(f32[32,1,128]{2,1,0:T(1,128)S(1)} %shard_map.72), channel_id=1, replica_groups=mesh['stu'=4,'que'=8] {'stu','que'}, dimensions={0} | all-to-all | bytes 32768 | tf_op jit(solution)/shard_map/all_to_all | solution.py:414
  46.1 0.9 %shard_map.73 = (f32[32,64]{1,0:T(8,128)}, f32[32,64]{1,0:T(8,128)}, f32[1,32]{1,0:T(1,128)}) custom-call(f32[32,1,128]{2,1,0:T(1,128)S(1)} %all_to_all.5.dots_ref, f32[168,128]{1,0:T(8,128)S(1)} %get-tuple-element.19.mine_ref.refs_4_.send_ref, f32[168,128]{1,0:T(8,128)S(1)} %collective-permute-done.13.other_ref.peer_ref, ...), custom_call_target="tpu_custom_call" | custom-call | tf_op jit(solution)/shard_map/pallas_call | solution.py:313
  (26 shorter events, 0.4 us)
Async XLA Ops:
  0.6 1.1 %copy-start.1 = (f32[32,64]{1,0:T(8,128)S(1)}, f32[32,64]{1,0:T(8,128)}, u32[]{:S(2)}) copy-start(f32[32,64]{1,0:T(8,128)} %param.5) | copy-start | bytes 24580
  0.6 2.0 %collective-permute-start.2 = (f32[32]{0:T(128)}, f32[32]{0:T(128)S(1)}, u32[]{:S(2)}, u32[]{:S(2)}) collective-permute-start(f32[32]{0:T(128)} %param.7), channel_id=1, source_target_pairs={{0,1},{1,0},{2,3},{3,2},{4,5},{5,4},{6,7},{7,6},{8,9},{9,8},{10,11... | collective-permute-start | bytes 392 | tf_op jit(solution)/shard_map/ppermute | solution.py:323
  1.2 1.6 %collective-permute-start = (f32[32,64]{1,0:T(8,128)}, f32[32,64]{1,0:T(8,128)S(1)}, u32[]{:S(2)}, u32[]{:S(2)}) collective-permute-start(f32[32,64]{1,0:T(8,128)} %param.5), channel_id=1, source_target_pairs={{0,1},{1,0},{2,3},{3,2},{4,5},{5,4},{6,7},{7,6},{8,9},{9,8},{10,11... | collective-permute-start | bytes 24584 | tf_op jit(solution)/shard_map/ppermute | solution.py:323
  1.2 1.5 %collective-permute-start.1 = (f32[32,64]{1,0:T(8,128)}, f32[32,64]{1,0:T(8,128)S(1)}, u32[]{:S(2)}, u32[]{:S(2)}) collective-permute-start(f32[32,64]{1,0:T(8,128)} %param.6), channel_id=1, source_target_pairs={{0,1},{1,0},{2,3},{3,2},{4,5},{5,4},{6,7},{7,6},{8,9},{9,8},{10,11... | collective-permute-start | bytes 24584 | tf_op jit(solution)/shard_map/ppermute | solution.py:323
  1.7 11.5 %collective-permute-start.9 = (s32[256,128]{1,0:T(8,128)}, s32[256,128]{1,0:T(8,128)S(1)}, u32[]{:S(2)}, u32[]{:S(2)}) collective-permute-start(s32[256,128]{1,0:T(8,128)} %own_ref.1), channel_id=1, source_target_pairs={{0,1},{1,0},{2,3},{3,2},{4,5},{5,4},{6,7},{7,6},{8,9},{9,8},{10,11... | collective-permute-start | bytes 393224 | tf_op jit(solution)/shard_map/ppermute | solution.py:323
  1.7 0.9 %copy-start.2 = (f32[32]{0:T(128)S(1)}, f32[32]{0:T(128)}, u32[]{:S(2)}) copy-start(f32[32]{0:T(128)} %param.7) | copy-start | bytes 388
  1.8 11.4 %copy-start = (s32[256,128]{1,0:T(8,128)S(1)}, s32[256,128]{1,0:T(8,128)}, u32[]{:S(2)}) copy-start(s32[256,128]{1,0:T(8,128)} %own_ref.1) | copy-start | bytes 393220
  2.9 8.1 %collective-permute-start.4 = (f32[40,128]{1,0:T(8,128)S(1)}, f32[40,128]{1,0:T(8,128)S(1)}, u32[]{:S(2)}, u32[]{:S(2)}) collective-permute-start(f32[40,128]{1,0:T(8,128)S(1)} %get-tuple-element.35.refs_4_), channel_id=1, source_target_pairs={{0,24},{1,7},{2,26},{3,5},{4,28},{5,3},{6,30},{7,1},{8,16},{9,15},... | collective-permute-start | bytes 61448 | tf_op jit(solution)/shard_map/ppermute | solution.py:332
  6.8 4.7 %collective-permute-start.6 = (f32[40,128]{1,0:T(8,128)S(1)}, f32[40,128]{1,0:T(8,128)S(1)}, u32[]{:S(2)}, u32[]{:S(2)}) collective-permute-start(f32[40,128]{1,0:T(8,128)S(1)} %get-tuple-element.36.refs_0_), channel_id=1, source_target_pairs={{0,4},{1,17},{2,6},{3,19},{4,0},{5,21},{6,2},{7,23},{8,12},{9,25},... | collective-permute-start | bytes 61448 | tf_op jit(solution)/shard_map/ppermute | solution.py:332
  9.4 3.8 %collective-permute-start.3 = (f32[40,128]{1,0:T(8,128)S(1)}, f32[40,128]{1,0:T(8,128)S(1)}, u32[]{:S(2)}, u32[]{:S(2)}) collective-permute-start(f32[40,128]{1,0:T(8,128)S(1)} %get-tuple-element.36.refs_0_), channel_id=1, source_target_pairs={{0,2},{1,9},{2,0},{3,11},{4,6},{5,13},{6,4},{7,15},{8,10},{9,1},{1... | collective-permute-start | bytes 61448 | tf_op jit(solution)/shard_map/ppermute | solution.py:332
  11.0 2.3 %collective-permute-start.5 = (f32[40,128]{1,0:T(8,128)S(1)}, f32[40,128]{1,0:T(8,128)S(1)}, u32[]{:S(2)}, u32[]{:S(2)}) collective-permute-start(f32[40,128]{1,0:T(8,128)S(1)} %collective-permute-done.4.refs_6_), channel_id=1, source_target_pairs={{0,1},{1,0},{2,3},{3,2},{4,5},{5,4},{6,7},{7,6},{8,9},{9,8},{10,11... | collective-permute-start | bytes 61448 | tf_op jit(solution)/shard_map/ppermute | solution.py:323
  11.5 1.8 %collective-permute-start.8 = (f32[40,128]{1,0:T(8,128)S(1)}, f32[40,128]{1,0:T(8,128)S(1)}, u32[]{:S(2)}, u32[]{:S(2)}) collective-permute-start(f32[40,128]{1,0:T(8,128)S(1)} %collective-permute-done.6.refs_3_), channel_id=1, source_target_pairs={{0,1},{1,0},{2,3},{3,2},{4,5},{5,4},{6,7},{7,6},{8,9},{9,8},{10,11... | collective-permute-start | bytes 61448 | tf_op jit(solution)/shard_map/ppermute | solution.py:323
  13.2 1.2 %collective-permute-start.7 = (f32[40,128]{1,0:T(8,128)S(1)}, f32[40,128]{1,0:T(8,128)S(1)}, u32[]{:S(2)}, u32[]{:S(2)}) collective-permute-start(f32[40,128]{1,0:T(8,128)S(1)} %collective-permute-done.3.refs_1_), channel_id=1, source_target_pairs={{0,1},{1,0},{2,3},{3,2},{4,5},{5,4},{6,7},{7,6},{8,9},{9,8},{10,11... | collective-permute-start | bytes 61448 | tf_op jit(solution)/shard_map/ppermute | solution.py:323
  15.3 7.4 %collective-permute-start.12 = (f32[264,128]{1,0:T(8,128)S(1)}, f32[264,128]{1,0:T(8,128)S(1)}, u32[]{:S(2)}, u32[]{:S(2)}) collective-permute-start(f32[264,128]{1,0:T(8,128)S(1)} %get-tuple-element.16.refs_0_), channel_id=1, source_target_pairs={{0,4},{1,17},{2,6},{3,19},{4,0},{5,21},{6,2},{7,23},{8,12},{9,25},... | collective-permute-start | bytes 405512 | tf_op jit(solution)/shard_map/ppermute | solution.py:332
  16.4 6.3 %collective-permute-start.11 = (f32[264,128]{1,0:T(8,128)S(1)}, f32[264,128]{1,0:T(8,128)S(1)}, u32[]{:S(2)}, u32[]{:S(2)}) collective-permute-start(f32[264,128]{1,0:T(8,128)S(1)} %get-tuple-element.16.refs_0_), channel_id=1, source_target_pairs={{0,2},{1,9},{2,0},{3,11},{4,6},{5,13},{6,4},{7,15},{8,10},{9,1},{1... | collective-permute-start | bytes 405512 | tf_op jit(solution)/shard_map/ppermute | solution.py:332
  18.1 7.2 %collective-permute-start.10 = (f32[264,128]{1,0:T(8,128)S(1)}, f32[264,128]{1,0:T(8,128)S(1)}, u32[]{:S(2)}, u32[]{:S(2)}) collective-permute-start(f32[264,128]{1,0:T(8,128)S(1)} %get-tuple-element.16.refs_0_), channel_id=1, source_target_pairs={{0,6},{1,25},{2,4},{3,27},{4,2},{5,29},{6,0},{7,31},{8,14},{9,17},... | collective-permute-start | bytes 405512 | tf_op jit(solution)/shard_map/ppermute | solution.py:332
  25.5 1.3 %collective-permute-start.13 = (f32[168,128]{1,0:T(8,128)S(1)}, f32[168,128]{1,0:T(8,128)S(1)}, u32[]{:S(2)}, u32[]{:S(2)}) collective-permute-start(f32[168,128]{1,0:T(8,128)S(1)} %get-tuple-element.19.mine_ref.refs_4_.send_ref), channel_id=1, source_target_pairs={{0,1},{1,0},{2,3},{3,2},{4,5},{5,4},{6,7},{7,6},{8,9},{9,8},{10,11... | collective-permute-start | bytes 258056 | tf_op jit(solution)/shard_map/ppermute | solution.py:323
  27.5 6.2 %collective-permute-start.16 = (f32[136,128]{1,0:T(8,128)S(1)}, f32[136,128]{1,0:T(8,128)S(1)}, u32[]{:S(2)}, u32[]{:S(2)}) collective-permute-start(f32[136,128]{1,0:T(8,128)S(1)} %shard_map.70.refs_0_), channel_id=1, source_target_pairs={{0,6},{1,25},{2,4},{3,27},{4,2},{5,29},{6,0},{7,31},{8,14},{9,17},... | collective-permute-start | bytes 208904 | tf_op jit(solution)/shard_map/ppermute | solution.py:332
  29.4 5.8 %collective-permute-start.15 = (f32[136,128]{1,0:T(8,128)S(1)}, f32[136,128]{1,0:T(8,128)S(1)}, u32[]{:S(2)}, u32[]{:S(2)}) collective-permute-start(f32[136,128]{1,0:T(8,128)S(1)} %shard_map.70.refs_0_), channel_id=1, source_target_pairs={{0,4},{1,17},{2,6},{3,19},{4,0},{5,21},{6,2},{7,23},{8,12},{9,25},... | collective-permute-start | bytes 208904 | tf_op jit(solution)/shard_map/ppermute | solution.py:332
  29.9 5.3 %collective-permute-start.14 = (f32[136,128]{1,0:T(8,128)S(1)}, f32[136,128]{1,0:T(8,128)S(1)}, u32[]{:S(2)}, u32[]{:S(2)}) collective-permute-start(f32[136,128]{1,0:T(8,128)S(1)} %shard_map.70.refs_0_), channel_id=1, source_target_pairs={{0,2},{1,9},{2,0},{3,11},{4,6},{5,13},{6,4},{7,15},{8,10},{9,1},{1... | collective-permute-start | bytes 208904 | tf_op jit(solution)/shard_map/ppermute | solution.py:332
  35.2 1.3 %collective-permute-start.17 = (f32[136,128]{1,0:T(8,128)S(1)}, f32[136,128]{1,0:T(8,128)S(1)}, u32[]{:S(2)}, u32[]{:S(2)}) collective-permute-start(f32[136,128]{1,0:T(8,128)S(1)} %get-tuple-element.23.mine_ref.second_ref), channel_id=1, source_target_pairs={{0,1},{1,0},{2,3},{3,2},{4,5},{5,4},{6,7},{7,6},{8,9},{9,8},{10,11... | collective-permute-start | bytes 208904 | tf_op jit(solution)/shard_map/ppermute | solution.py:323

commit v9 on v8

--- a/solution.py
+++ b/solution.py
@@ -75,8 +75,7 @@
 
 
 def column(rows):
-    wide = jnp.concatenate([rows, jnp.zeros((LANES - 2, LANES), jnp.float32)], 0)
-    tall = wide.T
+    tall = jnp.concatenate([rows, jnp.zeros((BIAS - 2, LANES), jnp.float32)], 0).T
     return jnp.concatenate([tall[:, 0:1], tall[:, 1:2]], 0)
 
 
@@ -121,7 +120,7 @@
     mine = pieces(refs[:parts], size)
     other = pieces(refs[parts : 2 * parts], size)
     rows = [jnp.where(core == 0, there[size : size + 1], here[size : size + 1]) for here, there in zip(mine, other)]
-    columns = jnp.concatenate(rows + [jnp.zeros((LANES - group, LANES), jnp.float32)], 0).T
+    columns = jnp.concatenate(rows + [jnp.zeros((-group % BIAS, LANES), jnp.float32)] * (group % BIAS > 0), 0).T
     place(list(zip(places, mine)), left_ref, core, columns, core, line, plane, group)
     place(list(zip(places, other)), right_ref, 1 - core, columns, 1 - core, line, plane, group)
     left = left_ref[...]
@@ -155,7 +154,7 @@
 
 
 def start_kernel(group, parts, *refs):
-    sum_refs, (left_ref, icpt_ref, send_ref, diag_ref, root_ref) = refs[:parts], refs[parts:]
+    sum_refs, (left_ref, icpt_ref, send_ref, diag_ref, whole_ref) = refs[:parts], refs[parts:]
     core, line, plane = position()
     total = sum_refs[0][...]
     for ref in sum_refs[1:]:
@@ -169,16 +168,16 @@
     grad_b = total[rows : rows + 2] + icpt_ref[:2]
     diag_b = total[rows + 2 : rows + 4] + 1.0
     first_b = -grad_b / diag_b
-    root_ref[...] = jnp.sqrt(diag)
+    whole_ref[...] = diag
     send_ref[:half, :] = pack(first)
     send_ref[half : half + BIAS, :] = jnp.concatenate(
-        [first_b, jnp.sqrt(diag_b), jnp.zeros((BIAS - 4, LANES), jnp.float32)], 0
+        [first_b, diag_b, jnp.zeros((BIAS - 4, LANES), jnp.float32)], 0
     )
     diag_ref[:half, :] = pack(diag)
     diag_ref[half:, :] = jnp.concatenate([diag_b, jnp.ones((BIAS - 2, LANES), jnp.float32)], 0)
     size = rows // (2 * group)
     at = block_of(core, 1 - core, line, plane, group) * size
-    send_ref[half + BIAS :, :] = root_ref[pl.ds(pl.multiple_of(at, size), size), :]
+    send_ref[half + BIAS :, :] = whole_ref[pl.ds(pl.multiple_of(at, size), size), :]
 
 
 def change_of(mine_ref, other_ref, left, right, half):
@@ -269,7 +268,7 @@
 
 
 def finish_kernel(
-    group, dots_ref, send_ref, peer_ref, second_ref, peer_second_ref, root_ref, theta_ref, disc_ref, icpt_ref
+    group, dots_ref, send_ref, peer_ref, second_ref, peer_second_ref, whole_ref, theta_ref, disc_ref, icpt_ref
 ):
     core, line, plane = position()
     dots = jnp.sum(dots_ref[...], axis=0)
@@ -282,7 +281,7 @@
     det = b * d - e * e
     s = (a * d - e * f) / det
     t = (f * f - a * h) / det
-    rows = root_ref.shape[0]
+    rows = whole_ref.shape[0]
     half = rows // 2
     size = rows // (2 * group)
 
@@ -295,13 +294,13 @@
     mine_at = block_of(core, core, line, plane, group)
     other_at = block_of(1 - core, core, line, plane, group)
     mine = direction(send_ref, second_ref, mine_at)
-    mine = mine * root_ref[pl.ds(pl.multiple_of(mine_at * size, size), size), :]
-    other = direction(peer_ref, peer_second_ref, other_at) * peer_ref[half + BIAS :, :]
+    mine = mine * jnp.sqrt(whole_ref[pl.ds(pl.multiple_of(mine_at * size, size), size), :])
+    other = direction(peer_ref, peer_second_ref, other_at) * jnp.sqrt(peer_ref[half + BIAS :, :])
     theta_ref[...] = jnp.where(core == 0, mine, other)[:, : LANES // 2]
     disc_ref[...] = jnp.where(core == 0, other, mine)[:, : LANES // 2]
     ask = jnp.where(core == 0, peer_ref[half : half + BIAS, :], send_ref[half : half + BIAS, :])
     ask_next = jnp.where(core == 0, peer_second_ref[half : half + 2, :], second_ref[half : half + 2, :])
-    bias = (s * ask[0:2] + t * ask_next) * ask[2:4]
+    bias = (s * ask[0:2] + t * ask_next) * jnp.sqrt(ask[2:4])
     disc_at = jnp.where(core == 0, other_at, mine_at)
     row = jnp.where(disc_at // group == 1, bias[1:2], bias[0:1])
     back = lax.rem(LANES - lax.rem(disc_at, group) * size, LANES)
@@ -391,7 +390,7 @@
         code,
     )
     parts = totals(sums, FIRST_ORDER)
-    first, diag, root = call(
+    first, diag, whole = call(
         functools.partial(start_kernel, group, len(parts)),
         [(half + BIAS + size, LANES), (half + BIAS, LANES), (rows, LANES)],
         *parts,
@@ -420,7 +419,7 @@
         peer,
         second,
         peer_second,
-        root,
+        whole,
     )
     return abilities, discs, icpts[0]
 

time: 47.2 us -> 47.2 us (level)
  no operation moved by 1% of the time
where the time goes in v9:
time: 47.2 us; the launch traced here: 47 us
  starting transfers between devices  18.3 us (39%)
  waiting for transfers between devices  14.6 us (31%)
  blocking collectives  9.13 us (19%)
  Pallas kernels  3.12 us (7%)
  other arithmetic  0.85 us (2%)
  between operations  0.74 us (2%)
    ppermute x9, starting transfers between devices, send_over(): return lax.ppermute(value, AXES, pairs)  17 us
    ppermute x9, waiting for transfers between devices, send_over(): return lax.ppermute(value, AXES, pairs)  11 us
    all_to_all x1, blocking collectives, shards(): dots = lax.all_to_all(dots, AXES, 0, 0, tiled=True)  9.13 us
    ppermute x9, waiting for transfers between devices, swap_cores(): return lax.ppermute(value, AXES, [(i, i ^ 1) for i in range(n_stu * n_que)])  3.65 us
    pallas_call x7, Pallas kernels, call(): pl.pallas_call(kernel, out_shape=out, in_specs=[pl.BlockSpec(memory_space...  3.12 us
    ppermute x9, starting transfers between devices, swap_cores(): return lax.ppermute(value, AXES, [(i, i ^ 1) for i in range(n_stu * n_que)])  1.26 us
  transfers between devices with their start and end apart: 18, of which 9 were waited for; matrix products, arithmetic and copies ran while one was open for 2% of the time, Pallas kernels for 0%

profile of v9, /device:TPU:0, one launch (start us, length us, event | category | flops | bytes accessed | tf_op | source)
XLA Modules:
  0.0 47.0 jit_solution(459477617752139717)
XLA Ops:
  0.6 0.5 %collective-permute-start.2 = (f32[32]{0:T(128)}, f32[32]{0:T(128)S(1)}, u32[]{:S(2)}, u32[]{:S(2)}) collective-permute-start(f32[32]{0:T(128)} %param.7), channel_id=1, source_target_pairs={{0,1},{1,0},{2,3},{3,2},{4,5},{5,4},{6,7},{7,6},{8,9},{9,8},{10,11... | collective-permute-start | bytes 392 | tf_op jit(solution)/shard_map/ppermute | solution.py:322
  1.2 0.1 collective-permute-start
  1.2 0.4 collective-permute-start.1
  1.7 0.1 collective-permute-start.9
  1.8 0.8 %broadcast_select_fusion = (f32[32,64]{1,0:T(8,128)S(1)}, f32[32,64]{1,0:T(8,128)S(1)}) fusion(f32[32,64]{1,0:T(8,128)} %param.6, f32[32,64]{1,0:T(8,128)S(1)} %copy-done.1, pred[]{:T(512)S(6)} %eq.2), kind=kLoop, calls=%fused_computation.2 | loop fusion | flops 4096 | bytes 32769 | tf_op jit(solution)/shard_map/jit(_where)/select_n | solution.py:361
  2.6 0.1 reshape.13
  2.7 0.1 reshape.12
  2.8 0.1 maximum_maximum_fusion.1
  2.9 3.9 %collective-permute-start.4 = (f32[40,128]{1,0:T(8,128)S(1)}, f32[40,128]{1,0:T(8,128)S(1)}, u32[]{:S(2)}, u32[]{:S(2)}) collective-permute-start(f32[40,128]{1,0:T(8,128)S(1)} %get-tuple-element.35.refs_4_), channel_id=1, source_target_pairs={{0,24},{1,7},{2,26},{3,5},{4,28},{5,3},{6,30},{7,1},{8,16},{9,15},... | collective-permute-start | bytes 61448 | tf_op jit(solution)/shard_map/ppermute | solution.py:331
  6.8 2.6 %collective-permute-start.6 = (f32[40,128]{1,0:T(8,128)S(1)}, f32[40,128]{1,0:T(8,128)S(1)}, u32[]{:S(2)}, u32[]{:S(2)}) collective-permute-start(f32[40,128]{1,0:T(8,128)S(1)} %get-tuple-element.36.refs_0_), channel_id=1, source_target_pairs={{0,4},{1,17},{2,6},{3,19},{4,0},{5,21},{6,2},{7,23},{8,12},{9,25},... | collective-permute-start | bytes 61448 | tf_op jit(solution)/shard_map/ppermute | solution.py:331
  9.4 1.6 %collective-permute-start.3 = (f32[40,128]{1,0:T(8,128)S(1)}, f32[40,128]{1,0:T(8,128)S(1)}, u32[]{:S(2)}, u32[]{:S(2)}) collective-permute-start(f32[40,128]{1,0:T(8,128)S(1)} %get-tuple-element.36.refs_0_), channel_id=1, source_target_pairs={{0,2},{1,9},{2,0},{3,11},{4,6},{5,13},{6,4},{7,15},{8,10},{9,1},{1... | collective-permute-start | bytes 61448 | tf_op jit(solution)/shard_map/ppermute | solution.py:331
  11.0 0.5 %collective-permute-done.6.refs_3_ = f32[40,128]{1,0:T(8,128)S(1)} collective-permute-done((f32[40,128]{1,0:T(8,128)S(1)}, f32[40,128]{1,0:T(8,128)S(1)}, u32[]{:S(2)}, u32[]{:S(2)}) %collective-permute-start.6) | collective-permute-done | bytes 20512 | tf_op jit(solution)/shard_map/ppermute | solution.py:331
  11.5 1.7 %collective-permute-done.3.refs_1_ = f32[40,128]{1,0:T(8,128)S(1)} collective-permute-done((f32[40,128]{1,0:T(8,128)S(1)}, f32[40,128]{1,0:T(8,128)S(1)}, u32[]{:S(2)}, u32[]{:S(2)}) %collective-permute-start.3) | collective-permute-done | bytes 20512 | tf_op jit(solution)/shard_map/ppermute | solution.py:331
  13.2 1.1 %collective-permute-done.7.refs_5_ = f32[40,128]{1,0:T(8,128)S(1)} collective-permute-done((f32[40,128]{1,0:T(8,128)S(1)}, f32[40,128]{1,0:T(8,128)S(1)}, u32[]{:S(2)}, u32[]{:S(2)}) %collective-permute-start.7) | collective-permute-done | bytes 20512 | tf_op jit(solution)/shard_map/ppermute | solution.py:322
  14.4 0.9 %shard_map.68 = (f32[264,128]{1,0:T(8,128)S(1)}, f32[256,128]{1,0:T(8,128)S(1)}, f32[256,128]{1,0:T(8,128)S(1)}, f32[256,256]{1,0:T(8,128)S(1)}, f32[8,128]{1,0:T(8,128)S(1)}) custom-call(f32[40,128]{1,0:T(8,128)S(1)} %get-tuple-element.36.refs_0_, f32[40,128]{1,0:T(8,128)S(1)} %collective-permute-done.3.refs_1_, ...), custom_call_target="tpu_custom_call" | custom-call | tf_op jit(solution)/shard_map/pallas_call | solution.py:312
  15.3 1.1 %collective-permute-start.12 = (f32[264,128]{1,0:T(8,128)S(1)}, f32[264,128]{1,0:T(8,128)S(1)}, u32[]{:S(2)}, u32[]{:S(2)}) collective-permute-start(f32[264,128]{1,0:T(8,128)S(1)} %get-tuple-element.16.refs_0_), channel_id=1, source_target_pairs={{0,4},{1,17},{2,6},{3,19},{4,0},{5,21},{6,2},{7,23},{8,12},{9,25},... | collective-permute-start | bytes 405512 | tf_op jit(solution)/shard_map/ppermute | solution.py:331
  16.4 1.7 %collective-permute-start.11 = (f32[264,128]{1,0:T(8,128)S(1)}, f32[264,128]{1,0:T(8,128)S(1)}, u32[]{:S(2)}, u32[]{:S(2)}) collective-permute-start(f32[264,128]{1,0:T(8,128)S(1)} %get-tuple-element.16.refs_0_), channel_id=1, source_target_pairs={{0,2},{1,9},{2,0},{3,11},{4,6},{5,13},{6,4},{7,15},{8,10},{9,1},{1... | collective-permute-start | bytes 405512 | tf_op jit(solution)/shard_map/ppermute | solution.py:331
  18.1 1.6 %collective-permute-start.10 = (f32[264,128]{1,0:T(8,128)S(1)}, f32[264,128]{1,0:T(8,128)S(1)}, u32[]{:S(2)}, u32[]{:S(2)}) collective-permute-start(f32[264,128]{1,0:T(8,128)S(1)} %get-tuple-element.16.refs_0_), channel_id=1, source_target_pairs={{0,6},{1,25},{2,4},{3,27},{4,2},{5,29},{6,0},{7,31},{8,14},{9,17},... | collective-permute-start | bytes 405512 | tf_op jit(solution)/shard_map/ppermute | solution.py:331
  19.7 3.0 %collective-permute-done.12.refs_3_ = f32[264,128]{1,0:T(8,128)S(1)} collective-permute-done((f32[264,128]{1,0:T(8,128)S(1)}, f32[264,128]{1,0:T(8,128)S(1)}, u32[]{:S(2)}, u32[]{:S(2)}) %collective-permute-start.12) | collective-permute-done | bytes 135200 | tf_op jit(solution)/shard_map/ppermute | solution.py:331
  22.7 2.6 %collective-permute-done.10.refs_1_ = f32[264,128]{1,0:T(8,128)S(1)} collective-permute-done((f32[264,128]{1,0:T(8,128)S(1)}, f32[264,128]{1,0:T(8,128)S(1)}, u32[]{:S(2)}, u32[]{:S(2)}) %collective-permute-start.10) | collective-permute-done | bytes 135200 | tf_op jit(solution)/shard_map/ppermute | solution.py:331
  25.3 0.2 shard_map.69
  25.6 1.3 %collective-permute-done.13.other_ref.peer_ref = f32[168,128]{1,0:T(8,128)S(1)} collective-permute-done((f32[168,128]{1,0:T(8,128)S(1)}, f32[168,128]{1,0:T(8,128)S(1)}, u32[]{:S(2)}, u32[]{:S(2)}) %collective-permute-start.13) | collective-permute-done | bytes 86048 | tf_op jit(solution)/shard_map/ppermute | solution.py:322
  26.9 0.6 %shard_map.70.refs_0_ = f32[136,128]{1,0:T(8,128)S(1)} custom-call(f32[168,128]{1,0:T(8,128)S(1)} %get-tuple-element.19.mine_ref.refs_4_.send_ref, f32[168,128]{1,0:T(8,128)S(1)} %collective-permute-done.13.other_ref.peer_ref, f32[256,128]{1,0:T(8,128)S(1)} %get-tuple-element.17.refs_4_.left_ref, f32[256,128]{1,0:T(8,128)S(1)} %get-tuple-element.20.right_ref, ...), custom_call_target="tpu_custom_call" | custom-call | tf_op jit(solution)/shard_map/pallas_call | solution.py:312
  27.5 1.9 %collective-permute-start.16 = (f32[136,128]{1,0:T(8,128)S(1)}, f32[136,128]{1,0:T(8,128)S(1)}, u32[]{:S(2)}, u32[]{:S(2)}) collective-permute-start(f32[136,128]{1,0:T(8,128)S(1)} %shard_map.70.refs_0_), channel_id=1, source_target_pairs={{0,6},{1,25},{2,4},{3,27},{4,2},{5,29},{6,0},{7,31},{8,14},{9,17},... | collective-permute-start | bytes 208904 | tf_op jit(solution)/shard_map/ppermute | solution.py:331
  29.3 0.5 %collective-permute-start.15 = (f32[136,128]{1,0:T(8,128)S(1)}, f32[136,128]{1,0:T(8,128)S(1)}, u32[]{:S(2)}, u32[]{:S(2)}) collective-permute-start(f32[136,128]{1,0:T(8,128)S(1)} %shard_map.70.refs_0_), channel_id=1, source_target_pairs={{0,4},{1,17},{2,6},{3,19},{4,0},{5,21},{6,2},{7,23},{8,12},{9,25},... | collective-permute-start | bytes 208904 | tf_op jit(solution)/shard_map/ppermute | solution.py:331
  29.9 2.1 %collective-permute-start.14 = (f32[136,128]{1,0:T(8,128)S(1)}, f32[136,128]{1,0:T(8,128)S(1)}, u32[]{:S(2)}, u32[]{:S(2)}) collective-permute-start(f32[136,128]{1,0:T(8,128)S(1)} %shard_map.70.refs_0_), channel_id=1, source_target_pairs={{0,2},{1,9},{2,0},{3,11},{4,6},{5,13},{6,4},{7,15},{8,10},{9,1},{1... | collective-permute-start | bytes 208904 | tf_op jit(solution)/shard_map/ppermute | solution.py:331
  31.9 1.7 %collective-permute-done.16.refs_3_ = f32[136,128]{1,0:T(8,128)S(1)} collective-permute-done((f32[136,128]{1,0:T(8,128)S(1)}, f32[136,128]{1,0:T(8,128)S(1)}, u32[]{:S(2)}, u32[]{:S(2)}) %collective-permute-start.16) | collective-permute-done | bytes 69664 | tf_op jit(solution)/shard_map/ppermute | solution.py:331
  33.7 1.5 %collective-permute-done.15.refs_2_ = f32[136,128]{1,0:T(8,128)S(1)} collective-permute-done((f32[136,128]{1,0:T(8,128)S(1)}, f32[136,128]{1,0:T(8,128)S(1)}, u32[]{:S(2)}, u32[]{:S(2)}) %collective-permute-start.15) | collective-permute-done | bytes 69664 | tf_op jit(solution)/shard_map/ppermute | solution.py:331
  35.3 1.2 %collective-permute-done.17.other_ref.peer_second_ref = f32[136,128]{1,0:T(8,128)S(1)} collective-permute-done((f32[136,128]{1,0:T(8,128)S(1)}, f32[136,128]{1,0:T(8,128)S(1)}, u32[]{:S(2)}, u32[]{:S(2)}) %collective-permute-start.17) | collective-permute-done | bytes 69664 | tf_op jit(solution)/shard_map/ppermute | solution.py:322
  36.5 0.5 shard_map.72
  37.0 9.1 %all_to_all.5.dots_ref = f32[32,1,128]{2,1,0:T(1,128)S(1)} all-to-all(f32[32,1,128]{2,1,0:T(1,128)S(1)} %shard_map.72), channel_id=1, replica_groups=mesh['stu'=4,'que'=8] {'stu','que'}, dimensions={0} | all-to-all | bytes 32768 | tf_op jit(solution)/shard_map/all_to_all | solution.py:413
  46.1 0.9 %shard_map.73 = (f32[32,64]{1,0:T(8,128)}, f32[32,64]{1,0:T(8,128)}, f32[1,32]{1,0:T(1,128)}) custom-call(f32[32,1,128]{2,1,0:T(1,128)S(1)} %all_to_all.5.dots_ref, f32[168,128]{1,0:T(8,128)S(1)} %get-tuple-element.19.mine_ref.refs_4_.send_ref, f32[168,128]{1,0:T(8,128)S(1)} %collective-permute-done.13.other_ref.peer_ref, ...), custom_call_target="tpu_custom_call" | custom-call | tf_op jit(solution)/shard_map/pallas_call | solution.py:312
  (26 shorter events, 0.4 us)
Async XLA Ops:
  0.6 1.1 %copy-start.1 = (f32[32,64]{1,0:T(8,128)S(1)}, f32[32,64]{1,0:T(8,128)}, u32[]{:S(2)}) copy-start(f32[32,64]{1,0:T(8,128)} %param.5) | copy-start | bytes 24580
  0.6 2.0 %collective-permute-start.2 = (f32[32]{0:T(128)}, f32[32]{0:T(128)S(1)}, u32[]{:S(2)}, u32[]{:S(2)}) collective-permute-start(f32[32]{0:T(128)} %param.7), channel_id=1, source_target_pairs={{0,1},{1,0},{2,3},{3,2},{4,5},{5,4},{6,7},{7,6},{8,9},{9,8},{10,11... | collective-permute-start | bytes 392 | tf_op jit(solution)/shard_map/ppermute | solution.py:322
  1.2 1.6 %collective-permute-start = (f32[32,64]{1,0:T(8,128)}, f32[32,64]{1,0:T(8,128)S(1)}, u32[]{:S(2)}, u32[]{:S(2)}) collective-permute-start(f32[32,64]{1,0:T(8,128)} %param.5), channel_id=1, source_target_pairs={{0,1},{1,0},{2,3},{3,2},{4,5},{5,4},{6,7},{7,6},{8,9},{9,8},{10,11... | collective-permute-start | bytes 24584 | tf_op jit(solution)/shard_map/ppermute | solution.py:322
  1.2 1.5 %collective-permute-start.1 = (f32[32,64]{1,0:T(8,128)}, f32[32,64]{1,0:T(8,128)S(1)}, u32[]{:S(2)}, u32[]{:S(2)}) collective-permute-start(f32[32,64]{1,0:T(8,128)} %param.6), channel_id=1, source_target_pairs={{0,1},{1,0},{2,3},{3,2},{4,5},{5,4},{6,7},{7,6},{8,9},{9,8},{10,11... | collective-permute-start | bytes 24584 | tf_op jit(solution)/shard_map/ppermute | solution.py:322
  1.7 11.5 %collective-permute-start.9 = (s32[256,128]{1,0:T(8,128)}, s32[256,128]{1,0:T(8,128)S(1)}, u32[]{:S(2)}, u32[]{:S(2)}) collective-permute-start(s32[256,128]{1,0:T(8,128)} %own_ref.1), channel_id=1, source_target_pairs={{0,1},{1,0},{2,3},{3,2},{4,5},{5,4},{6,7},{7,6},{8,9},{9,8},{10,11... | collective-permute-start | bytes 393224 | tf_op jit(solution)/shard_map/ppermute | solution.py:322
  1.7 0.9 %copy-start.2 = (f32[32]{0:T(128)S(1)}, f32[32]{0:T(128)}, u32[]{:S(2)}) copy-start(f32[32]{0:T(128)} %param.7) | copy-start | bytes 388
  1.8 11.4 %copy-start = (s32[256,128]{1,0:T(8,128)S(1)}, s32[256,128]{1,0:T(8,128)}, u32[]{:S(2)}) copy-start(s32[256,128]{1,0:T(8,128)} %own_ref.1) | copy-start | bytes 393220
  2.9 8.1 %collective-permute-start.4 = (f32[40,128]{1,0:T(8,128)S(1)}, f32[40,128]{1,0:T(8,128)S(1)}, u32[]{:S(2)}, u32[]{:S(2)}) collective-permute-start(f32[40,128]{1,0:T(8,128)S(1)} %get-tuple-element.35.refs_4_), channel_id=1, source_target_pairs={{0,24},{1,7},{2,26},{3,5},{4,28},{5,3},{6,30},{7,1},{8,16},{9,15},... | collective-permute-start | bytes 61448 | tf_op jit(solution)/shard_map/ppermute | solution.py:331
  6.8 4.7 %collective-permute-start.6 = (f32[40,128]{1,0:T(8,128)S(1)}, f32[40,128]{1,0:T(8,128)S(1)}, u32[]{:S(2)}, u32[]{:S(2)}) collective-permute-start(f32[40,128]{1,0:T(8,128)S(1)} %get-tuple-element.36.refs_0_), channel_id=1, source_target_pairs={{0,4},{1,17},{2,6},{3,19},{4,0},{5,21},{6,2},{7,23},{8,12},{9,25},... | collective-permute-start | bytes 61448 | tf_op jit(solution)/shard_map/ppermute | solution.py:331
  9.4 3.8 %collective-permute-start.3 = (f32[40,128]{1,0:T(8,128)S(1)}, f32[40,128]{1,0:T(8,128)S(1)}, u32[]{:S(2)}, u32[]{:S(2)}) collective-permute-start(f32[40,128]{1,0:T(8,128)S(1)} %get-tuple-element.36.refs_0_), channel_id=1, source_target_pairs={{0,2},{1,9},{2,0},{3,11},{4,6},{5,13},{6,4},{7,15},{8,10},{9,1},{1... | collective-permute-start | bytes 61448 | tf_op jit(solution)/shard_map/ppermute | solution.py:331
  11.0 2.3 %collective-permute-start.5 = (f32[40,128]{1,0:T(8,128)S(1)}, f32[40,128]{1,0:T(8,128)S(1)}, u32[]{:S(2)}, u32[]{:S(2)}) collective-permute-start(f32[40,128]{1,0:T(8,128)S(1)} %collective-permute-done.4.refs_6_), channel_id=1, source_target_pairs={{0,1},{1,0},{2,3},{3,2},{4,5},{5,4},{6,7},{7,6},{8,9},{9,8},{10,11... | collective-permute-start | bytes 61448 | tf_op jit(solution)/shard_map/ppermute | solution.py:322
  11.5 1.8 %collective-permute-start.8 = (f32[40,128]{1,0:T(8,128)S(1)}, f32[40,128]{1,0:T(8,128)S(1)}, u32[]{:S(2)}, u32[]{:S(2)}) collective-permute-start(f32[40,128]{1,0:T(8,128)S(1)} %collective-permute-done.6.refs_3_), channel_id=1, source_target_pairs={{0,1},{1,0},{2,3},{3,2},{4,5},{5,4},{6,7},{7,6},{8,9},{9,8},{10,11... | collective-permute-start | bytes 61448 | tf_op jit(solution)/shard_map/ppermute | solution.py:322
  13.2 1.2 %collective-permute-start.7 = (f32[40,128]{1,0:T(8,128)S(1)}, f32[40,128]{1,0:T(8,128)S(1)}, u32[]{:S(2)}, u32[]{:S(2)}) collective-permute-start(f32[40,128]{1,0:T(8,128)S(1)} %collective-permute-done.3.refs_1_), channel_id=1, source_target_pairs={{0,1},{1,0},{2,3},{3,2},{4,5},{5,4},{6,7},{7,6},{8,9},{9,8},{10,11... | collective-permute-start | bytes 61448 | tf_op jit(solution)/shard_map/ppermute | solution.py:322
  15.3 7.4 %collective-permute-start.12 = (f32[264,128]{1,0:T(8,128)S(1)}, f32[264,128]{1,0:T(8,128)S(1)}, u32[]{:S(2)}, u32[]{:S(2)}) collective-permute-start(f32[264,128]{1,0:T(8,128)S(1)} %get-tuple-element.16.refs_0_), channel_id=1, source_target_pairs={{0,4},{1,17},{2,6},{3,19},{4,0},{5,21},{6,2},{7,23},{8,12},{9,25},... | collective-permute-start | bytes 405512 | tf_op jit(solution)/shard_map/ppermute | solution.py:331
  16.4 6.3 %collective-permute-start.11 = (f32[264,128]{1,0:T(8,128)S(1)}, f32[264,128]{1,0:T(8,128)S(1)}, u32[]{:S(2)}, u32[]{:S(2)}) collective-permute-start(f32[264,128]{1,0:T(8,128)S(1)} %get-tuple-element.16.refs_0_), channel_id=1, source_target_pairs={{0,2},{1,9},{2,0},{3,11},{4,6},{5,13},{6,4},{7,15},{8,10},{9,1},{1... | collective-permute-start | bytes 405512 | tf_op jit(solution)/shard_map/ppermute | solution.py:331
  18.1 7.2 %collective-permute-start.10 = (f32[264,128]{1,0:T(8,128)S(1)}, f32[264,128]{1,0:T(8,128)S(1)}, u32[]{:S(2)}, u32[]{:S(2)}) collective-permute-start(f32[264,128]{1,0:T(8,128)S(1)} %get-tuple-element.16.refs_0_), channel_id=1, source_target_pairs={{0,6},{1,25},{2,4},{3,27},{4,2},{5,29},{6,0},{7,31},{8,14},{9,17},... | collective-permute-start | bytes 405512 | tf_op jit(solution)/shard_map/ppermute | solution.py:331
  25.5 1.3 %collective-permute-start.13 = (f32[168,128]{1,0:T(8,128)S(1)}, f32[168,128]{1,0:T(8,128)S(1)}, u32[]{:S(2)}, u32[]{:S(2)}) collective-permute-start(f32[168,128]{1,0:T(8,128)S(1)} %get-tuple-element.19.mine_ref.refs_4_.send_ref), channel_id=1, source_target_pairs={{0,1},{1,0},{2,3},{3,2},{4,5},{5,4},{6,7},{7,6},{8,9},{9,8},{10,11... | collective-permute-start | bytes 258056 | tf_op jit(solution)/shard_map/ppermute | solution.py:322
  27.5 6.2 %collective-permute-start.16 = (f32[136,128]{1,0:T(8,128)S(1)}, f32[136,128]{1,0:T(8,128)S(1)}, u32[]{:S(2)}, u32[]{:S(2)}) collective-permute-start(f32[136,128]{1,0:T(8,128)S(1)} %shard_map.70.refs_0_), channel_id=1, source_target_pairs={{0,6},{1,25},{2,4},{3,27},{4,2},{5,29},{6,0},{7,31},{8,14},{9,17},... | collective-permute-start | bytes 208904 | tf_op jit(solution)/shard_map/ppermute | solution.py:331
  29.3 5.8 %collective-permute-start.15 = (f32[136,128]{1,0:T(8,128)S(1)}, f32[136,128]{1,0:T(8,128)S(1)}, u32[]{:S(2)}, u32[]{:S(2)}) collective-permute-start(f32[136,128]{1,0:T(8,128)S(1)} %shard_map.70.refs_0_), channel_id=1, source_target_pairs={{0,4},{1,17},{2,6},{3,19},{4,0},{5,21},{6,2},{7,23},{8,12},{9,25},... | collective-permute-start | bytes 208904 | tf_op jit(solution)/shard_map/ppermute | solution.py:331
  29.9 5.3 %collective-permute-start.14 = (f32[136,128]{1,0:T(8,128)S(1)}, f32[136,128]{1,0:T(8,128)S(1)}, u32[]{:S(2)}, u32[]{:S(2)}) collective-permute-start(f32[136,128]{1,0:T(8,128)S(1)} %shard_map.70.refs_0_), channel_id=1, source_target_pairs={{0,2},{1,9},{2,0},{3,11},{4,6},{5,13},{6,4},{7,15},{8,10},{9,1},{1... | collective-permute-start | bytes 208904 | tf_op jit(solution)/shard_map/ppermute | solution.py:331
  35.2 1.3 %collective-permute-start.17 = (f32[136,128]{1,0:T(8,128)S(1)}, f32[136,128]{1,0:T(8,128)S(1)}, u32[]{:S(2)}, u32[]{:S(2)}) collective-permute-start(f32[136,128]{1,0:T(8,128)S(1)} %get-tuple-element.23.mine_ref.second_ref), channel_id=1, source_target_pairs={{0,1},{1,0},{2,3},{3,2},{4,5},{5,4},{6,7},{7,6},{8,9},{9,8},{10,11... | collective-permute-start | bytes 208904 | tf_op jit(solution)/shard_map/ppermute | solution.py:322

commit v10 on v9

--- a/solution.py
+++ b/solution.py
@@ -252,19 +252,27 @@
 
 
 def form_kernel(mine_ref, other_ref, left_ref, right_ref, weight_ref, dots_ref, out_ref):
+    core, _, _ = position()
     half = left_ref.shape[0] // 2
-    change = change_of(mine_ref, other_ref, left_ref[...], right_ref[...], half)
-
-    def use(value):
-        form = 0.5 * jnp.sum(weight_ref[...] * value * value, axis=0, keepdims=True)
+
+    def give(terms):
         row = lax.broadcasted_iota(jnp.int32, (8, LANES), 0)
-        terms = dots_ref[...] + jnp.where(row == 3, form[:, :LANES] + form[:, LANES:], 0.0)
+        lane = lax.broadcasted_iota(jnp.int32, (8, LANES), 1)
         sums = jnp.sum(terms, axis=1, keepdims=True)
-        lane = lax.broadcasted_iota(jnp.int32, (8, LANES), 1)
         dots = jnp.sum(jnp.where(lane == row, sums, 0.0), axis=0, keepdims=True)
         out_ref[...] = jnp.broadcast_to(dots[None], out_ref.shape)
 
-    with_bias(change, mine_ref, other_ref, half, use)
+    @pl.when(core == 0)
+    def _():
+        change = change_of(mine_ref, other_ref, left_ref[...], right_ref[...], half)
+        change = change + bias_lanes(other_ref[half : half + 2, :])
+        form = jnp.sum(weight_ref[...] * change * change, axis=0, keepdims=True)
+        row = lax.broadcasted_iota(jnp.int32, (8, LANES), 0)
+        give(dots_ref[...] + jnp.where(row == 3, form[:, :LANES] + form[:, LANES:], 0.0))
+
+    @pl.when(core == 1)
+    def _():
+        give(dots_ref[...])
 
 
 def finish_kernel(

time: 47.2 us -> 47.2 us (level)
  no operation moved by 1% of the time
where the time goes in v10:
time: 47.2 us; the launch traced here: 47 us
  starting transfers between devices  18.3 us (39%)
  waiting for transfers between devices  14.6 us (31%)
  blocking collectives  9.12 us (19%)
  Pallas kernels  3.11 us (7%)
  other arithmetic  0.85 us (2%)
  between operations  0.74 us (2%)
    ppermute x9, starting transfers between devices, send_over(): return lax.ppermute(value, AXES, pairs)  17 us
    ppermute x9, waiting for transfers between devices, send_over(): return lax.ppermute(value, AXES, pairs)  11 us
    all_to_all x1, blocking collectives, shards(): dots = lax.all_to_all(dots, AXES, 0, 0, tiled=True)  9.12 us
    ppermute x9, waiting for transfers between devices, swap_cores(): return lax.ppermute(value, AXES, [(i, i ^ 1) for i in range(n_stu * n_que)])  3.65 us
    pallas_call x7, Pallas kernels, call(): pl.pallas_call(kernel, out_shape=out, in_specs=[pl.BlockSpec(memory_space...  3.11 us
    ppermute x9, starting transfers between devices, swap_cores(): return lax.ppermute(value, AXES, [(i, i ^ 1) for i in range(n_stu * n_que)])  1.26 us
  transfers between devices with their start and end apart: 18, of which 9 were waited for; matrix products, arithmetic and copies ran while one was open for 2% of the time, Pallas kernels for 0%

profile of v10, /device:TPU:0, one launch (start us, length us, event | category | flops | bytes accessed | tf_op | source)
XLA Modules:
  0.0 47.0 jit_solution(17565489112149559008)
XLA Ops:
  0.6 0.5 %collective-permute-start.2 = (f32[32]{0:T(128)}, f32[32]{0:T(128)S(1)}, u32[]{:S(2)}, u32[]{:S(2)}) collective-permute-start(f32[32]{0:T(128)} %param.7), channel_id=1, source_target_pairs={{0,1},{1,0},{2,3},{3,2},{4,5},{5,4},{6,7},{7,6},{8,9},{9,8},{10,11... | collective-permute-start | bytes 392 | tf_op jit(solution)/shard_map/ppermute | solution.py:330
  1.2 0.1 collective-permute-start
  1.2 0.4 collective-permute-start.1
  1.7 0.1 collective-permute-start.9
  1.8 0.8 %broadcast_select_fusion = (f32[32,64]{1,0:T(8,128)S(1)}, f32[32,64]{1,0:T(8,128)S(1)}) fusion(f32[32,64]{1,0:T(8,128)} %param.6, f32[32,64]{1,0:T(8,128)S(1)} %copy-done.1, pred[]{:T(512)S(6)} %eq.2), kind=kLoop, calls=%fused_computation.2 | loop fusion | flops 4096 | bytes 32769 | tf_op jit(solution)/shard_map/jit(_where)/select_n | solution.py:369
  2.6 0.1 reshape.13
  2.7 0.1 reshape.12
  2.8 0.1 maximum_maximum_fusion.1
  2.9 3.9 %collective-permute-start.4 = (f32[40,128]{1,0:T(8,128)S(1)}, f32[40,128]{1,0:T(8,128)S(1)}, u32[]{:S(2)}, u32[]{:S(2)}) collective-permute-start(f32[40,128]{1,0:T(8,128)S(1)} %get-tuple-element.35.refs_4_), channel_id=1, source_target_pairs={{0,24},{1,7},{2,26},{3,5},{4,28},{5,3},{6,30},{7,1},{8,16},{9,15},... | collective-permute-start | bytes 61448 | tf_op jit(solution)/shard_map/ppermute | solution.py:339
  6.8 2.6 %collective-permute-start.6 = (f32[40,128]{1,0:T(8,128)S(1)}, f32[40,128]{1,0:T(8,128)S(1)}, u32[]{:S(2)}, u32[]{:S(2)}) collective-permute-start(f32[40,128]{1,0:T(8,128)S(1)} %get-tuple-element.36.refs_0_), channel_id=1, source_target_pairs={{0,4},{1,17},{2,6},{3,19},{4,0},{5,21},{6,2},{7,23},{8,12},{9,25},... | collective-permute-start | bytes 61448 | tf_op jit(solution)/shard_map/ppermute | solution.py:339
  9.4 1.6 %collective-permute-start.3 = (f32[40,128]{1,0:T(8,128)S(1)}, f32[40,128]{1,0:T(8,128)S(1)}, u32[]{:S(2)}, u32[]{:S(2)}) collective-permute-start(f32[40,128]{1,0:T(8,128)S(1)} %get-tuple-element.36.refs_0_), channel_id=1, source_target_pairs={{0,2},{1,9},{2,0},{3,11},{4,6},{5,13},{6,4},{7,15},{8,10},{9,1},{1... | collective-permute-start | bytes 61448 | tf_op jit(solution)/shard_map/ppermute | solution.py:339
  11.0 0.5 %collective-permute-done.6.refs_3_ = f32[40,128]{1,0:T(8,128)S(1)} collective-permute-done((f32[40,128]{1,0:T(8,128)S(1)}, f32[40,128]{1,0:T(8,128)S(1)}, u32[]{:S(2)}, u32[]{:S(2)}) %collective-permute-start.6) | collective-permute-done | bytes 20512 | tf_op jit(solution)/shard_map/ppermute | solution.py:339
  11.5 1.7 %collective-permute-done.3.refs_1_ = f32[40,128]{1,0:T(8,128)S(1)} collective-permute-done((f32[40,128]{1,0:T(8,128)S(1)}, f32[40,128]{1,0:T(8,128)S(1)}, u32[]{:S(2)}, u32[]{:S(2)}) %collective-permute-start.3) | collective-permute-done | bytes 20512 | tf_op jit(solution)/shard_map/ppermute | solution.py:339
  13.2 1.1 %collective-permute-done.7.refs_5_ = f32[40,128]{1,0:T(8,128)S(1)} collective-permute-done((f32[40,128]{1,0:T(8,128)S(1)}, f32[40,128]{1,0:T(8,128)S(1)}, u32[]{:S(2)}, u32[]{:S(2)}) %collective-permute-start.7) | collective-permute-done | bytes 20512 | tf_op jit(solution)/shard_map/ppermute | solution.py:330
  14.4 0.9 %shard_map.68 = (f32[264,128]{1,0:T(8,128)S(1)}, f32[256,128]{1,0:T(8,128)S(1)}, f32[256,128]{1,0:T(8,128)S(1)}, f32[256,256]{1,0:T(8,128)S(1)}, f32[8,128]{1,0:T(8,128)S(1)}) custom-call(f32[40,128]{1,0:T(8,128)S(1)} %get-tuple-element.36.refs_0_, f32[40,128]{1,0:T(8,128)S(1)} %collective-permute-done.3.refs_1_, ...), custom_call_target="tpu_custom_call" | custom-call | tf_op jit(solution)/shard_map/pallas_call | solution.py:320
  15.3 1.1 %collective-permute-start.12 = (f32[264,128]{1,0:T(8,128)S(1)}, f32[264,128]{1,0:T(8,128)S(1)}, u32[]{:S(2)}, u32[]{:S(2)}) collective-permute-start(f32[264,128]{1,0:T(8,128)S(1)} %get-tuple-element.16.refs_0_), channel_id=1, source_target_pairs={{0,4},{1,17},{2,6},{3,19},{4,0},{5,21},{6,2},{7,23},{8,12},{9,25},... | collective-permute-start | bytes 405512 | tf_op jit(solution)/shard_map/ppermute | solution.py:339
  16.4 1.7 %collective-permute-start.11 = (f32[264,128]{1,0:T(8,128)S(1)}, f32[264,128]{1,0:T(8,128)S(1)}, u32[]{:S(2)}, u32[]{:S(2)}) collective-permute-start(f32[264,128]{1,0:T(8,128)S(1)} %get-tuple-element.16.refs_0_), channel_id=1, source_target_pairs={{0,2},{1,9},{2,0},{3,11},{4,6},{5,13},{6,4},{7,15},{8,10},{9,1},{1... | collective-permute-start | bytes 405512 | tf_op jit(solution)/shard_map/ppermute | solution.py:339
  18.1 1.6 %collective-permute-start.10 = (f32[264,128]{1,0:T(8,128)S(1)}, f32[264,128]{1,0:T(8,128)S(1)}, u32[]{:S(2)}, u32[]{:S(2)}) collective-permute-start(f32[264,128]{1,0:T(8,128)S(1)} %get-tuple-element.16.refs_0_), channel_id=1, source_target_pairs={{0,6},{1,25},{2,4},{3,27},{4,2},{5,29},{6,0},{7,31},{8,14},{9,17},... | collective-permute-start | bytes 405512 | tf_op jit(solution)/shard_map/ppermute | solution.py:339
  19.7 3.0 %collective-permute-done.12.refs_3_ = f32[264,128]{1,0:T(8,128)S(1)} collective-permute-done((f32[264,128]{1,0:T(8,128)S(1)}, f32[264,128]{1,0:T(8,128)S(1)}, u32[]{:S(2)}, u32[]{:S(2)}) %collective-permute-start.12) | collective-permute-done | bytes 135200 | tf_op jit(solution)/shard_map/ppermute | solution.py:339
  22.7 2.6 %collective-permute-done.10.refs_1_ = f32[264,128]{1,0:T(8,128)S(1)} collective-permute-done((f32[264,128]{1,0:T(8,128)S(1)}, f32[264,128]{1,0:T(8,128)S(1)}, u32[]{:S(2)}, u32[]{:S(2)}) %collective-permute-start.10) | collective-permute-done | bytes 135200 | tf_op jit(solution)/shard_map/ppermute | solution.py:339
  25.3 0.2 shard_map.69
  25.6 1.3 %collective-permute-done.13.other_ref.peer_ref = f32[168,128]{1,0:T(8,128)S(1)} collective-permute-done((f32[168,128]{1,0:T(8,128)S(1)}, f32[168,128]{1,0:T(8,128)S(1)}, u32[]{:S(2)}, u32[]{:S(2)}) %collective-permute-start.13) | collective-permute-done | bytes 86048 | tf_op jit(solution)/shard_map/ppermute | solution.py:330
  26.9 0.6 %shard_map.70.refs_0_ = f32[136,128]{1,0:T(8,128)S(1)} custom-call(f32[168,128]{1,0:T(8,128)S(1)} %get-tuple-element.19.mine_ref.refs_4_.send_ref, f32[168,128]{1,0:T(8,128)S(1)} %collective-permute-done.13.other_ref.peer_ref, f32[256,128]{1,0:T(8,128)S(1)} %get-tuple-element.17.refs_4_.left_ref, f32[256,128]{1,0:T(8,128)S(1)} %get-tuple-element.20.right_ref, ...), custom_call_target="tpu_custom_call" | custom-call | tf_op jit(solution)/shard_map/pallas_call | solution.py:320
  27.5 1.9 %collective-permute-start.16 = (f32[136,128]{1,0:T(8,128)S(1)}, f32[136,128]{1,0:T(8,128)S(1)}, u32[]{:S(2)}, u32[]{:S(2)}) collective-permute-start(f32[136,128]{1,0:T(8,128)S(1)} %shard_map.70.refs_0_), channel_id=1, source_target_pairs={{0,6},{1,25},{2,4},{3,27},{4,2},{5,29},{6,0},{7,31},{8,14},{9,17},... | collective-permute-start | bytes 208904 | tf_op jit(solution)/shard_map/ppermute | solution.py:339
  29.3 0.5 %collective-permute-start.15 = (f32[136,128]{1,0:T(8,128)S(1)}, f32[136,128]{1,0:T(8,128)S(1)}, u32[]{:S(2)}, u32[]{:S(2)}) collective-permute-start(f32[136,128]{1,0:T(8,128)S(1)} %shard_map.70.refs_0_), channel_id=1, source_target_pairs={{0,4},{1,17},{2,6},{3,19},{4,0},{5,21},{6,2},{7,23},{8,12},{9,25},... | collective-permute-start | bytes 208904 | tf_op jit(solution)/shard_map/ppermute | solution.py:339
  29.9 2.1 %collective-permute-start.14 = (f32[136,128]{1,0:T(8,128)S(1)}, f32[136,128]{1,0:T(8,128)S(1)}, u32[]{:S(2)}, u32[]{:S(2)}) collective-permute-start(f32[136,128]{1,0:T(8,128)S(1)} %shard_map.70.refs_0_), channel_id=1, source_target_pairs={{0,2},{1,9},{2,0},{3,11},{4,6},{5,13},{6,4},{7,15},{8,10},{9,1},{1... | collective-permute-start | bytes 208904 | tf_op jit(solution)/shard_map/ppermute | solution.py:339
  31.9 1.7 %collective-permute-done.16.refs_3_ = f32[136,128]{1,0:T(8,128)S(1)} collective-permute-done((f32[136,128]{1,0:T(8,128)S(1)}, f32[136,128]{1,0:T(8,128)S(1)}, u32[]{:S(2)}, u32[]{:S(2)}) %collective-permute-start.16) | collective-permute-done | bytes 69664 | tf_op jit(solution)/shard_map/ppermute | solution.py:339
  33.7 1.5 %collective-permute-done.15.refs_2_ = f32[136,128]{1,0:T(8,128)S(1)} collective-permute-done((f32[136,128]{1,0:T(8,128)S(1)}, f32[136,128]{1,0:T(8,128)S(1)}, u32[]{:S(2)}, u32[]{:S(2)}) %collective-permute-start.15) | collective-permute-done | bytes 69664 | tf_op jit(solution)/shard_map/ppermute | solution.py:339
  35.3 1.2 %collective-permute-done.17.other_ref.peer_second_ref = f32[136,128]{1,0:T(8,128)S(1)} collective-permute-done((f32[136,128]{1,0:T(8,128)S(1)}, f32[136,128]{1,0:T(8,128)S(1)}, u32[]{:S(2)}, u32[]{:S(2)}) %collective-permute-start.17) | collective-permute-done | bytes 69664 | tf_op jit(solution)/shard_map/ppermute | solution.py:330
  36.5 0.4 shard_map.72
  37.0 9.1 %all_to_all.5.dots_ref = f32[32,1,128]{2,1,0:T(1,128)S(1)} all-to-all(f32[32,1,128]{2,1,0:T(1,128)S(1)} %shard_map.72), channel_id=1, replica_groups=mesh['stu'=4,'que'=8] {'stu','que'}, dimensions={0} | all-to-all | bytes 32768 | tf_op jit(solution)/shard_map/all_to_all | solution.py:421
  46.1 0.9 %shard_map.73 = (f32[32,64]{1,0:T(8,128)}, f32[32,64]{1,0:T(8,128)}, f32[1,32]{1,0:T(1,128)}) custom-call(f32[32,1,128]{2,1,0:T(1,128)S(1)} %all_to_all.5.dots_ref, f32[168,128]{1,0:T(8,128)S(1)} %get-tuple-element.19.mine_ref.refs_4_.send_ref, f32[168,128]{1,0:T(8,128)S(1)} %collective-permute-done.13.other_ref.peer_ref, ...), custom_call_target="tpu_custom_call" | custom-call | tf_op jit(solution)/shard_map/pallas_call | solution.py:320
  (26 shorter events, 0.4 us)
Async XLA Ops:
  0.6 1.1 %copy-start.1 = (f32[32,64]{1,0:T(8,128)S(1)}, f32[32,64]{1,0:T(8,128)}, u32[]{:S(2)}) copy-start(f32[32,64]{1,0:T(8,128)} %param.5) | copy-start | bytes 24580
  0.6 2.0 %collective-permute-start.2 = (f32[32]{0:T(128)}, f32[32]{0:T(128)S(1)}, u32[]{:S(2)}, u32[]{:S(2)}) collective-permute-start(f32[32]{0:T(128)} %param.7), channel_id=1, source_target_pairs={{0,1},{1,0},{2,3},{3,2},{4,5},{5,4},{6,7},{7,6},{8,9},{9,8},{10,11... | collective-permute-start | bytes 392 | tf_op jit(solution)/shard_map/ppermute | solution.py:330
  1.2 1.6 %collective-permute-start = (f32[32,64]{1,0:T(8,128)}, f32[32,64]{1,0:T(8,128)S(1)}, u32[]{:S(2)}, u32[]{:S(2)}) collective-permute-start(f32[32,64]{1,0:T(8,128)} %param.5), channel_id=1, source_target_pairs={{0,1},{1,0},{2,3},{3,2},{4,5},{5,4},{6,7},{7,6},{8,9},{9,8},{10,11... | collective-permute-start | bytes 24584 | tf_op jit(solution)/shard_map/ppermute | solution.py:330
  1.2 1.5 %collective-permute-start.1 = (f32[32,64]{1,0:T(8,128)}, f32[32,64]{1,0:T(8,128)S(1)}, u32[]{:S(2)}, u32[]{:S(2)}) collective-permute-start(f32[32,64]{1,0:T(8,128)} %param.6), channel_id=1, source_target_pairs={{0,1},{1,0},{2,3},{3,2},{4,5},{5,4},{6,7},{7,6},{8,9},{9,8},{10,11... | collective-permute-start | bytes 24584 | tf_op jit(solution)/shard_map/ppermute | solution.py:330
  1.7 11.5 %collective-permute-start.9 = (s32[256,128]{1,0:T(8,128)}, s32[256,128]{1,0:T(8,128)S(1)}, u32[]{:S(2)}, u32[]{:S(2)}) collective-permute-start(s32[256,128]{1,0:T(8,128)} %own_ref.1), channel_id=1, source_target_pairs={{0,1},{1,0},{2,3},{3,2},{4,5},{5,4},{6,7},{7,6},{8,9},{9,8},{10,11... | collective-permute-start | bytes 393224 | tf_op jit(solution)/shard_map/ppermute | solution.py:330
  1.7 0.9 %copy-start.2 = (f32[32]{0:T(128)S(1)}, f32[32]{0:T(128)}, u32[]{:S(2)}) copy-start(f32[32]{0:T(128)} %param.7) | copy-start | bytes 388
  1.8 11.4 %copy-start = (s32[256,128]{1,0:T(8,128)S(1)}, s32[256,128]{1,0:T(8,128)}, u32[]{:S(2)}) copy-start(s32[256,128]{1,0:T(8,128)} %own_ref.1) | copy-start | bytes 393220
  2.9 8.1 %collective-permute-start.4 = (f32[40,128]{1,0:T(8,128)S(1)}, f32[40,128]{1,0:T(8,128)S(1)}, u32[]{:S(2)}, u32[]{:S(2)}) collective-permute-start(f32[40,128]{1,0:T(8,128)S(1)} %get-tuple-element.35.refs_4_), channel_id=1, source_target_pairs={{0,24},{1,7},{2,26},{3,5},{4,28},{5,3},{6,30},{7,1},{8,16},{9,15},... | collective-permute-start | bytes 61448 | tf_op jit(solution)/shard_map/ppermute | solution.py:339
  6.8 4.7 %collective-permute-start.6 = (f32[40,128]{1,0:T(8,128)S(1)}, f32[40,128]{1,0:T(8,128)S(1)}, u32[]{:S(2)}, u32[]{:S(2)}) collective-permute-start(f32[40,128]{1,0:T(8,128)S(1)} %get-tuple-element.36.refs_0_), channel_id=1, source_target_pairs={{0,4},{1,17},{2,6},{3,19},{4,0},{5,21},{6,2},{7,23},{8,12},{9,25},... | collective-permute-start | bytes 61448 | tf_op jit(solution)/shard_map/ppermute | solution.py:339
  9.4 3.8 %collective-permute-start.3 = (f32[40,128]{1,0:T(8,128)S(1)}, f32[40,128]{1,0:T(8,128)S(1)}, u32[]{:S(2)}, u32[]{:S(2)}) collective-permute-start(f32[40,128]{1,0:T(8,128)S(1)} %get-tuple-element.36.refs_0_), channel_id=1, source_target_pairs={{0,2},{1,9},{2,0},{3,11},{4,6},{5,13},{6,4},{7,15},{8,10},{9,1},{1... | collective-permute-start | bytes 61448 | tf_op jit(solution)/shard_map/ppermute | solution.py:339
  11.0 2.3 %collective-permute-start.5 = (f32[40,128]{1,0:T(8,128)S(1)}, f32[40,128]{1,0:T(8,128)S(1)}, u32[]{:S(2)}, u32[]{:S(2)}) collective-permute-start(f32[40,128]{1,0:T(8,128)S(1)} %collective-permute-done.4.refs_6_), channel_id=1, source_target_pairs={{0,1},{1,0},{2,3},{3,2},{4,5},{5,4},{6,7},{7,6},{8,9},{9,8},{10,11... | collective-permute-start | bytes 61448 | tf_op jit(solution)/shard_map/ppermute | solution.py:330
  11.5 1.8 %collective-permute-start.8 = (f32[40,128]{1,0:T(8,128)S(1)}, f32[40,128]{1,0:T(8,128)S(1)}, u32[]{:S(2)}, u32[]{:S(2)}) collective-permute-start(f32[40,128]{1,0:T(8,128)S(1)} %collective-permute-done.6.refs_3_), channel_id=1, source_target_pairs={{0,1},{1,0},{2,3},{3,2},{4,5},{5,4},{6,7},{7,6},{8,9},{9,8},{10,11... | collective-permute-start | bytes 61448 | tf_op jit(solution)/shard_map/ppermute | solution.py:330
  13.2 1.2 %collective-permute-start.7 = (f32[40,128]{1,0:T(8,128)S(1)}, f32[40,128]{1,0:T(8,128)S(1)}, u32[]{:S(2)}, u32[]{:S(2)}) collective-permute-start(f32[40,128]{1,0:T(8,128)S(1)} %collective-permute-done.3.refs_1_), channel_id=1, source_target_pairs={{0,1},{1,0},{2,3},{3,2},{4,5},{5,4},{6,7},{7,6},{8,9},{9,8},{10,11... | collective-permute-start | bytes 61448 | tf_op jit(solution)/shard_map/ppermute | solution.py:330
  15.3 7.4 %collective-permute-start.12 = (f32[264,128]{1,0:T(8,128)S(1)}, f32[264,128]{1,0:T(8,128)S(1)}, u32[]{:S(2)}, u32[]{:S(2)}) collective-permute-start(f32[264,128]{1,0:T(8,128)S(1)} %get-tuple-element.16.refs_0_), channel_id=1, source_target_pairs={{0,4},{1,17},{2,6},{3,19},{4,0},{5,21},{6,2},{7,23},{8,12},{9,25},... | collective-permute-start | bytes 405512 | tf_op jit(solution)/shard_map/ppermute | solution.py:339
  16.4 6.3 %collective-permute-start.11 = (f32[264,128]{1,0:T(8,128)S(1)}, f32[264,128]{1,0:T(8,128)S(1)}, u32[]{:S(2)}, u32[]{:S(2)}) collective-permute-start(f32[264,128]{1,0:T(8,128)S(1)} %get-tuple-element.16.refs_0_), channel_id=1, source_target_pairs={{0,2},{1,9},{2,0},{3,11},{4,6},{5,13},{6,4},{7,15},{8,10},{9,1},{1... | collective-permute-start | bytes 405512 | tf_op jit(solution)/shard_map/ppermute | solution.py:339
  18.1 7.2 %collective-permute-start.10 = (f32[264,128]{1,0:T(8,128)S(1)}, f32[264,128]{1,0:T(8,128)S(1)}, u32[]{:S(2)}, u32[]{:S(2)}) collective-permute-start(f32[264,128]{1,0:T(8,128)S(1)} %get-tuple-element.16.refs_0_), channel_id=1, source_target_pairs={{0,6},{1,25},{2,4},{3,27},{4,2},{5,29},{6,0},{7,31},{8,14},{9,17},... | collective-permute-start | bytes 405512 | tf_op jit(solution)/shard_map/ppermute | solution.py:339
  25.5 1.3 %collective-permute-start.13 = (f32[168,128]{1,0:T(8,128)S(1)}, f32[168,128]{1,0:T(8,128)S(1)}, u32[]{:S(2)}, u32[]{:S(2)}) collective-permute-start(f32[168,128]{1,0:T(8,128)S(1)} %get-tuple-element.19.mine_ref.refs_4_.send_ref), channel_id=1, source_target_pairs={{0,1},{1,0},{2,3},{3,2},{4,5},{5,4},{6,7},{7,6},{8,9},{9,8},{10,11... | collective-permute-start | bytes 258056 | tf_op jit(solution)/shard_map/ppermute | solution.py:330
  27.5 6.2 %collective-permute-start.16 = (f32[136,128]{1,0:T(8,128)S(1)}, f32[136,128]{1,0:T(8,128)S(1)}, u32[]{:S(2)}, u32[]{:S(2)}) collective-permute-start(f32[136,128]{1,0:T(8,128)S(1)} %shard_map.70.refs_0_), channel_id=1, source_target_pairs={{0,6},{1,25},{2,4},{3,27},{4,2},{5,29},{6,0},{7,31},{8,14},{9,17},... | collective-permute-start | bytes 208904 | tf_op jit(solution)/shard_map/ppermute | solution.py:339
  29.3 5.8 %collective-permute-start.15 = (f32[136,128]{1,0:T(8,128)S(1)}, f32[136,128]{1,0:T(8,128)S(1)}, u32[]{:S(2)}, u32[]{:S(2)}) collective-permute-start(f32[136,128]{1,0:T(8,128)S(1)} %shard_map.70.refs_0_), channel_id=1, source_target_pairs={{0,4},{1,17},{2,6},{3,19},{4,0},{5,21},{6,2},{7,23},{8,12},{9,25},... | collective-permute-start | bytes 208904 | tf_op jit(solution)/shard_map/ppermute | solution.py:339
  29.9 5.3 %collective-permute-start.14 = (f32[136,128]{1,0:T(8,128)S(1)}, f32[136,128]{1,0:T(8,128)S(1)}, u32[]{:S(2)}, u32[]{:S(2)}) collective-permute-start(f32[136,128]{1,0:T(8,128)S(1)} %shard_map.70.refs_0_), channel_id=1, source_target_pairs={{0,2},{1,9},{2,0},{3,11},{4,6},{5,13},{6,4},{7,15},{8,10},{9,1},{1... | collective-permute-start | bytes 208904 | tf_op jit(solution)/shard_map/ppermute | solution.py:339
  35.2 1.3 %collective-permute-start.17 = (f32[136,128]{1,0:T(8,128)S(1)}, f32[136,128]{1,0:T(8,128)S(1)}, u32[]{:S(2)}, u32[]{:S(2)}) collective-permute-start(f32[136,128]{1,0:T(8,128)S(1)} %get-tuple-element.23.mine_ref.second_ref), channel_id=1, source_target_pairs={{0,1},{1,0},{2,3},{3,2},{4,5},{5,4},{6,7},{7,6},{8,9},{9,8},{10,11... | collective-permute-start | bytes 208904 | tf_op jit(solution)/shard_map/ppermute | solution.py:330

commit v11 on v10

--- a/solution.py
+++ b/solution.py
@@ -286,9 +286,9 @@
     a, f, h, d = [sums[at : at + 1] for at in range(4)]
     b = a + f
     e = f + h
-    det = b * d - e * e
-    s = (a * d - e * f) / det
-    t = (f * f - a * h) / det
+    scale = 1.0 / (b * d - e * e)
+    s = (a * d - e * f) * scale
+    t = (f * f - a * h) * scale
     rows = whole_ref.shape[0]
     half = rows // 2
     size = rows // (2 * group)

time: 47.2 us -> 47.2 us (level)
  no operation moved by 1% of the time
where the time goes in v11:
time: 47.2 us; the launch traced here: 47 us
  starting transfers between devices  18.3 us (39%)
  waiting for transfers between devices  14.6 us (31%)
  blocking collectives  9.12 us (19%)
  Pallas kernels  3.11 us (7%)
  other arithmetic  0.85 us (2%)
  between operations  0.74 us (2%)
    ppermute x9, starting transfers between devices, send_over(): return lax.ppermute(value, AXES, pairs)  17 us
    ppermute x9, waiting for transfers between devices, send_over(): return lax.ppermute(value, AXES, pairs)  11 us
    all_to_all x1, blocking collectives, shards(): dots = lax.all_to_all(dots, AXES, 0, 0, tiled=True)  9.12 us
    ppermute x9, waiting for transfers between devices, swap_cores(): return lax.ppermute(value, AXES, [(i, i ^ 1) for i in range(n_stu * n_que)])  3.65 us
    pallas_call x7, Pallas kernels, call(): pl.pallas_call(kernel, out_shape=out, in_specs=[pl.BlockSpec(memory_space...  3.11 us
    ppermute x9, starting transfers between devices, swap_cores(): return lax.ppermute(value, AXES, [(i, i ^ 1) for i in range(n_stu * n_que)])  1.26 us
  transfers between devices with their start and end apart: 18, of which 9 were waited for; matrix products, arithmetic and copies ran while one was open for 2% of the time, Pallas kernels for 0%

profile of v11, /device:TPU:0, one launch (start us, length us, event | category | flops | bytes accessed | tf_op | source)
XLA Modules:
  0.0 47.0 jit_solution(921389382254203142)
XLA Ops:
  0.6 0.5 %collective-permute-start.2 = (f32[32]{0:T(128)}, f32[32]{0:T(128)S(1)}, u32[]{:S(2)}, u32[]{:S(2)}) collective-permute-start(f32[32]{0:T(128)} %param.7), channel_id=1, source_target_pairs={{0,1},{1,0},{2,3},{3,2},{4,5},{5,4},{6,7},{7,6},{8,9},{9,8},{10,11... | collective-permute-start | bytes 392 | tf_op jit(solution)/shard_map/ppermute | solution.py:330
  1.2 0.1 collective-permute-start
  1.2 0.4 collective-permute-start.1
  1.7 0.1 collective-permute-start.9
  1.8 0.8 %broadcast_select_fusion = (f32[32,64]{1,0:T(8,128)S(1)}, f32[32,64]{1,0:T(8,128)S(1)}) fusion(f32[32,64]{1,0:T(8,128)} %param.6, f32[32,64]{1,0:T(8,128)S(1)} %copy-done.1, pred[]{:T(512)S(6)} %eq.2), kind=kLoop, calls=%fused_computation.2 | loop fusion | flops 4096 | bytes 32769 | tf_op jit(solution)/shard_map/jit(_where)/select_n | solution.py:369
  2.6 0.1 reshape.13
  2.7 0.1 reshape.12
  2.8 0.1 maximum_maximum_fusion.1
  2.9 3.9 %collective-permute-start.4 = (f32[40,128]{1,0:T(8,128)S(1)}, f32[40,128]{1,0:T(8,128)S(1)}, u32[]{:S(2)}, u32[]{:S(2)}) collective-permute-start(f32[40,128]{1,0:T(8,128)S(1)} %get-tuple-element.35.refs_4_), channel_id=1, source_target_pairs={{0,24},{1,7},{2,26},{3,5},{4,28},{5,3},{6,30},{7,1},{8,16},{9,15},... | collective-permute-start | bytes 61448 | tf_op jit(solution)/shard_map/ppermute | solution.py:339
  6.8 2.6 %collective-permute-start.6 = (f32[40,128]{1,0:T(8,128)S(1)}, f32[40,128]{1,0:T(8,128)S(1)}, u32[]{:S(2)}, u32[]{:S(2)}) collective-permute-start(f32[40,128]{1,0:T(8,128)S(1)} %get-tuple-element.36.refs_0_), channel_id=1, source_target_pairs={{0,4},{1,17},{2,6},{3,19},{4,0},{5,21},{6,2},{7,23},{8,12},{9,25},... | collective-permute-start | bytes 61448 | tf_op jit(solution)/shard_map/ppermute | solution.py:339
  9.4 1.6 %collective-permute-start.3 = (f32[40,128]{1,0:T(8,128)S(1)}, f32[40,128]{1,0:T(8,128)S(1)}, u32[]{:S(2)}, u32[]{:S(2)}) collective-permute-start(f32[40,128]{1,0:T(8,128)S(1)} %get-tuple-element.36.refs_0_), channel_id=1, source_target_pairs={{0,2},{1,9},{2,0},{3,11},{4,6},{5,13},{6,4},{7,15},{8,10},{9,1},{1... | collective-permute-start | bytes 61448 | tf_op jit(solution)/shard_map/ppermute | solution.py:339
  11.0 0.5 %collective-permute-done.6.refs_3_ = f32[40,128]{1,0:T(8,128)S(1)} collective-permute-done((f32[40,128]{1,0:T(8,128)S(1)}, f32[40,128]{1,0:T(8,128)S(1)}, u32[]{:S(2)}, u32[]{:S(2)}) %collective-permute-start.6) | collective-permute-done | bytes 20512 | tf_op jit(solution)/shard_map/ppermute | solution.py:339
  11.5 1.7 %collective-permute-done.3.refs_1_ = f32[40,128]{1,0:T(8,128)S(1)} collective-permute-done((f32[40,128]{1,0:T(8,128)S(1)}, f32[40,128]{1,0:T(8,128)S(1)}, u32[]{:S(2)}, u32[]{:S(2)}) %collective-permute-start.3) | collective-permute-done | bytes 20512 | tf_op jit(solution)/shard_map/ppermute | solution.py:339
  13.2 1.1 %collective-permute-done.7.refs_5_ = f32[40,128]{1,0:T(8,128)S(1)} collective-permute-done((f32[40,128]{1,0:T(8,128)S(1)}, f32[40,128]{1,0:T(8,128)S(1)}, u32[]{:S(2)}, u32[]{:S(2)}) %collective-permute-start.7) | collective-permute-done | bytes 20512 | tf_op jit(solution)/shard_map/ppermute | solution.py:330
  14.4 0.9 %shard_map.68 = (f32[264,128]{1,0:T(8,128)S(1)}, f32[256,128]{1,0:T(8,128)S(1)}, f32[256,128]{1,0:T(8,128)S(1)}, f32[256,256]{1,0:T(8,128)S(1)}, f32[8,128]{1,0:T(8,128)S(1)}) custom-call(f32[40,128]{1,0:T(8,128)S(1)} %get-tuple-element.36.refs_0_, f32[40,128]{1,0:T(8,128)S(1)} %collective-permute-done.3.refs_1_, ...), custom_call_target="tpu_custom_call" | custom-call | tf_op jit(solution)/shard_map/pallas_call | solution.py:320
  15.3 1.1 %collective-permute-start.12 = (f32[264,128]{1,0:T(8,128)S(1)}, f32[264,128]{1,0:T(8,128)S(1)}, u32[]{:S(2)}, u32[]{:S(2)}) collective-permute-start(f32[264,128]{1,0:T(8,128)S(1)} %get-tuple-element.16.refs_0_), channel_id=1, source_target_pairs={{0,4},{1,17},{2,6},{3,19},{4,0},{5,21},{6,2},{7,23},{8,12},{9,25},... | collective-permute-start | bytes 405512 | tf_op jit(solution)/shard_map/ppermute | solution.py:339
  16.4 1.7 %collective-permute-start.11 = (f32[264,128]{1,0:T(8,128)S(1)}, f32[264,128]{1,0:T(8,128)S(1)}, u32[]{:S(2)}, u32[]{:S(2)}) collective-permute-start(f32[264,128]{1,0:T(8,128)S(1)} %get-tuple-element.16.refs_0_), channel_id=1, source_target_pairs={{0,2},{1,9},{2,0},{3,11},{4,6},{5,13},{6,4},{7,15},{8,10},{9,1},{1... | collective-permute-start | bytes 405512 | tf_op jit(solution)/shard_map/ppermute | solution.py:339
  18.1 1.6 %collective-permute-start.10 = (f32[264,128]{1,0:T(8,128)S(1)}, f32[264,128]{1,0:T(8,128)S(1)}, u32[]{:S(2)}, u32[]{:S(2)}) collective-permute-start(f32[264,128]{1,0:T(8,128)S(1)} %get-tuple-element.16.refs_0_), channel_id=1, source_target_pairs={{0,6},{1,25},{2,4},{3,27},{4,2},{5,29},{6,0},{7,31},{8,14},{9,17},... | collective-permute-start | bytes 405512 | tf_op jit(solution)/shard_map/ppermute | solution.py:339
  19.7 3.0 %collective-permute-done.12.refs_3_ = f32[264,128]{1,0:T(8,128)S(1)} collective-permute-done((f32[264,128]{1,0:T(8,128)S(1)}, f32[264,128]{1,0:T(8,128)S(1)}, u32[]{:S(2)}, u32[]{:S(2)}) %collective-permute-start.12) | collective-permute-done | bytes 135200 | tf_op jit(solution)/shard_map/ppermute | solution.py:339
  22.7 2.6 %collective-permute-done.10.refs_1_ = f32[264,128]{1,0:T(8,128)S(1)} collective-permute-done((f32[264,128]{1,0:T(8,128)S(1)}, f32[264,128]{1,0:T(8,128)S(1)}, u32[]{:S(2)}, u32[]{:S(2)}) %collective-permute-start.10) | collective-permute-done | bytes 135200 | tf_op jit(solution)/shard_map/ppermute | solution.py:339
  25.3 0.2 shard_map.69
  25.6 1.3 %collective-permute-done.13.other_ref.peer_ref = f32[168,128]{1,0:T(8,128)S(1)} collective-permute-done((f32[168,128]{1,0:T(8,128)S(1)}, f32[168,128]{1,0:T(8,128)S(1)}, u32[]{:S(2)}, u32[]{:S(2)}) %collective-permute-start.13) | collective-permute-done | bytes 86048 | tf_op jit(solution)/shard_map/ppermute | solution.py:330
  26.9 0.6 %shard_map.70.refs_0_ = f32[136,128]{1,0:T(8,128)S(1)} custom-call(f32[168,128]{1,0:T(8,128)S(1)} %get-tuple-element.19.mine_ref.refs_4_.send_ref, f32[168,128]{1,0:T(8,128)S(1)} %collective-permute-done.13.other_ref.peer_ref, f32[256,128]{1,0:T(8,128)S(1)} %get-tuple-element.17.refs_4_.left_ref, f32[256,128]{1,0:T(8,128)S(1)} %get-tuple-element.20.right_ref, ...), custom_call_target="tpu_custom_call" | custom-call | tf_op jit(solution)/shard_map/pallas_call | solution.py:320
  27.5 1.9 %collective-permute-start.16 = (f32[136,128]{1,0:T(8,128)S(1)}, f32[136,128]{1,0:T(8,128)S(1)}, u32[]{:S(2)}, u32[]{:S(2)}) collective-permute-start(f32[136,128]{1,0:T(8,128)S(1)} %shard_map.70.refs_0_), channel_id=1, source_target_pairs={{0,6},{1,25},{2,4},{3,27},{4,2},{5,29},{6,0},{7,31},{8,14},{9,17},... | collective-permute-start | bytes 208904 | tf_op jit(solution)/shard_map/ppermute | solution.py:339
  29.3 0.5 %collective-permute-start.15 = (f32[136,128]{1,0:T(8,128)S(1)}, f32[136,128]{1,0:T(8,128)S(1)}, u32[]{:S(2)}, u32[]{:S(2)}) collective-permute-start(f32[136,128]{1,0:T(8,128)S(1)} %shard_map.70.refs_0_), channel_id=1, source_target_pairs={{0,4},{1,17},{2,6},{3,19},{4,0},{5,21},{6,2},{7,23},{8,12},{9,25},... | collective-permute-start | bytes 208904 | tf_op jit(solution)/shard_map/ppermute | solution.py:339
  29.9 2.1 %collective-permute-start.14 = (f32[136,128]{1,0:T(8,128)S(1)}, f32[136,128]{1,0:T(8,128)S(1)}, u32[]{:S(2)}, u32[]{:S(2)}) collective-permute-start(f32[136,128]{1,0:T(8,128)S(1)} %shard_map.70.refs_0_), channel_id=1, source_target_pairs={{0,2},{1,9},{2,0},{3,11},{4,6},{5,13},{6,4},{7,15},{8,10},{9,1},{1... | collective-permute-start | bytes 208904 | tf_op jit(solution)/shard_map/ppermute | solution.py:339
  31.9 1.7 %collective-permute-done.16.refs_3_ = f32[136,128]{1,0:T(8,128)S(1)} collective-permute-done((f32[136,128]{1,0:T(8,128)S(1)}, f32[136,128]{1,0:T(8,128)S(1)}, u32[]{:S(2)}, u32[]{:S(2)}) %collective-permute-start.16) | collective-permute-done | bytes 69664 | tf_op jit(solution)/shard_map/ppermute | solution.py:339
  33.7 1.5 %collective-permute-done.15.refs_2_ = f32[136,128]{1,0:T(8,128)S(1)} collective-permute-done((f32[136,128]{1,0:T(8,128)S(1)}, f32[136,128]{1,0:T(8,128)S(1)}, u32[]{:S(2)}, u32[]{:S(2)}) %collective-permute-start.15) | collective-permute-done | bytes 69664 | tf_op jit(solution)/shard_map/ppermute | solution.py:339
  35.3 1.2 %collective-permute-done.17.other_ref.peer_second_ref = f32[136,128]{1,0:T(8,128)S(1)} collective-permute-done((f32[136,128]{1,0:T(8,128)S(1)}, f32[136,128]{1,0:T(8,128)S(1)}, u32[]{:S(2)}, u32[]{:S(2)}) %collective-permute-start.17) | collective-permute-done | bytes 69664 | tf_op jit(solution)/shard_map/ppermute | solution.py:330
  36.5 0.4 shard_map.72
  37.0 9.1 %all_to_all.5.dots_ref = f32[32,1,128]{2,1,0:T(1,128)S(1)} all-to-all(f32[32,1,128]{2,1,0:T(1,128)S(1)} %shard_map.72), channel_id=1, replica_groups=mesh['stu'=4,'que'=8] {'stu','que'}, dimensions={0} | all-to-all | bytes 32768 | tf_op jit(solution)/shard_map/all_to_all | solution.py:421
  46.1 0.9 %shard_map.73 = (f32[32,64]{1,0:T(8,128)}, f32[32,64]{1,0:T(8,128)}, f32[1,32]{1,0:T(1,128)}) custom-call(f32[32,1,128]{2,1,0:T(1,128)S(1)} %all_to_all.5.dots_ref, f32[168,128]{1,0:T(8,128)S(1)} %get-tuple-element.19.mine_ref.refs_4_.send_ref, f32[168,128]{1,0:T(8,128)S(1)} %collective-permute-done.13.other_ref.peer_ref, ...), custom_call_target="tpu_custom_call" | custom-call | tf_op jit(solution)/shard_map/pallas_call | solution.py:320
  (26 shorter events, 0.4 us)
Async XLA Ops:
  0.6 1.1 %copy-start.1 = (f32[32,64]{1,0:T(8,128)S(1)}, f32[32,64]{1,0:T(8,128)}, u32[]{:S(2)}) copy-start(f32[32,64]{1,0:T(8,128)} %param.5) | copy-start | bytes 24580
  0.6 2.0 %collective-permute-start.2 = (f32[32]{0:T(128)}, f32[32]{0:T(128)S(1)}, u32[]{:S(2)}, u32[]{:S(2)}) collective-permute-start(f32[32]{0:T(128)} %param.7), channel_id=1, source_target_pairs={{0,1},{1,0},{2,3},{3,2},{4,5},{5,4},{6,7},{7,6},{8,9},{9,8},{10,11... | collective-permute-start | bytes 392 | tf_op jit(solution)/shard_map/ppermute | solution.py:330
  1.2 1.6 %collective-permute-start = (f32[32,64]{1,0:T(8,128)}, f32[32,64]{1,0:T(8,128)S(1)}, u32[]{:S(2)}, u32[]{:S(2)}) collective-permute-start(f32[32,64]{1,0:T(8,128)} %param.5), channel_id=1, source_target_pairs={{0,1},{1,0},{2,3},{3,2},{4,5},{5,4},{6,7},{7,6},{8,9},{9,8},{10,11... | collective-permute-start | bytes 24584 | tf_op jit(solution)/shard_map/ppermute | solution.py:330
  1.2 1.5 %collective-permute-start.1 = (f32[32,64]{1,0:T(8,128)}, f32[32,64]{1,0:T(8,128)S(1)}, u32[]{:S(2)}, u32[]{:S(2)}) collective-permute-start(f32[32,64]{1,0:T(8,128)} %param.6), channel_id=1, source_target_pairs={{0,1},{1,0},{2,3},{3,2},{4,5},{5,4},{6,7},{7,6},{8,9},{9,8},{10,11... | collective-permute-start | bytes 24584 | tf_op jit(solution)/shard_map/ppermute | solution.py:330
  1.7 11.5 %collective-permute-start.9 = (s32[256,128]{1,0:T(8,128)}, s32[256,128]{1,0:T(8,128)S(1)}, u32[]{:S(2)}, u32[]{:S(2)}) collective-permute-start(s32[256,128]{1,0:T(8,128)} %own_ref.1), channel_id=1, source_target_pairs={{0,1},{1,0},{2,3},{3,2},{4,5},{5,4},{6,7},{7,6},{8,9},{9,8},{10,11... | collective-permute-start | bytes 393224 | tf_op jit(solution)/shard_map/ppermute | solution.py:330
  1.7 0.9 %copy-start.2 = (f32[32]{0:T(128)S(1)}, f32[32]{0:T(128)}, u32[]{:S(2)}) copy-start(f32[32]{0:T(128)} %param.7) | copy-start | bytes 388
  1.8 11.4 %copy-start = (s32[256,128]{1,0:T(8,128)S(1)}, s32[256,128]{1,0:T(8,128)}, u32[]{:S(2)}) copy-start(s32[256,128]{1,0:T(8,128)} %own_ref.1) | copy-start | bytes 393220
  2.9 8.1 %collective-permute-start.4 = (f32[40,128]{1,0:T(8,128)S(1)}, f32[40,128]{1,0:T(8,128)S(1)}, u32[]{:S(2)}, u32[]{:S(2)}) collective-permute-start(f32[40,128]{1,0:T(8,128)S(1)} %get-tuple-element.35.refs_4_), channel_id=1, source_target_pairs={{0,24},{1,7},{2,26},{3,5},{4,28},{5,3},{6,30},{7,1},{8,16},{9,15},... | collective-permute-start | bytes 61448 | tf_op jit(solution)/shard_map/ppermute | solution.py:339
  6.8 4.7 %collective-permute-start.6 = (f32[40,128]{1,0:T(8,128)S(1)}, f32[40,128]{1,0:T(8,128)S(1)}, u32[]{:S(2)}, u32[]{:S(2)}) collective-permute-start(f32[40,128]{1,0:T(8,128)S(1)} %get-tuple-element.36.refs_0_), channel_id=1, source_target_pairs={{0,4},{1,17},{2,6},{3,19},{4,0},{5,21},{6,2},{7,23},{8,12},{9,25},... | collective-permute-start | bytes 61448 | tf_op jit(solution)/shard_map/ppermute | solution.py:339
  9.4 3.8 %collective-permute-start.3 = (f32[40,128]{1,0:T(8,128)S(1)}, f32[40,128]{1,0:T(8,128)S(1)}, u32[]{:S(2)}, u32[]{:S(2)}) collective-permute-start(f32[40,128]{1,0:T(8,128)S(1)} %get-tuple-element.36.refs_0_), channel_id=1, source_target_pairs={{0,2},{1,9},{2,0},{3,11},{4,6},{5,13},{6,4},{7,15},{8,10},{9,1},{1... | collective-permute-start | bytes 61448 | tf_op jit(solution)/shard_map/ppermute | solution.py:339
  11.0 2.3 %collective-permute-start.5 = (f32[40,128]{1,0:T(8,128)S(1)}, f32[40,128]{1,0:T(8,128)S(1)}, u32[]{:S(2)}, u32[]{:S(2)}) collective-permute-start(f32[40,128]{1,0:T(8,128)S(1)} %collective-permute-done.4.refs_6_), channel_id=1, source_target_pairs={{0,1},{1,0},{2,3},{3,2},{4,5},{5,4},{6,7},{7,6},{8,9},{9,8},{10,11... | collective-permute-start | bytes 61448 | tf_op jit(solution)/shard_map/ppermute | solution.py:330
  11.5 1.8 %collective-permute-start.8 = (f32[40,128]{1,0:T(8,128)S(1)}, f32[40,128]{1,0:T(8,128)S(1)}, u32[]{:S(2)}, u32[]{:S(2)}) collective-permute-start(f32[40,128]{1,0:T(8,128)S(1)} %collective-permute-done.6.refs_3_), channel_id=1, source_target_pairs={{0,1},{1,0},{2,3},{3,2},{4,5},{5,4},{6,7},{7,6},{8,9},{9,8},{10,11... | collective-permute-start | bytes 61448 | tf_op jit(solution)/shard_map/ppermute | solution.py:330
  13.2 1.2 %collective-permute-start.7 = (f32[40,128]{1,0:T(8,128)S(1)}, f32[40,128]{1,0:T(8,128)S(1)}, u32[]{:S(2)}, u32[]{:S(2)}) collective-permute-start(f32[40,128]{1,0:T(8,128)S(1)} %collective-permute-done.3.refs_1_), channel_id=1, source_target_pairs={{0,1},{1,0},{2,3},{3,2},{4,5},{5,4},{6,7},{7,6},{8,9},{9,8},{10,11... | collective-permute-start | bytes 61448 | tf_op jit(solution)/shard_map/ppermute | solution.py:330
  15.3 7.4 %collective-permute-start.12 = (f32[264,128]{1,0:T(8,128)S(1)}, f32[264,128]{1,0:T(8,128)S(1)}, u32[]{:S(2)}, u32[]{:S(2)}) collective-permute-start(f32[264,128]{1,0:T(8,128)S(1)} %get-tuple-element.16.refs_0_), channel_id=1, source_target_pairs={{0,4},{1,17},{2,6},{3,19},{4,0},{5,21},{6,2},{7,23},{8,12},{9,25},... | collective-permute-start | bytes 405512 | tf_op jit(solution)/shard_map/ppermute | solution.py:339
  16.4 6.3 %collective-permute-start.11 = (f32[264,128]{1,0:T(8,128)S(1)}, f32[264,128]{1,0:T(8,128)S(1)}, u32[]{:S(2)}, u32[]{:S(2)}) collective-permute-start(f32[264,128]{1,0:T(8,128)S(1)} %get-tuple-element.16.refs_0_), channel_id=1, source_target_pairs={{0,2},{1,9},{2,0},{3,11},{4,6},{5,13},{6,4},{7,15},{8,10},{9,1},{1... | collective-permute-start | bytes 405512 | tf_op jit(solution)/shard_map/ppermute | solution.py:339
  18.1 7.2 %collective-permute-start.10 = (f32[264,128]{1,0:T(8,128)S(1)}, f32[264,128]{1,0:T(8,128)S(1)}, u32[]{:S(2)}, u32[]{:S(2)}) collective-permute-start(f32[264,128]{1,0:T(8,128)S(1)} %get-tuple-element.16.refs_0_), channel_id=1, source_target_pairs={{0,6},{1,25},{2,4},{3,27},{4,2},{5,29},{6,0},{7,31},{8,14},{9,17},... | collective-permute-start | bytes 405512 | tf_op jit(solution)/shard_map/ppermute | solution.py:339
  25.5 1.3 %collective-permute-start.13 = (f32[168,128]{1,0:T(8,128)S(1)}, f32[168,128]{1,0:T(8,128)S(1)}, u32[]{:S(2)}, u32[]{:S(2)}) collective-permute-start(f32[168,128]{1,0:T(8,128)S(1)} %get-tuple-element.19.mine_ref.refs_4_.send_ref), channel_id=1, source_target_pairs={{0,1},{1,0},{2,3},{3,2},{4,5},{5,4},{6,7},{7,6},{8,9},{9,8},{10,11... | collective-permute-start | bytes 258056 | tf_op jit(solution)/shard_map/ppermute | solution.py:330
  27.5 6.2 %collective-permute-start.16 = (f32[136,128]{1,0:T(8,128)S(1)}, f32[136,128]{1,0:T(8,128)S(1)}, u32[]{:S(2)}, u32[]{:S(2)}) collective-permute-start(f32[136,128]{1,0:T(8,128)S(1)} %shard_map.70.refs_0_), channel_id=1, source_target_pairs={{0,6},{1,25},{2,4},{3,27},{4,2},{5,29},{6,0},{7,31},{8,14},{9,17},... | collective-permute-start | bytes 208904 | tf_op jit(solution)/shard_map/ppermute | solution.py:339
  29.3 5.8 %collective-permute-start.15 = (f32[136,128]{1,0:T(8,128)S(1)}, f32[136,128]{1,0:T(8,128)S(1)}, u32[]{:S(2)}, u32[]{:S(2)}) collective-permute-start(f32[136,128]{1,0:T(8,128)S(1)} %shard_map.70.refs_0_), channel_id=1, source_target_pairs={{0,4},{1,17},{2,6},{3,19},{4,0},{5,21},{6,2},{7,23},{8,12},{9,25},... | collective-permute-start | bytes 208904 | tf_op jit(solution)/shard_map/ppermute | solution.py:339
  29.9 5.3 %collective-permute-start.14 = (f32[136,128]{1,0:T(8,128)S(1)}, f32[136,128]{1,0:T(8,128)S(1)}, u32[]{:S(2)}, u32[]{:S(2)}) collective-permute-start(f32[136,128]{1,0:T(8,128)S(1)} %shard_map.70.refs_0_), channel_id=1, source_target_pairs={{0,2},{1,9},{2,0},{3,11},{4,6},{5,13},{6,4},{7,15},{8,10},{9,1},{1... | collective-permute-start | bytes 208904 | tf_op jit(solution)/shard_map/ppermute | solution.py:339
  35.2 1.3 %collective-permute-start.17 = (f32[136,128]{1,0:T(8,128)S(1)}, f32[136,128]{1,0:T(8,128)S(1)}, u32[]{:S(2)}, u32[]{:S(2)}) collective-permute-start(f32[136,128]{1,0:T(8,128)S(1)} %get-tuple-element.23.mine_ref.second_ref), channel_id=1, source_target_pairs={{0,1},{1,0},{2,3},{3,2},{4,5},{5,4},{6,7},{7,6},{8,9},{9,8},{10,11... | collective-permute-start | bytes 208904 | tf_op jit(solution)/shard_map/ppermute | solution.py:330

commit v12 on v10

--- a/solution.py
+++ b/solution.py
@@ -114,7 +114,8 @@
 
 
 def gradient_kernel(group, places, parts, *refs):
-    code_ref, sums_ref, left_ref, right_ref, weight_ref, icpt_ref = refs[2 * parts :]
+    code_ref, refs = refs[0], refs[1:]
+    sums_ref, left_ref, right_ref, weight_ref, icpt_ref = refs[2 * parts :]
     core, line, plane = position()
     size = left_ref.shape[0] // (2 * group)
     mine = pieces(refs[:parts], size)
@@ -393,9 +394,9 @@
     sums, left, right, weight, icpt = call(
         functools.partial(gradient_kernel, group, tuple(places), len(mine)),
         [(rows + BIAS, LANES), (rows, LANES), (rows, LANES), (rows, rows), (BIAS, LANES)],
+        code,
         *mine,
         *other,
-        code,
     )
     parts = totals(sums, FIRST_ORDER)
     first, diag, whole = call(

time: 47.2 us -> 47.2 us (level)
  no operation moved by 1% of the time
where the time goes in v12:
time: 47.2 us; the launch traced here: 47 us
  starting transfers between devices  18.3 us (39%)
  waiting for transfers between devices  14.6 us (31%)
  blocking collectives  9.12 us (19%)
  Pallas kernels  3.11 us (7%)
  other arithmetic  0.85 us (2%)
  between operations  0.74 us (2%)
    ppermute x9, starting transfers between devices, send_over(): return lax.ppermute(value, AXES, pairs)  17 us
    ppermute x9, waiting for transfers between devices, send_over(): return lax.ppermute(value, AXES, pairs)  11 us
    all_to_all x1, blocking collectives, shards(): dots = lax.all_to_all(dots, AXES, 0, 0, tiled=True)  9.12 us
    ppermute x9, waiting for transfers between devices, swap_cores(): return lax.ppermute(value, AXES, [(i, i ^ 1) for i in range(n_stu * n_que)])  3.65 us
    pallas_call x7, Pallas kernels, call(): pl.pallas_call(kernel, out_shape=out, in_specs=[pl.BlockSpec(memory_space...  3.11 us
    ppermute x9, starting transfers between devices, swap_cores(): return lax.ppermute(value, AXES, [(i, i ^ 1) for i in range(n_stu * n_que)])  1.26 us
  transfers between devices with their start and end apart: 18, of which 9 were waited for; matrix products, arithmetic and copies ran while one was open for 2% of the time, Pallas kernels for 0%

profile of v12, /device:TPU:0, one launch (start us, length us, event | category | flops | bytes accessed | tf_op | source)
XLA Modules:
  0.0 47.0 jit_solution(16505845287356488302)
XLA Ops:
  0.6 0.5 %collective-permute-start.3 = (f32[32]{0:T(128)}, f32[32]{0:T(128)S(1)}, u32[]{:S(2)}, u32[]{:S(2)}) collective-permute-start(f32[32]{0:T(128)} %param.7), channel_id=1, source_target_pairs={{0,1},{1,0},{2,3},{3,2},{4,5},{5,4},{6,7},{7,6},{8,9},{9,8},{10,11... | collective-permute-start | bytes 392 | tf_op jit(solution)/shard_map/ppermute | solution.py:331
  1.2 0.1 collective-permute-start.1
  1.2 0.4 collective-permute-start.2
  1.7 0.1 collective-permute-start
  1.8 0.8 %broadcast_select_fusion = (f32[32,64]{1,0:T(8,128)S(1)}, f32[32,64]{1,0:T(8,128)S(1)}) fusion(f32[32,64]{1,0:T(8,128)} %param.6, f32[32,64]{1,0:T(8,128)S(1)} %copy-done.1, pred[]{:T(512)S(6)} %eq.2), kind=kLoop, calls=%fused_computation.2 | loop fusion | flops 4096 | bytes 32769 | tf_op jit(solution)/shard_map/jit(_where)/select_n | solution.py:370
  2.6 0.1 reshape.13
  2.7 0.1 reshape.12
  2.8 0.1 maximum_maximum_fusion.1
  2.9 3.9 %collective-permute-start.5 = (f32[40,128]{1,0:T(8,128)S(1)}, f32[40,128]{1,0:T(8,128)S(1)}, u32[]{:S(2)}, u32[]{:S(2)}) collective-permute-start(f32[40,128]{1,0:T(8,128)S(1)} %get-tuple-element.35.refs_5_), channel_id=1, source_target_pairs={{0,24},{1,7},{2,26},{3,5},{4,28},{5,3},{6,30},{7,1},{8,16},{9,15},... | collective-permute-start | bytes 61448 | tf_op jit(solution)/shard_map/ppermute | solution.py:340
  6.8 2.6 %collective-permute-start.7 = (f32[40,128]{1,0:T(8,128)S(1)}, f32[40,128]{1,0:T(8,128)S(1)}, u32[]{:S(2)}, u32[]{:S(2)}) collective-permute-start(f32[40,128]{1,0:T(8,128)S(1)} %get-tuple-element.36.refs_1_), channel_id=1, source_target_pairs={{0,4},{1,17},{2,6},{3,19},{4,0},{5,21},{6,2},{7,23},{8,12},{9,25},... | collective-permute-start | bytes 61448 | tf_op jit(solution)/shard_map/ppermute | solution.py:340
  9.4 1.6 %collective-permute-start.4 = (f32[40,128]{1,0:T(8,128)S(1)}, f32[40,128]{1,0:T(8,128)S(1)}, u32[]{:S(2)}, u32[]{:S(2)}) collective-permute-start(f32[40,128]{1,0:T(8,128)S(1)} %get-tuple-element.36.refs_1_), channel_id=1, source_target_pairs={{0,2},{1,9},{2,0},{3,11},{4,6},{5,13},{6,4},{7,15},{8,10},{9,1},{1... | collective-permute-start | bytes 61448 | tf_op jit(solution)/shard_map/ppermute | solution.py:340
  11.0 0.5 %collective-permute-done.7.refs_4_ = f32[40,128]{1,0:T(8,128)S(1)} collective-permute-done((f32[40,128]{1,0:T(8,128)S(1)}, f32[40,128]{1,0:T(8,128)S(1)}, u32[]{:S(2)}, u32[]{:S(2)}) %collective-permute-start.7) | collective-permute-done | bytes 20512 | tf_op jit(solution)/shard_map/ppermute | solution.py:340
  11.5 1.7 %collective-permute-done.4.refs_2_ = f32[40,128]{1,0:T(8,128)S(1)} collective-permute-done((f32[40,128]{1,0:T(8,128)S(1)}, f32[40,128]{1,0:T(8,128)S(1)}, u32[]{:S(2)}, u32[]{:S(2)}) %collective-permute-start.4) | collective-permute-done | bytes 20512 | tf_op jit(solution)/shard_map/ppermute | solution.py:340
  13.2 1.1 %collective-permute-done.8.refs_6_ = f32[40,128]{1,0:T(8,128)S(1)} collective-permute-done((f32[40,128]{1,0:T(8,128)S(1)}, f32[40,128]{1,0:T(8,128)S(1)}, u32[]{:S(2)}, u32[]{:S(2)}) %collective-permute-start.8) | collective-permute-done | bytes 20512 | tf_op jit(solution)/shard_map/ppermute | solution.py:331
  14.4 0.9 %shard_map.68 = (f32[264,128]{1,0:T(8,128)S(1)}, f32[256,128]{1,0:T(8,128)S(1)}, f32[256,128]{1,0:T(8,128)S(1)}, f32[256,256]{1,0:T(8,128)S(1)}, f32[8,128]{1,0:T(8,128)S(1)}) custom-call(f32[256,256]{1,0:T(8,128)S(1)} %shard_map.67.refs_0_, f32[40,128]{1,0:T(8,128)S(1)} %get-tuple-element.36.refs_1_, f32[40,128]{1,0:T(8,128)S(1)} %collective-permute-done.4.refs_2_, ...), custom_call_target="tpu_custom_call" | custom-call | tf_op jit(solution)/shard_map/pallas_call | solution.py:321
  15.3 1.1 %collective-permute-start.12 = (f32[264,128]{1,0:T(8,128)S(1)}, f32[264,128]{1,0:T(8,128)S(1)}, u32[]{:S(2)}, u32[]{:S(2)}) collective-permute-start(f32[264,128]{1,0:T(8,128)S(1)} %get-tuple-element.16.refs_0_), channel_id=1, source_target_pairs={{0,4},{1,17},{2,6},{3,19},{4,0},{5,21},{6,2},{7,23},{8,12},{9,25},... | collective-permute-start | bytes 405512 | tf_op jit(solution)/shard_map/ppermute | solution.py:340
  16.4 1.7 %collective-permute-start.11 = (f32[264,128]{1,0:T(8,128)S(1)}, f32[264,128]{1,0:T(8,128)S(1)}, u32[]{:S(2)}, u32[]{:S(2)}) collective-permute-start(f32[264,128]{1,0:T(8,128)S(1)} %get-tuple-element.16.refs_0_), channel_id=1, source_target_pairs={{0,2},{1,9},{2,0},{3,11},{4,6},{5,13},{6,4},{7,15},{8,10},{9,1},{1... | collective-permute-start | bytes 405512 | tf_op jit(solution)/shard_map/ppermute | solution.py:340
  18.1 1.6 %collective-permute-start.10 = (f32[264,128]{1,0:T(8,128)S(1)}, f32[264,128]{1,0:T(8,128)S(1)}, u32[]{:S(2)}, u32[]{:S(2)}) collective-permute-start(f32[264,128]{1,0:T(8,128)S(1)} %get-tuple-element.16.refs_0_), channel_id=1, source_target_pairs={{0,6},{1,25},{2,4},{3,27},{4,2},{5,29},{6,0},{7,31},{8,14},{9,17},... | collective-permute-start | bytes 405512 | tf_op jit(solution)/shard_map/ppermute | solution.py:340
  19.7 3.0 %collective-permute-done.12.refs_3_ = f32[264,128]{1,0:T(8,128)S(1)} collective-permute-done((f32[264,128]{1,0:T(8,128)S(1)}, f32[264,128]{1,0:T(8,128)S(1)}, u32[]{:S(2)}, u32[]{:S(2)}) %collective-permute-start.12) | collective-permute-done | bytes 135200 | tf_op jit(solution)/shard_map/ppermute | solution.py:340
  22.7 2.6 %collective-permute-done.10.refs_1_ = f32[264,128]{1,0:T(8,128)S(1)} collective-permute-done((f32[264,128]{1,0:T(8,128)S(1)}, f32[264,128]{1,0:T(8,128)S(1)}, u32[]{:S(2)}, u32[]{:S(2)}) %collective-permute-start.10) | collective-permute-done | bytes 135200 | tf_op jit(solution)/shard_map/ppermute | solution.py:340
  25.3 0.2 shard_map.69
  25.6 1.3 %collective-permute-done.13.other_ref.peer_ref = f32[168,128]{1,0:T(8,128)S(1)} collective-permute-done((f32[168,128]{1,0:T(8,128)S(1)}, f32[168,128]{1,0:T(8,128)S(1)}, u32[]{:S(2)}, u32[]{:S(2)}) %collective-permute-start.13) | collective-permute-done | bytes 86048 | tf_op jit(solution)/shard_map/ppermute | solution.py:331
  26.9 0.6 %shard_map.70.refs_0_ = f32[136,128]{1,0:T(8,128)S(1)} custom-call(f32[168,128]{1,0:T(8,128)S(1)} %get-tuple-element.19.mine_ref.refs_4_.send_ref, f32[168,128]{1,0:T(8,128)S(1)} %collective-permute-done.13.other_ref.peer_ref, f32[256,128]{1,0:T(8,128)S(1)} %get-tuple-element.17.refs_4_.left_ref, f32[256,128]{1,0:T(8,128)S(1)} %get-tuple-element.20.right_ref, ...), custom_call_target="tpu_custom_call" | custom-call | tf_op jit(solution)/shard_map/pallas_call | solution.py:321
  27.5 1.9 %collective-permute-start.16 = (f32[136,128]{1,0:T(8,128)S(1)}, f32[136,128]{1,0:T(8,128)S(1)}, u32[]{:S(2)}, u32[]{:S(2)}) collective-permute-start(f32[136,128]{1,0:T(8,128)S(1)} %shard_map.70.refs_0_), channel_id=1, source_target_pairs={{0,6},{1,25},{2,4},{3,27},{4,2},{5,29},{6,0},{7,31},{8,14},{9,17},... | collective-permute-start | bytes 208904 | tf_op jit(solution)/shard_map/ppermute | solution.py:340
  29.3 0.5 %collective-permute-start.15 = (f32[136,128]{1,0:T(8,128)S(1)}, f32[136,128]{1,0:T(8,128)S(1)}, u32[]{:S(2)}, u32[]{:S(2)}) collective-permute-start(f32[136,128]{1,0:T(8,128)S(1)} %shard_map.70.refs_0_), channel_id=1, source_target_pairs={{0,4},{1,17},{2,6},{3,19},{4,0},{5,21},{6,2},{7,23},{8,12},{9,25},... | collective-permute-start | bytes 208904 | tf_op jit(solution)/shard_map/ppermute | solution.py:340
  29.9 2.1 %collective-permute-start.14 = (f32[136,128]{1,0:T(8,128)S(1)}, f32[136,128]{1,0:T(8,128)S(1)}, u32[]{:S(2)}, u32[]{:S(2)}) collective-permute-start(f32[136,128]{1,0:T(8,128)S(1)} %shard_map.70.refs_0_), channel_id=1, source_target_pairs={{0,2},{1,9},{2,0},{3,11},{4,6},{5,13},{6,4},{7,15},{8,10},{9,1},{1... | collective-permute-start | bytes 208904 | tf_op jit(solution)/shard_map/ppermute | solution.py:340
  31.9 1.7 %collective-permute-done.16.refs_3_ = f32[136,128]{1,0:T(8,128)S(1)} collective-permute-done((f32[136,128]{1,0:T(8,128)S(1)}, f32[136,128]{1,0:T(8,128)S(1)}, u32[]{:S(2)}, u32[]{:S(2)}) %collective-permute-start.16) | collective-permute-done | bytes 69664 | tf_op jit(solution)/shard_map/ppermute | solution.py:340
  33.7 1.5 %collective-permute-done.15.refs_2_ = f32[136,128]{1,0:T(8,128)S(1)} collective-permute-done((f32[136,128]{1,0:T(8,128)S(1)}, f32[136,128]{1,0:T(8,128)S(1)}, u32[]{:S(2)}, u32[]{:S(2)}) %collective-permute-start.15) | collective-permute-done | bytes 69664 | tf_op jit(solution)/shard_map/ppermute | solution.py:340
  35.3 1.2 %collective-permute-done.17.other_ref.peer_second_ref = f32[136,128]{1,0:T(8,128)S(1)} collective-permute-done((f32[136,128]{1,0:T(8,128)S(1)}, f32[136,128]{1,0:T(8,128)S(1)}, u32[]{:S(2)}, u32[]{:S(2)}) %collective-permute-start.17) | collective-permute-done | bytes 69664 | tf_op jit(solution)/shard_map/ppermute | solution.py:331
  36.5 0.4 shard_map.72
  37.0 9.1 %all_to_all.5.dots_ref = f32[32,1,128]{2,1,0:T(1,128)S(1)} all-to-all(f32[32,1,128]{2,1,0:T(1,128)S(1)} %shard_map.72), channel_id=1, replica_groups=mesh['stu'=4,'que'=8] {'stu','que'}, dimensions={0} | all-to-all | bytes 32768 | tf_op jit(solution)/shard_map/all_to_all | solution.py:422
  46.1 0.9 %shard_map.73 = (f32[32,64]{1,0:T(8,128)}, f32[32,64]{1,0:T(8,128)}, f32[1,32]{1,0:T(1,128)}) custom-call(f32[32,1,128]{2,1,0:T(1,128)S(1)} %all_to_all.5.dots_ref, f32[168,128]{1,0:T(8,128)S(1)} %get-tuple-element.19.mine_ref.refs_4_.send_ref, f32[168,128]{1,0:T(8,128)S(1)} %collective-permute-done.13.other_ref.peer_ref, ...), custom_call_target="tpu_custom_call" | custom-call | tf_op jit(solution)/shard_map/pallas_call | solution.py:321
  (26 shorter events, 0.4 us)
Async XLA Ops:
  0.6 1.1 %copy-start.1 = (f32[32,64]{1,0:T(8,128)S(1)}, f32[32,64]{1,0:T(8,128)}, u32[]{:S(2)}) copy-start(f32[32,64]{1,0:T(8,128)} %param.5) | copy-start | bytes 24580
  0.6 2.0 %collective-permute-start.3 = (f32[32]{0:T(128)}, f32[32]{0:T(128)S(1)}, u32[]{:S(2)}, u32[]{:S(2)}) collective-permute-start(f32[32]{0:T(128)} %param.7), channel_id=1, source_target_pairs={{0,1},{1,0},{2,3},{3,2},{4,5},{5,4},{6,7},{7,6},{8,9},{9,8},{10,11... | collective-permute-start | bytes 392 | tf_op jit(solution)/shard_map/ppermute | solution.py:331
  1.2 1.6 %collective-permute-start.1 = (f32[32,64]{1,0:T(8,128)}, f32[32,64]{1,0:T(8,128)S(1)}, u32[]{:S(2)}, u32[]{:S(2)}) collective-permute-start(f32[32,64]{1,0:T(8,128)} %param.5), channel_id=1, source_target_pairs={{0,1},{1,0},{2,3},{3,2},{4,5},{5,4},{6,7},{7,6},{8,9},{9,8},{10,11... | collective-permute-start | bytes 24584 | tf_op jit(solution)/shard_map/ppermute | solution.py:331
  1.2 1.5 %collective-permute-start.2 = (f32[32,64]{1,0:T(8,128)}, f32[32,64]{1,0:T(8,128)S(1)}, u32[]{:S(2)}, u32[]{:S(2)}) collective-permute-start(f32[32,64]{1,0:T(8,128)} %param.6), channel_id=1, source_target_pairs={{0,1},{1,0},{2,3},{3,2},{4,5},{5,4},{6,7},{7,6},{8,9},{9,8},{10,11... | collective-permute-start | bytes 24584 | tf_op jit(solution)/shard_map/ppermute | solution.py:331
  1.7 11.5 %collective-permute-start = (s32[256,128]{1,0:T(8,128)}, s32[256,128]{1,0:T(8,128)S(1)}, u32[]{:S(2)}, u32[]{:S(2)}) collective-permute-start(s32[256,128]{1,0:T(8,128)} %own_ref.1), channel_id=1, source_target_pairs={{0,1},{1,0},{2,3},{3,2},{4,5},{5,4},{6,7},{7,6},{8,9},{9,8},{10,11... | collective-permute-start | bytes 393224 | tf_op jit(solution)/shard_map/ppermute | solution.py:331
  1.7 0.9 %copy-start.2 = (f32[32]{0:T(128)S(1)}, f32[32]{0:T(128)}, u32[]{:S(2)}) copy-start(f32[32]{0:T(128)} %param.7) | copy-start | bytes 388
  1.8 11.4 %copy-start = (s32[256,128]{1,0:T(8,128)S(1)}, s32[256,128]{1,0:T(8,128)}, u32[]{:S(2)}) copy-start(s32[256,128]{1,0:T(8,128)} %own_ref.1) | copy-start | bytes 393220
  2.9 8.1 %collective-permute-start.5 = (f32[40,128]{1,0:T(8,128)S(1)}, f32[40,128]{1,0:T(8,128)S(1)}, u32[]{:S(2)}, u32[]{:S(2)}) collective-permute-start(f32[40,128]{1,0:T(8,128)S(1)} %get-tuple-element.35.refs_5_), channel_id=1, source_target_pairs={{0,24},{1,7},{2,26},{3,5},{4,28},{5,3},{6,30},{7,1},{8,16},{9,15},... | collective-permute-start | bytes 61448 | tf_op jit(solution)/shard_map/ppermute | solution.py:340
  6.8 4.7 %collective-permute-start.7 = (f32[40,128]{1,0:T(8,128)S(1)}, f32[40,128]{1,0:T(8,128)S(1)}, u32[]{:S(2)}, u32[]{:S(2)}) collective-permute-start(f32[40,128]{1,0:T(8,128)S(1)} %get-tuple-element.36.refs_1_), channel_id=1, source_target_pairs={{0,4},{1,17},{2,6},{3,19},{4,0},{5,21},{6,2},{7,23},{8,12},{9,25},... | collective-permute-start | bytes 61448 | tf_op jit(solution)/shard_map/ppermute | solution.py:340
  9.4 3.8 %collective-permute-start.4 = (f32[40,128]{1,0:T(8,128)S(1)}, f32[40,128]{1,0:T(8,128)S(1)}, u32[]{:S(2)}, u32[]{:S(2)}) collective-permute-start(f32[40,128]{1,0:T(8,128)S(1)} %get-tuple-element.36.refs_1_), channel_id=1, source_target_pairs={{0,2},{1,9},{2,0},{3,11},{4,6},{5,13},{6,4},{7,15},{8,10},{9,1},{1... | collective-permute-start | bytes 61448 | tf_op jit(solution)/shard_map/ppermute | solution.py:340
  11.0 2.3 %collective-permute-start.6 = (f32[40,128]{1,0:T(8,128)S(1)}, f32[40,128]{1,0:T(8,128)S(1)}, u32[]{:S(2)}, u32[]{:S(2)}) collective-permute-start(f32[40,128]{1,0:T(8,128)S(1)} %collective-permute-done.5.refs_7_), channel_id=1, source_target_pairs={{0,1},{1,0},{2,3},{3,2},{4,5},{5,4},{6,7},{7,6},{8,9},{9,8},{10,11... | collective-permute-start | bytes 61448 | tf_op jit(solution)/shard_map/ppermute | solution.py:331
  11.5 1.8 %collective-permute-start.9 = (f32[40,128]{1,0:T(8,128)S(1)}, f32[40,128]{1,0:T(8,128)S(1)}, u32[]{:S(2)}, u32[]{:S(2)}) collective-permute-start(f32[40,128]{1,0:T(8,128)S(1)} %collective-permute-done.7.refs_4_), channel_id=1, source_target_pairs={{0,1},{1,0},{2,3},{3,2},{4,5},{5,4},{6,7},{7,6},{8,9},{9,8},{10,11... | collective-permute-start | bytes 61448 | tf_op jit(solution)/shard_map/ppermute | solution.py:331
  13.2 1.2 %collective-permute-start.8 = (f32[40,128]{1,0:T(8,128)S(1)}, f32[40,128]{1,0:T(8,128)S(1)}, u32[]{:S(2)}, u32[]{:S(2)}) collective-permute-start(f32[40,128]{1,0:T(8,128)S(1)} %collective-permute-done.4.refs_2_), channel_id=1, source_target_pairs={{0,1},{1,0},{2,3},{3,2},{4,5},{5,4},{6,7},{7,6},{8,9},{9,8},{10,11... | collective-permute-start | bytes 61448 | tf_op jit(solution)/shard_map/ppermute | solution.py:331
  15.3 7.4 %collective-permute-start.12 = (f32[264,128]{1,0:T(8,128)S(1)}, f32[264,128]{1,0:T(8,128)S(1)}, u32[]{:S(2)}, u32[]{:S(2)}) collective-permute-start(f32[264,128]{1,0:T(8,128)S(1)} %get-tuple-element.16.refs_0_), channel_id=1, source_target_pairs={{0,4},{1,17},{2,6},{3,19},{4,0},{5,21},{6,2},{7,23},{8,12},{9,25},... | collective-permute-start | bytes 405512 | tf_op jit(solution)/shard_map/ppermute | solution.py:340
  16.4 6.3 %collective-permute-start.11 = (f32[264,128]{1,0:T(8,128)S(1)}, f32[264,128]{1,0:T(8,128)S(1)}, u32[]{:S(2)}, u32[]{:S(2)}) collective-permute-start(f32[264,128]{1,0:T(8,128)S(1)} %get-tuple-element.16.refs_0_), channel_id=1, source_target_pairs={{0,2},{1,9},{2,0},{3,11},{4,6},{5,13},{6,4},{7,15},{8,10},{9,1},{1... | collective-permute-start | bytes 405512 | tf_op jit(solution)/shard_map/ppermute | solution.py:340
  18.1 7.2 %collective-permute-start.10 = (f32[264,128]{1,0:T(8,128)S(1)}, f32[264,128]{1,0:T(8,128)S(1)}, u32[]{:S(2)}, u32[]{:S(2)}) collective-permute-start(f32[264,128]{1,0:T(8,128)S(1)} %get-tuple-element.16.refs_0_), channel_id=1, source_target_pairs={{0,6},{1,25},{2,4},{3,27},{4,2},{5,29},{6,0},{7,31},{8,14},{9,17},... | collective-permute-start | bytes 405512 | tf_op jit(solution)/shard_map/ppermute | solution.py:340
  25.5 1.3 %collective-permute-start.13 = (f32[168,128]{1,0:T(8,128)S(1)}, f32[168,128]{1,0:T(8,128)S(1)}, u32[]{:S(2)}, u32[]{:S(2)}) collective-permute-start(f32[168,128]{1,0:T(8,128)S(1)} %get-tuple-element.19.mine_ref.refs_4_.send_ref), channel_id=1, source_target_pairs={{0,1},{1,0},{2,3},{3,2},{4,5},{5,4},{6,7},{7,6},{8,9},{9,8},{10,11... | collective-permute-start | bytes 258056 | tf_op jit(solution)/shard_map/ppermute | solution.py:331
  27.5 6.2 %collective-permute-start.16 = (f32[136,128]{1,0:T(8,128)S(1)}, f32[136,128]{1,0:T(8,128)S(1)}, u32[]{:S(2)}, u32[]{:S(2)}) collective-permute-start(f32[136,128]{1,0:T(8,128)S(1)} %shard_map.70.refs_0_), channel_id=1, source_target_pairs={{0,6},{1,25},{2,4},{3,27},{4,2},{5,29},{6,0},{7,31},{8,14},{9,17},... | collective-permute-start | bytes 208904 | tf_op jit(solution)/shard_map/ppermute | solution.py:340
  29.3 5.8 %collective-permute-start.15 = (f32[136,128]{1,0:T(8,128)S(1)}, f32[136,128]{1,0:T(8,128)S(1)}, u32[]{:S(2)}, u32[]{:S(2)}) collective-permute-start(f32[136,128]{1,0:T(8,128)S(1)} %shard_map.70.refs_0_), channel_id=1, source_target_pairs={{0,4},{1,17},{2,6},{3,19},{4,0},{5,21},{6,2},{7,23},{8,12},{9,25},... | collective-permute-start | bytes 208904 | tf_op jit(solution)/shard_map/ppermute | solution.py:340
  29.9 5.3 %collective-permute-start.14 = (f32[136,128]{1,0:T(8,128)S(1)}, f32[136,128]{1,0:T(8,128)S(1)}, u32[]{:S(2)}, u32[]{:S(2)}) collective-permute-start(f32[136,128]{1,0:T(8,128)S(1)} %shard_map.70.refs_0_), channel_id=1, source_target_pairs={{0,2},{1,9},{2,0},{3,11},{4,6},{5,13},{6,4},{7,15},{8,10},{9,1},{1... | collective-permute-start | bytes 208904 | tf_op jit(solution)/shard_map/ppermute | solution.py:340
  35.2 1.3 %collective-permute-start.17 = (f32[136,128]{1,0:T(8,128)S(1)}, f32[136,128]{1,0:T(8,128)S(1)}, u32[]{:S(2)}, u32[]{:S(2)}) collective-permute-start(f32[136,128]{1,0:T(8,128)S(1)} %get-tuple-element.23.mine_ref.second_ref), channel_id=1, source_target_pairs={{0,1},{1,0},{2,3},{3,2},{4,5},{5,4},{6,7},{7,6},{8,9},{9,8},{10,11... | collective-permute-start | bytes 208904 | tf_op jit(solution)/shard_map/ppermute | solution.py:331

commit v13 on v10

--- a/solution.py
+++ b/solution.py
@@ -9,7 +9,7 @@
 
 AXES = ("stu", "que")
 LANES = 128
-GATHER_ORDER = (1, 3, 2)
+GATHER_ORDER = (3, 2, 1)
 FIRST_ORDER = (3, 1, 2)
 SECOND_ORDER = (1, 2, 3)
 BIAS = 8

time: 47.2 us -> 47.8 us (1.013)
  starting transfers between devices: 18.3 us -> 18.8 us
    ppermute x9, starting transfers between devices: 1.26 us -> 1.76 us  [swap_cores(): return lax.ppermute(value, AXES, [(i, i ^ 1) for i in range(n_stu * n_que)])]
  transfers between devices with their start and end apart: 18 -> 18, of which waited for: 9 -> 8; matrix products, arithmetic and copies ran while one was open for 2% -> 2% of each run, Pallas kernels for 0% -> 0%
where the time goes in v13:
time: 47.8 us; the launch traced here: 47.5 us
  starting transfers between devices  18.8 us (39%)
  waiting for transfers between devices  14.3 us (30%)
  blocking collectives  9.52 us (20%)
  Pallas kernels  3.11 us (7%)
  other arithmetic  0.85 us (2%)
  between operations  0.75 us (2%)
    ppermute x9, starting transfers between devices, send_over(): return lax.ppermute(value, AXES, pairs)  17 us
    ppermute x9, waiting for transfers between devices, send_over(): return lax.ppermute(value, AXES, pairs)  10.6 us
    all_to_all x1, blocking collectives, shards(): dots = lax.all_to_all(dots, AXES, 0, 0, tiled=True)  9.52 us
    ppermute x9, waiting for transfers between devices, swap_cores(): return lax.ppermute(value, AXES, [(i, i ^ 1) for i in range(n_stu * n_que)])  3.65 us
    pallas_call x7, Pallas kernels, call(): pl.pallas_call(kernel, out_shape=out, in_specs=[pl.BlockSpec(memory_space...  3.11 us
    ppermute x9, starting transfers between devices, swap_cores(): return lax.ppermute(value, AXES, [(i, i ^ 1) for i in range(n_stu * n_que)])  1.76 us
  transfers between devices with their start and end apart: 18, of which 8 were waited for; matrix products, arithmetic and copies ran while one was open for 2% of the time, Pallas kernels for 0%

profile of v13, /device:TPU:0, one launch (start us, length us, event | category | flops | bytes accessed | tf_op | source)
XLA Modules:
  0.0 47.5 jit_solution(6936177495259107211)
XLA Ops:
  0.6 0.5 %collective-permute-start.2 = (f32[32]{0:T(128)}, f32[32]{0:T(128)S(1)}, u32[]{:S(2)}, u32[]{:S(2)}) collective-permute-start(f32[32]{0:T(128)} %param.7), channel_id=1, source_target_pairs={{0,1},{1,0},{2,3},{3,2},{4,5},{5,4},{6,7},{7,6},{8,9},{9,8},{10,11... | collective-permute-start | bytes 392 | tf_op jit(solution)/shard_map/ppermute | solution.py:330
  1.2 0.1 collective-permute-start
  1.2 0.4 collective-permute-start.1
  1.7 0.1 collective-permute-start.9
  1.8 0.8 %broadcast_select_fusion = (f32[32,64]{1,0:T(8,128)S(1)}, f32[32,64]{1,0:T(8,128)S(1)}) fusion(f32[32,64]{1,0:T(8,128)} %param.6, f32[32,64]{1,0:T(8,128)S(1)} %copy-done.1, pred[]{:T(512)S(6)} %eq.2), kind=kLoop, calls=%fused_computation.2 | loop fusion | flops 4096 | bytes 32769 | tf_op jit(solution)/shard_map/jit(_where)/select_n | solution.py:369
  2.6 0.1 reshape.13
  2.7 0.1 reshape.12
  2.8 0.1 maximum_maximum_fusion.1
  2.9 3.9 %collective-permute-start.3 = (f32[40,128]{1,0:T(8,128)S(1)}, f32[40,128]{1,0:T(8,128)S(1)}, u32[]{:S(2)}, u32[]{:S(2)}) collective-permute-start(f32[40,128]{1,0:T(8,128)S(1)} %get-tuple-element.35.refs_4_), channel_id=1, source_target_pairs={{0,24},{1,7},{2,26},{3,5},{4,28},{5,3},{6,30},{7,1},{8,16},{9,15},... | collective-permute-start | bytes 61448 | tf_op jit(solution)/shard_map/ppermute | solution.py:339
  6.8 1.6 %collective-permute-start.6 = (f32[40,128]{1,0:T(8,128)S(1)}, f32[40,128]{1,0:T(8,128)S(1)}, u32[]{:S(2)}, u32[]{:S(2)}) collective-permute-start(f32[40,128]{1,0:T(8,128)S(1)} %get-tuple-element.36.refs_0_), channel_id=1, source_target_pairs={{0,2},{1,9},{2,0},{3,11},{4,6},{5,13},{6,4},{7,15},{8,10},{9,1},{1... | collective-permute-start | bytes 61448 | tf_op jit(solution)/shard_map/ppermute | solution.py:339
  8.4 2.6 %collective-permute-start.5 = (f32[40,128]{1,0:T(8,128)S(1)}, f32[40,128]{1,0:T(8,128)S(1)}, u32[]{:S(2)}, u32[]{:S(2)}) collective-permute-start(f32[40,128]{1,0:T(8,128)S(1)} %get-tuple-element.36.refs_0_), channel_id=1, source_target_pairs={{0,4},{1,17},{2,6},{3,19},{4,0},{5,21},{6,2},{7,23},{8,12},{9,25},... | collective-permute-start | bytes 61448 | tf_op jit(solution)/shard_map/ppermute | solution.py:339
  11.0 0.5 %collective-permute-start.8 = (f32[40,128]{1,0:T(8,128)S(1)}, f32[40,128]{1,0:T(8,128)S(1)}, u32[]{:S(2)}, u32[]{:S(2)}) collective-permute-start(f32[40,128]{1,0:T(8,128)S(1)} %collective-permute-done.6.refs_3_), channel_id=1, source_target_pairs={{0,1},{1,0},{2,3},{3,2},{4,5},{5,4},{6,7},{7,6},{8,9},{9,8},{10,11... | collective-permute-start | bytes 61448 | tf_op jit(solution)/shard_map/ppermute | solution.py:330
  11.5 1.7 %collective-permute-done.5.refs_2_ = f32[40,128]{1,0:T(8,128)S(1)} collective-permute-done((f32[40,128]{1,0:T(8,128)S(1)}, f32[40,128]{1,0:T(8,128)S(1)}, u32[]{:S(2)}, u32[]{:S(2)}) %collective-permute-start.5) | collective-permute-done | bytes 20512 | tf_op jit(solution)/shard_map/ppermute | solution.py:339
  13.2 1.1 %collective-permute-done.7.refs_6_ = f32[40,128]{1,0:T(8,128)S(1)} collective-permute-done((f32[40,128]{1,0:T(8,128)S(1)}, f32[40,128]{1,0:T(8,128)S(1)}, u32[]{:S(2)}, u32[]{:S(2)}) %collective-permute-start.7) | collective-permute-done | bytes 20512 | tf_op jit(solution)/shard_map/ppermute | solution.py:330
  14.4 0.9 %shard_map.68 = (f32[264,128]{1,0:T(8,128)S(1)}, f32[256,128]{1,0:T(8,128)S(1)}, f32[256,128]{1,0:T(8,128)S(1)}, f32[256,256]{1,0:T(8,128)S(1)}, f32[8,128]{1,0:T(8,128)S(1)}) custom-call(f32[40,128]{1,0:T(8,128)S(1)} %get-tuple-element.36.refs_0_, f32[40,128]{1,0:T(8,128)S(1)} %collective-permute-done.4.refs_1_, ...), custom_call_target="tpu_custom_call" | custom-call | tf_op jit(solution)/shard_map/pallas_call | solution.py:320
  15.3 2.5 %collective-permute-start.12 = (f32[264,128]{1,0:T(8,128)S(1)}, f32[264,128]{1,0:T(8,128)S(1)}, u32[]{:S(2)}, u32[]{:S(2)}) collective-permute-start(f32[264,128]{1,0:T(8,128)S(1)} %get-tuple-element.16.refs_0_), channel_id=1, source_target_pairs={{0,4},{1,17},{2,6},{3,19},{4,0},{5,21},{6,2},{7,23},{8,12},{9,25},... | collective-permute-start | bytes 405512 | tf_op jit(solution)/shard_map/ppermute | solution.py:339
  17.8 0.4 collective-permute-start.11
  18.3 1.5 %collective-permute-start.10 = (f32[264,128]{1,0:T(8,128)S(1)}, f32[264,128]{1,0:T(8,128)S(1)}, u32[]{:S(2)}, u32[]{:S(2)}) collective-permute-start(f32[264,128]{1,0:T(8,128)S(1)} %get-tuple-element.16.refs_0_), channel_id=1, source_target_pairs={{0,6},{1,25},{2,4},{3,27},{4,2},{5,29},{6,0},{7,31},{8,14},{9,17},... | collective-permute-start | bytes 405512 | tf_op jit(solution)/shard_map/ppermute | solution.py:339
  19.7 2.9 %collective-permute-done.12.refs_3_ = f32[264,128]{1,0:T(8,128)S(1)} collective-permute-done((f32[264,128]{1,0:T(8,128)S(1)}, f32[264,128]{1,0:T(8,128)S(1)}, u32[]{:S(2)}, u32[]{:S(2)}) %collective-permute-start.12) | collective-permute-done | bytes 135200 | tf_op jit(solution)/shard_map/ppermute | solution.py:339
  22.6 2.8 %collective-permute-done.11.refs_2_ = f32[264,128]{1,0:T(8,128)S(1)} collective-permute-done((f32[264,128]{1,0:T(8,128)S(1)}, f32[264,128]{1,0:T(8,128)S(1)}, u32[]{:S(2)}, u32[]{:S(2)}) %collective-permute-start.11) | collective-permute-done | bytes 135200 | tf_op jit(solution)/shard_map/ppermute | solution.py:339
  25.4 0.2 shard_map.69
  25.7 1.3 %collective-permute-done.13.other_ref.peer_ref = f32[168,128]{1,0:T(8,128)S(1)} collective-permute-done((f32[168,128]{1,0:T(8,128)S(1)}, f32[168,128]{1,0:T(8,128)S(1)}, u32[]{:S(2)}, u32[]{:S(2)}) %collective-permute-start.13) | collective-permute-done | bytes 86048 | tf_op jit(solution)/shard_map/ppermute | solution.py:330
  26.9 0.6 %shard_map.70.refs_0_ = f32[136,128]{1,0:T(8,128)S(1)} custom-call(f32[168,128]{1,0:T(8,128)S(1)} %get-tuple-element.19.mine_ref.refs_4_.send_ref, f32[168,128]{1,0:T(8,128)S(1)} %collective-permute-done.13.other_ref.peer_ref, f32[256,128]{1,0:T(8,128)S(1)} %get-tuple-element.17.refs_4_.left_ref, f32[256,128]{1,0:T(8,128)S(1)} %get-tuple-element.20.right_ref, ...), custom_call_target="tpu_custom_call" | custom-call | tf_op jit(solution)/shard_map/pallas_call | solution.py:320
  27.5 2.4 %collective-permute-start.16 = (f32[136,128]{1,0:T(8,128)S(1)}, f32[136,128]{1,0:T(8,128)S(1)}, u32[]{:S(2)}, u32[]{:S(2)}) collective-permute-start(f32[136,128]{1,0:T(8,128)S(1)} %shard_map.70.refs_0_), channel_id=1, source_target_pairs={{0,6},{1,25},{2,4},{3,27},{4,2},{5,29},{6,0},{7,31},{8,14},{9,17},... | collective-permute-start | bytes 208904 | tf_op jit(solution)/shard_map/ppermute | solution.py:339
  29.9 0.1 collective-permute-start.15
  30.0 2.0 %collective-permute-start.14 = (f32[136,128]{1,0:T(8,128)S(1)}, f32[136,128]{1,0:T(8,128)S(1)}, u32[]{:S(2)}, u32[]{:S(2)}) collective-permute-start(f32[136,128]{1,0:T(8,128)S(1)} %shard_map.70.refs_0_), channel_id=1, source_target_pairs={{0,2},{1,9},{2,0},{3,11},{4,6},{5,13},{6,4},{7,15},{8,10},{9,1},{1... | collective-permute-start | bytes 208904 | tf_op jit(solution)/shard_map/ppermute | solution.py:339
  32.0 1.7 %collective-permute-done.16.refs_3_ = f32[136,128]{1,0:T(8,128)S(1)} collective-permute-done((f32[136,128]{1,0:T(8,128)S(1)}, f32[136,128]{1,0:T(8,128)S(1)}, u32[]{:S(2)}, u32[]{:S(2)}) %collective-permute-start.16) | collective-permute-done | bytes 69664 | tf_op jit(solution)/shard_map/ppermute | solution.py:339
  33.7 1.6 %collective-permute-done.15.refs_2_ = f32[136,128]{1,0:T(8,128)S(1)} collective-permute-done((f32[136,128]{1,0:T(8,128)S(1)}, f32[136,128]{1,0:T(8,128)S(1)}, u32[]{:S(2)}, u32[]{:S(2)}) %collective-permute-start.15) | collective-permute-done | bytes 69664 | tf_op jit(solution)/shard_map/ppermute | solution.py:339
  35.4 1.2 %collective-permute-done.17.other_ref.peer_second_ref = f32[136,128]{1,0:T(8,128)S(1)} collective-permute-done((f32[136,128]{1,0:T(8,128)S(1)}, f32[136,128]{1,0:T(8,128)S(1)}, u32[]{:S(2)}, u32[]{:S(2)}) %collective-permute-start.17) | collective-permute-done | bytes 69664 | tf_op jit(solution)/shard_map/ppermute | solution.py:330
  36.7 0.4 shard_map.72
  37.1 9.5 %all_to_all.5.dots_ref = f32[32,1,128]{2,1,0:T(1,128)S(1)} all-to-all(f32[32,1,128]{2,1,0:T(1,128)S(1)} %shard_map.72), channel_id=1, replica_groups=mesh['stu'=4,'que'=8] {'stu','que'}, dimensions={0} | all-to-all | bytes 32768 | tf_op jit(solution)/shard_map/all_to_all | solution.py:421
  46.7 0.9 %shard_map.73 = (f32[32,64]{1,0:T(8,128)}, f32[32,64]{1,0:T(8,128)}, f32[1,32]{1,0:T(1,128)}) custom-call(f32[32,1,128]{2,1,0:T(1,128)S(1)} %all_to_all.5.dots_ref, f32[168,128]{1,0:T(8,128)S(1)} %get-tuple-element.19.mine_ref.refs_4_.send_ref, f32[168,128]{1,0:T(8,128)S(1)} %collective-permute-done.13.other_ref.peer_ref, ...), custom_call_target="tpu_custom_call" | custom-call | tf_op jit(solution)/shard_map/pallas_call | solution.py:320
  (26 shorter events, 0.4 us)
Async XLA Ops:
  0.6 1.1 %copy-start.1 = (f32[32,64]{1,0:T(8,128)S(1)}, f32[32,64]{1,0:T(8,128)}, u32[]{:S(2)}) copy-start(f32[32,64]{1,0:T(8,128)} %param.5) | copy-start | bytes 24580
  0.6 2.0 %collective-permute-start.2 = (f32[32]{0:T(128)}, f32[32]{0:T(128)S(1)}, u32[]{:S(2)}, u32[]{:S(2)}) collective-permute-start(f32[32]{0:T(128)} %param.7), channel_id=1, source_target_pairs={{0,1},{1,0},{2,3},{3,2},{4,5},{5,4},{6,7},{7,6},{8,9},{9,8},{10,11... | collective-permute-start | bytes 392 | tf_op jit(solution)/shard_map/ppermute | solution.py:330
  1.2 1.6 %collective-permute-start = (f32[32,64]{1,0:T(8,128)}, f32[32,64]{1,0:T(8,128)S(1)}, u32[]{:S(2)}, u32[]{:S(2)}) collective-permute-start(f32[32,64]{1,0:T(8,128)} %param.5), channel_id=1, source_target_pairs={{0,1},{1,0},{2,3},{3,2},{4,5},{5,4},{6,7},{7,6},{8,9},{9,8},{10,11... | collective-permute-start | bytes 24584 | tf_op jit(solution)/shard_map/ppermute | solution.py:330
  1.2 1.5 %collective-permute-start.1 = (f32[32,64]{1,0:T(8,128)}, f32[32,64]{1,0:T(8,128)S(1)}, u32[]{:S(2)}, u32[]{:S(2)}) collective-permute-start(f32[32,64]{1,0:T(8,128)} %param.6), channel_id=1, source_target_pairs={{0,1},{1,0},{2,3},{3,2},{4,5},{5,4},{6,7},{7,6},{8,9},{9,8},{10,11... | collective-permute-start | bytes 24584 | tf_op jit(solution)/shard_map/ppermute | solution.py:330
  1.7 11.5 %collective-permute-start.9 = (s32[256,128]{1,0:T(8,128)}, s32[256,128]{1,0:T(8,128)S(1)}, u32[]{:S(2)}, u32[]{:S(2)}) collective-permute-start(s32[256,128]{1,0:T(8,128)} %own_ref.1), channel_id=1, source_target_pairs={{0,1},{1,0},{2,3},{3,2},{4,5},{5,4},{6,7},{7,6},{8,9},{9,8},{10,11... | collective-permute-start | bytes 393224 | tf_op jit(solution)/shard_map/ppermute | solution.py:330
  1.7 0.9 %copy-start.2 = (f32[32]{0:T(128)S(1)}, f32[32]{0:T(128)}, u32[]{:S(2)}) copy-start(f32[32]{0:T(128)} %param.7) | copy-start | bytes 388
  1.8 11.4 %copy-start = (s32[256,128]{1,0:T(8,128)S(1)}, s32[256,128]{1,0:T(8,128)}, u32[]{:S(2)}) copy-start(s32[256,128]{1,0:T(8,128)} %own_ref.1) | copy-start | bytes 393220
  2.9 8.1 %collective-permute-start.3 = (f32[40,128]{1,0:T(8,128)S(1)}, f32[40,128]{1,0:T(8,128)S(1)}, u32[]{:S(2)}, u32[]{:S(2)}) collective-permute-start(f32[40,128]{1,0:T(8,128)S(1)} %get-tuple-element.35.refs_4_), channel_id=1, source_target_pairs={{0,24},{1,7},{2,26},{3,5},{4,28},{5,3},{6,30},{7,1},{8,16},{9,15},... | collective-permute-start | bytes 61448 | tf_op jit(solution)/shard_map/ppermute | solution.py:339
  6.8 4.2 %collective-permute-start.6 = (f32[40,128]{1,0:T(8,128)S(1)}, f32[40,128]{1,0:T(8,128)S(1)}, u32[]{:S(2)}, u32[]{:S(2)}) collective-permute-start(f32[40,128]{1,0:T(8,128)S(1)} %get-tuple-element.36.refs_0_), channel_id=1, source_target_pairs={{0,2},{1,9},{2,0},{3,11},{4,6},{5,13},{6,4},{7,15},{8,10},{9,1},{1... | collective-permute-start | bytes 61448 | tf_op jit(solution)/shard_map/ppermute | solution.py:339
  8.4 4.8 %collective-permute-start.5 = (f32[40,128]{1,0:T(8,128)S(1)}, f32[40,128]{1,0:T(8,128)S(1)}, u32[]{:S(2)}, u32[]{:S(2)}) collective-permute-start(f32[40,128]{1,0:T(8,128)S(1)} %get-tuple-element.36.refs_0_), channel_id=1, source_target_pairs={{0,4},{1,17},{2,6},{3,19},{4,0},{5,21},{6,2},{7,23},{8,12},{9,25},... | collective-permute-start | bytes 61448 | tf_op jit(solution)/shard_map/ppermute | solution.py:339
  11.0 2.3 %collective-permute-start.4 = (f32[40,128]{1,0:T(8,128)S(1)}, f32[40,128]{1,0:T(8,128)S(1)}, u32[]{:S(2)}, u32[]{:S(2)}) collective-permute-start(f32[40,128]{1,0:T(8,128)S(1)} %collective-permute-done.3.refs_5_), channel_id=1, source_target_pairs={{0,1},{1,0},{2,3},{3,2},{4,5},{5,4},{6,7},{7,6},{8,9},{9,8},{10,11... | collective-permute-start | bytes 61448 | tf_op jit(solution)/shard_map/ppermute | solution.py:330
  11.0 2.3 %collective-permute-start.8 = (f32[40,128]{1,0:T(8,128)S(1)}, f32[40,128]{1,0:T(8,128)S(1)}, u32[]{:S(2)}, u32[]{:S(2)}) collective-permute-start(f32[40,128]{1,0:T(8,128)S(1)} %collective-permute-done.6.refs_3_), channel_id=1, source_target_pairs={{0,1},{1,0},{2,3},{3,2},{4,5},{5,4},{6,7},{7,6},{8,9},{9,8},{10,11... | collective-permute-start | bytes 61448 | tf_op jit(solution)/shard_map/ppermute | solution.py:330
  13.2 1.2 %collective-permute-start.7 = (f32[40,128]{1,0:T(8,128)S(1)}, f32[40,128]{1,0:T(8,128)S(1)}, u32[]{:S(2)}, u32[]{:S(2)}) collective-permute-start(f32[40,128]{1,0:T(8,128)S(1)} %collective-permute-done.5.refs_2_), channel_id=1, source_target_pairs={{0,1},{1,0},{2,3},{3,2},{4,5},{5,4},{6,7},{7,6},{8,9},{9,8},{10,11... | collective-permute-start | bytes 61448 | tf_op jit(solution)/shard_map/ppermute | solution.py:330
  15.3 7.3 %collective-permute-start.12 = (f32[264,128]{1,0:T(8,128)S(1)}, f32[264,128]{1,0:T(8,128)S(1)}, u32[]{:S(2)}, u32[]{:S(2)}) collective-permute-start(f32[264,128]{1,0:T(8,128)S(1)} %get-tuple-element.16.refs_0_), channel_id=1, source_target_pairs={{0,4},{1,17},{2,6},{3,19},{4,0},{5,21},{6,2},{7,23},{8,12},{9,25},... | collective-permute-start | bytes 405512 | tf_op jit(solution)/shard_map/ppermute | solution.py:339
  17.8 7.6 %collective-permute-start.11 = (f32[264,128]{1,0:T(8,128)S(1)}, f32[264,128]{1,0:T(8,128)S(1)}, u32[]{:S(2)}, u32[]{:S(2)}) collective-permute-start(f32[264,128]{1,0:T(8,128)S(1)} %get-tuple-element.16.refs_0_), channel_id=1, source_target_pairs={{0,2},{1,9},{2,0},{3,11},{4,6},{5,13},{6,4},{7,15},{8,10},{9,1},{1... | collective-permute-start | bytes 405512 | tf_op jit(solution)/shard_map/ppermute | solution.py:339
  18.3 7.1 %collective-permute-start.10 = (f32[264,128]{1,0:T(8,128)S(1)}, f32[264,128]{1,0:T(8,128)S(1)}, u32[]{:S(2)}, u32[]{:S(2)}) collective-permute-start(f32[264,128]{1,0:T(8,128)S(1)} %get-tuple-element.16.refs_0_), channel_id=1, source_target_pairs={{0,6},{1,25},{2,4},{3,27},{4,2},{5,29},{6,0},{7,31},{8,14},{9,17},... | collective-permute-start | bytes 405512 | tf_op jit(solution)/shard_map/ppermute | solution.py:339
  25.6 1.3 %collective-permute-start.13 = (f32[168,128]{1,0:T(8,128)S(1)}, f32[168,128]{1,0:T(8,128)S(1)}, u32[]{:S(2)}, u32[]{:S(2)}) collective-permute-start(f32[168,128]{1,0:T(8,128)S(1)} %get-tuple-element.19.mine_ref.refs_4_.send_ref), channel_id=1, source_target_pairs={{0,1},{1,0},{2,3},{3,2},{4,5},{5,4},{6,7},{7,6},{8,9},{9,8},{10,11... | collective-permute-start | bytes 258056 | tf_op jit(solution)/shard_map/ppermute | solution.py:330
  27.5 6.2 %collective-permute-start.16 = (f32[136,128]{1,0:T(8,128)S(1)}, f32[136,128]{1,0:T(8,128)S(1)}, u32[]{:S(2)}, u32[]{:S(2)}) collective-permute-start(f32[136,128]{1,0:T(8,128)S(1)} %shard_map.70.refs_0_), channel_id=1, source_target_pairs={{0,6},{1,25},{2,4},{3,27},{4,2},{5,29},{6,0},{7,31},{8,14},{9,17},... | collective-permute-start | bytes 208904 | tf_op jit(solution)/shard_map/ppermute | solution.py:339
  29.9 5.4 %collective-permute-start.15 = (f32[136,128]{1,0:T(8,128)S(1)}, f32[136,128]{1,0:T(8,128)S(1)}, u32[]{:S(2)}, u32[]{:S(2)}) collective-permute-start(f32[136,128]{1,0:T(8,128)S(1)} %shard_map.70.refs_0_), channel_id=1, source_target_pairs={{0,4},{1,17},{2,6},{3,19},{4,0},{5,21},{6,2},{7,23},{8,12},{9,25},... | collective-permute-start | bytes 208904 | tf_op jit(solution)/shard_map/ppermute | solution.py:339
  30.0 5.3 %collective-permute-start.14 = (f32[136,128]{1,0:T(8,128)S(1)}, f32[136,128]{1,0:T(8,128)S(1)}, u32[]{:S(2)}, u32[]{:S(2)}) collective-permute-start(f32[136,128]{1,0:T(8,128)S(1)} %shard_map.70.refs_0_), channel_id=1, source_target_pairs={{0,2},{1,9},{2,0},{3,11},{4,6},{5,13},{6,4},{7,15},{8,10},{9,1},{1... | collective-permute-start | bytes 208904 | tf_op jit(solution)/shard_map/ppermute | solution.py:339
  35.4 1.3 %collective-permute-start.17 = (f32[136,128]{1,0:T(8,128)S(1)}, f32[136,128]{1,0:T(8,128)S(1)}, u32[]{:S(2)}, u32[]{:S(2)}) collective-permute-start(f32[136,128]{1,0:T(8,128)S(1)} %get-tuple-element.23.mine_ref.second_ref), channel_id=1, source_target_pairs={{0,1},{1,0},{2,3},{3,2},{4,5},{5,4},{6,7},{7,6},{8,9},{9,8},{10,11... | collective-permute-start | bytes 208904 | tf_op jit(solution)/shard_map/ppermute | solution.py:330
